TPU v7x, 32 devices: a whole 2x2x4 slice. The times are simulated.
32 devices in a mesh: row: 16 (over z, y, core), col: 2 (over x).
Axes of the slice: x: 2, y: 2, z: 4, core: 2. Of those that a mesh axis runs over, the one named last changes fastest.
Arguments:
- velocity: float32 [6, 3, 2048], P(None, None, ('row', 'col')), may hold values from -3 to 3
- points: float32 [3, 2048], P(None, ('row', 'col')), may hold values from -1 to 1
- panel_area: float32 [2048], P(('row', 'col')), may hold values from 0.00390625 to 0.0390625
- self_term: float32 [2048], P(('row', 'col')), may hold values from 0.5 to 4
- near_index: int32 [2048, 32], P('row', 'col'), may hold values from 0 to 1023
- near_weight: float32 [2048, 32], P('row', 'col'), may hold values from -0.5 to 0.5
Outputs:
- density: float32 [6, 3, 2048], P(None, None, ('row', 'col'))
Inputs may be any that keep to these rules, and one draw needn't show every extreme that they name: `near_index`: each entry is a place in the source block of its column of 16 entries; places may repeat, and every listing counts.
All inputs are finite; a program needn't handle non-finite values.
Results may differ from a plain program's by a relative error of at most 0.0003.
Values sent between devices are 32-bit elements; how exact they have to be, the bound alone decides.
No kernel may reach another device: no remote copies, remote signals or barrier semaphores. Data moves between devices by JAX's collectives and lax.ppermute only.
A program may use at most 128 MiB of HBM per device.

v0:
```python
import math

import jax
import jax.numpy as jnp
from jax import lax
from jax.sharding import PartitionSpec as P

ITERS = 3


BLOB_SQ = 0.0025
INV_EIGHT_PI = 1.0 / (8.0 * math.pi)


def build_columns(values, src_points):
    rhs_count = values.shape[0]
    count = values.shape[2]
    inner_prod = jnp.sum(src_points[None] * values, axis=1)
    direct_cols = values.reshape(rhs_count * 3, count)
    outer_cols = (src_points[None, :, None, :] * values[:, None, :, :]).reshape(
        rhs_count * 9, count
    )
    scaled = (src_points[None] * inner_prod[:, None]).reshape(rhs_count * 3, count)
    return (direct_cols, jnp.concatenate([direct_cols, inner_prod, outer_cols, scaled], axis=0))


def tile_terms(tgt_points, src_points, src_area, direct_cols, columns):
    offsets = tgt_points[:, :, None] - src_points[:, None, :]
    dist_sq = jnp.sum(offsets * offsets, axis=0)
    inv_root = lax.rsqrt(dist_sq + BLOB_SQ)
    kernel_two = src_area[None, :] * inv_root * inv_root * inv_root * INV_EIGHT_PI
    kernel_one = (dist_sq + 2.0 * BLOB_SQ) * kernel_two
    dims = (((1,), (1,)), ((), ()))
    near_one = lax.dot_general(direct_cols, kernel_one, dims, precision=lax.Precision.HIGHEST)
    products = lax.dot_general(columns, kernel_two, dims, precision=lax.Precision.HIGHEST)
    rhs_count = direct_cols.shape[0] // 3
    tgt_count = tgt_points.shape[1]
    direct = near_one.reshape(rhs_count, 3, tgt_count)
    along_f = products[: 3 * rhs_count].reshape(rhs_count, 3, tgt_count)
    along_g = products[3 * rhs_count : 4 * rhs_count]
    along_yf = products[4 * rhs_count : 13 * rhs_count].reshape(rhs_count, 3, 3, tgt_count)
    along_yg = products[13 * rhs_count :].reshape(rhs_count, 3, tgt_count)
    x_dot = jnp.sum(tgt_points[None] * along_f, axis=1)
    cross_term = jnp.sum(tgt_points[None, None] * along_yf, axis=2)
    return direct + tgt_points[None] * (x_dot - along_g)[:, None] - cross_term + along_yg


def solve_small(hessen, start_norm, count):
    zero = jnp.zeros_like(start_norm)
    target = [start_norm] + [zero] * count
    cosines = []
    sines = []
    triangle = {}
    for k in range(count):
        column = [hessen[i, k] for i in range(k + 2)]
        for j in range(k):
            first_val = column[j]
            second_val = column[j + 1]
            column[j] = cosines[j] * first_val + sines[j] * second_val
            column[j + 1] = cosines[j] * second_val - sines[j] * first_val
        radius = jnp.sqrt(column[k] * column[k] + column[k + 1] * column[k + 1])
        cosine = column[k] / radius
        sine = column[k + 1] / radius
        cosines.append(cosine)
        sines.append(sine)
        for i in range(k):
            triangle[i, k] = column[i]
        triangle[k, k] = radius
        target[k + 1] = -sine * target[k]
        target[k] = cosine * target[k]
    coeffs = [None] * count
    for k in range(count - 1, -1, -1):
        accum = target[k]
        for i in range(k + 1, count):
            accum = accum - triangle[k, i] * coeffs[i]
        coeffs[k] = accum / triangle[k, k]
    return coeffs


def block_size(length):
    best = 1
    for cand in range(1, min(length, 1024) + 1):
        if length % cand == 0:
            best = cand
    return best


def body(velocity, points, panel_area, self_term, near_index, near_weight):
    tgt_points = lax.all_gather(points, "col", axis=1, tiled=True)
    src_points, src_area = (
        lax.all_gather(points, "row", axis=1, tiled=True),
        lax.all_gather(panel_area, "row", axis=0, tiled=True),
    )
    rhs_count = velocity.shape[0]
    tgt_count = tgt_points.shape[1]
    empty = jnp.zeros((rhs_count, 3, tgt_count), jnp.float32)

    def norm_of(field):
        return jnp.sqrt(lax.psum(jnp.sum(field * field, axis=(1, 2)), ("row", "col")))

    start_norm = norm_of(velocity)
    basis = [velocity / start_norm[:, None, None]]
    hessen = {}
    for k in range(ITERS):
        vector = basis[k]
        gathered = lax.all_gather(vector, "row", axis=2, tiled=True)
        length = gathered.shape[2]
        step = block_size(length)
        turns = length // step
        direct_cols, columns = build_columns(gathered, src_points)

        def one_turn(turn, acc):
            begin = turn * step
            return acc + tile_terms(
                tgt_points,
                lax.dynamic_slice_in_dim(src_points, begin, step, 1),
                lax.dynamic_slice_in_dim(src_area, begin, step, 0),
                lax.dynamic_slice_in_dim(direct_cols, begin, step, 1),
                lax.dynamic_slice_in_dim(columns, begin, step, 1),
            )

        partial_sum = lax.fori_loop(0, turns, one_turn, empty)
        picked = jnp.take(gathered, near_index, axis=2)
        partial_sum = partial_sum + jnp.sum(picked * near_weight[None, None], axis=-1)
        summed = lax.psum_scatter(partial_sum, "col", scatter_dimension=2, tiled=True)
        image = self_term[None, None] * vector + summed
        stacked = jnp.stack([jnp.sum(basis[j] * image, axis=(1, 2)) for j in range(k + 1)])
        totals = lax.psum(stacked, ("row", "col"))
        for j in range(k + 1):
            hessen[j, k] = totals[j]
            image = image - totals[j][:, None, None] * basis[j]
        length = norm_of(image)
        hessen[k + 1, k] = length
        if k + 1 < ITERS:
            basis.append(image / length[:, None, None])
    coeffs = solve_small(hessen, start_norm, ITERS)
    density = coeffs[0][:, None, None] * basis[0]
    for k in range(1, ITERS):
        density = density + coeffs[k][:, None, None] * basis[k]
    return density


def solution(mesh):
    return jax.shard_map(
        body,
        mesh=mesh,
        in_specs=(
            P(None, None, ("row", "col")),
            P(None, ("row", "col")),
            P(("row", "col")),
            P(("row", "col")),
            P("row", "col"),
            P("row", "col"),
        ),
        out_specs=P(None, None, ("row", "col")),
        check_vma=False,
    )
```

profile of v0, /device:TPU:0, one launch (start us, length us, event | category | flops | bytes accessed | tf_op | source)
XLA Modules:
  0.0 638.5 jit_solution(4090428311999120731)
XLA Ops:
  9.1 23.4 %all-gather.1 = f32[16,64,3]{1,2,0:T(4,128)S(1)} all-gather(f32[1,64,3]{1,2,0:T(4,128)} %bitcast.126), channel_id=1, replica_groups=mesh['row'=16,'col'=2] {'row'}, dimensions={0}, use_global_device_ids=true | all-gather | bytes 13056 | tf_op jit(solution)/shard_map/all_gather | solution.py:91
  32.5 5.3 all-gather
  38.7 36.9 %psum.49 = f32[6]{0:T(128)S(1)} all-reduce(f32[6]{0:T(128)S(1)} %multiply_reduce_fusion.16), channel_id=1, replica_groups=mesh['row'=16,'col'=2] {'row','col'}, use_global_device_ids=true, to_apply=%region_1.0 | all-reduce | flops 6 | bytes 48 | tf_op jit(solution)/shard_map/psum | solution.py:99
  77.6 33.4 %all_gather.18 = f32[6,3,1024]{0,1,2:T(4,128)S(1)} all-gather(f32[6,3,64]{0,1,2:T(4,128)S(1)} %copy.141), channel_id=1, replica_groups=mesh['row'=16,'col'=2] {'row'}, dimensions={2}, use_global_device_ids=true | all-gather | bytes 78336 | tf_op jit(solution)/shard_map/all_gather | solution.py:106
  112.1 5.6 multiply_reduce_fusion.2
  117.7 4.8 broadcast_multiply_fusion.2
  127.9 34.0 %all-reduce = f32[1024]{0:T(1024)} all-reduce(f32[1024]{0:T(1024)S(1)} %dynamic-update-slice), channel_id=1, replica_groups=mesh['row'=16,'col'=2] {'row'}, use_global_device_ids=true, to_apply=%add | all-reduce | flops 1024 | bytes 8192
  167.2 15.4 %gather_fusion = f32[2048,6,3]{1,2,0:T(4,128)} fusion(f32[6,3,1024]{0,1,2:T(4,128)S(1)} %all_gather.18, s32[2048]{0:T(1024)S(1)} %broadcast_clamp_fusion), kind=kCustom, calls=%fused_computation.clone | custom fusion | bytes 303104 | tf_op jit(solution)/shard_map/jit(_take)/gather | solution.py:123
  182.7 5.8 copy.182
  190.5 2.6 fusion.18
  194.2 5.8 reduce-scatter.10.cloned.1.call-done
  201.2 39.4 %psum.50 = f32[6]{0:T(128)S(1)} all-reduce(f32[6]{0:T(128)S(1)} %multiply_reduce_fusion.15), channel_id=1, replica_groups=mesh['row'=16,'col'=2] {'row','col'}, use_global_device_ids=true, to_apply=%region_9.11 | all-reduce | flops 6 | bytes 48 | tf_op jit(solution)/shard_map/psum | solution.py:128
  240.7 41.0 %psum.51 = f32[6]{0:T(128)S(1)} all-reduce(f32[6]{0:T(128)S(1)} %multiply_reduce_fusion.14), channel_id=1, replica_groups=mesh['row'=16,'col'=2] {'row','col'}, use_global_device_ids=true, to_apply=%region_11.13 | all-reduce | flops 6 | bytes 48 | tf_op jit(solution)/shard_map/psum | solution.py:99
  282.5 33.4 %all_gather.22 = f32[6,3,1024]{0,1,2:T(4,128)S(1)} all-gather(f32[6,3,64]{0,1,2:T(4,128)S(1)} %copy.157), channel_id=1, replica_groups=mesh['row'=16,'col'=2] {'row'}, dimensions={2}, use_global_device_ids=true | all-gather | bytes 78336 | tf_op jit(solution)/shard_map/all_gather | solution.py:106
  315.9 15.4 %gather_fusion.1 = f32[2048,6,3]{1,2,0:T(4,128)} fusion(f32[6,3,1024]{0,1,2:T(4,128)S(1)} %all_gather.22, s32[2048]{0:T(1024)S(1)} %broadcast_clamp_fusion), kind=kCustom, calls=%fused_computation.1.clone | custom fusion | bytes 303104 | tf_op jit(solution)/shard_map/jit(_take)/gather | solution.py:123
  331.3 6.4 %multiply_reduce_fusion.1 = f32[6,1024]{0,1:T(8,128)} fusion(f32[6,3,1024]{0,1,2:T(4,128)S(1)} %all_gather.22, f32[3,1024]{0,1:T(8,128)S(1)} %copy.146), kind=kLoop, calls=%fused_computation.4 | loop fusion | flops 30720 | bytes 110592 | tf_op jit(solution)/shard_map/reduce_sum | solution.py:18
  339.2 5.6 broadcast_multiply_fusion.1
  349.2 2.5 copy.161
  355.8 5.8 copy.183
  363.4 3.2 fusion.30
  368.3 10.3 %reduce-scatter.12.cloned.1.call-done = f32[64,18]{1,0:T(8,128)} async-done(((f32[128,18]{1,0:T(8,128)}), f32[64,18]{1,0:T(8,128)}) %reduce-scatter.12.cloned.1.call-update) | async-done | bytes 4624
  380.5 39.4 %psum.52 = f32[2,6]{1,0:T(2,128)S(1)} all-reduce(f32[2,6]{1,0:T(2,128)S(1)} %pad_maximum_fusion.1), channel_id=1, replica_groups=mesh['row'=16,'col'=2] {'row','col'}, use_global_device_ids=true, to_apply=%region_19.0 | all-reduce | flops 12 | bytes 96 | tf_op jit(solution)/shard_map/psum | solution.py:128
  420.7 41.0 %psum.53 = f32[6]{0:T(128)S(1)} all-reduce(f32[6]{0:T(128)S(1)} %get-tuple-element.68), channel_id=1, replica_groups=mesh['row'=16,'col'=2] {'row','col'}, use_global_device_ids=true, to_apply=%region_21.23 | all-reduce | flops 6 | bytes 48 | tf_op jit(solution)/shard_map/psum | solution.py:99
  462.0 33.4 %all_gather.23 = f32[6,3,1024]{0,1,2:T(4,128)S(1)} all-gather(f32[6,3,64]{0,1,2:T(4,128)S(1)} %copy.169), channel_id=1, replica_groups=mesh['row'=16,'col'=2] {'row'}, dimensions={2}, use_global_device_ids=true | all-gather | bytes 78336 | tf_op jit(solution)/shard_map/all_gather | solution.py:106
  495.4 15.4 %gather_fusion.2 = f32[2048,6,3]{1,2,0:T(4,128)} fusion(f32[6,3,1024]{0,1,2:T(4,128)S(1)} %all_gather.23, s32[2048]{0:T(1024)S(1)} %broadcast_clamp_fusion), kind=kCustom, calls=%fused_computation.2.clone | custom fusion | bytes 303104 | tf_op jit(solution)/shard_map/jit(_take)/gather | solution.py:123
  510.8 6.4 %multiply_reduce_fusion = f32[6,1024]{0,1:T(8,128)} fusion(f32[6,3,1024]{0,1,2:T(4,128)S(1)} %all_gather.23, f32[3,1024]{0,1:T(8,128)S(1)} %copy.146), kind=kLoop, calls=%fused_computation.3 | loop fusion | flops 30720 | bytes 110592 | tf_op jit(solution)/shard_map/reduce_sum | solution.py:18
  518.0 5.7 broadcast_multiply_fusion
  527.9 5.8 copy.184
  535.5 2.6 fusion.42
  539.0 10.4 %reduce-scatter.14.cloned.1.call-done = f32[64,18]{1,0:T(8,128)} async-done(((f32[128,18]{1,0:T(8,128)}), f32[64,18]{1,0:T(8,128)}) %reduce-scatter.14.cloned.1.call-update) | async-done | bytes 4624
  550.6 39.4 %psum.54 = f32[3,6]{1,0:T(4,128)S(1)} all-reduce(f32[3,6]{1,0:T(4,128)S(1)} %pad_maximum_fusion), channel_id=1, replica_groups=mesh['row'=16,'col'=2] {'row','col'}, use_global_device_ids=true, to_apply=%region_30.0 | all-reduce | flops 18 | bytes 144 | tf_op jit(solution)/shard_map/psum | solution.py:128
  590.2 41.0 %psum.55 = f32[6]{0:T(128)S(1)} all-reduce(f32[6]{0:T(128)S(1)} %multiply_reduce_fusion.7), channel_id=1, replica_groups=mesh['row'=16,'col'=2] {'row','col'}, use_global_device_ids=true, to_apply=%region_32.0 | all-reduce | flops 6 | bytes 48 | tf_op jit(solution)/shard_map/psum | solution.py:99
  (157 shorter events, 47.7 us)
Async XLA Ops:
  6.5 193.5 %reduce-scatter.10.cloned.1.call-start = ((), (), s32[]{:S(2)}) async-start(), calls=%async_computation.3 | async-start | bytes 98304
  75.6 0.6 copy-start.19
  76.2 0.5 copy-start.9
  124.8 3.1 copy-start.3
  164.5 2.6 copy-start.12
  182.6 5.8 copy-start.15
  182.6 5.9 copy-start.16
  182.7 6.1 copy-start.4
  182.7 7.9 %copy-start.6 = (f32[1024]{0:T(1024)S(1)}, f32[1024]{0:T(1024)}, u32[]{:S(2)}) copy-start(f32[1024]{0:T(1024)} %all-reduce) | copy-start | bytes 12292
  188.7 1.8 copy-start.1
  188.8 12.1 %copy-start = (f32[6,3,64]{2,1,0:T(4,128)S(1)}, f32[6,3,64]{2,1,0:T(4,128)}, u32[]{:S(2)}) copy-start(f32[6,3,64]{2,1,0:T(4,128)} %param.8) | copy-start | bytes 13828
  188.8 12.1 %copy-start.10 = (f32[6]{0:T(128)S(1)}, f32[6]{0:T(128)}, u32[]{:S(2)}) copy-start(f32[6]{0:T(128)} %copy-done.9) | copy-start | bytes 76
  188.8 12.1 %copy-start.13 = (f32[64]{0:T(128)S(1)}, f32[64]{0:T(128)}, u32[]{:S(2)}) copy-start(f32[64]{0:T(128)} %param.11) | copy-start | bytes 772
  194.1 184.5 %reduce-scatter.12.cloned.1.call-start = ((), (), s32[]{:S(2)}) async-start(), calls=%async_computation.4 | async-start | bytes 98304
  240.5 41.7 %copy-start.17 = (f32[6]{0:T(128)}, f32[6]{0:T(128)S(1)}, u32[]{:S(2)}) copy-start(f32[6]{0:T(128)S(1)} %psum.50) | copy-start | bytes 76
  281.7 0.5 copy-start.21
  355.8 5.8 copy-start.2
  355.8 7.5 %copy-start.5 = (f32[128,3]{0,1:T(4,128)S(1)}, f32[128,3]{0,1:T(4,128)}, u32[]{:S(2)}) copy-start(f32[128,3]{0,1:T(4,128)} %copy-done.3) | copy-start | bytes 4612
  355.8 7.6 %copy-start.7 = (f32[1024]{0:T(1024)S(1)}, f32[1024]{0:T(1024)}, u32[]{:S(2)}) copy-start(f32[1024]{0:T(1024)} %all-reduce) | copy-start | bytes 12292
  368.3 181.1 %reduce-scatter.14.cloned.1.call-start = ((), (), s32[]{:S(2)}) async-start(), calls=%async_computation.5 | async-start | bytes 98304
  461.7 49.1 %copy-start.23 = (f32[6]{0:T(128)}, f32[6]{0:T(128)S(1)}, u32[]{:S(2)}) copy-start(f32[6]{0:T(128)S(1)} %psum.53) | copy-start | bytes 76
  523.7 3.4 copy-start.8
  533.6 16.7 %copy-start.11 = (f32[6]{0:T(128)S(1)}, f32[6]{0:T(128)}, u32[]{:S(2)}) copy-start(f32[6]{0:T(128)} %copy-done.9) | copy-start | bytes 76
  533.7 16.7 %copy-start.14 = (f32[64]{0:T(128)S(1)}, f32[64]{0:T(128)}, u32[]{:S(2)}) copy-start(f32[64]{0:T(128)} %param.11) | copy-start | bytes 772
  533.7 97.5 %copy-start.18 = (f32[6]{0:T(128)S(1)}, f32[6]{0:T(128)}, u32[]{:S(2)}) copy-start(f32[6]{0:T(128)} %copy-done.17) | copy-start | bytes 76
  533.7 97.5 %copy-start.20 = (f32[6]{0:T(128)S(1)}, f32[6]{0:T(128)}, u32[]{:S(2)}) copy-start(f32[6]{0:T(128)} %copy-done.19) | copy-start | bytes 76
  533.7 97.5 %copy-start.22 = (f32[6]{0:T(128)S(1)}, f32[6]{0:T(128)}, u32[]{:S(2)}) copy-start(f32[6]{0:T(128)} %copy-done.21) | copy-start | bytes 76
  533.7 97.5 %copy-start.24 = (f32[6]{0:T(128)S(1)}, f32[6]{0:T(128)}, u32[]{:S(2)}) copy-start(f32[6]{0:T(128)} %copy-done.23) | copy-start | bytes 76
Sparse Core Ops, SparseCore 0:
  194.2 5.7 reduce-scatter.9
  368.4 10.1 reduce-scatter.11
  539.2 10.2 reduce-scatter.13
where the time goes:
time: 640 us; the launch traced here: 639 us
  blocking collectives  441 us (69%)
  local copies, waits for them, and re-layouts  96 us (15%)
  other arithmetic  48 us (8%)
  waiting for transfers between devices  26.6 us (4%)
  between operations  14.3 us (2%)
  matrix products  12.6 us (2%)
    psum x4, blocking collectives, norm_of(): lax.psum(jnp.sum(field * field, axis=(1, 2)), ('row', 'col'))  160 us
    psum x3, blocking collectives, body(): totals = lax.psum(stacked, ('row', 'col'))  118 us
    all_gather x3, blocking collectives, body(): gathered = lax.all_gather(vector, 'row', axis=2, tiled=True)  100 us
    gather x6, local copies, waits for them, and re-layouts, body(): picked = jnp.take(gathered, near_index, axis=2)  63.6 us
    unnamed x1, blocking collectives  34 us
    unnamed x6, waiting for transfers between devices  26.6 us
    all_gather x1, blocking collectives, body(): lax.all_gather(points, 'row', axis=1, tiled=True)  23.4 us
    reduce_sum x3, other arithmetic, build_columns(): inner_prod = jnp.sum(src_points[None] * values, axis=1)  18.5 us
  transfers between devices with their start and end apart: 3, of which 3 were waited for; matrix products, arithmetic and copies ran while one was open for 0% of the time, Pallas kernels for 0%

commit v1 on v0

v1 whole, which is shorter than its diff:
```python
import functools
import math

import jax
import jax.numpy as jnp
from jax import lax
from jax.experimental import pallas as pl
from jax.experimental.pallas import tpu as pltpu
from jax.sharding import PartitionSpec as P

ITERS = 3
BLOB_SQ = 0.0025
INV_EIGHT_PI = 1.0 / (8.0 * math.pi)
ROWS = 8
AXES = ("row", "col")
F32 = jnp.float32
BF16 = jnp.bfloat16


def low_half(shape):
    return lax.broadcasted_iota(jnp.int32, shape, len(shape) - 1) < 64


def pack(rows):
    return jnp.concatenate([rows[..., :4, :], rows[..., 4:, :]], axis=-1)


def xor_perm(n, m):
    return [(d, d ^ m) for d in range(n)]


def exchange(piece, n, mode):
    if mode == "gather" or n > 64:
        return [lax.all_gather(piece, AXES, axis=0)], None
    if mode == "alltoall":
        wide = jnp.broadcast_to(piece[None], (n,) + piece.shape)
        return [lax.all_to_all(wide, AXES, 0, 0, tiled=True)], None
    if mode == "direct":
        arrays = [piece[None]]
        for m in range(1, n):
            arrays.append(lax.ppermute(piece[None], AXES, xor_perm(n, m)))
        return arrays, [(m, 0) for m in range(n)]
    if mode == "double":
        held = piece[None]
        m = 1
        while m < n:
            other = lax.ppermute(held, AXES, xor_perm(n, m))
            if 2 * m == n:
                return [held, other], [(i // m, i % m) for i in range(n)]
            held = jnp.concatenate([held, other], axis=0)
            m *= 2
    raise ValueError(mode)


def assemble(piece_refs, where, slots, me):
    n = slots.shape[0]
    if where is None:

        @pl.loop(0, n)
        def _(m):
            slots[m] = piece_refs[0][me ^ m]
    else:
        for m, (k, i) in enumerate(where):
            slots[m] = piece_refs[k][i]


def chunk_parts(slots, chunk, n_row, n_col, part):
    half = n_row // 2
    o = chunk // half
    u = chunk % half
    even = slots[(2 * u) * n_col + o, part]
    odd = slots[(2 * u + 1) * n_col + o, part]
    low = low_half((4, 128))
    first = jnp.where(low, even, pltpu.roll(odd, 64, 1))
    second = jnp.where(low, pltpu.roll(even, 64, 1), odd)
    return first, second


def row_sum(acc):
    return jnp.sum(acc, axis=1, keepdims=True)


def dot_of(left, right, n_chunk):
    def step(chunk, acc):
        return acc + jnp.sum(left[chunk] * right[chunk], axis=0)

    acc = lax.fori_loop(0, n_chunk, step, jnp.zeros((ROWS, 128), F32), unroll=4)
    return row_sum(acc)


def write_columns(cols, places, chunk, vec):
    y = places[chunk]
    ys = [y[a : a + 1] for a in range(3)]
    f = [vec[a] for a in range(3)]
    g = ys[0] * f[0] + ys[1] * f[1] + ys[2] * f[2]
    groups = f + [g]
    groups += [ys[p] * f[v] for p in range(3) for v in range(3)]
    groups += [ys[a] * g for a in range(3)]
    full = jnp.concatenate(groups, axis=0)
    high = full.astype(BF16)
    low = (full - high.astype(F32)).astype(BF16)
    at = pl.ds(pl.multiple_of(chunk * 128, 128), 128)
    cols[0:128, at] = high
    cols[128:256, at] = low


def apply_rows(cols, kernels, targets, self_row, own, out):
    total = cols.shape[1]
    step = min(total, 2048)

    def turn(i, acc):
        at = pl.ds(pl.multiple_of(i * step, step), step)
        return acc + jnp.dot(cols[:, at], kernels[at, :], preferred_element_type=F32)

    if total == step:
        prod = jnp.dot(cols[...], kernels[...], preferred_element_type=F32)
    else:
        prod = lax.fori_loop(0, total // step, turn, jnp.zeros((256, 256), F32))
    both = prod[:128, :128] + (prod[128:, :128] + prod[:128, 128:])
    two = pltpu.roll(both, 64, 1)

    def group(k):
        return two[8 * k : 8 * k + 8]

    x = [targets[a : a + 1] for a in range(3)]
    along = x[0] * group(0) + x[1] * group(1) + x[2] * group(2) - group(3)
    for a in range(3):
        cross = sum(x[b] * group(4 + 3 * a + b) for b in range(3))
        image = both[8 * a : 8 * a + 8] + x[a] * along - cross + group(13 + a)
        image = image + self_row * own[a]
        top, bottom = image[:4], pltpu.roll(image[4:], 64, 1)
        out[a] = jnp.where(low_half((4, 128)), top, bottom)


def first_kernel(n_row, n_col, where, n_pieces, *refs):
    pieces = refs[:n_pieces]
    near = refs[n_pieces : n_pieces + n_col]
    tgt, me_ref = refs[n_pieces + n_col : n_pieces + n_col + 2]
    kernels, places, basis, norm_out, out, slots, cols = refs[n_pieces + n_col + 2 :]
    n_chunk = n_row * n_col // 2
    half = n_row // 2
    assemble(pieces, where, slots, me_ref[0])

    def unpack(chunk, acc):
        first, _ = chunk_parts(slots, chunk, n_row, n_col, 3)
        places[chunk] = jnp.concatenate([first, first], axis=0)
        for a in range(3):
            vec = jnp.concatenate(chunk_parts(slots, chunk, n_row, n_col, a), axis=0)
            basis[chunk, a] = vec
            acc = acc + vec * vec
        return acc

    acc = lax.fori_loop(0, n_chunk, unpack, jnp.zeros((ROWS, 128), F32))
    norm = jnp.sqrt(row_sum(acc))
    norm_out[...] = jnp.broadcast_to(norm, (ROWS, 128))

    low = low_half((128, 128))
    x = [tgt[a : a + 1] for a in range(3)]
    lines = lax.broadcasted_iota(jnp.int32, (128, 128), 0)

    for o in range(n_col):
        index = near[o][0]
        weight = near[o][1]
        count = index.shape[0]

        def build(u, carry):
            chunk = o * half + u
            vec = [basis[chunk, a] / norm for a in range(3)]
            for a in range(3):
                basis[chunk, a] = vec[a]
            write_columns(cols, places, chunk, vec)
            col = places[chunk].T
            d = [x[a] - col[:, a : a + 1] for a in range(3)]
            dist = d[0] * d[0] + d[1] * d[1] + d[2] * d[2]
            root = lax.rsqrt(dist + BLOB_SQ)
            two = col[:, 3:4] * root * root * root * INV_EIGHT_PI
            one = (dist + 2.0 * BLOB_SQ) * two
            line = (lines + u * 128).astype(F32)
            extra = jnp.zeros((128, 128), F32)
            for k in range(count):
                extra = extra + jnp.where(line == index[k : k + 1], weight[k : k + 1], 0.0)
            one = one + (extra + pltpu.roll(extra, 64, 1))
            value = jnp.where(low, one, two)
            high = value.astype(BF16)
            at = pl.ds(pl.multiple_of(chunk * 128, 128), 128)
            kernels[at, 0:128] = high
            kernels[at, 128:256] = (value - high.astype(F32)).astype(BF16)
            return carry

        lax.fori_loop(0, half, build, 0)

    apply_rows(cols, kernels, tgt, tgt[3:4], basis[0], out)


def load_image(pieces, where, slots, image, me, n_row, n_col):
    assemble(pieces, where, slots, me)

    def unpack(chunk, carry):
        for a in range(3):
            image[chunk, a] = jnp.concatenate(
                chunk_parts(slots, chunk, n_row, n_col, a), axis=0
            )
        return carry

    lax.fori_loop(0, n_row * n_col // 2, unpack, 0)


def orthogonalize(image, bases, n_chunk):
    column = []
    for base in bases:
        h = dot_of(image, base, n_chunk)
        column.append(h)

        def take(chunk, carry):
            image[chunk] = image[chunk] - h[None] * base[chunk]
            return carry

        lax.fori_loop(0, n_chunk, take, 0, unroll=4)
    column.append(jnp.sqrt(dot_of(image, image, n_chunk)))
    return column


def middle_kernel(n_row, n_col, where, n_pieces, n_base, *refs):
    pieces = refs[:n_pieces]
    bases = refs[n_pieces : n_pieces + n_base]
    kernels, places, tgt, me_ref, basis, h_out, out, slots, cols = refs[n_pieces + n_base :]
    n_chunk = n_row * n_col // 2
    load_image(pieces, where, slots, basis, me_ref[0], n_row, n_col)
    column = orthogonalize(basis, bases, n_chunk)
    for j, h in enumerate(column):
        h_out[j] = jnp.broadcast_to(h, (ROWS, 128))

    def scale(chunk, carry):
        vec = [basis[chunk, a] / column[-1] for a in range(3)]
        for a in range(3):
            basis[chunk, a] = vec[a]
        write_columns(cols, places, chunk, vec)
        return carry

    lax.fori_loop(0, n_chunk, scale, 0)
    apply_rows(cols, kernels, tgt, tgt[3:4], basis[0], out)


def solve_small(hessen, start_norm, count):
    zero = jnp.zeros_like(start_norm)
    target = [start_norm] + [zero] * count
    cosines = []
    sines = []
    triangle = {}
    for k in range(count):
        column = [hessen[i, k] for i in range(k + 2)]
        for j in range(k):
            first_val = column[j]
            second_val = column[j + 1]
            column[j] = cosines[j] * first_val + sines[j] * second_val
            column[j + 1] = cosines[j] * second_val - sines[j] * first_val
        radius = jnp.sqrt(column[k] * column[k] + column[k + 1] * column[k + 1])
        cosine = column[k] / radius
        sine = column[k + 1] / radius
        cosines.append(cosine)
        sines.append(sine)
        for i in range(k):
            triangle[i, k] = column[i]
        triangle[k, k] = radius
        target[k + 1] = -sine * target[k]
        target[k] = cosine * target[k]
    coeffs = [None] * count
    for k in range(count - 1, -1, -1):
        accum = target[k]
        for i in range(k + 1, count):
            accum = accum - triangle[k, i] * coeffs[i]
        coeffs[k] = accum / triangle[k, k]
    return coeffs


def last_kernel(n_row, n_col, where, n_pieces, *refs):
    pieces = refs[:n_pieces]
    bases = refs[n_pieces : n_pieces + ITERS]
    columns = refs[n_pieces + ITERS : n_pieces + 2 * ITERS - 1]
    norm, me_ref, out, slots, image = refs[n_pieces + 2 * ITERS - 1 :]
    n_chunk = n_row * n_col // 2
    load_image(pieces, where, slots, image, me_ref[0], n_row, n_col)
    last = orthogonalize(image, bases, n_chunk)
    hessen = {}
    for k in range(ITERS - 1):
        for j in range(k + 2):
            hessen[j, k] = columns[k][j]
    for j in range(ITERS + 1):
        hessen[j, ITERS - 1] = jnp.broadcast_to(last[j], (ROWS, 128))
    coeffs = solve_small(hessen, norm[...], ITERS)
    for a in range(3):
        out[a] = sum(coeffs[k] * bases[k][0, a] for k in range(ITERS))


def call(kernel, outs, scratch, operands, n_smem):
    vmem = pl.BlockSpec(memory_space=pltpu.VMEM)
    smem = pl.BlockSpec(memory_space=pltpu.SMEM)
    count = len(operands)
    specs = [smem if i in n_smem else vmem for i in range(count)]
    return pl.pallas_call(
        kernel,
        out_shape=[jax.ShapeDtypeStruct(s, t) for s, t in outs],
        in_specs=specs,
        out_specs=[vmem] * len(outs),
        scratch_shapes=[pltpu.VMEM(s, t) for s, t in scratch],
        compiler_params=pltpu.CompilerParams(vmem_limit_bytes=48 * 1024 * 1024),
    )(*operands)


def body(n_row, n_col, velocity, points, panel_area, self_term, near_index, near_weight):
    n = n_row * n_col
    n_chunk = n // 2
    total = n * 64
    row = lax.axis_index("row")
    col = lax.axis_index("col")
    me = (row * n_col + col).astype(jnp.int32).reshape(1)
    rhs = velocity.shape[0]
    vec = velocity.transpose(1, 0, 2)
    vec = jnp.concatenate([vec, vec[:, : ROWS - rhs]], axis=1)
    place = jnp.concatenate([points, panel_area[None]], axis=0)
    place = jnp.concatenate([place, jnp.zeros_like(place)], axis=0)
    piece = jnp.concatenate([pack(vec), pack(place)[None]], axis=0)

    tgt = jnp.concatenate([points, self_term[None]], axis=0)
    tgt = jnp.concatenate([tgt, tgt], axis=1)
    tgt = jnp.concatenate([tgt, tgt], axis=0)

    near = []
    count = near_index.shape[1] // 2
    for o in range(n_col):
        begin = (col ^ o) * 64
        index = lax.dynamic_slice_in_dim(near_index, begin, 64, 0)
        index = ((index // 64) ^ row) * 64 + index % 64
        weight = lax.dynamic_slice_in_dim(near_weight, begin, 64, 0)
        pair = jnp.stack([index.astype(F32), weight]).transpose(0, 2, 1)
        pair = jnp.concatenate([pair[:, :count], pair[:, count:]], axis=-1)
        if o:
            pair = lax.ppermute(pair, "col", xor_perm(n_col, o))
        near.append(pair)

    vec_shape = (n_chunk, 3, ROWS, 128)
    out_piece = ((3, 4, 128), F32)
    cols = ((256, total), BF16)

    arrays, where = exchange(piece, n, "gather")
    kernels, places, basis, norm, image = call(
        functools.partial(first_kernel, n_row, n_col, where, len(arrays)),
        [
            ((total, 256), BF16),
            ((n_chunk, ROWS, 128), F32),
            (vec_shape, F32),
            ((ROWS, 128), F32),
            out_piece,
        ],
        [((n, 4, 4, 128), F32), cols],
        [*arrays, *near, tgt, me],
        {len(arrays) + n_col + 1},
    )
    bases = [basis]
    columns = []
    for k, mode in ((1, "double"), (2, "direct")):
        arrays, where = exchange(image, n, mode)
        basis, column, image = call(
            functools.partial(middle_kernel, n_row, n_col, where, len(arrays), k),
            [(vec_shape, F32), ((k + 1, ROWS, 128), F32), out_piece],
            [((n, 3, 4, 128), F32), cols],
            [*arrays, *bases, kernels, places, tgt, me],
            {len(arrays) + k + 3},
        )
        bases.append(basis)
        columns.append(column)
    arrays, where = exchange(image, n, "alltoall")
    (density,) = call(
        functools.partial(last_kernel, n_row, n_col, where, len(arrays)),
        [((3, ROWS, 128), F32)],
        [((n, 3, 4, 128), F32), (vec_shape, F32)],
        [*arrays, *bases, *columns, norm, me],
        {len(arrays) + 2 * ITERS},
    )
    return density[:, :rhs, :64].transpose(1, 0, 2)


def solution(mesh):
    n_row, n_col = mesh.shape["row"], mesh.shape["col"]
    return jax.shard_map(
        functools.partial(body, n_row, n_col),
        mesh=mesh,
        in_specs=(
            P(None, None, AXES),
            P(None, AXES),
            P(AXES),
            P(AXES),
            P("row", "col"),
            P("row", "col"),
        ),
        out_specs=P(None, None, AXES),
        check_vma=False,
    )
```

time: 640 us -> 173 us (0.27)
  blocking collectives: 441 us -> 80.5 us
  local copies, waits for them, and re-layouts: 96 us -> 3.42 us
  starting transfers between devices: 0.09 us -> 54.2 us
  other arithmetic: 48 us -> 0.44 us
  between operations: 14.3 us -> 0.22 us
  Pallas kernels: 0 us -> 13.7 us
  matrix products: 12.6 us -> 0 us
    psum x7 -> x0, blocking collectives: 278 us -> none  [the longest x4 160 us: norm_of(): lax.psum(jnp.sum(field * field, axis=(1, 2)), ('row', 'col'))]
    gather x6 -> x0, local copies, waits for them, and re-layouts: 63.6 us -> none  [body(): picked = jnp.take(gathered, near_index, axis=2)]
    all_gather x5 -> x1, blocking collectives: 129 us -> 68.7 us  [exchange(): return ([lax.all_gather(piece, AXES, axis=0)], None)]
    ppermute x0 -> x37, starting transfers between devices: none -> 54.2 us  [the longest x31 51 us: exchange(): arrays.append(lax.ppermute(piece[None], AXES, xor_perm(n, m)))]
    unnamed x1 -> x0, blocking collectives: 34 us -> none
    reduce_sum x20 -> x0, other arithmetic: 27.2 us -> none  [the longest x3 18.5 us: build_columns(): inner_prod = jnp.sum(src_points[None] * values, axis=1)]
    unnamed x6 -> x0, waiting for transfers between devices: 26.6 us -> none
    ppermute x0 -> x37, waiting for transfers between devices: none -> 20.3 us  [the longest x5 18.6 us: exchange(): other = lax.ppermute(held, AXES, xor_perm(n, m))]
  transfers between devices with their start and end apart: 3 -> 37, of which waited for: 3 -> 7; matrix products, arithmetic and copies ran while one was open for 0% -> 0% of each run, Pallas kernels for 0% -> 0%
where the time goes in v1:
time: 173 us
  blocking collectives  80.5 us (47%)
  starting transfers between devices  54.2 us (31%)
  waiting for transfers between devices  20.3 us (12%)
  Pallas kernels  13.7 us (8%)
  local copies, waits for them, and re-layouts  3.42 us (2%)
    all_gather x1, blocking collectives, exchange(): return ([lax.all_gather(piece, AXES, axis=0)], None)  68.7 us
    ppermute x31, starting transfers between devices, exchange(): arrays.append(lax.ppermute(piece[None], AXES, xor_perm(n, m)))  51 us
    ppermute x5, waiting for transfers between devices, exchange(): other = lax.ppermute(held, AXES, xor_perm(n, m))  18.6 us
    pallas_call x4, Pallas kernels, call(): pl.pallas_call(kernel, out_shape=[jax.ShapeDtypeStruct(s, t) for s, t in...  13.7 us
    all_to_all x1, blocking collectives, exchange(): return ([lax.all_to_all(wide, AXES, 0, 0, tiled=True)], None)  11.8 us
  transfers between devices with their start and end apart: 37, of which 7 were waited for; matrix products, arithmetic and copies ran while one was open for 0% of the time, Pallas kernels for 0%

profile of v1, /device:TPU:0, one launch (start us, length us, event | category | flops | bytes accessed | tf_op | source)
XLA Modules:
  0.0 172.8 jit_solution(1127928583727491547)
XLA Ops:
  0.0 0.7 copy-done
  1.6 2.9 %collective-permute-start = (f32[2,8,128]{2,1,0:T(8,128)S(1)}, f32[2,8,128]{2,1,0:T(8,128)S(1)}, u32[]{:S(2)}, u32[]{:S(2)}) collective-permute-start(f32[2,8,128]{2,1,0:T(8,128)S(1)} %pad_maximum_fusion.5), channel_id=1, source_target_pairs={{0,1},{1,0},{2,3},{3,2},{4,5},{5,4},{6,7},{7,6},{8,9},{9,8},{10,11... | collective-permute-start | bytes 24584 | tf_op jit(solution)/shard_map/ppermute | solution.py:338
  5.3 68.7 %all-gather = f32[128,4,128]{2,1,0:T(4,128)S(1)} all-gather(f32[4,4,128]{2,1,0:T(4,128)S(1)} %fusion.11), channel_id=2, replica_groups=mesh['row'=16,'col'=2] {'row','col'}, dimensions={0}, use_global_device_ids=true | all-gather | bytes 270336 | tf_op jit(solution)/shard_map/all_gather | solution.py:34
  74.1 0.7 copy-done.5
  74.9 6.5 %shard_map.64 = (bf16[2048,256]{1,0:T(8,128)(2,1)S(1)}, f32[16,8,128]{2,1,0:T(8,128)S(1)}, f32[16,3,8,128]{3,2,1,0:T(8,128)S(1)}, f32[8,128]{1,0:T(8,128)S(1)}, f32[3,4,128]{2,1,0:T(4,128)S(1)}) custom-call(f32[32,4,4,128]{3,2,1,0:T(4,128)S(1)} %bitcast.26, f32[2,8,128]{2,1,0:T(8,128)S(1)} %pad_maximum_fusion.4.refs_1_, ...), custom_call_target="tpu_custom_call" | custom-call | tf_op jit(solution)/shard_map/pallas_call | solution.py:300
  81.5 3.6 %collective-permute-done.1 = f32[1,3,4,128]{3,2,1,0:T(4,128)S(1)} collective-permute-done((f32[1,3,4,128]{3,2,1,0:T(4,128)S(1)}, f32[1,3,4,128]{3,2,1,0:T(4,128)S(1)}, u32[]{:S(2)}, u32[]{:S(2)}) %collective-permute-start.1) | collective-permute-done | bytes 6176 | tf_op jit(solution)/shard_map/ppermute | solution.py:47
  85.1 1.2 collective-permute-done.2
  86.3 3.8 %collective-permute-done.3 = f32[4,3,4,128]{3,2,1,0:T(4,128)S(1)} collective-permute-done((f32[4,3,4,128]{3,2,1,0:T(4,128)S(1)}, f32[4,3,4,128]{3,2,1,0:T(4,128)S(1)}, u32[]{:S(2)}, u32[]{:S(2)}) %collective-permute-start.3) | collective-permute-done | bytes 24608 | tf_op jit(solution)/shard_map/ppermute | solution.py:47
  90.2 4.1 %collective-permute-done.4 = f32[8,3,4,128]{3,2,1,0:T(4,128)S(1)} collective-permute-done((f32[8,3,4,128]{3,2,1,0:T(4,128)S(1)}, f32[8,3,4,128]{3,2,1,0:T(4,128)S(1)}, u32[]{:S(2)}, u32[]{:S(2)}) %collective-permute-start.4) | collective-permute-done | bytes 49184 | tf_op jit(solution)/shard_map/ppermute | solution.py:47
  94.4 6.0 %collective-permute-done.5.refs_1_ = f32[16,3,4,128]{3,2,1,0:T(4,128)S(1)} collective-permute-done((f32[16,3,4,128]{3,2,1,0:T(4,128)S(1)}, f32[16,3,4,128]{3,2,1,0:T(4,128)S(1)}, u32[]{:S(2)}, u32[]{:S(2)}) %collective-permute-start.5) | collective-permute-done | bytes 98336 | tf_op jit(solution)/shard_map/ppermute | solution.py:47
  100.4 2.5 %shard_map.65 = (f32[16,3,8,128]{3,2,1,0:T(8,128)S(1)}, f32[2,8,128]{2,1,0:T(8,128)S(1)}, f32[3,4,128]{2,1,0:T(4,128)S(1)}) custom-call(f32[16,3,4,128]{3,2,1,0:T(4,128)S(1)} %constant_dynamic-update-slice_fusion.refs_0_, f32[16,3,4,128]{3,2,1,0:T(4,128)S(1)} %collective-permute-done.5.refs_1_, ...), custom_call_target="tpu_custom_call" | custom-call | tf_op jit(solution)/shard_map/pallas_call | solution.py:300
  102.9 3.9 %collective-permute-start.35 = (f32[1,3,4,128]{3,2,1,0:T(4,128)S(1)}, f32[1,3,4,128]{3,2,1,0:T(4,128)S(1)}, u32[]{:S(2)}, u32[]{:S(2)}) collective-permute-start(f32[1,3,4,128]{3,2,1,0:T(4,128)S(1)} %bitcast.32), channel_id=1, source_target_pairs={{0,30},{1,31},{2,28},{3,29},{4,26},{5,27},{6,24},{7,25},{8,22},{9,... | collective-permute-start | bytes 18440 | tf_op jit(solution)/shard_map/ppermute | solution.py:41
  106.8 6.2 %collective-permute-start.33 = (f32[1,3,4,128]{3,2,1,0:T(4,128)S(1)}, f32[1,3,4,128]{3,2,1,0:T(4,128)S(1)}, u32[]{:S(2)}, u32[]{:S(2)}) collective-permute-start(f32[1,3,4,128]{3,2,1,0:T(4,128)S(1)} %bitcast.34), channel_id=1, source_target_pairs={{0,28},{1,29},{2,30},{3,31},{4,24},{5,25},{6,26},{7,27},{8,20},{9,... | collective-permute-start | bytes 18440 | tf_op jit(solution)/shard_map/ppermute | solution.py:41
  113.0 3.0 %collective-permute-start.31 = (f32[1,3,4,128]{3,2,1,0:T(4,128)S(1)}, f32[1,3,4,128]{3,2,1,0:T(4,128)S(1)}, u32[]{:S(2)}, u32[]{:S(2)}) collective-permute-start(f32[1,3,4,128]{3,2,1,0:T(4,128)S(1)} %bitcast.36), channel_id=1, source_target_pairs={{0,26},{1,27},{2,24},{3,25},{4,30},{5,31},{6,28},{7,29},{8,18},{9,... | collective-permute-start | bytes 18440 | tf_op jit(solution)/shard_map/ppermute | solution.py:41
  116.4 4.9 %collective-permute-start.29 = (f32[1,3,4,128]{3,2,1,0:T(4,128)S(1)}, f32[1,3,4,128]{3,2,1,0:T(4,128)S(1)}, u32[]{:S(2)}, u32[]{:S(2)}) collective-permute-start(f32[1,3,4,128]{3,2,1,0:T(4,128)S(1)} %bitcast.38), channel_id=1, source_target_pairs={{0,24},{1,25},{2,26},{3,27},{4,28},{5,29},{6,30},{7,31},{8,16},{9,... | collective-permute-start | bytes 18440 | tf_op jit(solution)/shard_map/ppermute | solution.py:41
  121.3 3.0 %collective-permute-start.27 = (f32[1,3,4,128]{3,2,1,0:T(4,128)S(1)}, f32[1,3,4,128]{3,2,1,0:T(4,128)S(1)}, u32[]{:S(2)}, u32[]{:S(2)}) collective-permute-start(f32[1,3,4,128]{3,2,1,0:T(4,128)S(1)} %bitcast.40), channel_id=1, source_target_pairs={{0,22},{1,23},{2,20},{3,21},{4,18},{5,19},{6,16},{7,17},{8,30},{9,... | collective-permute-start | bytes 18440 | tf_op jit(solution)/shard_map/ppermute | solution.py:41
  124.2 5.3 %collective-permute-start.25 = (f32[1,3,4,128]{3,2,1,0:T(4,128)S(1)}, f32[1,3,4,128]{3,2,1,0:T(4,128)S(1)}, u32[]{:S(2)}, u32[]{:S(2)}) collective-permute-start(f32[1,3,4,128]{3,2,1,0:T(4,128)S(1)} %bitcast.42), channel_id=1, source_target_pairs={{0,20},{1,21},{2,22},{3,23},{4,16},{5,17},{6,18},{7,19},{8,28},{9,... | collective-permute-start | bytes 18440 | tf_op jit(solution)/shard_map/ppermute | solution.py:41
  129.5 2.1 %collective-permute-start.23 = (f32[1,3,4,128]{3,2,1,0:T(4,128)S(1)}, f32[1,3,4,128]{3,2,1,0:T(4,128)S(1)}, u32[]{:S(2)}, u32[]{:S(2)}) collective-permute-start(f32[1,3,4,128]{3,2,1,0:T(4,128)S(1)} %bitcast.44), channel_id=1, source_target_pairs={{0,18},{1,19},{2,16},{3,17},{4,22},{5,23},{6,20},{7,21},{8,26},{9,... | collective-permute-start | bytes 18440 | tf_op jit(solution)/shard_map/ppermute | solution.py:41
  131.7 4.3 %collective-permute-start.21 = (f32[1,3,4,128]{3,2,1,0:T(4,128)S(1)}, f32[1,3,4,128]{3,2,1,0:T(4,128)S(1)}, u32[]{:S(2)}, u32[]{:S(2)}) collective-permute-start(f32[1,3,4,128]{3,2,1,0:T(4,128)S(1)} %bitcast.46), channel_id=1, source_target_pairs={{0,16},{1,17},{2,18},{3,19},{4,20},{5,21},{6,22},{7,23},{8,24},{9,... | collective-permute-start | bytes 18440 | tf_op jit(solution)/shard_map/ppermute | solution.py:41
  136.0 2.1 %collective-permute-start.19 = (f32[1,3,4,128]{3,2,1,0:T(4,128)S(1)}, f32[1,3,4,128]{3,2,1,0:T(4,128)S(1)}, u32[]{:S(2)}, u32[]{:S(2)}) collective-permute-start(f32[1,3,4,128]{3,2,1,0:T(4,128)S(1)} %bitcast.48), channel_id=1, source_target_pairs={{0,14},{1,15},{2,12},{3,13},{4,10},{5,11},{6,8},{7,9},{8,6},{9,7},... | collective-permute-start | bytes 18440 | tf_op jit(solution)/shard_map/ppermute | solution.py:41
  138.1 4.4 %collective-permute-start.17 = (f32[1,3,4,128]{3,2,1,0:T(4,128)S(1)}, f32[1,3,4,128]{3,2,1,0:T(4,128)S(1)}, u32[]{:S(2)}, u32[]{:S(2)}) collective-permute-start(f32[1,3,4,128]{3,2,1,0:T(4,128)S(1)} %bitcast.50), channel_id=1, source_target_pairs={{0,12},{1,13},{2,14},{3,15},{4,8},{5,9},{6,10},{7,11},{8,4},{9,5},... | collective-permute-start | bytes 18440 | tf_op jit(solution)/shard_map/ppermute | solution.py:41
  142.5 1.2 collective-permute-start.15
  143.8 3.4 %collective-permute-start.13 = (f32[1,3,4,128]{3,2,1,0:T(4,128)S(1)}, f32[1,3,4,128]{3,2,1,0:T(4,128)S(1)}, u32[]{:S(2)}, u32[]{:S(2)}) collective-permute-start(f32[1,3,4,128]{3,2,1,0:T(4,128)S(1)} %bitcast.54), channel_id=1, source_target_pairs={{0,8},{1,9},{2,10},{3,11},{4,12},{5,13},{6,14},{7,15},{8,0},{9,1},... | collective-permute-start | bytes 18440 | tf_op jit(solution)/shard_map/ppermute | solution.py:41
  147.2 1.2 collective-permute-start.11
  148.4 1.5 collective-permute-start.10
  149.8 2.0 %collective-permute-start.9 = (f32[1,3,4,128]{3,2,1,0:T(4,128)S(1)}, f32[1,3,4,128]{3,2,1,0:T(4,128)S(1)}, u32[]{:S(2)}, u32[]{:S(2)}) collective-permute-start(f32[1,3,4,128]{3,2,1,0:T(4,128)S(1)} %bitcast.58), channel_id=1, source_target_pairs={{0,4},{1,5},{2,6},{3,7},{4,0},{5,1},{6,2},{7,3},{8,12},{9,13},{10,... | collective-permute-start | bytes 18440 | tf_op jit(solution)/shard_map/ppermute | solution.py:41
  152.0 2.0 %collective-permute-start.6 = (f32[1,3,4,128]{3,2,1,0:T(4,128)S(1)}, f32[1,3,4,128]{3,2,1,0:T(4,128)S(1)}, u32[]{:S(2)}, u32[]{:S(2)}) collective-permute-start(f32[1,3,4,128]{3,2,1,0:T(4,128)S(1)} %bitcast.61), channel_id=1, source_target_pairs={{0,1},{1,0},{2,3},{3,2},{4,5},{5,4},{6,7},{7,6},{8,9},{9,8},{10,11... | collective-permute-start | bytes 18440 | tf_op jit(solution)/shard_map/ppermute | solution.py:41
  154.0 0.9 collective-permute-done.8.refs_3_
  154.9 0.7 collective-permute-done.6.refs_1_
  155.7 2.7 %shard_map.66 = (f32[16,3,8,128]{3,2,1,0:T(8,128)S(1)}, f32[3,8,128]{2,1,0:T(8,128)S(1)}, f32[3,4,128]{2,1,0:T(4,128)S(1)}) custom-call(f32[1,3,4,128]{3,2,1,0:T(4,128)S(1)} %bitcast.62, f32[1,3,4,128]{3,2,1,0:T(4,128)S(1)} %collective-permute-done.6.refs_1_, f32[1,3,4,128]{3,2,1,0:T(4,128)S(1)} %collective-permute-done.7.refs_2_, ...), custom_call_target="tpu_custom_call" | custom-call | tf_op jit(solution)/shard_map/pallas_call | solution.py:300
  158.4 11.8 %all_to_all.5.refs_0_ = f32[32,3,4,128]{3,2,1,0:T(4,128)S(1)} all-to-all(f32[32,3,4,128]{3,2,1,0:T(4,128)S(1)} %broadcast_in_dim.17), channel_id=1, replica_groups=mesh['row'=16,'col'=2] {'row','col'}, dimensions={0} | all-to-all | bytes 393216 | tf_op jit(solution)/shard_map/all_to_all | solution.py:37
  170.2 2.0 %shard_map.67 = f32[3,8,128]{2,1,0:T(8,128)S(1)} custom-call(f32[32,3,4,128]{3,2,1,0:T(4,128)S(1)} %all_to_all.5.refs_0_, f32[16,3,8,128]{3,2,1,0:T(8,128)S(1)} %get-tuple-element.17.refs_2_.refs_32_.refs_1_, f32[16,3,8,128]{3,2,1,0:T(8,128)S(1)} %get-tuple-element.21.refs_33_.refs_2_, f32[16,3,8,128]{3,2,1,0:T(8,128)S(1)} %get-tuple-element.23.refs_3_, ...), custom_call_target="tpu_custom_call" | custom-call | tf_op jit(solution)/shard_map/pallas_call | solution.py:300
  (84 shorter events, 3.5 us)
Async XLA Ops:
  1.6 73.3 %collective-permute-start = (f32[2,8,128]{2,1,0:T(8,128)S(1)}, f32[2,8,128]{2,1,0:T(8,128)S(1)}, u32[]{:S(2)}, u32[]{:S(2)}) collective-permute-start(f32[2,8,128]{2,1,0:T(8,128)S(1)} %pad_maximum_fusion.5), channel_id=1, source_target_pairs={{0,1},{1,0},{2,3},{3,2},{4,5},{5,4},{6,7},{7,6},{8,9},{9,8},{10,11... | collective-permute-start | bytes 24584 | tf_op jit(solution)/shard_map/ppermute | solution.py:338
  86.2 3.9 %collective-permute-start.3 = (f32[4,3,4,128]{3,2,1,0:T(4,128)S(1)}, f32[4,3,4,128]{3,2,1,0:T(4,128)S(1)}, u32[]{:S(2)}, u32[]{:S(2)}) collective-permute-start(f32[4,3,4,128]{3,2,1,0:T(4,128)S(1)} %pad_maximum_fusion.1), channel_id=1, source_target_pairs={{0,4},{1,5},{2,6},{3,7},{4,0},{5,1},{6,2},{7,3},{8,12},{9,13},{10,... | collective-permute-start | bytes 73736 | tf_op jit(solution)/shard_map/ppermute | solution.py:47
  90.2 4.2 %collective-permute-start.4 = (f32[8,3,4,128]{3,2,1,0:T(4,128)S(1)}, f32[8,3,4,128]{3,2,1,0:T(4,128)S(1)}, u32[]{:S(2)}, u32[]{:S(2)}) collective-permute-start(f32[8,3,4,128]{3,2,1,0:T(4,128)S(1)} %pad_maximum_fusion), channel_id=1, source_target_pairs={{0,8},{1,9},{2,10},{3,11},{4,12},{5,13},{6,14},{7,15},{8,0},{9,1},... | collective-permute-start | bytes 147464 | tf_op jit(solution)/shard_map/ppermute | solution.py:47
  94.3 6.1 %collective-permute-start.5 = (f32[16,3,4,128]{3,2,1,0:T(4,128)S(1)}, f32[16,3,4,128]{3,2,1,0:T(4,128)S(1)}, u32[]{:S(2)}, u32[]{:S(2)}) collective-permute-start(f32[16,3,4,128]{3,2,1,0:T(4,128)S(1)} %constant_dynamic-update-slice_fusion.refs_0_), channel_id=1, source_target_pairs={{0,16},{1,17},{2,18},{3,19},{4,20},{5,21},{6,22},{7,23},{8,24},{9,... | collective-permute-start | bytes 294920 | tf_op jit(solution)/shard_map/ppermute | solution.py:47
  102.9 10.1 %collective-permute-start.36 = (f32[1,3,4,128]{3,2,1,0:T(4,128)S(1)}, f32[1,3,4,128]{3,2,1,0:T(4,128)S(1)}, u32[]{:S(2)}, u32[]{:S(2)}) collective-permute-start(f32[1,3,4,128]{3,2,1,0:T(4,128)S(1)} %bitcast.31), channel_id=1, source_target_pairs={{0,31},{1,30},{2,29},{3,28},{4,27},{5,26},{6,25},{7,24},{8,23},{9,... | collective-permute-start | bytes 18440 | tf_op jit(solution)/shard_map/ppermute | solution.py:41
  102.9 13.0 %collective-permute-start.35 = (f32[1,3,4,128]{3,2,1,0:T(4,128)S(1)}, f32[1,3,4,128]{3,2,1,0:T(4,128)S(1)}, u32[]{:S(2)}, u32[]{:S(2)}) collective-permute-start(f32[1,3,4,128]{3,2,1,0:T(4,128)S(1)} %bitcast.32), channel_id=1, source_target_pairs={{0,30},{1,31},{2,28},{3,29},{4,26},{5,27},{6,24},{7,25},{8,22},{9,... | collective-permute-start | bytes 18440 | tf_op jit(solution)/shard_map/ppermute | solution.py:41
  106.8 9.6 %collective-permute-start.34 = (f32[1,3,4,128]{3,2,1,0:T(4,128)S(1)}, f32[1,3,4,128]{3,2,1,0:T(4,128)S(1)}, u32[]{:S(2)}, u32[]{:S(2)}) collective-permute-start(f32[1,3,4,128]{3,2,1,0:T(4,128)S(1)} %bitcast.33), channel_id=1, source_target_pairs={{0,29},{1,28},{2,31},{3,30},{4,25},{5,24},{6,27},{7,26},{8,21},{9,... | collective-permute-start | bytes 18440 | tf_op jit(solution)/shard_map/ppermute | solution.py:41
  106.8 14.5 %collective-permute-start.33 = (f32[1,3,4,128]{3,2,1,0:T(4,128)S(1)}, f32[1,3,4,128]{3,2,1,0:T(4,128)S(1)}, u32[]{:S(2)}, u32[]{:S(2)}) collective-permute-start(f32[1,3,4,128]{3,2,1,0:T(4,128)S(1)} %bitcast.34), channel_id=1, source_target_pairs={{0,28},{1,29},{2,30},{3,31},{4,24},{5,25},{6,26},{7,27},{8,20},{9,... | collective-permute-start | bytes 18440 | tf_op jit(solution)/shard_map/ppermute | solution.py:41
  113.0 8.3 %collective-permute-start.32 = (f32[1,3,4,128]{3,2,1,0:T(4,128)S(1)}, f32[1,3,4,128]{3,2,1,0:T(4,128)S(1)}, u32[]{:S(2)}, u32[]{:S(2)}) collective-permute-start(f32[1,3,4,128]{3,2,1,0:T(4,128)S(1)} %bitcast.35), channel_id=1, source_target_pairs={{0,27},{1,26},{2,25},{3,24},{4,31},{5,30},{6,29},{7,28},{8,19},{9,... | collective-permute-start | bytes 18440 | tf_op jit(solution)/shard_map/ppermute | solution.py:41
  113.0 11.3 %collective-permute-start.31 = (f32[1,3,4,128]{3,2,1,0:T(4,128)S(1)}, f32[1,3,4,128]{3,2,1,0:T(4,128)S(1)}, u32[]{:S(2)}, u32[]{:S(2)}) collective-permute-start(f32[1,3,4,128]{3,2,1,0:T(4,128)S(1)} %bitcast.36), channel_id=1, source_target_pairs={{0,26},{1,27},{2,24},{3,25},{4,30},{5,31},{6,28},{7,29},{8,18},{9,... | collective-permute-start | bytes 18440 | tf_op jit(solution)/shard_map/ppermute | solution.py:41
  116.0 8.3 %collective-permute-start.30 = (f32[1,3,4,128]{3,2,1,0:T(4,128)S(1)}, f32[1,3,4,128]{3,2,1,0:T(4,128)S(1)}, u32[]{:S(2)}, u32[]{:S(2)}) collective-permute-start(f32[1,3,4,128]{3,2,1,0:T(4,128)S(1)} %bitcast.37), channel_id=1, source_target_pairs={{0,25},{1,24},{2,27},{3,26},{4,29},{5,28},{6,31},{7,30},{8,17},{9,... | collective-permute-start | bytes 18440 | tf_op jit(solution)/shard_map/ppermute | solution.py:41
  116.4 13.2 %collective-permute-start.29 = (f32[1,3,4,128]{3,2,1,0:T(4,128)S(1)}, f32[1,3,4,128]{3,2,1,0:T(4,128)S(1)}, u32[]{:S(2)}, u32[]{:S(2)}) collective-permute-start(f32[1,3,4,128]{3,2,1,0:T(4,128)S(1)} %bitcast.38), channel_id=1, source_target_pairs={{0,24},{1,25},{2,26},{3,27},{4,28},{5,29},{6,30},{7,31},{8,16},{9,... | collective-permute-start | bytes 18440 | tf_op jit(solution)/shard_map/ppermute | solution.py:41
  121.2 8.3 %collective-permute-start.28 = (f32[1,3,4,128]{3,2,1,0:T(4,128)S(1)}, f32[1,3,4,128]{3,2,1,0:T(4,128)S(1)}, u32[]{:S(2)}, u32[]{:S(2)}) collective-permute-start(f32[1,3,4,128]{3,2,1,0:T(4,128)S(1)} %bitcast.39), channel_id=1, source_target_pairs={{0,23},{1,22},{2,21},{3,20},{4,19},{5,18},{6,17},{7,16},{8,31},{9,... | collective-permute-start | bytes 18440 | tf_op jit(solution)/shard_map/ppermute | solution.py:41
  121.3 10.4 %collective-permute-start.27 = (f32[1,3,4,128]{3,2,1,0:T(4,128)S(1)}, f32[1,3,4,128]{3,2,1,0:T(4,128)S(1)}, u32[]{:S(2)}, u32[]{:S(2)}) collective-permute-start(f32[1,3,4,128]{3,2,1,0:T(4,128)S(1)} %bitcast.40), channel_id=1, source_target_pairs={{0,22},{1,23},{2,20},{3,21},{4,18},{5,19},{6,16},{7,17},{8,30},{9,... | collective-permute-start | bytes 18440 | tf_op jit(solution)/shard_map/ppermute | solution.py:41
  124.2 7.5 %collective-permute-start.26 = (f32[1,3,4,128]{3,2,1,0:T(4,128)S(1)}, f32[1,3,4,128]{3,2,1,0:T(4,128)S(1)}, u32[]{:S(2)}, u32[]{:S(2)}) collective-permute-start(f32[1,3,4,128]{3,2,1,0:T(4,128)S(1)} %bitcast.41), channel_id=1, source_target_pairs={{0,21},{1,20},{2,23},{3,22},{4,17},{5,16},{6,19},{7,18},{8,29},{9,... | collective-permute-start | bytes 18440 | tf_op jit(solution)/shard_map/ppermute | solution.py:41
  124.2 11.8 %collective-permute-start.25 = (f32[1,3,4,128]{3,2,1,0:T(4,128)S(1)}, f32[1,3,4,128]{3,2,1,0:T(4,128)S(1)}, u32[]{:S(2)}, u32[]{:S(2)}) collective-permute-start(f32[1,3,4,128]{3,2,1,0:T(4,128)S(1)} %bitcast.42), channel_id=1, source_target_pairs={{0,20},{1,21},{2,22},{3,23},{4,16},{5,17},{6,18},{7,19},{8,28},{9,... | collective-permute-start | bytes 18440 | tf_op jit(solution)/shard_map/ppermute | solution.py:41
  129.5 6.5 %collective-permute-start.24 = (f32[1,3,4,128]{3,2,1,0:T(4,128)S(1)}, f32[1,3,4,128]{3,2,1,0:T(4,128)S(1)}, u32[]{:S(2)}, u32[]{:S(2)}) collective-permute-start(f32[1,3,4,128]{3,2,1,0:T(4,128)S(1)} %bitcast.43), channel_id=1, source_target_pairs={{0,19},{1,18},{2,17},{3,16},{4,23},{5,22},{6,21},{7,20},{8,27},{9,... | collective-permute-start | bytes 18440 | tf_op jit(solution)/shard_map/ppermute | solution.py:41
  129.5 8.6 %collective-permute-start.23 = (f32[1,3,4,128]{3,2,1,0:T(4,128)S(1)}, f32[1,3,4,128]{3,2,1,0:T(4,128)S(1)}, u32[]{:S(2)}, u32[]{:S(2)}) collective-permute-start(f32[1,3,4,128]{3,2,1,0:T(4,128)S(1)} %bitcast.44), channel_id=1, source_target_pairs={{0,18},{1,19},{2,16},{3,17},{4,22},{5,23},{6,20},{7,21},{8,26},{9,... | collective-permute-start | bytes 18440 | tf_op jit(solution)/shard_map/ppermute | solution.py:41
  131.6 6.5 %collective-permute-start.22 = (f32[1,3,4,128]{3,2,1,0:T(4,128)S(1)}, f32[1,3,4,128]{3,2,1,0:T(4,128)S(1)}, u32[]{:S(2)}, u32[]{:S(2)}) collective-permute-start(f32[1,3,4,128]{3,2,1,0:T(4,128)S(1)} %bitcast.45), channel_id=1, source_target_pairs={{0,17},{1,16},{2,19},{3,18},{4,21},{5,20},{6,23},{7,22},{8,25},{9,... | collective-permute-start | bytes 18440 | tf_op jit(solution)/shard_map/ppermute | solution.py:41
  131.7 10.8 %collective-permute-start.21 = (f32[1,3,4,128]{3,2,1,0:T(4,128)S(1)}, f32[1,3,4,128]{3,2,1,0:T(4,128)S(1)}, u32[]{:S(2)}, u32[]{:S(2)}) collective-permute-start(f32[1,3,4,128]{3,2,1,0:T(4,128)S(1)} %bitcast.46), channel_id=1, source_target_pairs={{0,16},{1,17},{2,18},{3,19},{4,20},{5,21},{6,22},{7,23},{8,24},{9,... | collective-permute-start | bytes 18440 | tf_op jit(solution)/shard_map/ppermute | solution.py:41
  136.0 6.5 %collective-permute-start.20 = (f32[1,3,4,128]{3,2,1,0:T(4,128)S(1)}, f32[1,3,4,128]{3,2,1,0:T(4,128)S(1)}, u32[]{:S(2)}, u32[]{:S(2)}) collective-permute-start(f32[1,3,4,128]{3,2,1,0:T(4,128)S(1)} %bitcast.47), channel_id=1, source_target_pairs={{0,15},{1,14},{2,13},{3,12},{4,11},{5,10},{6,9},{7,8},{8,7},{9,6},... | collective-permute-start | bytes 18440 | tf_op jit(solution)/shard_map/ppermute | solution.py:41
  136.0 7.7 %collective-permute-start.19 = (f32[1,3,4,128]{3,2,1,0:T(4,128)S(1)}, f32[1,3,4,128]{3,2,1,0:T(4,128)S(1)}, u32[]{:S(2)}, u32[]{:S(2)}) collective-permute-start(f32[1,3,4,128]{3,2,1,0:T(4,128)S(1)} %bitcast.48), channel_id=1, source_target_pairs={{0,14},{1,15},{2,12},{3,13},{4,10},{5,11},{6,8},{7,9},{8,6},{9,7},... | collective-permute-start | bytes 18440 | tf_op jit(solution)/shard_map/ppermute | solution.py:41
  138.1 5.7 %collective-permute-start.18 = (f32[1,3,4,128]{3,2,1,0:T(4,128)S(1)}, f32[1,3,4,128]{3,2,1,0:T(4,128)S(1)}, u32[]{:S(2)}, u32[]{:S(2)}) collective-permute-start(f32[1,3,4,128]{3,2,1,0:T(4,128)S(1)} %bitcast.49), channel_id=1, source_target_pairs={{0,13},{1,12},{2,15},{3,14},{4,9},{5,8},{6,11},{7,10},{8,5},{9,4},... | collective-permute-start | bytes 18440 | tf_op jit(solution)/shard_map/ppermute | solution.py:41
  138.1 9.1 %collective-permute-start.17 = (f32[1,3,4,128]{3,2,1,0:T(4,128)S(1)}, f32[1,3,4,128]{3,2,1,0:T(4,128)S(1)}, u32[]{:S(2)}, u32[]{:S(2)}) collective-permute-start(f32[1,3,4,128]{3,2,1,0:T(4,128)S(1)} %bitcast.50), channel_id=1, source_target_pairs={{0,12},{1,13},{2,14},{3,15},{4,8},{5,9},{6,10},{7,11},{8,4},{9,5},... | collective-permute-start | bytes 18440 | tf_op jit(solution)/shard_map/ppermute | solution.py:41
  142.5 4.7 %collective-permute-start.16 = (f32[1,3,4,128]{3,2,1,0:T(4,128)S(1)}, f32[1,3,4,128]{3,2,1,0:T(4,128)S(1)}, u32[]{:S(2)}, u32[]{:S(2)}) collective-permute-start(f32[1,3,4,128]{3,2,1,0:T(4,128)S(1)} %bitcast.51), channel_id=1, source_target_pairs={{0,11},{1,10},{2,9},{3,8},{4,15},{5,14},{6,13},{7,12},{8,3},{9,2},... | collective-permute-start | bytes 18440 | tf_op jit(solution)/shard_map/ppermute | solution.py:41
  142.5 5.9 %collective-permute-start.15 = (f32[1,3,4,128]{3,2,1,0:T(4,128)S(1)}, f32[1,3,4,128]{3,2,1,0:T(4,128)S(1)}, u32[]{:S(2)}, u32[]{:S(2)}) collective-permute-start(f32[1,3,4,128]{3,2,1,0:T(4,128)S(1)} %bitcast.52), channel_id=1, source_target_pairs={{0,10},{1,11},{2,8},{3,9},{4,14},{5,15},{6,12},{7,13},{8,2},{9,3},... | collective-permute-start | bytes 18440 | tf_op jit(solution)/shard_map/ppermute | solution.py:41
  143.7 6.2 %collective-permute-start.14 = (f32[1,3,4,128]{3,2,1,0:T(4,128)S(1)}, f32[1,3,4,128]{3,2,1,0:T(4,128)S(1)}, u32[]{:S(2)}, u32[]{:S(2)}) collective-permute-start(f32[1,3,4,128]{3,2,1,0:T(4,128)S(1)} %bitcast.53), channel_id=1, source_target_pairs={{0,9},{1,8},{2,11},{3,10},{4,13},{5,12},{6,15},{7,14},{8,1},{9,0},... | collective-permute-start | bytes 18440 | tf_op jit(solution)/shard_map/ppermute | solution.py:41
  143.8 8.1 %collective-permute-start.13 = (f32[1,3,4,128]{3,2,1,0:T(4,128)S(1)}, f32[1,3,4,128]{3,2,1,0:T(4,128)S(1)}, u32[]{:S(2)}, u32[]{:S(2)}) collective-permute-start(f32[1,3,4,128]{3,2,1,0:T(4,128)S(1)} %bitcast.54), channel_id=1, source_target_pairs={{0,8},{1,9},{2,10},{3,11},{4,12},{5,13},{6,14},{7,15},{8,0},{9,1},... | collective-permute-start | bytes 18440 | tf_op jit(solution)/shard_map/ppermute | solution.py:41
  147.2 4.7 %collective-permute-start.12 = (f32[1,3,4,128]{3,2,1,0:T(4,128)S(1)}, f32[1,3,4,128]{3,2,1,0:T(4,128)S(1)}, u32[]{:S(2)}, u32[]{:S(2)}) collective-permute-start(f32[1,3,4,128]{3,2,1,0:T(4,128)S(1)} %bitcast.55), channel_id=1, source_target_pairs={{0,7},{1,6},{2,5},{3,4},{4,3},{5,2},{6,1},{7,0},{8,15},{9,14},{10,... | collective-permute-start | bytes 18440 | tf_op jit(solution)/shard_map/ppermute | solution.py:41
  147.2 4.8 %collective-permute-start.11 = (f32[1,3,4,128]{3,2,1,0:T(4,128)S(1)}, f32[1,3,4,128]{3,2,1,0:T(4,128)S(1)}, u32[]{:S(2)}, u32[]{:S(2)}) collective-permute-start(f32[1,3,4,128]{3,2,1,0:T(4,128)S(1)} %bitcast.56), channel_id=1, source_target_pairs={{0,6},{1,7},{2,4},{3,5},{4,2},{5,3},{6,0},{7,1},{8,14},{9,15},{10,... | collective-permute-start | bytes 18440 | tf_op jit(solution)/shard_map/ppermute | solution.py:41
  148.4 5.6 %collective-permute-start.10 = (f32[1,3,4,128]{3,2,1,0:T(4,128)S(1)}, f32[1,3,4,128]{3,2,1,0:T(4,128)S(1)}, u32[]{:S(2)}, u32[]{:S(2)}) collective-permute-start(f32[1,3,4,128]{3,2,1,0:T(4,128)S(1)} %bitcast.57), channel_id=1, source_target_pairs={{0,5},{1,4},{2,7},{3,6},{4,1},{5,0},{6,3},{7,2},{8,13},{9,12},{10,... | collective-permute-start | bytes 18440 | tf_op jit(solution)/shard_map/ppermute | solution.py:41
  149.8 4.2 %collective-permute-start.9 = (f32[1,3,4,128]{3,2,1,0:T(4,128)S(1)}, f32[1,3,4,128]{3,2,1,0:T(4,128)S(1)}, u32[]{:S(2)}, u32[]{:S(2)}) collective-permute-start(f32[1,3,4,128]{3,2,1,0:T(4,128)S(1)} %bitcast.58), channel_id=1, source_target_pairs={{0,4},{1,5},{2,6},{3,7},{4,0},{5,1},{6,2},{7,3},{8,12},{9,13},{10,... | collective-permute-start | bytes 18440 | tf_op jit(solution)/shard_map/ppermute | solution.py:41
  (11 other events, 21.0 us)

commit v2 on v1

--- a/solution.py
+++ b/solution.py
@@ -12,7 +12,7 @@
 BLOB_SQ = 0.0025
 INV_EIGHT_PI = 1.0 / (8.0 * math.pi)
 ROWS = 8
-AXES = ("row", "col")
+AXES = ("top", "mid", "core", "col")
 F32 = jnp.float32
 BF16 = jnp.bfloat16
 
@@ -29,39 +29,37 @@
     return [(d, d ^ m) for d in range(n)]
 
 
-def exchange(piece, n, mode):
-    if mode == "gather" or n > 64:
-        return [lax.all_gather(piece, AXES, axis=0)], None
-    if mode == "alltoall":
-        wide = jnp.broadcast_to(piece[None], (n,) + piece.shape)
-        return [lax.all_to_all(wide, AXES, 0, 0, tiled=True)], None
-    if mode == "direct":
-        arrays = [piece[None]]
-        for m in range(1, n):
-            arrays.append(lax.ppermute(piece[None], AXES, xor_perm(n, m)))
-        return arrays, [(m, 0) for m in range(n)]
-    if mode == "double":
-        held = piece[None]
-        m = 1
-        while m < n:
-            other = lax.ppermute(held, AXES, xor_perm(n, m))
-            if 2 * m == n:
-                return [held, other], [(i // m, i % m) for i in range(n)]
-            held = jnp.concatenate([held, other], axis=0)
-            m *= 2
+def spread(piece, axes, size):
+    wide = jnp.broadcast_to(piece[None], (size,) + piece.shape)
+    return lax.all_to_all(wide, axes, 0, 0, tiled=True)
+
+
+def exchange(piece, sizes, mode):
+    top, mid, core, col = sizes
+    n = top * mid * core * col
+    if mode == "all":
+        return [spread(piece, AXES, n)], lambda m, me: (0, me ^ m)
+    if mode == "two":
+        near = spread(piece, AXES[1:], n // top)
+        far = spread(near, AXES[0], top)
+        return [far.reshape((n,) + piece.shape)], lambda m, me: (0, me ^ m)
+    if mode == "chips":
+        own = spread(piece, ("top", "mid", "col"), n // 2)
+        other = lax.ppermute(own, "core", xor_perm(2, 1))
+
+        def where(m, me):
+            dev = me ^ m
+            chip = dev // (2 * col) * col + dev % col
+            return (m // col) % 2, chip
+
+        return [own, other], where
     raise ValueError(mode)
 
 
 def assemble(piece_refs, where, slots, me):
-    n = slots.shape[0]
-    if where is None:
-
-        @pl.loop(0, n)
-        def _(m):
-            slots[m] = piece_refs[0][me ^ m]
-    else:
-        for m, (k, i) in enumerate(where):
-            slots[m] = piece_refs[k][i]
+    for m in range(slots.shape[0]):
+        k, i = where(m, me)
+        slots[m] = piece_refs[k][i]
 
 
 def chunk_parts(slots, chunk, n_row, n_col, part):
@@ -74,6 +72,14 @@
     first = jnp.where(low, even, pltpu.roll(odd, 64, 1))
     second = jnp.where(low, pltpu.roll(even, 64, 1), odd)
     return first, second
+
+
+PAIRS = [(i, j) for i in range(ITERS) for j in range(i, ITERS)]
+
+
+def place_of(j):
+    lane = lax.broadcasted_iota(jnp.int32, (ROWS, 128), 1)
+    return lane == lax.broadcasted_iota(jnp.int32, (ROWS, 128), 0) * (ITERS + 1) + j
 
 
 def row_sum(acc):
@@ -104,7 +110,7 @@
     cols[128:256, at] = low
 
 
-def apply_rows(cols, kernels, targets, self_row, own, out):
+def apply_rows(cols, kernels, targets, own):
     total = cols.shape[1]
     step = min(total, 2048)
 
@@ -123,11 +129,17 @@
         return two[8 * k : 8 * k + 8]
 
     x = [targets[a : a + 1] for a in range(3)]
+    images = []
     along = x[0] * group(0) + x[1] * group(1) + x[2] * group(2) - group(3)
     for a in range(3):
         cross = sum(x[b] * group(4 + 3 * a + b) for b in range(3))
         image = both[8 * a : 8 * a + 8] + x[a] * along - cross + group(13 + a)
-        image = image + self_row * own[a]
+        images.append(image + targets[3:4] * own[a])
+    return images
+
+
+def write_piece(images, out):
+    for a, image in enumerate(images):
         top, bottom = image[:4], pltpu.roll(image[4:], 64, 1)
         out[a] = jnp.where(low_half((4, 128)), top, bottom)
 
@@ -189,7 +201,7 @@
 
         lax.fori_loop(0, half, build, 0)
 
-    apply_rows(cols, kernels, tgt, tgt[3:4], basis[0], out)
+    write_piece(apply_rows(cols, kernels, tgt, basis[0]), out)
 
 
 def load_image(pieces, where, slots, image, me, n_row, n_col):
@@ -220,7 +232,7 @@
     return column
 
 
-def middle_kernel(n_row, n_col, where, n_pieces, n_base, *refs):
+def middle_kernel(n_row, n_col, where, n_pieces, n_base, final, *refs):
     pieces = refs[:n_pieces]
     bases = refs[n_pieces : n_pieces + n_base]
     kernels, places, tgt, me_ref, basis, h_out, out, slots, cols = refs[n_pieces + n_base :]
@@ -238,7 +250,22 @@
         return carry
 
     lax.fori_loop(0, n_chunk, scale, 0)
-    apply_rows(cols, kernels, tgt, tgt[3:4], basis[0], out)
+    images = apply_rows(cols, kernels, tgt, basis[0])
+    if not final:
+        write_piece(images, out)
+        return
+    every = [*bases, basis]
+    for at, (i, j) in enumerate(PAIRS):
+        gram = dot_of(every[i], every[j], n_chunk)
+        h_out[len(column) + at] = jnp.broadcast_to(gram, (ROWS, 128))
+    low = low_half((ROWS, 128))
+    row = jnp.zeros((ROWS, 128), F32)
+    for j in range(ITERS + 1):
+        other = images if j == ITERS else [every[j][0, a] for a in range(3)]
+        part = sum(images[a] * other[a] for a in range(3))
+        part = row_sum(jnp.where(low, part, 0.0))
+        row = row + jnp.where(place_of(j), part, 0.0)
+    out[...] = jnp.sum(row, axis=0, keepdims=True)
 
 
 def solve_small(hessen, start_norm, count):
@@ -273,23 +300,37 @@
     return coeffs
 
 
-def last_kernel(n_row, n_col, where, n_pieces, *refs):
-    pieces = refs[:n_pieces]
-    bases = refs[n_pieces : n_pieces + ITERS]
-    columns = refs[n_pieces + ITERS : n_pieces + 2 * ITERS - 1]
-    norm, me_ref, out, slots, image = refs[n_pieces + 2 * ITERS - 1 :]
-    n_chunk = n_row * n_col // 2
-    load_image(pieces, where, slots, image, me_ref[0], n_row, n_col)
-    last = orthogonalize(image, bases, n_chunk)
+def last_kernel(sums, *refs):
+    bases = refs[:ITERS]
+    columns = refs[ITERS : 2 * ITERS - 1]
+    norm, out = refs[2 * ITERS - 1 :]
     hessen = {}
     for k in range(ITERS - 1):
         for j in range(k + 2):
             hessen[j, k] = columns[k][j]
-    for j in range(ITERS + 1):
-        hessen[j, ITERS - 1] = jnp.broadcast_to(last[j], (ROWS, 128))
+    gram = {}
+    for at, (i, j) in enumerate(PAIRS):
+        gram[i, j] = gram[j, i] = columns[-1][ITERS + at]
+    row = jnp.broadcast_to(jnp.sum(sums[...], axis=0), (ROWS, 128))
+    inner = [
+        jnp.broadcast_to(row_sum(jnp.where(place_of(j), row, 0.0)), (ROWS, 128))
+        for j in range(ITERS + 1)
+    ]
+    square = inner[ITERS]
+    for j in range(ITERS):
+        h = inner[j]
+        for i in range(j):
+            h = h - hessen[i, ITERS - 1] * gram[i, j]
+        hessen[j, ITERS - 1] = h
+    for j in range(ITERS):
+        rest = -2.0 * inner[j]
+        for i in range(ITERS):
+            rest = rest + hessen[i, ITERS - 1] * gram[i, j]
+        square = square + hessen[j, ITERS - 1] * rest
+    hessen[ITERS, ITERS - 1] = jnp.sqrt(jnp.maximum(square, 0.0))
     coeffs = solve_small(hessen, norm[...], ITERS)
     for a in range(3):
-        out[a] = sum(coeffs[k] * bases[k][0, a] for k in range(ITERS))
+        out[a] = sum(coeffs[k] * bases[k][a] for k in range(ITERS))
 
 
 def call(kernel, outs, scratch, operands, n_smem):
@@ -307,11 +348,12 @@
     )(*operands)
 
 
-def body(n_row, n_col, velocity, points, panel_area, self_term, near_index, near_weight):
+def body(sizes, velocity, points, panel_area, self_term, near_index, near_weight):
+    n_row, n_col = sizes[0] * sizes[1] * sizes[2], sizes[3]
     n = n_row * n_col
     n_chunk = n // 2
     total = n * 64
-    row = lax.axis_index("row")
+    row = lax.axis_index(AXES[:3])
     col = lax.axis_index("col")
     me = (row * n_col + col).astype(jnp.int32).reshape(1)
     rhs = velocity.shape[0]
@@ -342,7 +384,7 @@
     out_piece = ((3, 4, 128), F32)
     cols = ((256, total), BF16)
 
-    arrays, where = exchange(piece, n, "gather")
+    arrays, where = exchange(piece, sizes, "all")
     kernels, places, basis, norm, image = call(
         functools.partial(first_kernel, n_row, n_col, where, len(arrays)),
         [
@@ -358,40 +400,47 @@
     )
     bases = [basis]
     columns = []
-    for k, mode in ((1, "double"), (2, "direct")):
-        arrays, where = exchange(image, n, mode)
+    for k, mode in ((1, "chips"), (2, "two")):
+        arrays, where = exchange(image, sizes, mode)
+        final = k == ITERS - 1
         basis, column, image = call(
-            functools.partial(middle_kernel, n_row, n_col, where, len(arrays), k),
-            [(vec_shape, F32), ((k + 1, ROWS, 128), F32), out_piece],
+            functools.partial(middle_kernel, n_row, n_col, where, len(arrays), k, final),
+            [
+                (vec_shape, F32),
+                ((k + 1 + (6 if final else 0), ROWS, 128), F32),
+                ((1, 128), F32) if final else out_piece,
+            ],
             [((n, 3, 4, 128), F32), cols],
             [*arrays, *bases, kernels, places, tgt, me],
             {len(arrays) + k + 3},
         )
         bases.append(basis)
         columns.append(column)
-    arrays, where = exchange(image, n, "alltoall")
+    sums = spread(image, AXES, n)
     (density,) = call(
-        functools.partial(last_kernel, n_row, n_col, where, len(arrays)),
+        last_kernel,
         [((3, ROWS, 128), F32)],
-        [((n, 3, 4, 128), F32), (vec_shape, F32)],
-        [*arrays, *bases, *columns, norm, me],
-        {len(arrays) + 2 * ITERS},
+        [],
+        [sums, *[base[0] for base in bases], *columns, norm],
+        {},
     )
     return density[:, :rhs, :64].transpose(1, 0, 2)
 
 
 def solution(mesh):
     n_row, n_col = mesh.shape["row"], mesh.shape["col"]
+    sizes = (n_row // 4, 2, 2, n_col)
+    split = jax.sharding.Mesh(mesh.devices.reshape(sizes), AXES)
     return jax.shard_map(
-        functools.partial(body, n_row, n_col),
-        mesh=mesh,
+        functools.partial(body, sizes),
+        mesh=split,
         in_specs=(
             P(None, None, AXES),
             P(None, AXES),
             P(AXES),
             P(AXES),
-            P("row", "col"),
-            P("row", "col"),
+            P(AXES[:3], "col"),
+            P(AXES[:3], "col"),
         ),
         out_specs=P(None, None, AXES),
         check_vma=False,

time: 173 us -> 75.5 us (0.44)
  blocking collectives: 80.5 us -> 18 us
  starting transfers between devices: 54.2 us -> 14.9 us
  local copies, waits for them, and re-layouts: 3.42 us -> 6.19 us
  waiting for transfers between devices: 20.3 us -> 22.9 us
    all_gather x1 -> x0, blocking collectives: 68.7 us -> none  [exchange(): return ([lax.all_gather(piece, AXES, axis=0)], None)]
    ppermute x36 -> x1, starting transfers between devices: 51.2 us -> 0.01 us  [exchange(): other = lax.ppermute(own, 'core', xor_perm(2, 1))]
    all_to_all x0 -> x3, waiting for transfers between devices: none -> 20.5 us  [spread(): return lax.all_to_all(wide, axes, 0, 0, tiled=True)]
    ppermute x36 -> x1, waiting for transfers between devices: 20.3 us -> 1.3 us  [exchange(): other = lax.ppermute(own, 'core', xor_perm(2, 1))]
    all_to_all x0 -> x3, starting transfers between devices: none -> 13.2 us  [spread(): return lax.all_to_all(wide, axes, 0, 0, tiled=True)]
    all_to_all x1 -> x2, blocking collectives: 11.8 us -> 18 us  [spread(): return lax.all_to_all(wide, axes, 0, 0, tiled=True)]
    broadcast_in_dim x1 -> x5, local copies, waits for them, and re-layouts: 0.03 us -> 2.07 us  [spread(): wide = jnp.broadcast_to(piece[None], (size,) + piece.shape)]
  transfers between devices with their start and end apart: 37 -> 5, of which waited for: 7 -> 5; matrix products, arithmetic and copies ran while one was open for 0% -> 1% of each run, Pallas kernels for 0% -> 0%
where the time goes in v2:
time: 75.5 us; the launch traced here: 75 us
  waiting for transfers between devices  22.9 us (30%)
  blocking collectives  18 us (24%)
  starting transfers between devices  14.9 us (20%)
  Pallas kernels  12.4 us (16%)
  local copies, waits for them, and re-layouts  6.19 us (8%)
    all_to_all x3, waiting for transfers between devices, spread(): return lax.all_to_all(wide, axes, 0, 0, tiled=True)  20.5 us
    all_to_all x2, blocking collectives, spread(): return lax.all_to_all(wide, axes, 0, 0, tiled=True)  18 us
    all_to_all x3, starting transfers between devices, spread(): return lax.all_to_all(wide, axes, 0, 0, tiled=True)  13.2 us
    pallas_call x4, Pallas kernels, call(): pl.pallas_call(kernel, out_shape=[jax.ShapeDtypeStruct(s, t) for s, t in...  12.4 us
    unnamed x12, local copies, waits for them, and re-layouts  2.64 us
    broadcast_in_dim x5, local copies, waits for them, and re-layouts, spread(): wide = jnp.broadcast_to(piece[None], (size,) + piece.shape)  2.07 us
    ppermute x1, starting transfers between devices, body(): pair = lax.ppermute(pair, 'col', xor_perm(n_col, o))  1.77 us
  transfers between devices with their start and end apart: 5, of which 5 were waited for; matrix products, arithmetic and copies ran while one was open for 1% of the time, Pallas kernels for 0%

profile of v2, /device:TPU:0, one launch (start us, length us, event | category | flops | bytes accessed | tf_op | source)
XLA Modules:
  0.0 75.0 jit_solution(5009749547522103730)
XLA Ops:
  0.0 0.8 %slice.44 = f32[3,4,64]{2,0,1:T(4,128)S(1)} slice(f32[3,6,64]{2,0,1:T(4,128)} %bitcast.31), slice={[0:3], [0:4], [0:64]} | slice | bytes 6144 | tf_op jit(solution)/shard_map/slice | solution.py:25
  0.8 0.0 copy-start.4
  0.8 0.7 copy-done.3
  1.5 0.1 fusion.11
  1.6 0.7 broadcast_in_dim.20
  2.3 7.3 %all-to-all-start = ((f32[32,4,4,128]{3,2,1,0:T(4,128)}), f32[32,4,4,128]{3,2,1,0:T(4,128)S(1)}, u32[]{:S(2)}, u32[]{:S(2)}) async-start(f32[32,4,4,128]{3,2,1,0:T(4,128)} %broadcast_in_dim.20), calls=%async_computation | async-start | bytes 524288 | tf_op jit(solution)/shard_map/all_to_all | solution.py:34
  9.6 0.0 copy-start.1
  9.6 0.7 copy-done.1
  10.3 0.1 dynamic-slice_bitcast_fusion
  10.4 0.6 copy-done.2
  11.0 0.1 fusion.9
  11.1 0.1 pad_maximum_fusion.2
  11.2 1.8 %collective-permute-start = (f32[2,8,128]{2,1,0:T(8,128)S(1)}, f32[2,8,128]{2,1,0:T(8,128)S(1)}, u32[]{:S(2)}, u32[]{:S(2)}) collective-permute-start(f32[2,8,128]{2,1,0:T(8,128)S(1)} %pad_maximum_fusion.2), channel_id=1, source_target_pairs={{0,1},{1,0},{2,3},{3,2},{4,5},{5,4},{6,7},{7,6},{8,9},{9,8},{10,11... | collective-permute-start | bytes 24584 | tf_op jit(solution)/shard_map/ppermute | solution.py:380
  13.0 0.1 pad_maximum_fusion.1.refs_1_
  13.1 0.7 copy-done.5
  13.7 0.1 maximum_maximum_fusion.refs_3_.refs_5_
  13.8 1.2 %collective-permute-done.refs_2_ = f32[2,8,128]{2,1,0:T(8,128)S(1)} collective-permute-done((f32[2,8,128]{2,1,0:T(8,128)S(1)}, f32[2,8,128]{2,1,0:T(8,128)S(1)}, u32[]{:S(2)}, u32[]{:S(2)}) %collective-permute-start) | collective-permute-done | bytes 8224 | tf_op jit(solution)/shard_map/ppermute | solution.py:380
  15.0 5.3 %all-to-all-done.refs_0_ = f32[32,4,4,128]{3,2,1,0:T(4,128)S(1)} async-done(((f32[32,4,4,128]{3,2,1,0:T(4,128)}), f32[32,4,4,128]{3,2,1,0:T(4,128)S(1)}, u32[]{:S(2)}, u32[]{:S(2)}) %all-to-all-start) | async-done | bytes 262176 | tf_op jit(solution)/shard_map/all_to_all | solution.py:34
  20.3 6.3 %shard_map.64 = (bf16[2048,256]{1,0:T(8,128)(2,1)S(1)}, f32[16,8,128]{2,1,0:T(8,128)S(1)}, f32[16,3,8,128]{3,2,1,0:T(8,128)S(1)}, f32[8,128]{1,0:T(8,128)S(1)}, f32[3,4,128]{2,1,0:T(4,128)S(1)}) custom-call(f32[32,4,4,128]{3,2,1,0:T(4,128)S(1)} %all-to-all-done.refs_0_, f32[2,8,128]{2,1,0:T(8,128)S(1)} %pad_maximum_fusion.1.refs_1_, ...), custom_call_target="tpu_custom_call" | custom-call | tf_op jit(solution)/shard_map/pallas_call | solution.py:341
  26.7 10.8 %all_to_all.25.refs_0_ = f32[16,3,4,128]{3,2,1,0:T(4,128)S(1)} all-to-all(f32[16,3,4,128]{3,2,1,0:T(4,128)S(1)} %broadcast_in_dim.22), channel_id=1, replica_groups=mesh['top'=4,'mid'=2,'core'=2,'col'=2] {'top','mid','col'}, dimensions={0} | all-to-all | bytes 196608 | tf_op jit(solution)/shard_map/all_to_all | solution.py:34
  37.5 1.3 %collective-permute-done.1.refs_1_ = f32[16,3,4,128]{3,2,1,0:T(4,128)S(1)} collective-permute-done((f32[16,3,4,128]{3,2,1,0:T(4,128)S(1)}, f32[16,3,4,128]{3,2,1,0:T(4,128)S(1)}, u32[]{:S(2)}, u32[]{:S(2)}) %collective-permute-start.1) | collective-permute-done | bytes 98336 | tf_op jit(solution)/shard_map/ppermute | solution.py:48
  38.8 2.7 %shard_map.65 = (f32[16,3,8,128]{3,2,1,0:T(8,128)S(1)}, f32[2,8,128]{2,1,0:T(8,128)S(1)}, f32[3,4,128]{2,1,0:T(4,128)S(1)}) custom-call(f32[16,3,4,128]{3,2,1,0:T(4,128)S(1)} %all_to_all.25.refs_0_, f32[16,3,4,128]{3,2,1,0:T(4,128)S(1)} %collective-permute-done.1.refs_1_, f32[16,3,8,128]{3,2,1,0:T(8,128)S(1)} %get-tuple-element.17.refs_2_.refs_1_, ...), custom_call_target="tpu_custom_call" | custom-call | tf_op jit(solution)/shard_map/pallas_call | solution.py:341
  41.4 7.2 %all_to_all.26 = f32[8,3,4,128]{3,2,1,0:T(4,128)S(1)} all-to-all(f32[8,3,4,128]{3,2,1,0:T(4,128)S(1)} %broadcast_in_dim.23), channel_id=1, replica_groups=mesh['top'=4,'mid'=2,'core'=2,'col'=2] {'mid','core','col'}, dimensions={0} | all-to-all | bytes 98304 | tf_op jit(solution)/shard_map/all_to_all | solution.py:34
  48.6 0.7 broadcast_in_dim.48
  49.3 3.4 %all-to-all-start.3 = ((f32[4,8,3,4,128]{4,3,2,1,0:T(4,128)}), f32[4,8,3,4,128]{4,3,2,1,0:T(4,128)S(1)}, u32[]{:S(2)}, u32[]{:S(2)}) async-start(f32[4,8,3,4,128]{4,3,2,1,0:T(4,128)} %broadcast_in_dim.48), calls=%async_computation.3 | async-start | bytes 393216 | tf_op jit(solution)/shard_map/all_to_all | solution.py:34
  52.7 8.0 %all-to-all-done.3 = f32[4,8,3,4,128]{4,3,2,1,0:T(4,128)S(1)} async-done(((f32[4,8,3,4,128]{4,3,2,1,0:T(4,128)}), f32[4,8,3,4,128]{4,3,2,1,0:T(4,128)S(1)}, u32[]{:S(2)}, u32[]{:S(2)}) %all-to-all-start.3) | async-done | bytes 196640 | tf_op jit(solution)/shard_map/all_to_all | solution.py:34
  60.7 3.3 %shard_map.66 = (f32[16,3,8,128]{3,2,1,0:T(8,128)S(1)}, f32[9,8,128]{2,1,0:T(8,128)S(1)}, f32[1,128]{1,0:T(1,128)S(1)}) custom-call(f32[32,3,4,128]{3,2,1,0:T(4,128)S(1)} %bitcast.29, f32[16,3,8,128]{3,2,1,0:T(8,128)S(1)} %get-tuple-element.17.refs_2_.refs_1_, f32[16,3,8,128]{3,2,1,0:T(8,128)S(1)} %get-tuple-element.21.refs_2_, ...), custom_call_target="tpu_custom_call" | custom-call | tf_op jit(solution)/shard_map/pallas_call | solution.py:341
  63.9 0.6 broadcast_in_dim.50
  64.5 2.5 %all-to-all-start.4 = ((f32[32,1,128]{2,1,0:T(1,128)}), f32[32,1,128]{2,1,0:T(1,128)S(1)}, u32[]{:S(2)}, u32[]{:S(2)}) async-start(f32[32,1,128]{2,1,0:T(1,128)} %broadcast_in_dim.50), calls=%async_computation.4 | async-start | bytes 32768 | tf_op jit(solution)/shard_map/all_to_all | solution.py:34
  67.0 7.2 %all-to-all-done.4.sums = f32[32,1,128]{2,1,0:T(1,128)S(1)} async-done(((f32[32,1,128]{2,1,0:T(1,128)}), f32[32,1,128]{2,1,0:T(1,128)S(1)}, u32[]{:S(2)}, u32[]{:S(2)}) %all-to-all-start.4) | async-done | bytes 16416 | tf_op jit(solution)/shard_map/all_to_all | solution.py:34
  74.2 0.1 shard_map.67
  74.4 0.6 copy.9
  (19 shorter events, 0.1 us)
Async XLA Ops:
  0.0 0.8 %copy-start = (f32[6,3,64]{2,1,0:T(4,128)S(1)}, f32[6,3,64]{2,1,0:T(4,128)}, u32[]{:S(2)}) copy-start(f32[6,3,64]{2,1,0:T(4,128)} %param.6) | copy-start | bytes 13828
  0.8 0.7 copy-start.3
  0.8 0.7 copy-start.4
  2.3 18.0 %all-to-all-start = ((f32[32,4,4,128]{3,2,1,0:T(4,128)}), f32[32,4,4,128]{3,2,1,0:T(4,128)S(1)}, u32[]{:S(2)}, u32[]{:S(2)}) async-start(f32[32,4,4,128]{3,2,1,0:T(4,128)} %broadcast_in_dim.20), calls=%async_computation | async-start | bytes 524288 | tf_op jit(solution)/shard_map/all_to_all | solution.py:34
  9.6 0.7 copy-start.1
  10.3 0.7 copy-start.2
  11.2 3.8 %collective-permute-start = (f32[2,8,128]{2,1,0:T(8,128)S(1)}, f32[2,8,128]{2,1,0:T(8,128)S(1)}, u32[]{:S(2)}, u32[]{:S(2)}) collective-permute-start(f32[2,8,128]{2,1,0:T(8,128)S(1)} %pad_maximum_fusion.2), channel_id=1, source_target_pairs={{0,1},{1,0},{2,3},{3,2},{4,5},{5,4},{6,7},{7,6},{8,9},{9,8},{10,11... | collective-permute-start | bytes 24584 | tf_op jit(solution)/shard_map/ppermute | solution.py:380
  13.1 0.7 copy-start.5
  37.5 1.3 %collective-permute-start.1 = (f32[16,3,4,128]{3,2,1,0:T(4,128)S(1)}, f32[16,3,4,128]{3,2,1,0:T(4,128)S(1)}, u32[]{:S(2)}, u32[]{:S(2)}) collective-permute-start(f32[16,3,4,128]{3,2,1,0:T(4,128)S(1)} %all_to_all.25.refs_0_), channel_id=1, source_target_pairs={{0,2},{2,0},{1,3},{3,1},{4,6},{6,4},{5,7},{7,5},{8,10},{10,8},{9,1... | collective-permute-start | bytes 294920 | tf_op jit(solution)/shard_map/ppermute | solution.py:48
  49.3 11.4 %all-to-all-start.3 = ((f32[4,8,3,4,128]{4,3,2,1,0:T(4,128)}), f32[4,8,3,4,128]{4,3,2,1,0:T(4,128)S(1)}, u32[]{:S(2)}, u32[]{:S(2)}) async-start(f32[4,8,3,4,128]{4,3,2,1,0:T(4,128)} %broadcast_in_dim.48), calls=%async_computation.3 | async-start | bytes 393216 | tf_op jit(solution)/shard_map/all_to_all | solution.py:34
  64.5 9.7 %all-to-all-start.4 = ((f32[32,1,128]{2,1,0:T(1,128)}), f32[32,1,128]{2,1,0:T(1,128)S(1)}, u32[]{:S(2)}, u32[]{:S(2)}) async-start(f32[32,1,128]{2,1,0:T(1,128)} %broadcast_in_dim.50), calls=%async_computation.4 | async-start | bytes 32768 | tf_op jit(solution)/shard_map/all_to_all | solution.py:34

commit v3 on v2

v3 whole, which is shorter than its diff:
```python
import functools
import math

import jax
import jax.numpy as jnp
from jax import lax
from jax.experimental import pallas as pl
from jax.experimental.pallas import tpu as pltpu
from jax.sharding import PartitionSpec as P

ITERS = 3
BLOB_SQ = 0.0025
INV_EIGHT_PI = 1.0 / (8.0 * math.pi)
ROWS = 8
AXES = ("top", "mid", "core", "col")
F32 = jnp.float32
BF16 = jnp.bfloat16


def low_half(shape):
    return lax.broadcasted_iota(jnp.int32, shape, len(shape) - 1) < 64


def pack(rows):
    return jnp.concatenate([rows[..., :4, :], rows[..., 4:, :]], axis=-1)


def xor_perm(n, m):
    return [(d, d ^ m) for d in range(n)]


def spread(piece, axes, size):
    wide = jnp.broadcast_to(piece[None], (size,) + piece.shape)
    return lax.all_to_all(wide, axes, 0, 0, tiled=True)


def each(count, step):
    if count <= 16:
        for i in range(count):
            step(i)
    else:
        pl.loop(0, count)(step)


def dots(pairs, n_chunk):
    lanes = 4
    zero = jnp.zeros((ROWS, 128), F32)

    def step(chunk, accs):
        slot = chunk % lanes if isinstance(chunk, int) else 0
        for at, (left, right) in enumerate(pairs):
            part = sum(left[chunk, a] * right[chunk, a] for a in range(3))
            accs[at][slot] = accs[at][slot] + part
        return accs

    accs = [[zero] * lanes for _ in pairs]
    if n_chunk <= 16:
        for chunk in range(n_chunk):
            accs = step(chunk, accs)
    else:
        accs = lax.fori_loop(0, n_chunk, step, accs)
    sums = [(acc[0] + acc[1]) + (acc[2] + acc[3]) for acc in accs]
    return [jnp.sum(acc, axis=1, keepdims=True) for acc in sums]


def chunk_parts(piece, chunk, me, n_row, n_col, part):
    half = n_row // 2
    o = chunk // half
    u = chunk % half
    even = piece[me ^ ((2 * u) * n_col + o), part]
    odd = piece[me ^ ((2 * u + 1) * n_col + o), part]
    low = low_half((4, 128))
    first = jnp.where(low, even, pltpu.roll(odd, 64, 1))
    second = jnp.where(low, pltpu.roll(even, 64, 1), odd)
    return first, second


PAIRS = [(i, j) for i in range(ITERS) for j in range(i, ITERS)]


def place_of(j):
    lane = lax.broadcasted_iota(jnp.int32, (ROWS, 128), 1)
    return lane == lax.broadcasted_iota(jnp.int32, (ROWS, 128), 0) * (ITERS + 1) + j


def row_sum(acc):
    return jnp.sum(acc, axis=1, keepdims=True)


def lines_of(chunk):
    if isinstance(chunk, int):
        return pl.ds(chunk * 128, 128)
    return pl.ds(pl.multiple_of(chunk * 128, 128), 128)


def write_columns(cols, places, chunk, vec):
    y = places[chunk]
    ys = [y[a : a + 1] for a in range(3)]
    f = [vec[a] for a in range(3)]
    g = ys[0] * f[0] + ys[1] * f[1] + ys[2] * f[2]
    groups = f + [g]
    groups += [ys[p] * f[v] for p in range(3) for v in range(3)]
    groups += [ys[a] * g for a in range(3)]
    full = jnp.concatenate(groups, axis=0)
    high = full.astype(BF16)
    low = (full - high.astype(F32)).astype(BF16)
    at = lines_of(chunk)
    cols[0:128, at] = high
    cols[128:256, at] = low


def apply_rows(cols, kernels, targets, own):
    total = cols.shape[1]
    step = min(total, 2048)

    def turn(i, acc):
        at = pl.ds(pl.multiple_of(i * step, step), step)
        return acc + jnp.dot(cols[:, at], kernels[at, :], preferred_element_type=F32)

    if total == step:
        prod = jnp.dot(cols[...], kernels[...], preferred_element_type=F32)
    else:
        prod = lax.fori_loop(0, total // step, turn, jnp.zeros((256, 256), F32))
    both = prod[:128, :128] + (prod[128:, :128] + prod[:128, 128:])
    two = pltpu.roll(both, 64, 1)

    def group(k):
        return two[8 * k : 8 * k + 8]

    x = [targets[a : a + 1] for a in range(3)]
    images = []
    along = x[0] * group(0) + x[1] * group(1) + x[2] * group(2) - group(3)
    for a in range(3):
        cross = sum(x[b] * group(4 + 3 * a + b) for b in range(3))
        image = both[8 * a : 8 * a + 8] + x[a] * along - cross + group(13 + a)
        images.append(image + targets[3:4] * own[a])
    return images


def write_piece(images, out):
    rows = []
    for image in images:
        top, bottom = image[:4], pltpu.roll(image[4:], 64, 1)
        rows.append(jnp.where(low_half((4, 128)), top, bottom))

    def put(m):
        for a in range(3):
            out[m, a] = rows[a]

    each_wide(out.shape[0], put)


def each_wide(count, put):
    if count <= 64:
        for m in range(count):
            put(m)
    else:
        pl.loop(0, count)(put)


def pack_kernel(velocity, points, area, self_term, out, tgt):
    rhs = velocity.shape[0]
    field = velocity[...]
    rows = []
    for a in range(3):
        vec = field[:, a, :]
        rows.append(jnp.concatenate([vec[:4], jnp.concatenate([vec[4:], vec[: ROWS - rhs]], axis=0)], axis=1))
    where = points[...]
    place = jnp.concatenate([where, area[...]], axis=0)
    rows.append(jnp.concatenate([place, place], axis=1))
    mine = jnp.concatenate([where, self_term[...]], axis=0)
    mine = jnp.concatenate([mine, mine], axis=1)
    tgt[...] = jnp.concatenate([mine, mine], axis=0)

    def put(m):
        for a in range(4):
            out[m, a] = rows[a]

    each_wide(out.shape[0], put)


def near_kernel(index, weight, me, *outs):
    row, col = me[1], me[2]
    half = index.shape[0] // 2
    low = low_half((half, 128))
    for o, out in enumerate(outs):
        to = col ^ o
        at = lines_of(to // 2)
        odd = to % 2 == 1
        place = index[:, at]
        place = (((place // 64) ^ row) * 64 + place % 64).astype(F32)
        for i, value in enumerate((place, weight[:, at])):
            top, bottom = value[:half], value[half:]
            lower = jnp.where(low, top, pltpu.roll(bottom, 64, 1))
            upper = jnp.where(low, pltpu.roll(top, 64, 1), bottom)
            out[i] = jnp.where(odd, upper, lower)


def extra_kernel(half_chunks, *refs):
    near, out = refs[:-1], refs[-1]
    low = low_half((128, 128))
    lines = lax.broadcasted_iota(jnp.int32, (128, 128), 0)
    for o, pair in enumerate(near):
        index, weight = pair[0], pair[1]

        def build(u):
            line = (lines + u * 128).astype(F32)
            total = jnp.zeros((128, 128), F32)
            for k in range(index.shape[0]):
                total = total + jnp.where(line == index[k : k + 1], weight[k : k + 1], 0.0)
            total = total + pltpu.roll(total, 64, 1)
            out[o * half_chunks + u] = jnp.where(low, total, 0.0)

        pl.loop(0, half_chunks)(build)


def first_kernel(n_row, n_col, piece, extra, tgt, me_ref, kernels, places, basis, norm_out, out, cols):
    n_chunk = n_row * n_col // 2
    me = me_ref[0]

    def unpack(chunk):
        first, _ = chunk_parts(piece, chunk, me, n_row, n_col, 3)
        places[chunk] = jnp.concatenate([first, first], axis=0)
        for a in range(3):
            parts = chunk_parts(piece, chunk, me, n_row, n_col, a)
            basis[chunk, a] = jnp.concatenate(parts, axis=0)

    each(n_chunk, unpack)
    (square,) = dots([(basis, basis)], n_chunk)
    norm = jnp.sqrt(square)
    norm_out[...] = jnp.broadcast_to(norm, (ROWS, 128))
    scale = jnp.broadcast_to(1.0 / norm, (ROWS, 128))
    low = low_half((128, 128))
    x = [tgt[a : a + 1] for a in range(3)]

    def build(chunk):
        vec = [basis[chunk, a] * scale for a in range(3)]
        for a in range(3):
            basis[chunk, a] = vec[a]
        write_columns(cols, places, chunk, vec)
        col = places[chunk].T
        d = [x[a] - col[:, a : a + 1] for a in range(3)]
        dist = d[0] * d[0] + d[1] * d[1] + d[2] * d[2]
        root = lax.rsqrt(dist + BLOB_SQ)
        two = (col[:, 3:4] * INV_EIGHT_PI) * root * root * root
        one = (dist + 2.0 * BLOB_SQ) * two
        value = jnp.where(low, one, two) + extra[chunk]
        high = value.astype(BF16)
        at = lines_of(chunk)
        kernels[at, 0:128] = high
        kernels[at, 128:256] = (value - high.astype(F32)).astype(BF16)

    each(n_chunk, build)
    write_piece(apply_rows(cols, kernels, tgt, basis[0]), out)


def middle_kernel(n_row, n_col, n_base, final, piece, *refs):
    bases = refs[:n_base]
    kernels, places, tgt, me_ref, basis, h_out, out, own, cols = refs[n_base:]
    n_chunk = n_row * n_col // 2
    me = me_ref[0]

    def unpack(chunk):
        for a in range(3):
            parts = chunk_parts(piece, chunk, me, n_row, n_col, a)
            basis[chunk, a] = jnp.concatenate(parts, axis=0)

    each(n_chunk, unpack)
    column = []
    for base in bases:
        (h,) = dots([(basis, base)], n_chunk)
        h = jnp.broadcast_to(h, (ROWS, 128))
        column.append(h)

        def take(chunk):
            for a in range(3):
                basis[chunk, a] = basis[chunk, a] - h * base[chunk, a]

        each(n_chunk, take)
    (square,) = dots([(basis, basis)], n_chunk)
    length = jnp.broadcast_to(jnp.sqrt(square), (ROWS, 128))
    column.append(length)
    for j, h in enumerate(column):
        h_out[j] = h
    scale = 1.0 / length

    def columns(chunk):
        vec = [basis[chunk, a] * scale for a in range(3)]
        for a in range(3):
            basis[chunk, a] = vec[a]
        write_columns(cols, places, chunk, vec)

    each(n_chunk, columns)
    images = apply_rows(cols, kernels, tgt, basis[0])
    every = [*bases, basis]
    for j, base in enumerate(every):
        own[j] = base[0]
    if not final:
        write_piece(images, out)
        return
    grams = dots([(every[i], every[j]) for i, j in PAIRS], n_chunk)
    for at, gram in enumerate(grams):
        h_out[len(column) + at] = jnp.broadcast_to(gram, (ROWS, 128))
    low = low_half((ROWS, 128))
    row = jnp.zeros((ROWS, 128), F32)
    for j in range(ITERS + 1):
        other = images if j == ITERS else [every[j][0, a] for a in range(3)]
        part = sum(images[a] * other[a] for a in range(3))
        part = row_sum(jnp.where(low, part, 0.0))
        row = row + jnp.where(place_of(j), part, 0.0)
    row = jnp.sum(row, axis=0, keepdims=True)

    def put(m):
        out[m] = row

    each_wide(out.shape[0], put)


def solve_small(hessen, start_norm, count):
    zero = jnp.zeros_like(start_norm)
    target = [start_norm] + [zero] * count
    cosines = []
    sines = []
    triangle = {}
    for k in range(count):
        column = [hessen[i, k] for i in range(k + 2)]
        for j in range(k):
            first_val = column[j]
            second_val = column[j + 1]
            column[j] = cosines[j] * first_val + sines[j] * second_val
            column[j + 1] = cosines[j] * second_val - sines[j] * first_val
        radius = jnp.sqrt(column[k] * column[k] + column[k + 1] * column[k + 1])
        cosine = column[k] / radius
        sine = column[k + 1] / radius
        cosines.append(cosine)
        sines.append(sine)
        for i in range(k):
            triangle[i, k] = column[i]
        triangle[k, k] = radius
        target[k + 1] = -sine * target[k]
        target[k] = cosine * target[k]
    coeffs = [None] * count
    for k in range(count - 1, -1, -1):
        accum = target[k]
        for i in range(k + 1, count):
            accum = accum - triangle[k, i] * coeffs[i]
        coeffs[k] = accum / triangle[k, k]
    return coeffs


def last_kernel(sums, own, *refs):
    columns = refs[: ITERS - 1]
    norm, out = refs[ITERS - 1 :]
    hessen = {}
    for k in range(ITERS - 1):
        for j in range(k + 2):
            hessen[j, k] = columns[k][j]
    gram = {}
    for at, (i, j) in enumerate(PAIRS):
        gram[i, j] = gram[j, i] = columns[-1][ITERS + at]
    row = jnp.broadcast_to(jnp.sum(sums[...], axis=0), (ROWS, 128))
    inner = [
        jnp.broadcast_to(row_sum(jnp.where(place_of(j), row, 0.0)), (ROWS, 128))
        for j in range(ITERS + 1)
    ]
    square = inner[ITERS]
    for j in range(ITERS):
        h = inner[j]
        for i in range(j):
            h = h - hessen[i, ITERS - 1] * gram[i, j]
        hessen[j, ITERS - 1] = h
    for j in range(ITERS):
        rest = -2.0 * inner[j]
        for i in range(ITERS):
            rest = rest + hessen[i, ITERS - 1] * gram[i, j]
        square = square + hessen[j, ITERS - 1] * rest
    hessen[ITERS, ITERS - 1] = jnp.sqrt(jnp.maximum(square, 0.0))
    coeffs = solve_small(hessen, norm[...], ITERS)
    for a in range(3):
        density = sum(coeffs[k] * own[k, a] for k in range(ITERS))
        out[:, a, :] = density[: out.shape[0], :64]


def call(kernel, outs, scratch, operands, scalars=(), flops=0):
    vmem = pl.BlockSpec(memory_space=pltpu.VMEM)
    smem = pl.BlockSpec(memory_space=pltpu.SMEM)
    count = len(operands)
    specs = [smem if i in scalars else vmem for i in range(count)]
    moved = sum(x.size * x.dtype.itemsize for x in operands)
    return pl.pallas_call(
        kernel,
        out_shape=[jax.ShapeDtypeStruct(s, t) for s, t in outs],
        in_specs=specs,
        out_specs=[vmem] * len(outs),
        scratch_shapes=[pltpu.VMEM(s, t) for s, t in scratch],
        cost_estimate=pl.CostEstimate(flops=flops, bytes_accessed=moved, transcendentals=0),
        compiler_params=pltpu.CompilerParams(vmem_limit_bytes=48 * 1024 * 1024),
    )(*operands)


def body(sizes, velocity, points, panel_area, self_term, near_index, near_weight):
    n_row, n_col = sizes[0] * sizes[1] * sizes[2], sizes[3]
    n = n_row * n_col
    n_chunk = n // 2
    total = n * 64
    row = lax.axis_index(AXES[:3])
    col = lax.axis_index("col")
    me = jnp.stack([row * n_col + col, row, col]).astype(jnp.int32)
    rhs = velocity.shape[0]

    wide, tgt = call(
        pack_kernel,
        [((n, 4, 4, 128), F32), ((8, 128), F32)],
        [],
        [velocity, points, panel_area[None], self_term[None]],
    )
    piece = lax.all_to_all(wide, AXES, 0, 0, tiled=True)

    near = call(
        near_kernel,
        [((2, near_index.shape[1] // 2, 128), F32)] * n_col,
        [],
        [near_index.T, near_weight.T, me],
        {2},
    )
    near = [
        lax.ppermute(pair, "col", xor_perm(n_col, o)) if o else pair
        for o, pair in enumerate(near)
    ]
    (extra,) = call(
        functools.partial(extra_kernel, n_row // 2),
        [((n_chunk, 128, 128), F32)],
        [],
        near,
        flops=10**9,
    )

    vec_shape = (n_chunk, 3, ROWS, 128)
    cols = ((256, total), BF16)
    kernels, places, basis, norm, wide = call(
        functools.partial(first_kernel, n_row, n_col),
        [
            ((total, 256), BF16),
            ((n_chunk, ROWS, 128), F32),
            (vec_shape, F32),
            ((ROWS, 128), F32),
            ((n, 3, 4, 128), F32),
        ],
        [cols],
        [piece, extra, tgt, me],
        {3},
    )
    bases = [basis]
    columns = []
    for k in range(1, ITERS):
        final = k == ITERS - 1
        piece = lax.all_to_all(wide, AXES, 0, 0, tiled=True)
        basis, column, wide, own = call(
            functools.partial(middle_kernel, n_row, n_col, k, final),
            [
                (vec_shape, F32),
                ((k + 1 + (len(PAIRS) if final else 0), ROWS, 128), F32),
                ((n, 1, 128) if final else (n, 3, 4, 128), F32),
                ((k + 1, 3, ROWS, 128), F32),
            ],
            [cols],
            [piece, *bases, kernels, places, tgt, me],
            {k + 4},
        )
        bases.append(basis)
        columns.append(column)
    sums = lax.all_to_all(wide, AXES, 0, 0, tiled=True)
    (density,) = call(
        last_kernel, [((rhs, 3, 64), F32)], [], [sums, own, *columns, norm]
    )
    return density


def solution(mesh):
    n_row, n_col = mesh.shape["row"], mesh.shape["col"]
    sizes = (n_row // 4, 2, 2, n_col)
    split = jax.sharding.Mesh(mesh.devices.reshape(sizes), AXES)
    return jax.shard_map(
        functools.partial(body, sizes),
        mesh=split,
        in_specs=(
            P(None, None, AXES),
            P(None, AXES),
            P(AXES),
            P(AXES),
            P(AXES[:3], "col"),
            P(AXES[:3], "col"),
        ),
        out_specs=P(None, None, AXES),
        check_vma=False,
    )
```

time: 75.5 us -> 60.9 us (0.81)
  waiting for transfers between devices: 22.9 us -> 5.41 us
  blocking collectives: 18 us -> 32.1 us
  starting transfers between devices: 14.9 us -> 9.12 us
  local copies, waits for them, and re-layouts: 6.19 us -> 2.01 us
  Pallas kernels: 12.4 us -> 11.6 us
    all_to_all x3 -> x1, waiting for transfers between devices: 20.5 us -> 3.39 us  [body(): piece = lax.all_to_all(wide, AXES, 0, 0, tiled=True)]
    all_to_all x2 -> x3, blocking collectives: 18 us -> 32.1 us  [the longest x2 23.2 us: body(): piece = lax.all_to_all(wide, AXES, 0, 0, tiled=True)]
    all_to_all x3 -> x1, starting transfers between devices: 13.2 us -> 7.3 us  [body(): piece = lax.all_to_all(wide, AXES, 0, 0, tiled=True)]
    broadcast_in_dim x5 -> x0, local copies, waits for them, and re-layouts: 2.07 us -> none  [spread(): wide = jnp.broadcast_to(piece[None], (size,) + piece.shape)]
    pallas_call x4 -> x7, Pallas kernels: 12.4 us -> 11.6 us  [call(): pl.pallas_call(kernel, out_shape=[jax.ShapeDtypeStruct(s, t) for s, t in...]
    slice x4 -> x0, local copies, waits for them, and re-layouts: 0.78 us -> none  [the longest x1 0.77 us: pack(): return jnp.concatenate([rows[..., :4, :], rows[..., 4:, :]], axis=-1)]
    ppermute x2 -> x1, waiting for transfers between devices: 2.47 us -> 2.02 us  [body(): lax.ppermute(pair, 'col', xor_perm(n_col, o))]
    ppermute x2 -> x1, starting transfers between devices: 1.78 us -> 1.83 us  [body(): lax.ppermute(pair, 'col', xor_perm(n_col, o))]
  transfers between devices with their start and end apart: 5 -> 2, of which waited for: 5 -> 2; matrix products, arithmetic and copies ran while one was open for 1% -> 0% of each run, Pallas kernels for 0% -> 5%
where the time goes in v3:
time: 60.9 us; the launch traced here: 60.4 us
  blocking collectives  32.1 us (53%)
  Pallas kernels  11.6 us (19%)
  starting transfers between devices  9.12 us (15%)
  waiting for transfers between devices  5.41 us (9%)
  local copies, waits for them, and re-layouts  2.01 us (3%)
    all_to_all x2, blocking collectives, body(): piece = lax.all_to_all(wide, AXES, 0, 0, tiled=True)  23.2 us
    pallas_call x7, Pallas kernels, call(): pl.pallas_call(kernel, out_shape=[jax.ShapeDtypeStruct(s, t) for s, t in...  11.6 us
    all_to_all x1, blocking collectives, body(): sums = lax.all_to_all(wide, AXES, 0, 0, tiled=True)  8.94 us
    all_to_all x1, starting transfers between devices, body(): piece = lax.all_to_all(wide, AXES, 0, 0, tiled=True)  7.3 us
    all_to_all x1, waiting for transfers between devices, body(): piece = lax.all_to_all(wide, AXES, 0, 0, tiled=True)  3.39 us
    ppermute x1, waiting for transfers between devices, body(): lax.ppermute(pair, 'col', xor_perm(n_col, o))  2.02 us
    unnamed x12, local copies, waits for them, and re-layouts  2.01 us
    ppermute x1, starting transfers between devices, body(): lax.ppermute(pair, 'col', xor_perm(n_col, o))  1.83 us
  transfers between devices with their start and end apart: 2, of which 2 were waited for; matrix products, arithmetic and copies ran while one was open for 0% of the time, Pallas kernels for 5%

profile of v3, /device:TPU:0, one launch (start us, length us, event | category | flops | bytes accessed | tf_op | source)
XLA Modules:
  0.0 60.4 jit_solution(17438840632654966562)
XLA Ops:
  0.0 0.0 copy-start.3
  0.0 0.0 copy-start.4
  0.0 0.0 copy-start.5
  0.0 0.7 %copy-done.3 = f32[3,64]{1,0:T(4,128)S(1)} copy-done((f32[3,64]{1,0:T(4,128)S(1)}, f32[3,64]{1,0:T(4,128)}, u32[]{:S(2)}) %copy-start.3) | copy-done | bytes 792
  0.7 0.0 copy-done.4
  0.7 0.0 copy-done.5
  0.7 0.0 copy-start
  0.7 0.7 %copy-done = f32[6,3,64]{2,1,0:T(4,128)S(1)} copy-done((f32[6,3,64]{2,1,0:T(4,128)S(1)}, f32[6,3,64]{2,1,0:T(4,128)}, u32[]{:S(2)}) %copy-start) | copy-done | bytes 4632
  1.4 0.8 %shard_map.64 = (f32[32,4,4,128]{3,2,1,0:T(4,128)}, f32[8,128]{1,0:T(8,128)S(1)}) custom-call(f32[6,3,64]{2,1,0:T(4,128)S(1)} %copy-done, f32[3,64]{1,0:T(4,128)S(1)} %copy-done.3, f32[1,64]{1,0:T(1,128)S(1)} %bitcast.9, f32[1,64]{1,0:T(1,128)S(1)} %bitcast.10), custom_call_target="tpu_custom_call" | custom-call | bytes 5888 | tf_op jit(solution)/shard_map/pallas_call | solution.py:390
  2.2 7.3 %all-to-all-start = ((f32[32,4,4,128]{3,2,1,0:T(4,128)}), f32[32,4,4,128]{3,2,1,0:T(4,128)S(1)}, u32[]{:S(2)}, u32[]{:S(2)}) async-start(f32[32,4,4,128]{3,2,1,0:T(4,128)} %get-tuple-element.20), calls=%async_computation | async-start | bytes 524288 | tf_op jit(solution)/shard_map/all_to_all | solution.py:417
  9.5 0.0 copy-start.2
  9.5 0.0 copy-start.1
  9.5 0.1 pad_add_fusion.me.me_ref.refs_4_.refs_5_
  9.6 0.6 copy-done.2
  10.2 0.0 copy-done.1
  10.2 0.6 %shard_map.65 = (f32[2,8,128]{2,1,0:T(8,128)S(1)}, f32[2,8,128]{2,1,0:T(8,128)S(1)}) custom-call(s32[16,128]{1,0:T(8,128)S(1)} %bitcast.7, f32[16,128]{1,0:T(8,128)S(1)} %bitcast.8, s32[3]{0:T(128)S(1)} %pad_add_fusion.me.me_ref.refs_4_.refs_5_), custom_call_target="tpu_custom_call" | custom-call | bytes 16396 | tf_op jit(solution)/shard_map/pallas_call | solution.py:390
  10.9 1.8 %collective-permute-start = (f32[2,8,128]{2,1,0:T(8,128)S(1)}, f32[2,8,128]{2,1,0:T(8,128)S(1)}, u32[]{:S(2)}, u32[]{:S(2)}) collective-permute-start(f32[2,8,128]{2,1,0:T(8,128)S(1)} %get-tuple-element.22), channel_id=1, source_target_pairs={{0,1},{1,0},{2,3},{3,2},{4,5},{5,4},{6,7},{7,6},{8,9},{9,8},{10,11... | collective-permute-start | bytes 24584 | tf_op jit(solution)/shard_map/ppermute | solution.py:427
  12.7 2.0 %collective-permute-done.refs_1_ = f32[2,8,128]{2,1,0:T(8,128)S(1)} collective-permute-done((f32[2,8,128]{2,1,0:T(8,128)S(1)}, f32[2,8,128]{2,1,0:T(8,128)S(1)}, u32[]{:S(2)}, u32[]{:S(2)}) %collective-permute-start) | collective-permute-done | bytes 8224 | tf_op jit(solution)/shard_map/ppermute | solution.py:427
  14.7 2.1 %shard_map.66.extra = f32[16,128,128]{2,1,0:T(8,128)S(1)} custom-call(f32[2,8,128]{2,1,0:T(8,128)S(1)} %get-tuple-element.21.refs_0_, f32[2,8,128]{2,1,0:T(8,128)S(1)} %collective-permute-done.refs_1_), custom_call_target="tpu_custom_call" | custom-call | flops 1000000000 | bytes 16384 | tf_op jit(solution)/shard_map/pallas_call | solution.py:390
  16.8 3.4 %all-to-all-done.piece = f32[32,4,4,128]{3,2,1,0:T(4,128)S(1)} async-done(((f32[32,4,4,128]{3,2,1,0:T(4,128)}), f32[32,4,4,128]{3,2,1,0:T(4,128)S(1)}, u32[]{:S(2)}, u32[]{:S(2)}) %all-to-all-start) | async-done | bytes 262176 | tf_op jit(solution)/shard_map/all_to_all | solution.py:417
  20.2 2.9 %shard_map.67 = (bf16[2048,256]{1,0:T(8,128)(2,1)S(1)}, f32[16,8,128]{2,1,0:T(8,128)S(1)}, f32[16,3,8,128]{3,2,1,0:T(8,128)S(1)}, f32[8,128]{1,0:T(8,128)S(1)}, f32[32,3,4,128]{3,2,1,0:T(4,128)S(1)}) custom-call(f32[32,4,4,128]{3,2,1,0:T(4,128)S(1)} %all-to-all-done.piece, f32[16,128,128]{2,1,0:T(8,128)S(1)} %shard_map.66.extra, ...), custom_call_target="tpu_custom_call" | custom-call | bytes 1314828 | tf_op jit(solution)/shard_map/pallas_call | solution.py:390
  23.1 11.8 %all_to_all.20.piece = f32[32,3,4,128]{3,2,1,0:T(4,128)S(1)} all-to-all(f32[32,3,4,128]{3,2,1,0:T(4,128)S(1)} %get-tuple-element.24), channel_id=1, replica_groups=mesh['top'=4,'mid'=2,'core'=2,'col'=2] {'top','mid','core','col'}, dimensions={0} | all-to-all | bytes 393216 | tf_op jit(solution)/shard_map/all_to_all | solution.py:457
  34.9 2.1 %shard_map.68 = (f32[16,3,8,128]{3,2,1,0:T(8,128)S(1)}, f32[2,8,128]{2,1,0:T(8,128)S(1)}, f32[32,3,4,128]{3,2,1,0:T(4,128)S(1)}, f32[2,3,8,128]{3,2,1,0:T(8,128)}) custom-call(f32[32,3,4,128]{3,2,1,0:T(4,128)S(1)} %all_to_all.20.piece, f32[16,3,8,128]{3,2,1,0:T(8,128)S(1)} %get-tuple-element.25.refs_0_, ...), custom_call_target="tpu_custom_call" | custom-call | bytes 1511436 | tf_op jit(solution)/shard_map/pallas_call | solution.py:390
  37.0 11.4 %all_to_all.21.piece = f32[32,3,4,128]{3,2,1,0:T(4,128)S(1)} all-to-all(f32[32,3,4,128]{3,2,1,0:T(4,128)S(1)} %get-tuple-element.28), channel_id=1, replica_groups=mesh['top'=4,'mid'=2,'core'=2,'col'=2] {'top','mid','core','col'}, dimensions={0} | all-to-all | bytes 393216 | tf_op jit(solution)/shard_map/all_to_all | solution.py:457
  48.4 2.3 %shard_map.69 = (f32[16,3,8,128]{3,2,1,0:T(8,128)}, f32[9,8,128]{2,1,0:T(8,128)S(1)}, f32[32,1,128]{2,1,0:T(1,128)S(1)}, f32[3,3,8,128]{3,2,1,0:T(8,128)S(1)}) custom-call(f32[32,3,4,128]{3,2,1,0:T(4,128)S(1)} %all_to_all.21.piece, f32[16,3,8,128]{3,2,1,0:T(8,128)S(1)} %get-tuple-element.25.refs_0_, f32[16,3,8,128]{3,2,1,0:T(8,128)S(1)} %get-tuple-element.29.refs_1_, ...), custom_call_target="tpu_custom_call" | custom-call | bytes 1708044 | tf_op jit(solution)/shard_map/pallas_call | solution.py:390
  50.7 8.9 %all_to_all.22.sums = f32[32,1,128]{2,1,0:T(1,128)S(1)} all-to-all(f32[32,1,128]{2,1,0:T(1,128)S(1)} %get-tuple-element.30), channel_id=1, replica_groups=mesh['top'=4,'mid'=2,'core'=2,'col'=2] {'top','mid','core','col'}, dimensions={0} | all-to-all | bytes 32768 | tf_op jit(solution)/shard_map/all_to_all | solution.py:472
  59.6 0.8 %shard_map.70 = f32[6,3,64]{2,1,0:T(4,128)} custom-call(f32[32,1,128]{2,1,0:T(1,128)S(1)} %all_to_all.22.sums, f32[3,3,8,128]{3,2,1,0:T(8,128)S(1)} %get-tuple-element.31.own, f32[2,8,128]{2,1,0:T(8,128)S(1)} %get-tuple-element.32.refs_0_, f32[9,8,128]{2,1,0:T(8,128)S(1)} %get-tuple-element.33.refs_1_, f32[8,128]{1,0:T(8,128)S(1)} %get-tuple-element.34.refs_2_), custom_call_target="tpu_custom_call" | custom-call | bytes 102400 | tf_op jit(solution)/shard_map/pallas_call | solution.py:390
Async XLA Ops:
  0.0 0.7 %copy-start.3 = (f32[3,64]{1,0:T(4,128)S(1)}, f32[3,64]{1,0:T(4,128)}, u32[]{:S(2)}) copy-start(f32[3,64]{1,0:T(4,128)} %points.1) | copy-start | bytes 2308
  0.0 0.7 %copy-start.4 = (f32[64]{0:T(128)S(1)}, f32[64]{0:T(128)}, u32[]{:S(2)}) copy-start(f32[64]{0:T(128)} %param.8) | copy-start | bytes 772
  0.0 0.7 %copy-start.5 = (f32[64]{0:T(128)S(1)}, f32[64]{0:T(128)}, u32[]{:S(2)}) copy-start(f32[64]{0:T(128)} %param.9) | copy-start | bytes 772
  0.7 0.7 %copy-start = (f32[6,3,64]{2,1,0:T(4,128)S(1)}, f32[6,3,64]{2,1,0:T(4,128)}, u32[]{:S(2)}) copy-start(f32[6,3,64]{2,1,0:T(4,128)} %velocity.1) | copy-start | bytes 13828
  2.2 18.0 %all-to-all-start = ((f32[32,4,4,128]{3,2,1,0:T(4,128)}), f32[32,4,4,128]{3,2,1,0:T(4,128)S(1)}, u32[]{:S(2)}, u32[]{:S(2)}) async-start(f32[32,4,4,128]{3,2,1,0:T(4,128)} %get-tuple-element.20), calls=%async_computation | async-start | bytes 524288 | tf_op jit(solution)/shard_map/all_to_all | solution.py:417
  9.5 0.7 %copy-start.2 = (f32[128,16]{0,1:T(8,128)S(1)}, f32[128,16]{0,1:T(8,128)}, u32[]{:S(2)}) copy-start(f32[128,16]{0,1:T(8,128)} %param.11) | copy-start | bytes 24580
  9.5 0.7 %copy-start.1 = (s32[128,16]{0,1:T(8,128)S(1)}, s32[128,16]{0,1:T(8,128)}, u32[]{:S(2)}) copy-start(s32[128,16]{0,1:T(8,128)} %param.10) | copy-start | bytes 24580
  10.9 3.8 %collective-permute-start = (f32[2,8,128]{2,1,0:T(8,128)S(1)}, f32[2,8,128]{2,1,0:T(8,128)S(1)}, u32[]{:S(2)}, u32[]{:S(2)}) collective-permute-start(f32[2,8,128]{2,1,0:T(8,128)S(1)} %get-tuple-element.22), channel_id=1, source_target_pairs={{0,1},{1,0},{2,3},{3,2},{4,5},{5,4},{6,7},{7,6},{8,9},{9,8},{10,11... | collective-permute-start | bytes 24584 | tf_op jit(solution)/shard_map/ppermute | solution.py:427

commit v4 on v3

--- a/solution.py
+++ b/solution.py
@@ -42,25 +42,30 @@
         pl.loop(0, count)(step)
 
 
-def dots(pairs, n_chunk):
-    lanes = 4
-    zero = jnp.zeros((ROWS, 128), F32)
-
-    def step(chunk, accs):
-        slot = chunk % lanes if isinstance(chunk, int) else 0
-        for at, (left, right) in enumerate(pairs):
-            part = sum(left[chunk, a] * right[chunk, a] for a in range(3))
-            accs[at][slot] = accs[at][slot] + part
-        return accs
-
-    accs = [[zero] * lanes for _ in pairs]
-    if n_chunk <= 16:
-        for chunk in range(n_chunk):
-            accs = step(chunk, accs)
-    else:
-        accs = lax.fori_loop(0, n_chunk, step, accs)
-    sums = [(acc[0] + acc[1]) + (acc[2] + acc[3]) for acc in accs]
-    return [jnp.sum(acc, axis=1, keepdims=True) for acc in sums]
+class Sums:
+    def __init__(self, count, refs):
+        self.refs = refs
+        self.parts = [[None] * 4 for _ in range(count)]
+        if refs is not None:
+            for at in range(count):
+                refs[at] = jnp.zeros((ROWS, 128), F32)
+
+    def add(self, chunk, at, left, right):
+        part = sum(left[a] * right[a] for a in range(3))
+        if self.refs is not None:
+            self.refs[at] = self.refs[at] + part
+            return
+        held = self.parts[at]
+        slot = chunk % 4
+        held[slot] = part if held[slot] is None else held[slot] + part
+
+    def get(self, at):
+        if self.refs is not None:
+            total = self.refs[at]
+        else:
+            held = self.parts[at]
+            total = (held[0] + held[1]) + (held[2] + held[3])
+        return jnp.broadcast_to(jnp.sum(total, axis=1, keepdims=True), (ROWS, 128))
 
 
 def chunk_parts(piece, chunk, me, n_row, n_col, part):
@@ -75,7 +80,7 @@
     return first, second
 
 
-PAIRS = [(i, j) for i in range(ITERS) for j in range(i, ITERS)]
+PAIRS = [(i, j) for i in range(ITERS) for j in range(i + 1, ITERS)]
 
 
 def place_of(j):
@@ -93,8 +98,7 @@
     return pl.ds(pl.multiple_of(chunk * 128, 128), 128)
 
 
-def write_columns(cols, places, chunk, vec):
-    y = places[chunk]
+def write_columns(cols, y, chunk, vec):
     ys = [y[a : a + 1] for a in range(3)]
     f = [vec[a] for a in range(3)]
     g = ys[0] * f[0] + ys[1] * f[1] + ys[2] * f[2]
@@ -109,7 +113,7 @@
     cols[128:256, at] = low
 
 
-def apply_rows(cols, kernels, targets, own):
+def apply_rows(cols, kernels, targets, own, scale):
     total = cols.shape[1]
     step = min(total, 2048)
 
@@ -133,7 +137,7 @@
     for a in range(3):
         cross = sum(x[b] * group(4 + 3 * a + b) for b in range(3))
         image = both[8 * a : 8 * a + 8] + x[a] * along - cross + group(13 + a)
-        images.append(image + targets[3:4] * own[a])
+        images.append((image + targets[3:4] * own[a]) * scale)
     return images
 
 
@@ -158,42 +162,52 @@
         pl.loop(0, count)(put)
 
 
-def pack_kernel(velocity, points, area, self_term, out, tgt):
+def pack_kernel(n_col, *refs):
+    sources, me = refs[:6], refs[6]
+    out, tgt = refs[7:9]
+    near = refs[9 : 9 + n_col]
+    held, sems = refs[9 + n_col : 15 + n_col], refs[15 + n_col]
+    copies = [
+        pltpu.make_async_copy(src, dst, sems.at[i])
+        for i, (src, dst) in enumerate(zip(sources, held))
+    ]
+    for copy in copies:
+        copy.start()
+    for copy in copies:
+        copy.wait()
+    velocity, points, area, self_term, index, weight = held
     rhs = velocity.shape[0]
     field = velocity[...]
+    spot = points[...]
+    place = [jnp.concatenate([spot[2:3], area[...]], axis=0) if a == 1 else spot[:2] for a in range(3)]
     rows = []
     for a in range(3):
         vec = field[:, a, :]
-        rows.append(jnp.concatenate([vec[:4], jnp.concatenate([vec[4:], vec[: ROWS - rhs]], axis=0)], axis=1))
-    where = points[...]
-    place = jnp.concatenate([where, area[...]], axis=0)
-    rows.append(jnp.concatenate([place, place], axis=1))
-    mine = jnp.concatenate([where, self_term[...]], axis=0)
+        rows.append(jnp.concatenate([vec[:4], jnp.concatenate([vec[4:], place[a]], axis=0)], axis=1))
+    mine = jnp.concatenate([spot, self_term[...]], axis=0)
     mine = jnp.concatenate([mine, mine], axis=1)
     tgt[...] = jnp.concatenate([mine, mine], axis=0)
 
     def put(m):
-        for a in range(4):
+        for a in range(3):
             out[m, a] = rows[a]
 
     each_wide(out.shape[0], put)
 
-
-def near_kernel(index, weight, me, *outs):
     row, col = me[1], me[2]
     half = index.shape[0] // 2
     low = low_half((half, 128))
-    for o, out in enumerate(outs):
+    for o in range(n_col):
         to = col ^ o
         at = lines_of(to // 2)
         odd = to % 2 == 1
-        place = index[:, at]
-        place = (((place // 64) ^ row) * 64 + place % 64).astype(F32)
-        for i, value in enumerate((place, weight[:, at])):
+        at_source = index[:, at]
+        at_source = (((at_source // 64) ^ row) * 64 + at_source % 64).astype(F32)
+        for i, value in enumerate((at_source, weight[:, at])):
             top, bottom = value[:half], value[half:]
             lower = jnp.where(low, top, pltpu.roll(bottom, 64, 1))
             upper = jnp.where(low, pltpu.roll(top, 64, 1), bottom)
-            out[i] = jnp.where(odd, upper, lower)
+            near[o][i] = jnp.where(odd, upper, lower)
 
 
 def extra_kernel(half_chunks, *refs):
@@ -214,31 +228,28 @@
         pl.loop(0, half_chunks)(build)
 
 
-def first_kernel(n_row, n_col, piece, extra, tgt, me_ref, kernels, places, basis, norm_out, out, cols):
+def first_kernel(
+    n_row, n_col, piece, extra, tgt, me_ref, kernels, places, basis, norm_out, out, cols, *sums
+):
     n_chunk = n_row * n_col // 2
     me = me_ref[0]
-
-    def unpack(chunk):
-        first, _ = chunk_parts(piece, chunk, me, n_row, n_col, 3)
-        places[chunk] = jnp.concatenate([first, first], axis=0)
-        for a in range(3):
-            parts = chunk_parts(piece, chunk, me, n_row, n_col, a)
-            basis[chunk, a] = jnp.concatenate(parts, axis=0)
-
-    each(n_chunk, unpack)
-    (square,) = dots([(basis, basis)], n_chunk)
-    norm = jnp.sqrt(square)
-    norm_out[...] = jnp.broadcast_to(norm, (ROWS, 128))
-    scale = jnp.broadcast_to(1.0 / norm, (ROWS, 128))
     low = low_half((128, 128))
     x = [tgt[a : a + 1] for a in range(3)]
+    total = Sums(1, sums[0] if sums else None)
 
     def build(chunk):
-        vec = [basis[chunk, a] * scale for a in range(3)]
+        vec = [
+            jnp.concatenate(chunk_parts(piece, chunk, me, n_row, n_col, a), axis=0)
+            for a in range(3)
+        ]
+        spot = jnp.concatenate([vec[0][6:8], vec[1][6:8]], axis=0)
+        spot = jnp.concatenate([spot, spot], axis=0)
+        places[chunk] = spot
         for a in range(3):
             basis[chunk, a] = vec[a]
-        write_columns(cols, places, chunk, vec)
-        col = places[chunk].T
+        total.add(chunk, 0, vec, vec)
+        write_columns(cols, spot, chunk, vec)
+        col = spot.T
         d = [x[a] - col[:, a : a + 1] for a in range(3)]
         dist = d[0] * d[0] + d[1] * d[1] + d[2] * d[2]
         root = lax.rsqrt(dist + BLOB_SQ)
@@ -251,60 +262,85 @@
         kernels[at, 128:256] = (value - high.astype(F32)).astype(BF16)
 
     each(n_chunk, build)
-    write_piece(apply_rows(cols, kernels, tgt, basis[0]), out)
+    norm = jnp.sqrt(total.get(0))
+    scale = 1.0 / norm
+    norm_out[0] = norm
+    norm_out[1] = scale
+    write_piece(apply_rows(cols, kernels, tgt, basis[0], scale), out)
 
 
 def middle_kernel(n_row, n_col, n_base, final, piece, *refs):
-    bases = refs[:n_base]
-    kernels, places, tgt, me_ref, basis, h_out, out, own, cols = refs[n_base:]
+    bases, norms = refs[:n_base], refs[n_base : 2 * n_base]
+    kernels, places, tgt, me_ref, basis, h_out, out, own, cols, *held = refs[2 * n_base :]
     n_chunk = n_row * n_col // 2
     me = me_ref[0]
+    scales = [norm[norm.shape[0] - 1] for norm in norms]
+    cross = [(i, j) for i in range(n_base) for j in range(i)]
+    sums = Sums(2 * n_base + 1 + len(cross), held[0] if held else None)
 
     def unpack(chunk):
-        for a in range(3):
-            parts = chunk_parts(piece, chunk, me, n_row, n_col, a)
-            basis[chunk, a] = jnp.concatenate(parts, axis=0)
-
-    each(n_chunk, unpack)
-    column = []
-    for base in bases:
-        (h,) = dots([(basis, base)], n_chunk)
-        h = jnp.broadcast_to(h, (ROWS, 128))
-        column.append(h)
-
-        def take(chunk):
-            for a in range(3):
-                basis[chunk, a] = basis[chunk, a] - h * base[chunk, a]
-
-        each(n_chunk, take)
-    (square,) = dots([(basis, basis)], n_chunk)
-    length = jnp.broadcast_to(jnp.sqrt(square), (ROWS, 128))
-    column.append(length)
-    for j, h in enumerate(column):
-        h_out[j] = h
-    scale = 1.0 / length
-
-    def columns(chunk):
-        vec = [basis[chunk, a] * scale for a in range(3)]
+        vec = [
+            jnp.concatenate(chunk_parts(piece, chunk, me, n_row, n_col, a), axis=0)
+            for a in range(3)
+        ]
+        old = [[base[chunk, a] for a in range(3)] for base in bases]
         for a in range(3):
             basis[chunk, a] = vec[a]
-        write_columns(cols, places, chunk, vec)
+        for j in range(n_base):
+            sums.add(chunk, j, vec, old[j])
+        for at, (i, j) in enumerate(cross):
+            sums.add(chunk, 2 * n_base + 1 + at, old[i], old[j])
+
+    each(n_chunk, unpack)
+    gram = {}
+    for at, (i, j) in enumerate(cross):
+        gram[j, i] = sums.get(2 * n_base + 1 + at) * (scales[i] * scales[j])
+    column = []
+    for j in range(n_base):
+        h = sums.get(j) * scales[j]
+        for i in range(j):
+            h = h - column[i] * gram[i, j]
+        column.append(h)
+        h_out[j] = h
+    factors = [h * scale for h, scale in zip(column, scales)]
+
+    def columns(chunk):
+        old = [[base[chunk, a] for a in range(3)] for base in bases]
+        vec = []
+        for a in range(3):
+            value = basis[chunk, a]
+            for j in range(n_base):
+                value = value - factors[j] * old[j][a]
+            vec.append(value)
+            basis[chunk, a] = value
+        sums.add(chunk, n_base, vec, vec)
+        write_columns(cols, places[chunk], chunk, vec)
+        if final:
+            for j in range(n_base):
+                sums.add(chunk, n_base + 1 + j, vec, old[j])
 
     each(n_chunk, columns)
-    images = apply_rows(cols, kernels, tgt, basis[0])
+    norm = jnp.sqrt(sums.get(n_base))
+    scale = 1.0 / norm
+    h_out[n_base] = norm
+    images = apply_rows(cols, kernels, tgt, basis[0], scale)
     every = [*bases, basis]
+    scales = [*scales, scale]
     for j, base in enumerate(every):
-        own[j] = base[0]
+        for a in range(3):
+            own[j, a] = base[0, a] * scales[j]
     if not final:
+        h_out[n_base + 1] = scale
         write_piece(images, out)
         return
-    grams = dots([(every[i], every[j]) for i, j in PAIRS], n_chunk)
-    for at, gram in enumerate(grams):
-        h_out[len(column) + at] = jnp.broadcast_to(gram, (ROWS, 128))
+    for j in range(n_base):
+        gram[j, n_base] = sums.get(n_base + 1 + j) * (scale * scales[j])
+    for at, pair in enumerate(PAIRS):
+        h_out[n_base + 1 + at] = gram[pair]
     low = low_half((ROWS, 128))
     row = jnp.zeros((ROWS, 128), F32)
     for j in range(ITERS + 1):
-        other = images if j == ITERS else [every[j][0, a] for a in range(3)]
+        other = images if j == ITERS else [own[j, a] for a in range(3)]
         part = sum(images[a] * other[a] for a in range(3))
         part = row_sum(jnp.where(low, part, 0.0))
         row = row + jnp.where(place_of(j), part, 0.0)
@@ -355,7 +391,7 @@
     for k in range(ITERS - 1):
         for j in range(k + 2):
             hessen[j, k] = columns[k][j]
-    gram = {}
+    gram = {(j, j): 1.0 for j in range(ITERS)}
     for at, (i, j) in enumerate(PAIRS):
         gram[i, j] = gram[j, i] = columns[-1][ITERS + at]
     row = jnp.broadcast_to(jnp.sum(sums[...], axis=0), (ROWS, 128))
@@ -375,24 +411,25 @@
             rest = rest + hessen[i, ITERS - 1] * gram[i, j]
         square = square + hessen[j, ITERS - 1] * rest
     hessen[ITERS, ITERS - 1] = jnp.sqrt(jnp.maximum(square, 0.0))
-    coeffs = solve_small(hessen, norm[...], ITERS)
+    coeffs = solve_small(hessen, norm[0], ITERS)
     for a in range(3):
         density = sum(coeffs[k] * own[k, a] for k in range(ITERS))
         out[:, a, :] = density[: out.shape[0], :64]
 
 
-def call(kernel, outs, scratch, operands, scalars=(), flops=0):
+def call(kernel, outs, scratch, operands, scalars=(), far=(), flops=0):
     vmem = pl.BlockSpec(memory_space=pltpu.VMEM)
     smem = pl.BlockSpec(memory_space=pltpu.SMEM)
+    anywhere = pl.BlockSpec(memory_space=pl.ANY)
     count = len(operands)
-    specs = [smem if i in scalars else vmem for i in range(count)]
+    specs = [smem if i in scalars else anywhere if i in far else vmem for i in range(count)]
     moved = sum(x.size * x.dtype.itemsize for x in operands)
     return pl.pallas_call(
         kernel,
         out_shape=[jax.ShapeDtypeStruct(s, t) for s, t in outs],
         in_specs=specs,
         out_specs=[vmem] * len(outs),
-        scratch_shapes=[pltpu.VMEM(s, t) for s, t in scratch],
+        scratch_shapes=scratch,
         cost_estimate=pl.CostEstimate(flops=flops, bytes_accessed=moved, transcendentals=0),
         compiler_params=pltpu.CompilerParams(vmem_limit_bytes=48 * 1024 * 1024),
     )(*operands)
@@ -408,25 +445,29 @@
     me = jnp.stack([row * n_col + col, row, col]).astype(jnp.int32)
     rhs = velocity.shape[0]
 
-    wide, tgt = call(
-        pack_kernel,
-        [((n, 4, 4, 128), F32), ((8, 128), F32)],
-        [],
-        [velocity, points, panel_area[None], self_term[None]],
-    )
-    piece = lax.all_to_all(wide, AXES, 0, 0, tiled=True)
-
-    near = call(
-        near_kernel,
-        [((2, near_index.shape[1] // 2, 128), F32)] * n_col,
-        [],
-        [near_index.T, near_weight.T, me],
-        {2},
+    sources = [
+        velocity,
+        points,
+        panel_area[None],
+        self_term[None],
+        near_index.T,
+        near_weight.T,
+    ]
+    message = ((n, 3, 4, 128), F32)
+    wide, tgt, *near = call(
+        functools.partial(pack_kernel, n_col),
+        [message, ((8, 128), F32)]
+        + [((2, near_index.shape[1] // 2, 128), F32)] * n_col,
+        [pltpu.VMEM(x.shape, x.dtype) for x in sources] + [pltpu.SemaphoreType.DMA((6,))],
+        [*sources, me],
+        {6},
+        range(6),
     )
     near = [
         lax.ppermute(pair, "col", xor_perm(n_col, o)) if o else pair
         for o, pair in enumerate(near)
     ]
+    piece = lax.all_to_all(wide, AXES, 0, 0, tiled=True)
     (extra,) = call(
         functools.partial(extra_kernel, n_row // 2),
         [((n_chunk, 128, 128), F32)],
@@ -436,22 +477,23 @@
     )
 
     vec_shape = (n_chunk, 3, ROWS, 128)
-    cols = ((256, total), BF16)
+    cols = pltpu.VMEM((256, total), BF16)
+    held = [] if n_chunk <= 16 else [pltpu.VMEM((8, ROWS, 128), F32)]
     kernels, places, basis, norm, wide = call(
         functools.partial(first_kernel, n_row, n_col),
         [
             ((total, 256), BF16),
             ((n_chunk, ROWS, 128), F32),
             (vec_shape, F32),
-            ((ROWS, 128), F32),
-            ((n, 3, 4, 128), F32),
+            ((2, ROWS, 128), F32),
+            message,
         ],
-        [cols],
+        [cols, *held],
         [piece, extra, tgt, me],
         {3},
     )
     bases = [basis]
-    columns = []
+    columns = [norm]
     for k in range(1, ITERS):
         final = k == ITERS - 1
         piece = lax.all_to_all(wide, AXES, 0, 0, tiled=True)
@@ -459,19 +501,19 @@
             functools.partial(middle_kernel, n_row, n_col, k, final),
             [
                 (vec_shape, F32),
-                ((k + 1 + (len(PAIRS) if final else 0), ROWS, 128), F32),
-                ((n, 1, 128) if final else (n, 3, 4, 128), F32),
+                ((k + 1 + (len(PAIRS) if final else 1), ROWS, 128), F32),
+                ((n, 1, 128), F32) if final else message,
                 ((k + 1, 3, ROWS, 128), F32),
             ],
-            [cols],
-            [piece, *bases, kernels, places, tgt, me],
-            {k + 4},
+            [cols, *held],
+            [piece, *bases, *columns, kernels, places, tgt, me],
+            {2 * k + 4},
         )
         bases.append(basis)
         columns.append(column)
     sums = lax.all_to_all(wide, AXES, 0, 0, tiled=True)
     (density,) = call(
-        last_kernel, [((rhs, 3, 64), F32)], [], [sums, own, *columns, norm]
+        last_kernel, [((rhs, 3, 64), F32)], [], [sums, own, *columns[1:], columns[0]]
     )
     return density
 

time: 60.9 us -> 60.2 us (0.989)
  local copies, waits for them, and re-layouts: 2.01 us -> 0.68 us
  Pallas kernels: 11.6 us -> 12.4 us
    unnamed x12, local copies, waits for them, and re-layouts: 2.01 us -> 0.68 us
    pallas_call x7 -> x6, Pallas kernels: 11.6 us -> 12.4 us  [call(): pl.pallas_call(kernel, out_shape=[jax.ShapeDtypeStruct(s, t) for s, t in...]
  transfers between devices with their start and end apart: 2 -> 2, of which waited for: 2 -> 2; matrix products, arithmetic and copies ran while one was open for 0% -> 0% of each run, Pallas kernels for 5% -> 3%
where the time goes in v4:
time: 60.2 us; the launch traced here: 59.9 us
  blocking collectives  31.8 us (53%)
  Pallas kernels  12.4 us (21%)
  starting transfers between devices  9.14 us (15%)
  waiting for transfers between devices  5.74 us (10%)
  local copies, waits for them, and re-layouts  0.68 us (1%)
    all_to_all x2, blocking collectives, body(): piece = lax.all_to_all(wide, AXES, 0, 0, tiled=True)  22.9 us
    pallas_call x6, Pallas kernels, call(): pl.pallas_call(kernel, out_shape=[jax.ShapeDtypeStruct(s, t) for s, t in...  12.4 us
    all_to_all x1, blocking collectives, body(): sums = lax.all_to_all(wide, AXES, 0, 0, tiled=True)  8.94 us
    all_to_all x1, starting transfers between devices, body(): piece = lax.all_to_all(wide, AXES, 0, 0, tiled=True)  7.3 us
    all_to_all x1, waiting for transfers between devices, body(): piece = lax.all_to_all(wide, AXES, 0, 0, tiled=True)  3.82 us
    ppermute x1, waiting for transfers between devices, body(): lax.ppermute(pair, 'col', xor_perm(n_col, o))  1.92 us
    ppermute x1, starting transfers between devices, body(): lax.ppermute(pair, 'col', xor_perm(n_col, o))  1.83 us
  transfers between devices with their start and end apart: 2, of which 2 were waited for; matrix products, arithmetic and copies ran while one was open for 0% of the time, Pallas kernels for 3%

profile of v4, /device:TPU:0, one launch (start us, length us, event | category | flops | bytes accessed | tf_op | source)
XLA Modules:
  0.0 59.9 jit_solution(9329634625660810197)
XLA Ops:
  0.0 0.0 copy-start.4
  0.0 0.0 copy-start.5
  0.0 0.0 copy-start.3
  0.0 0.0 copy-start.2
  0.0 0.0 copy-start
  0.0 0.0 copy-start.1
  0.0 0.1 pad_add_fusion.refs_6_.me_ref.refs_5_.refs_7_
  0.1 0.6 copy-done.4
  0.7 0.0 copy-done.5
  0.7 0.0 copy-done.3
  0.7 0.0 copy-done.2
  0.7 0.0 copy-done
  0.8 0.0 copy-done.1
  0.8 1.4 %shard_map.64 = (f32[32,3,4,128]{3,2,1,0:T(4,128)}, f32[8,128]{1,0:T(8,128)S(1)}, f32[2,8,128]{2,1,0:T(8,128)S(1)}, f32[2,8,128]{2,1,0:T(8,128)S(1)}) custom-call(f32[6,3,64]{2,1,0:T(4,128)S(1)} %copy-done, f32[3,64]{1,0:T(4,128)S(1)} %copy-done.3, f32[1,64]{1,0:T(1,128)S(1)} %bitcast.9, f32[1,64]{1,0:T(1,128)S(1)} %bitcast.10, s32[16,128]{1,0:T(8,128)S(1)} %bitcast.7, ...), custom_call_target="tpu_custom_call" | custom-call | bytes 22284 | tf_op jit(solution)/shard_map/pallas_call | solution.py:427
  2.2 7.3 %all-to-all-start = ((f32[32,3,4,128]{3,2,1,0:T(4,128)}), f32[32,3,4,128]{3,2,1,0:T(4,128)S(1)}, u32[]{:S(2)}, u32[]{:S(2)}) async-start(f32[32,3,4,128]{3,2,1,0:T(4,128)} %get-tuple-element.20), calls=%async_computation | async-start | bytes 393216 | tf_op jit(solution)/shard_map/all_to_all | solution.py:470
  9.5 1.8 %collective-permute-start = (f32[2,8,128]{2,1,0:T(8,128)S(1)}, f32[2,8,128]{2,1,0:T(8,128)S(1)}, u32[]{:S(2)}, u32[]{:S(2)}) collective-permute-start(f32[2,8,128]{2,1,0:T(8,128)S(1)} %get-tuple-element.22), channel_id=1, source_target_pairs={{0,1},{1,0},{2,3},{3,2},{4,5},{5,4},{6,7},{7,6},{8,9},{9,8},{10,11... | collective-permute-start | bytes 24584 | tf_op jit(solution)/shard_map/ppermute | solution.py:467
  11.3 1.9 %collective-permute-done.refs_1_ = f32[2,8,128]{2,1,0:T(8,128)S(1)} collective-permute-done((f32[2,8,128]{2,1,0:T(8,128)S(1)}, f32[2,8,128]{2,1,0:T(8,128)S(1)}, u32[]{:S(2)}, u32[]{:S(2)}) %collective-permute-start) | collective-permute-done | bytes 8224 | tf_op jit(solution)/shard_map/ppermute | solution.py:467
  13.3 2.1 %shard_map.65.extra = f32[16,128,128]{2,1,0:T(8,128)S(1)} custom-call(f32[2,8,128]{2,1,0:T(8,128)S(1)} %get-tuple-element.21.refs_0_, f32[2,8,128]{2,1,0:T(8,128)S(1)} %collective-permute-done.refs_1_), custom_call_target="tpu_custom_call" | custom-call | flops 1000000000 | bytes 16384 | tf_op jit(solution)/shard_map/pallas_call | solution.py:427
  15.3 3.8 %all-to-all-done.piece = f32[32,3,4,128]{3,2,1,0:T(4,128)S(1)} async-done(((f32[32,3,4,128]{3,2,1,0:T(4,128)}), f32[32,3,4,128]{3,2,1,0:T(4,128)S(1)}, u32[]{:S(2)}, u32[]{:S(2)}) %all-to-all-start) | async-done | bytes 196640 | tf_op jit(solution)/shard_map/all_to_all | solution.py:470
  19.2 4.4 %shard_map.66 = (bf16[2048,256]{1,0:T(8,128)(2,1)S(1)}, f32[16,8,128]{2,1,0:T(8,128)S(1)}, f32[16,3,8,128]{3,2,1,0:T(8,128)S(1)}, f32[2,8,128]{2,1,0:T(8,128)S(1)}, f32[32,3,4,128]{3,2,1,0:T(4,128)S(1)}) custom-call(f32[32,3,4,128]{3,2,1,0:T(4,128)S(1)} %all-to-all-done.piece, f32[16,128,128]{2,1,0:T(8,128)S(1)} %shard_map.65.extra, ...), custom_call_target="tpu_custom_call" | custom-call | bytes 1249292 | tf_op jit(solution)/shard_map/pallas_call | solution.py:427
  23.6 11.5 %all_to_all.20.piece = f32[32,3,4,128]{3,2,1,0:T(4,128)S(1)} all-to-all(f32[32,3,4,128]{3,2,1,0:T(4,128)S(1)} %get-tuple-element.24), channel_id=1, replica_groups=mesh['top'=4,'mid'=2,'core'=2,'col'=2] {'top','mid','core','col'}, dimensions={0} | all-to-all | bytes 393216 | tf_op jit(solution)/shard_map/all_to_all | solution.py:499
  35.0 1.7 %shard_map.67 = (f32[16,3,8,128]{3,2,1,0:T(8,128)S(1)}, f32[3,8,128]{2,1,0:T(8,128)S(1)}, f32[32,3,4,128]{3,2,1,0:T(4,128)S(1)}, f32[2,3,8,128]{3,2,1,0:T(8,128)}) custom-call(f32[32,3,4,128]{3,2,1,0:T(4,128)S(1)} %all_to_all.20.piece, f32[16,3,8,128]{3,2,1,0:T(8,128)S(1)} %get-tuple-element.25.refs_0_, f32[2,8,128]{2,1,0:T(8,128)S(1)} %get-tuple-element.26.refs_1_.refs_2_, ...), custom_call_target="tpu_custom_call" | custom-call | bytes 1519628 | tf_op jit(solution)/shard_map/pallas_call | solution.py:427
  36.7 11.4 %all_to_all.21.piece = f32[32,3,4,128]{3,2,1,0:T(4,128)S(1)} all-to-all(f32[32,3,4,128]{3,2,1,0:T(4,128)S(1)} %get-tuple-element.29), channel_id=1, replica_groups=mesh['top'=4,'mid'=2,'core'=2,'col'=2] {'top','mid','core','col'}, dimensions={0} | all-to-all | bytes 393216 | tf_op jit(solution)/shard_map/all_to_all | solution.py:499
  48.1 2.1 %shard_map.68 = (f32[16,3,8,128]{3,2,1,0:T(8,128)}, f32[6,8,128]{2,1,0:T(8,128)S(1)}, f32[32,1,128]{2,1,0:T(1,128)S(1)}, f32[3,3,8,128]{3,2,1,0:T(8,128)S(1)}) custom-call(f32[32,3,4,128]{3,2,1,0:T(4,128)S(1)} %all_to_all.21.piece, f32[16,3,8,128]{3,2,1,0:T(8,128)S(1)} %get-tuple-element.25.refs_0_, f32[16,3,8,128]{3,2,1,0:T(8,128)S(1)} %get-tuple-element.30.refs_1_, ...), custom_call_target="tpu_custom_call" | custom-call | bytes 1728524 | tf_op jit(solution)/shard_map/pallas_call | solution.py:427
  50.2 8.9 %all_to_all.22.sums = f32[32,1,128]{2,1,0:T(1,128)S(1)} all-to-all(f32[32,1,128]{2,1,0:T(1,128)S(1)} %get-tuple-element.32), channel_id=1, replica_groups=mesh['top'=4,'mid'=2,'core'=2,'col'=2] {'top','mid','core','col'}, dimensions={0} | all-to-all | bytes 32768 | tf_op jit(solution)/shard_map/all_to_all | solution.py:514
  59.1 0.8 %shard_map.69 = f32[6,3,64]{2,1,0:T(4,128)} custom-call(f32[32,1,128]{2,1,0:T(1,128)S(1)} %all_to_all.22.sums, f32[3,3,8,128]{3,2,1,0:T(8,128)S(1)} %get-tuple-element.33.own, f32[3,8,128]{2,1,0:T(8,128)S(1)} %get-tuple-element.31.refs_3_.refs_0_, f32[6,8,128]{2,1,0:T(8,128)S(1)} %get-tuple-element.34.refs_1_, f32[2,8,128]{2,1,0:T(8,128)S(1)} %get-tuple-element.26.refs_1_.refs_2_), custom_call_target="tpu_custom_call" | custom-call | bytes 98304 | tf_op jit(solution)/shard_map/pallas_call | solution.py:427
Async XLA Ops:
  0.0 0.7 %copy-start.4 = (f32[64]{0:T(128)S(1)}, f32[64]{0:T(128)}, u32[]{:S(2)}) copy-start(f32[64]{0:T(128)} %param.8) | copy-start | bytes 772
  0.0 0.7 %copy-start.5 = (f32[64]{0:T(128)S(1)}, f32[64]{0:T(128)}, u32[]{:S(2)}) copy-start(f32[64]{0:T(128)} %param.9) | copy-start | bytes 772
  0.0 0.7 %copy-start.3 = (f32[3,64]{1,0:T(4,128)S(1)}, f32[3,64]{1,0:T(4,128)}, u32[]{:S(2)}) copy-start(f32[3,64]{1,0:T(4,128)} %refs_1_.1) | copy-start | bytes 2308
  0.0 0.7 %copy-start.2 = (f32[128,16]{0,1:T(8,128)S(1)}, f32[128,16]{0,1:T(8,128)}, u32[]{:S(2)}) copy-start(f32[128,16]{0,1:T(8,128)} %param.11) | copy-start | bytes 24580
  0.0 0.8 %copy-start = (f32[6,3,64]{2,1,0:T(4,128)S(1)}, f32[6,3,64]{2,1,0:T(4,128)}, u32[]{:S(2)}) copy-start(f32[6,3,64]{2,1,0:T(4,128)} %refs_0_.1) | copy-start | bytes 13828
  0.0 0.8 %copy-start.1 = (s32[128,16]{0,1:T(8,128)S(1)}, s32[128,16]{0,1:T(8,128)}, u32[]{:S(2)}) copy-start(s32[128,16]{0,1:T(8,128)} %param.10) | copy-start | bytes 24580
  2.2 17.0 %all-to-all-start = ((f32[32,3,4,128]{3,2,1,0:T(4,128)}), f32[32,3,4,128]{3,2,1,0:T(4,128)S(1)}, u32[]{:S(2)}, u32[]{:S(2)}) async-start(f32[32,3,4,128]{3,2,1,0:T(4,128)} %get-tuple-element.20), calls=%async_computation | async-start | bytes 393216 | tf_op jit(solution)/shard_map/all_to_all | solution.py:470
  9.5 3.8 %collective-permute-start = (f32[2,8,128]{2,1,0:T(8,128)S(1)}, f32[2,8,128]{2,1,0:T(8,128)S(1)}, u32[]{:S(2)}, u32[]{:S(2)}) collective-permute-start(f32[2,8,128]{2,1,0:T(8,128)S(1)} %get-tuple-element.22), channel_id=1, source_target_pairs={{0,1},{1,0},{2,3},{3,2},{4,5},{5,4},{6,7},{7,6},{8,9},{9,8},{10,11... | collective-permute-start | bytes 24584 | tf_op jit(solution)/shard_map/ppermute | solution.py:467

commit v5 on v4

--- a/solution.py
+++ b/solution.py
@@ -113,16 +113,21 @@
     cols[128:256, at] = low
 
 
+def contract(left, right):
+    dims = (((1,), (1,)), ((), ()))
+    return lax.dot_general(left, right, dims, preferred_element_type=F32)
+
+
 def apply_rows(cols, kernels, targets, own, scale):
     total = cols.shape[1]
     step = min(total, 2048)
 
     def turn(i, acc):
         at = pl.ds(pl.multiple_of(i * step, step), step)
-        return acc + jnp.dot(cols[:, at], kernels[at, :], preferred_element_type=F32)
+        return acc + contract(cols[:, at], kernels[:, at])
 
     if total == step:
-        prod = jnp.dot(cols[...], kernels[...], preferred_element_type=F32)
+        prod = contract(cols[...], kernels[...])
     else:
         prod = lax.fori_loop(0, total // step, turn, jnp.zeros((256, 256), F32))
     both = prod[:128, :128] + (prod[128:, :128] + prod[:128, 128:])
@@ -163,19 +168,8 @@
 
 
 def pack_kernel(n_col, *refs):
-    sources, me = refs[:6], refs[6]
-    out, tgt = refs[7:9]
-    near = refs[9 : 9 + n_col]
-    held, sems = refs[9 + n_col : 15 + n_col], refs[15 + n_col]
-    copies = [
-        pltpu.make_async_copy(src, dst, sems.at[i])
-        for i, (src, dst) in enumerate(zip(sources, held))
-    ]
-    for copy in copies:
-        copy.start()
-    for copy in copies:
-        copy.wait()
-    velocity, points, area, self_term, index, weight = held
+    velocity, points, area, self_term, index, weight, me, out, tgt = refs[:9]
+    near = refs[9:]
     rhs = velocity.shape[0]
     field = velocity[...]
     spot = points[...]
@@ -212,7 +206,6 @@
 
 def extra_kernel(half_chunks, *refs):
     near, out = refs[:-1], refs[-1]
-    low = low_half((128, 128))
     lines = lax.broadcasted_iota(jnp.int32, (128, 128), 0)
     for o, pair in enumerate(near):
         index, weight = pair[0], pair[1]
@@ -222,8 +215,8 @@
             total = jnp.zeros((128, 128), F32)
             for k in range(index.shape[0]):
                 total = total + jnp.where(line == index[k : k + 1], weight[k : k + 1], 0.0)
-            total = total + pltpu.roll(total, 64, 1)
-            out[o * half_chunks + u] = jnp.where(low, total, 0.0)
+            turned = total.T
+            out[o * half_chunks + u] = turned[:64] + turned[64:]
 
         pl.loop(0, half_chunks)(build)
 
@@ -233,11 +226,9 @@
 ):
     n_chunk = n_row * n_col // 2
     me = me_ref[0]
-    low = low_half((128, 128))
-    x = [tgt[a : a + 1] for a in range(3)]
     total = Sums(1, sums[0] if sums else None)
 
-    def build(chunk):
+    def unpack(chunk):
         vec = [
             jnp.concatenate(chunk_parts(piece, chunk, me, n_row, n_col, a), axis=0)
             for a in range(3)
@@ -249,17 +240,23 @@
             basis[chunk, a] = vec[a]
         total.add(chunk, 0, vec, vec)
         write_columns(cols, spot, chunk, vec)
-        col = spot.T
-        d = [x[a] - col[:, a : a + 1] for a in range(3)]
+
+    each(n_chunk, unpack)
+    turned = tgt[...].T
+    x = [jnp.broadcast_to(turned[:64, a : a + 1], (64, 128)) for a in range(3)]
+
+    def build(chunk):
+        y = places[chunk]
+        d = [x[a] - y[a : a + 1] for a in range(3)]
         dist = d[0] * d[0] + d[1] * d[1] + d[2] * d[2]
         root = lax.rsqrt(dist + BLOB_SQ)
-        two = (col[:, 3:4] * INV_EIGHT_PI) * root * root * root
-        one = (dist + 2.0 * BLOB_SQ) * two
-        value = jnp.where(low, one, two) + extra[chunk]
+        two = (y[3:4] * INV_EIGHT_PI) * root * root * root
+        one = (dist + 2.0 * BLOB_SQ) * two + extra[chunk]
+        value = jnp.concatenate([one, two], axis=0)
         high = value.astype(BF16)
         at = lines_of(chunk)
-        kernels[at, 0:128] = high
-        kernels[at, 128:256] = (value - high.astype(F32)).astype(BF16)
+        kernels[0:128, at] = high
+        kernels[128:256, at] = (value - high.astype(F32)).astype(BF16)
 
     each(n_chunk, build)
     norm = jnp.sqrt(total.get(0))
@@ -417,12 +414,11 @@
         out[:, a, :] = density[: out.shape[0], :64]
 
 
-def call(kernel, outs, scratch, operands, scalars=(), far=(), flops=0):
+def call(kernel, outs, scratch, operands, scalars=(), flops=0):
     vmem = pl.BlockSpec(memory_space=pltpu.VMEM)
     smem = pl.BlockSpec(memory_space=pltpu.SMEM)
-    anywhere = pl.BlockSpec(memory_space=pl.ANY)
     count = len(operands)
-    specs = [smem if i in scalars else anywhere if i in far else vmem for i in range(count)]
+    specs = [smem if i in scalars else vmem for i in range(count)]
     moved = sum(x.size * x.dtype.itemsize for x in operands)
     return pl.pallas_call(
         kernel,
@@ -458,10 +454,9 @@
         functools.partial(pack_kernel, n_col),
         [message, ((8, 128), F32)]
         + [((2, near_index.shape[1] // 2, 128), F32)] * n_col,
-        [pltpu.VMEM(x.shape, x.dtype) for x in sources] + [pltpu.SemaphoreType.DMA((6,))],
+        [],
         [*sources, me],
         {6},
-        range(6),
     )
     near = [
         lax.ppermute(pair, "col", xor_perm(n_col, o)) if o else pair
@@ -470,7 +465,7 @@
     piece = lax.all_to_all(wide, AXES, 0, 0, tiled=True)
     (extra,) = call(
         functools.partial(extra_kernel, n_row // 2),
-        [((n_chunk, 128, 128), F32)],
+        [((n_chunk, 64, 128), F32)],
         [],
         near,
         flops=10**9,
@@ -482,7 +477,7 @@
     kernels, places, basis, norm, wide = call(
         functools.partial(first_kernel, n_row, n_col),
         [
-            ((total, 256), BF16),
+            ((256, total), BF16),
             ((n_chunk, ROWS, 128), F32),
             (vec_shape, F32),
             ((2, ROWS, 128), F32),

time: 60.2 us -> 57.9 us (0.962)
  Pallas kernels: 12.4 us -> 10.1 us
    pallas_call x6, Pallas kernels: 12.4 us -> 10.1 us  [call(): pl.pallas_call(kernel, out_shape=[jax.ShapeDtypeStruct(s, t) for s, t in...]
  transfers between devices with their start and end apart: 2 -> 2, of which waited for: 2 -> 2; matrix products, arithmetic and copies ran while one was open for 0% -> 0% of each run, Pallas kernels for 3% -> 4%
where the time goes in v5:
time: 57.9 us; the launch traced here: 57.5 us
  blocking collectives  31.8 us (55%)
  Pallas kernels  10.1 us (17%)
  starting transfers between devices  9.13 us (16%)
  waiting for transfers between devices  5.76 us (10%)
  local copies, waits for them, and re-layouts  0.68 us (1%)
    all_to_all x2, blocking collectives, body(): piece = lax.all_to_all(wide, AXES, 0, 0, tiled=True)  22.8 us
    pallas_call x6, Pallas kernels, call(): pl.pallas_call(kernel, out_shape=[jax.ShapeDtypeStruct(s, t) for s, t in...  10.1 us
    all_to_all x1, blocking collectives, body(): sums = lax.all_to_all(wide, AXES, 0, 0, tiled=True)  8.93 us
    all_to_all x1, starting transfers between devices, body(): piece = lax.all_to_all(wide, AXES, 0, 0, tiled=True)  7.3 us
    all_to_all x1, waiting for transfers between devices, body(): piece = lax.all_to_all(wide, AXES, 0, 0, tiled=True)  3.83 us
    ppermute x1, waiting for transfers between devices, body(): lax.ppermute(pair, 'col', xor_perm(n_col, o))  1.92 us
    ppermute x1, starting transfers between devices, body(): lax.ppermute(pair, 'col', xor_perm(n_col, o))  1.83 us
  transfers between devices with their start and end apart: 2, of which 2 were waited for; matrix products, arithmetic and copies ran while one was open for 0% of the time, Pallas kernels for 4%

profile of v5, /device:TPU:0, one launch (start us, length us, event | category | flops | bytes accessed | tf_op | source)
XLA Modules:
  0.0 57.5 jit_solution(13831690935370450727)
XLA Ops:
  0.0 0.0 copy-start.4
  0.0 0.0 copy-start.5
  0.0 0.0 copy-start.3
  0.0 0.0 copy-start.2
  0.0 0.0 copy-start
  0.0 0.0 copy-start.1
  0.0 0.1 pad_add_fusion.refs_6_.me_ref.refs_5_.refs_7_
  0.1 0.6 copy-done.4
  0.7 0.0 copy-done.5
  0.7 0.0 copy-done.3
  0.7 0.0 copy-done.2
  0.7 0.0 copy-done
  0.8 0.0 copy-done.1
  0.8 1.3 %shard_map.64 = (f32[32,3,4,128]{3,2,1,0:T(4,128)}, f32[8,128]{1,0:T(8,128)S(1)}, f32[2,8,128]{2,1,0:T(8,128)S(1)}, f32[2,8,128]{2,1,0:T(8,128)S(1)}) custom-call(f32[6,3,64]{2,1,0:T(4,128)S(1)} %copy-done, f32[3,64]{1,0:T(4,128)S(1)} %copy-done.3, f32[1,64]{1,0:T(1,128)S(1)} %bitcast.9, f32[1,64]{1,0:T(1,128)S(1)} %bitcast.10, s32[16,128]{1,0:T(8,128)S(1)} %bitcast.7, ...), custom_call_target="tpu_custom_call" | custom-call | bytes 22284 | tf_op jit(solution)/shard_map/pallas_call | solution.py:423
  2.1 7.3 %all-to-all-start = ((f32[32,3,4,128]{3,2,1,0:T(4,128)}), f32[32,3,4,128]{3,2,1,0:T(4,128)S(1)}, u32[]{:S(2)}, u32[]{:S(2)}) async-start(f32[32,3,4,128]{3,2,1,0:T(4,128)} %get-tuple-element.20), calls=%async_computation | async-start | bytes 393216 | tf_op jit(solution)/shard_map/all_to_all | solution.py:465
  9.4 1.8 %collective-permute-start = (f32[2,8,128]{2,1,0:T(8,128)S(1)}, f32[2,8,128]{2,1,0:T(8,128)S(1)}, u32[]{:S(2)}, u32[]{:S(2)}) collective-permute-start(f32[2,8,128]{2,1,0:T(8,128)S(1)} %get-tuple-element.22), channel_id=1, source_target_pairs={{0,1},{1,0},{2,3},{3,2},{4,5},{5,4},{6,7},{7,6},{8,9},{9,8},{10,11... | collective-permute-start | bytes 24584 | tf_op jit(solution)/shard_map/ppermute | solution.py:462
  11.2 1.9 %collective-permute-done.refs_1_ = f32[2,8,128]{2,1,0:T(8,128)S(1)} collective-permute-done((f32[2,8,128]{2,1,0:T(8,128)S(1)}, f32[2,8,128]{2,1,0:T(8,128)S(1)}, u32[]{:S(2)}, u32[]{:S(2)}) %collective-permute-start) | collective-permute-done | bytes 8224 | tf_op jit(solution)/shard_map/ppermute | solution.py:462
  13.2 2.1 %shard_map.65.extra = f32[16,64,128]{2,1,0:T(8,128)S(1)} custom-call(f32[2,8,128]{2,1,0:T(8,128)S(1)} %get-tuple-element.21.refs_0_, f32[2,8,128]{2,1,0:T(8,128)S(1)} %collective-permute-done.refs_1_), custom_call_target="tpu_custom_call" | custom-call | flops 1000000000 | bytes 16384 | tf_op jit(solution)/shard_map/pallas_call | solution.py:423
  15.2 3.8 %all-to-all-done.piece = f32[32,3,4,128]{3,2,1,0:T(4,128)S(1)} async-done(((f32[32,3,4,128]{3,2,1,0:T(4,128)}), f32[32,3,4,128]{3,2,1,0:T(4,128)S(1)}, u32[]{:S(2)}, u32[]{:S(2)}) %all-to-all-start) | async-done | bytes 196640 | tf_op jit(solution)/shard_map/all_to_all | solution.py:465
  19.1 2.0 %shard_map.66 = (bf16[256,2048]{1,0:T(8,128)(2,1)S(1)}, f32[16,8,128]{2,1,0:T(8,128)S(1)}, f32[16,3,8,128]{3,2,1,0:T(8,128)S(1)}, f32[2,8,128]{2,1,0:T(8,128)S(1)}, f32[32,3,4,128]{3,2,1,0:T(4,128)S(1)}) custom-call(f32[32,3,4,128]{3,2,1,0:T(4,128)S(1)} %all-to-all-done.piece, f32[16,64,128]{2,1,0:T(8,128)S(1)} %shard_map.65.extra, ...), custom_call_target="tpu_custom_call" | custom-call | bytes 725004 | tf_op jit(solution)/shard_map/pallas_call | solution.py:423
  21.1 11.4 %all_to_all.20.piece = f32[32,3,4,128]{3,2,1,0:T(4,128)S(1)} all-to-all(f32[32,3,4,128]{3,2,1,0:T(4,128)S(1)} %get-tuple-element.24), channel_id=1, replica_groups=mesh['top'=4,'mid'=2,'core'=2,'col'=2] {'top','mid','core','col'}, dimensions={0} | all-to-all | bytes 393216 | tf_op jit(solution)/shard_map/all_to_all | solution.py:494
  32.5 1.8 %shard_map.67 = (f32[16,3,8,128]{3,2,1,0:T(8,128)S(1)}, f32[3,8,128]{2,1,0:T(8,128)S(1)}, f32[32,3,4,128]{3,2,1,0:T(4,128)S(1)}, f32[2,3,8,128]{3,2,1,0:T(8,128)}) custom-call(f32[32,3,4,128]{3,2,1,0:T(4,128)S(1)} %all_to_all.20.piece, f32[16,3,8,128]{3,2,1,0:T(8,128)S(1)} %get-tuple-element.25.refs_0_, f32[2,8,128]{2,1,0:T(8,128)S(1)} %get-tuple-element.26.refs_1_.refs_2_, ...), custom_call_target="tpu_custom_call" | custom-call | bytes 1519628 | tf_op jit(solution)/shard_map/pallas_call | solution.py:423
  34.3 11.4 %all_to_all.21.piece = f32[32,3,4,128]{3,2,1,0:T(4,128)S(1)} all-to-all(f32[32,3,4,128]{3,2,1,0:T(4,128)S(1)} %get-tuple-element.29), channel_id=1, replica_groups=mesh['top'=4,'mid'=2,'core'=2,'col'=2] {'top','mid','core','col'}, dimensions={0} | all-to-all | bytes 393216 | tf_op jit(solution)/shard_map/all_to_all | solution.py:494
  45.7 2.1 %shard_map.68 = (f32[16,3,8,128]{3,2,1,0:T(8,128)}, f32[6,8,128]{2,1,0:T(8,128)S(1)}, f32[32,1,128]{2,1,0:T(1,128)S(1)}, f32[3,3,8,128]{3,2,1,0:T(8,128)S(1)}) custom-call(f32[32,3,4,128]{3,2,1,0:T(4,128)S(1)} %all_to_all.21.piece, f32[16,3,8,128]{3,2,1,0:T(8,128)S(1)} %get-tuple-element.25.refs_0_, f32[16,3,8,128]{3,2,1,0:T(8,128)S(1)} %get-tuple-element.30.refs_1_, ...), custom_call_target="tpu_custom_call" | custom-call | bytes 1728524 | tf_op jit(solution)/shard_map/pallas_call | solution.py:423
  47.8 8.9 %all_to_all.22.sums = f32[32,1,128]{2,1,0:T(1,128)S(1)} all-to-all(f32[32,1,128]{2,1,0:T(1,128)S(1)} %get-tuple-element.32), channel_id=1, replica_groups=mesh['top'=4,'mid'=2,'core'=2,'col'=2] {'top','mid','core','col'}, dimensions={0} | all-to-all | bytes 32768 | tf_op jit(solution)/shard_map/all_to_all | solution.py:509
  56.8 0.8 %shard_map.69 = f32[6,3,64]{2,1,0:T(4,128)} custom-call(f32[32,1,128]{2,1,0:T(1,128)S(1)} %all_to_all.22.sums, f32[3,3,8,128]{3,2,1,0:T(8,128)S(1)} %get-tuple-element.33.own, f32[3,8,128]{2,1,0:T(8,128)S(1)} %get-tuple-element.31.refs_3_.refs_0_, f32[6,8,128]{2,1,0:T(8,128)S(1)} %get-tuple-element.34.refs_1_, f32[2,8,128]{2,1,0:T(8,128)S(1)} %get-tuple-element.26.refs_1_.refs_2_), custom_call_target="tpu_custom_call" | custom-call | bytes 98304 | tf_op jit(solution)/shard_map/pallas_call | solution.py:423
Async XLA Ops:
  0.0 0.7 %copy-start.4 = (f32[64]{0:T(128)S(1)}, f32[64]{0:T(128)}, u32[]{:S(2)}) copy-start(f32[64]{0:T(128)} %param.8) | copy-start | bytes 772
  0.0 0.7 %copy-start.5 = (f32[64]{0:T(128)S(1)}, f32[64]{0:T(128)}, u32[]{:S(2)}) copy-start(f32[64]{0:T(128)} %param.9) | copy-start | bytes 772
  0.0 0.7 %copy-start.3 = (f32[3,64]{1,0:T(4,128)S(1)}, f32[3,64]{1,0:T(4,128)}, u32[]{:S(2)}) copy-start(f32[3,64]{1,0:T(4,128)} %refs_1_.1) | copy-start | bytes 2308
  0.0 0.7 %copy-start.2 = (f32[128,16]{0,1:T(8,128)S(1)}, f32[128,16]{0,1:T(8,128)}, u32[]{:S(2)}) copy-start(f32[128,16]{0,1:T(8,128)} %param.11) | copy-start | bytes 24580
  0.0 0.8 %copy-start = (f32[6,3,64]{2,1,0:T(4,128)S(1)}, f32[6,3,64]{2,1,0:T(4,128)}, u32[]{:S(2)}) copy-start(f32[6,3,64]{2,1,0:T(4,128)} %refs_0_.1) | copy-start | bytes 13828
  0.0 0.8 %copy-start.1 = (s32[128,16]{0,1:T(8,128)S(1)}, s32[128,16]{0,1:T(8,128)}, u32[]{:S(2)}) copy-start(s32[128,16]{0,1:T(8,128)} %param.10) | copy-start | bytes 24580
  2.1 17.0 %all-to-all-start = ((f32[32,3,4,128]{3,2,1,0:T(4,128)}), f32[32,3,4,128]{3,2,1,0:T(4,128)S(1)}, u32[]{:S(2)}, u32[]{:S(2)}) async-start(f32[32,3,4,128]{3,2,1,0:T(4,128)} %get-tuple-element.20), calls=%async_computation | async-start | bytes 393216 | tf_op jit(solution)/shard_map/all_to_all | solution.py:465
  9.4 3.8 %collective-permute-start = (f32[2,8,128]{2,1,0:T(8,128)S(1)}, f32[2,8,128]{2,1,0:T(8,128)S(1)}, u32[]{:S(2)}, u32[]{:S(2)}) collective-permute-start(f32[2,8,128]{2,1,0:T(8,128)S(1)} %get-tuple-element.22), channel_id=1, source_target_pairs={{0,1},{1,0},{2,3},{3,2},{4,5},{5,4},{6,7},{7,6},{8,9},{9,8},{10,11... | collective-permute-start | bytes 24584 | tf_op jit(solution)/shard_map/ppermute | solution.py:462

commit v6 on v5

--- a/solution.py
+++ b/solution.py
@@ -12,6 +12,9 @@
 BLOB_SQ = 0.0025
 INV_EIGHT_PI = 1.0 / (8.0 * math.pi)
 ROWS = 8
+HALF = 3
+FIRST, LATER = 11, 10
+ORDER = (0, 2, 1)
 AXES = ("top", "mid", "core", "col")
 F32 = jnp.float32
 BF16 = jnp.bfloat16
@@ -21,17 +24,13 @@
     return lax.broadcasted_iota(jnp.int32, shape, len(shape) - 1) < 64
 
 
-def pack(rows):
-    return jnp.concatenate([rows[..., :4, :], rows[..., 4:, :]], axis=-1)
-
-
 def xor_perm(n, m):
     return [(d, d ^ m) for d in range(n)]
 
 
-def spread(piece, axes, size):
-    wide = jnp.broadcast_to(piece[None], (size,) + piece.shape)
-    return lax.all_to_all(wide, axes, 0, 0, tiled=True)
+def spread(rows, n):
+    wide = rows.reshape(n, -1, 1, 128)
+    return lax.all_to_all(wide, AXES, 0, 0, tiled=True).reshape(rows.shape)
 
 
 def each(count, step):
@@ -68,16 +67,16 @@
         return jnp.broadcast_to(jnp.sum(total, axis=1, keepdims=True), (ROWS, 128))
 
 
-def chunk_parts(piece, chunk, me, n_row, n_col, part):
+def chunk_parts(piece, chunk, me, n_row, n_col, size, at, count):
     half = n_row // 2
     o = chunk // half
     u = chunk % half
-    even = piece[me ^ ((2 * u) * n_col + o), part]
-    odd = piece[me ^ ((2 * u + 1) * n_col + o), part]
-    low = low_half((4, 128))
+    even = piece[pl.ds((me ^ ((2 * u) * n_col + o)) * size + at, count)]
+    odd = piece[pl.ds((me ^ ((2 * u + 1) * n_col + o)) * size + at, count)]
+    low = low_half((count, 128))
     first = jnp.where(low, even, pltpu.roll(odd, 64, 1))
     second = jnp.where(low, pltpu.roll(even, 64, 1), odd)
-    return first, second
+    return jnp.concatenate([first, second], axis=0)
 
 
 PAIRS = [(i, j) for i in range(ITERS) for j in range(i + 1, ITERS)]
@@ -99,7 +98,7 @@
 
 
 def write_columns(cols, y, chunk, vec):
-    ys = [y[a : a + 1] for a in range(3)]
+    ys = [y[a : a + 1] for a in ORDER]
     f = [vec[a] for a in range(3)]
     g = ys[0] * f[0] + ys[1] * f[1] + ys[2] * f[2]
     groups = f + [g]
@@ -154,9 +153,9 @@
 
     def put(m):
         for a in range(3):
-            out[m, a] = rows[a]
-
-    each_wide(out.shape[0], put)
+            out[pl.ds(m * LATER + HALF * a, 4)] = rows[a]
+
+    each_wide(out.shape[0] // LATER, put)
 
 
 def each_wide(count, put):
@@ -170,23 +169,24 @@
 def pack_kernel(n_col, *refs):
     velocity, points, area, self_term, index, weight, me, out, tgt = refs[:9]
     near = refs[9:]
-    rhs = velocity.shape[0]
     field = velocity[...]
     spot = points[...]
-    place = [jnp.concatenate([spot[2:3], area[...]], axis=0) if a == 1 else spot[:2] for a in range(3)]
     rows = []
     for a in range(3):
         vec = field[:, a, :]
-        rows.append(jnp.concatenate([vec[:4], jnp.concatenate([vec[4:], place[a]], axis=0)], axis=1))
+        rows.append(jnp.concatenate([vec[:HALF], vec[HALF:]], axis=1))
     mine = jnp.concatenate([spot, self_term[...]], axis=0)
     mine = jnp.concatenate([mine, mine], axis=1)
     tgt[...] = jnp.concatenate([mine, mine], axis=0)
+    left = jnp.concatenate([spot[0:1], spot[2:3]], axis=0)
+    right = jnp.concatenate([spot[1:2], area[...]], axis=0)
+    rows.append(jnp.concatenate([left, right], axis=1))
+    message = jnp.concatenate(rows, axis=0)
 
     def put(m):
-        for a in range(3):
-            out[m, a] = rows[a]
-
-    each_wide(out.shape[0], put)
+        out[pl.ds(m * FIRST, FIRST)] = message
+
+    each_wide(out.shape[0] // FIRST, put)
 
     row, col = me[1], me[2]
     half = index.shape[0] // 2
@@ -230,11 +230,10 @@
 
     def unpack(chunk):
         vec = [
-            jnp.concatenate(chunk_parts(piece, chunk, me, n_row, n_col, a), axis=0)
+            chunk_parts(piece, chunk, me, n_row, n_col, FIRST, HALF * a, 4)
             for a in range(3)
         ]
-        spot = jnp.concatenate([vec[0][6:8], vec[1][6:8]], axis=0)
-        spot = jnp.concatenate([spot, spot], axis=0)
+        spot = chunk_parts(piece, chunk, me, n_row, n_col, FIRST, 3 * HALF, 2)
         places[chunk] = spot
         for a in range(3):
             basis[chunk, a] = vec[a]
@@ -247,7 +246,7 @@
 
     def build(chunk):
         y = places[chunk]
-        d = [x[a] - y[a : a + 1] for a in range(3)]
+        d = [x[a] - y[k : k + 1] for a, k in enumerate(ORDER)]
         dist = d[0] * d[0] + d[1] * d[1] + d[2] * d[2]
         root = lax.rsqrt(dist + BLOB_SQ)
         two = (y[3:4] * INV_EIGHT_PI) * root * root * root
@@ -277,7 +276,7 @@
 
     def unpack(chunk):
         vec = [
-            jnp.concatenate(chunk_parts(piece, chunk, me, n_row, n_col, a), axis=0)
+            chunk_parts(piece, chunk, me, n_row, n_col, LATER, HALF * a, 4)
             for a in range(3)
         ]
         old = [[base[chunk, a] for a in range(3)] for base in bases]
@@ -344,7 +343,7 @@
     row = jnp.sum(row, axis=0, keepdims=True)
 
     def put(m):
-        out[m] = row
+        out[pl.ds(m, 1)] = row
 
     each_wide(out.shape[0], put)
 
@@ -391,7 +390,7 @@
     gram = {(j, j): 1.0 for j in range(ITERS)}
     for at, (i, j) in enumerate(PAIRS):
         gram[i, j] = gram[j, i] = columns[-1][ITERS + at]
-    row = jnp.broadcast_to(jnp.sum(sums[...], axis=0), (ROWS, 128))
+    row = jnp.broadcast_to(jnp.sum(sums[...], axis=0, keepdims=True), (ROWS, 128))
     inner = [
         jnp.broadcast_to(row_sum(jnp.where(place_of(j), row, 0.0)), (ROWS, 128))
         for j in range(ITERS + 1)
@@ -411,7 +410,8 @@
     coeffs = solve_small(hessen, norm[0], ITERS)
     for a in range(3):
         density = sum(coeffs[k] * own[k, a] for k in range(ITERS))
-        out[:, a, :] = density[: out.shape[0], :64]
+        out[:HALF, a, :] = density[:HALF, :64]
+        out[HALF:, a, :] = density[4 : 4 + HALF, :64]
 
 
 def call(kernel, outs, scratch, operands, scalars=(), flops=0):
@@ -449,10 +449,10 @@
         near_index.T,
         near_weight.T,
     ]
-    message = ((n, 3, 4, 128), F32)
+    message = ((n * LATER, 128), F32)
     wide, tgt, *near = call(
         functools.partial(pack_kernel, n_col),
-        [message, ((8, 128), F32)]
+        [((n * FIRST, 128), F32), ((8, 128), F32)]
         + [((2, near_index.shape[1] // 2, 128), F32)] * n_col,
         [],
         [*sources, me],
@@ -462,7 +462,7 @@
         lax.ppermute(pair, "col", xor_perm(n_col, o)) if o else pair
         for o, pair in enumerate(near)
     ]
-    piece = lax.all_to_all(wide, AXES, 0, 0, tiled=True)
+    piece = spread(wide, n)
     (extra,) = call(
         functools.partial(extra_kernel, n_row // 2),
         [((n_chunk, 64, 128), F32)],
@@ -478,7 +478,7 @@
         functools.partial(first_kernel, n_row, n_col),
         [
             ((256, total), BF16),
-            ((n_chunk, ROWS, 128), F32),
+            ((n_chunk, 4, 128), F32),
             (vec_shape, F32),
             ((2, ROWS, 128), F32),
             message,
@@ -491,13 +491,13 @@
     columns = [norm]
     for k in range(1, ITERS):
         final = k == ITERS - 1
-        piece = lax.all_to_all(wide, AXES, 0, 0, tiled=True)
+        piece = spread(wide, n)
         basis, column, wide, own = call(
             functools.partial(middle_kernel, n_row, n_col, k, final),
             [
                 (vec_shape, F32),
                 ((k + 1 + (len(PAIRS) if final else 1), ROWS, 128), F32),
-                ((n, 1, 128), F32) if final else message,
+                ((n, 128), F32) if final else message,
                 ((k + 1, 3, ROWS, 128), F32),
             ],
             [cols, *held],
@@ -506,7 +506,7 @@
         )
         bases.append(basis)
         columns.append(column)
-    sums = lax.all_to_all(wide, AXES, 0, 0, tiled=True)
+    sums = spread(wide, n)
     (density,) = call(
         last_kernel, [((rhs, 3, 64), F32)], [], [sums, own, *columns[1:], columns[0]]
     )

time: 57.9 us -> 56.7 us (0.979)
  blocking collectives: 31.8 us -> 30.9 us
    all_to_all x3, blocking collectives: 31.8 us -> 30.9 us  [spread(): return lax.all_to_all(wide, AXES, 0, 0, tiled=True).reshape(rows.shape)]
where the time goes in v6:
time: 56.7 us; the launch traced here: 56.4 us
  blocking collectives  30.9 us (54%)
  Pallas kernels  10.1 us (18%)
  starting transfers between devices  9.13 us (16%)
  waiting for transfers between devices  5.49 us (10%)
  local copies, waits for them, and re-layouts  0.68 us (1%)
    all_to_all x3, blocking collectives, spread(): return lax.all_to_all(wide, AXES, 0, 0, tiled=True).reshape(rows.shape)  30.9 us
    pallas_call x6, Pallas kernels, call(): pl.pallas_call(kernel, out_shape=[jax.ShapeDtypeStruct(s, t) for s, t in...  10.1 us
    all_to_all x1, starting transfers between devices, spread(): return lax.all_to_all(wide, AXES, 0, 0, tiled=True).reshape(rows.shape)  7.3 us
    all_to_all x1, waiting for transfers between devices, spread(): return lax.all_to_all(wide, AXES, 0, 0, tiled=True).reshape(rows.shape)  3.59 us
    ppermute x1, waiting for transfers between devices, body(): lax.ppermute(pair, 'col', xor_perm(n_col, o))  1.9 us
    ppermute x1, starting transfers between devices, body(): lax.ppermute(pair, 'col', xor_perm(n_col, o))  1.83 us
  transfers between devices with their start and end apart: 2, of which 2 were waited for; matrix products, arithmetic and copies ran while one was open for 0% of the time, Pallas kernels for 4%

profile of v6, /device:TPU:0, one launch (start us, length us, event | category | flops | bytes accessed | tf_op | source)
XLA Modules:
  0.0 56.4 jit_solution(17058290308971104818)
XLA Ops:
  0.0 0.0 copy-start.4
  0.0 0.0 copy-start.5
  0.0 0.0 copy-start.3
  0.0 0.0 copy-start.2
  0.0 0.0 copy-start
  0.0 0.0 copy-start.1
  0.0 0.1 pad_add_fusion.refs_6_.me_ref.refs_5_.refs_7_
  0.1 0.6 copy-done.4
  0.7 0.0 copy-done.5
  0.7 0.0 copy-done.3
  0.7 0.0 copy-done.2
  0.7 0.0 copy-done
  0.8 0.0 copy-done.1
  0.8 1.3 %shard_map.64 = (f32[352,128]{1,0:T(8,128)}, f32[8,128]{1,0:T(8,128)S(1)}, f32[2,8,128]{2,1,0:T(8,128)S(1)}, f32[2,8,128]{2,1,0:T(8,128)S(1)}) custom-call(f32[6,3,64]{2,1,0:T(4,128)S(1)} %copy-done, f32[3,64]{1,0:T(4,128)S(1)} %copy-done.3, f32[1,64]{1,0:T(1,128)S(1)} %bitcast.26, f32[1,64]{1,0:T(1,128)S(1)} %bitcast.27, s32[16,128]{1,0:T(8,128)S(1)} %bitcast.24, ...), custom_call_target="tpu_custom_call" | custom-call | bytes 22284 | tf_op jit(solution)/shard_map/pallas_call | solution.py:423
  2.1 7.3 %all-to-all-start = ((f32[32,11,1,128]{3,2,1,0:T(1,128)}), f32[32,11,1,128]{3,2,1,0:T(1,128)S(1)}, u32[]{:S(2)}, u32[]{:S(2)}) async-start(f32[32,11,1,128]{3,2,1,0:T(1,128)} %bitcast.7), calls=%async_computation | async-start | bytes 360448 | tf_op jit(solution)/shard_map/all_to_all | solution.py:33
  9.4 1.8 %collective-permute-start = (f32[2,8,128]{2,1,0:T(8,128)S(1)}, f32[2,8,128]{2,1,0:T(8,128)S(1)}, u32[]{:S(2)}, u32[]{:S(2)}) collective-permute-start(f32[2,8,128]{2,1,0:T(8,128)S(1)} %get-tuple-element.22), channel_id=1, source_target_pairs={{0,1},{1,0},{2,3},{3,2},{4,5},{5,4},{6,7},{7,6},{8,9},{9,8},{10,11... | collective-permute-start | bytes 24584 | tf_op jit(solution)/shard_map/ppermute | solution.py:462
  11.2 1.9 %collective-permute-done.refs_1_ = f32[2,8,128]{2,1,0:T(8,128)S(1)} collective-permute-done((f32[2,8,128]{2,1,0:T(8,128)S(1)}, f32[2,8,128]{2,1,0:T(8,128)S(1)}, u32[]{:S(2)}, u32[]{:S(2)}) %collective-permute-start) | collective-permute-done | bytes 8224 | tf_op jit(solution)/shard_map/ppermute | solution.py:462
  13.1 2.1 %shard_map.65.extra = f32[16,64,128]{2,1,0:T(8,128)S(1)} custom-call(f32[2,8,128]{2,1,0:T(8,128)S(1)} %get-tuple-element.21.refs_0_, f32[2,8,128]{2,1,0:T(8,128)S(1)} %collective-permute-done.refs_1_), custom_call_target="tpu_custom_call" | custom-call | flops 1000000000 | bytes 16384 | tf_op jit(solution)/shard_map/pallas_call | solution.py:423
  15.2 3.6 %all-to-all-done = f32[32,11,1,128]{3,2,1,0:T(1,128)S(1)} async-done(((f32[32,11,1,128]{3,2,1,0:T(1,128)}), f32[32,11,1,128]{3,2,1,0:T(1,128)S(1)}, u32[]{:S(2)}, u32[]{:S(2)}) %all-to-all-start) | async-done | bytes 180256 | tf_op jit(solution)/shard_map/all_to_all | solution.py:33
  18.8 2.0 %shard_map.66 = (bf16[256,2048]{1,0:T(8,128)(2,1)S(1)}, f32[16,4,128]{2,1,0:T(4,128)S(1)}, f32[16,3,8,128]{3,2,1,0:T(8,128)S(1)}, f32[2,8,128]{2,1,0:T(8,128)S(1)}, f32[320,128]{1,0:T(8,128)S(1)}) custom-call(f32[352,128]{1,0:T(8,128)S(1)} %bitcast.17, f32[16,64,128]{2,1,0:T(8,128)S(1)} %shard_map.65.extra, ...), custom_call_target="tpu_custom_call" | custom-call | bytes 708620 | tf_op jit(solution)/shard_map/pallas_call | solution.py:423
  20.8 11.2 %all_to_all.20 = f32[32,10,1,128]{3,2,1,0:T(1,128)S(1)} all-to-all(f32[32,10,1,128]{3,2,1,0:T(1,128)S(1)} %bitcast.20), channel_id=1, replica_groups=mesh['top'=4,'mid'=2,'core'=2,'col'=2] {'top','mid','core','col'}, dimensions={0} | all-to-all | bytes 327680 | tf_op jit(solution)/shard_map/all_to_all | solution.py:33
  32.1 1.8 %shard_map.67 = (f32[16,3,8,128]{3,2,1,0:T(8,128)S(1)}, f32[3,8,128]{2,1,0:T(8,128)S(1)}, f32[320,128]{1,0:T(8,128)S(1)}, f32[2,3,8,128]{3,2,1,0:T(8,128)}) custom-call(f32[320,128]{1,0:T(8,128)S(1)} %bitcast.19, f32[16,3,8,128]{3,2,1,0:T(8,128)S(1)} %get-tuple-element.25.refs_0_, f32[2,8,128]{2,1,0:T(8,128)S(1)} %get-tuple-element.26.refs_1_.refs_2_, ...), custom_call_target="tpu_custom_call" | custom-call | bytes 1454092 | tf_op jit(solution)/shard_map/pallas_call | solution.py:423
  33.9 10.8 %all_to_all.21 = f32[32,10,1,128]{3,2,1,0:T(1,128)S(1)} all-to-all(f32[32,10,1,128]{3,2,1,0:T(1,128)S(1)} %bitcast.21), channel_id=1, replica_groups=mesh['top'=4,'mid'=2,'core'=2,'col'=2] {'top','mid','core','col'}, dimensions={0} | all-to-all | bytes 327680 | tf_op jit(solution)/shard_map/all_to_all | solution.py:33
  44.7 2.1 %shard_map.68 = (f32[16,3,8,128]{3,2,1,0:T(8,128)}, f32[6,8,128]{2,1,0:T(8,128)S(1)}, f32[32,128]{1,0:T(8,128)S(1)}, f32[3,3,8,128]{3,2,1,0:T(8,128)S(1)}) custom-call(f32[320,128]{1,0:T(8,128)S(1)} %bitcast.18, f32[16,3,8,128]{3,2,1,0:T(8,128)S(1)} %get-tuple-element.25.refs_0_, f32[16,3,8,128]{3,2,1,0:T(8,128)S(1)} %get-tuple-element.30.refs_1_, ...), custom_call_target="tpu_custom_call" | custom-call | bytes 1662988 | tf_op jit(solution)/shard_map/pallas_call | solution.py:423
  46.8 8.9 %all_to_all.22 = f32[32,1,1,128]{3,2,1,0:T(1,128)S(1)} all-to-all(f32[32,1,1,128]{3,2,1,0:T(1,128)S(1)} %bitcast.23), channel_id=1, replica_groups=mesh['top'=4,'mid'=2,'core'=2,'col'=2] {'top','mid','core','col'}, dimensions={0} | all-to-all | bytes 32768 | tf_op jit(solution)/shard_map/all_to_all | solution.py:33
  55.7 0.7 %shard_map.69 = f32[6,3,64]{2,1,0:T(4,128)} custom-call(f32[32,128]{1,0:T(8,128)S(1)} %bitcast.22, f32[3,3,8,128]{3,2,1,0:T(8,128)S(1)} %get-tuple-element.33.own, f32[3,8,128]{2,1,0:T(8,128)S(1)} %get-tuple-element.31.refs_3_.refs_0_, f32[6,8,128]{2,1,0:T(8,128)S(1)} %get-tuple-element.34.refs_1_, f32[2,8,128]{2,1,0:T(8,128)S(1)} %get-tuple-element.26.refs_1_.refs_2_), custom_call_target="tpu_custom_call" | custom-call | bytes 98304 | tf_op jit(solution)/shard_map/pallas_call | solution.py:423
Async XLA Ops:
  0.0 0.7 %copy-start.4 = (f32[64]{0:T(128)S(1)}, f32[64]{0:T(128)}, u32[]{:S(2)}) copy-start(f32[64]{0:T(128)} %param.8) | copy-start | bytes 772
  0.0 0.7 %copy-start.5 = (f32[64]{0:T(128)S(1)}, f32[64]{0:T(128)}, u32[]{:S(2)}) copy-start(f32[64]{0:T(128)} %param.9) | copy-start | bytes 772
  0.0 0.7 %copy-start.3 = (f32[3,64]{1,0:T(4,128)S(1)}, f32[3,64]{1,0:T(4,128)}, u32[]{:S(2)}) copy-start(f32[3,64]{1,0:T(4,128)} %refs_1_.1) | copy-start | bytes 2308
  0.0 0.7 %copy-start.2 = (f32[128,16]{0,1:T(8,128)S(1)}, f32[128,16]{0,1:T(8,128)}, u32[]{:S(2)}) copy-start(f32[128,16]{0,1:T(8,128)} %param.11) | copy-start | bytes 24580
  0.0 0.8 %copy-start = (f32[6,3,64]{2,1,0:T(4,128)S(1)}, f32[6,3,64]{2,1,0:T(4,128)}, u32[]{:S(2)}) copy-start(f32[6,3,64]{2,1,0:T(4,128)} %refs_0_.1) | copy-start | bytes 13828
  0.0 0.8 %copy-start.1 = (s32[128,16]{0,1:T(8,128)S(1)}, s32[128,16]{0,1:T(8,128)}, u32[]{:S(2)}) copy-start(s32[128,16]{0,1:T(8,128)} %param.10) | copy-start | bytes 24580
  2.1 16.7 %all-to-all-start = ((f32[32,11,1,128]{3,2,1,0:T(1,128)}), f32[32,11,1,128]{3,2,1,0:T(1,128)S(1)}, u32[]{:S(2)}, u32[]{:S(2)}) async-start(f32[32,11,1,128]{3,2,1,0:T(1,128)} %bitcast.7), calls=%async_computation | async-start | bytes 360448 | tf_op jit(solution)/shard_map/all_to_all | solution.py:33
  9.4 3.7 %collective-permute-start = (f32[2,8,128]{2,1,0:T(8,128)S(1)}, f32[2,8,128]{2,1,0:T(8,128)S(1)}, u32[]{:S(2)}, u32[]{:S(2)}) collective-permute-start(f32[2,8,128]{2,1,0:T(8,128)S(1)} %get-tuple-element.22), channel_id=1, source_target_pairs={{0,1},{1,0},{2,3},{3,2},{4,5},{5,4},{6,7},{7,6},{8,9},{9,8},{10,11... | collective-permute-start | bytes 24584 | tf_op jit(solution)/shard_map/ppermute | solution.py:462

commit v7 on v6

--- a/solution.py
+++ b/solution.py
@@ -117,18 +117,27 @@
     return lax.dot_general(left, right, dims, preferred_element_type=F32)
 
 
-def apply_rows(cols, kernels, targets, own, scale):
-    total = cols.shape[1]
-    step = min(total, 2048)
+def products(n_chunk, columns, cols, kernels):
+    if n_chunk <= 16:
+        group = n_chunk // 4
+        prod = None
+        for begin in range(0, n_chunk, group):
+            for chunk in range(begin, begin + group):
+                columns(chunk)
+            at = pl.ds(begin * 128, group * 128)
+            part = contract(cols[:, at], kernels[:, at])
+            prod = part if prod is None else prod + part
+        return prod
+    pl.loop(0, n_chunk)(columns)
 
     def turn(i, acc):
-        at = pl.ds(pl.multiple_of(i * step, step), step)
+        at = pl.ds(pl.multiple_of(i * 2048, 2048), 2048)
         return acc + contract(cols[:, at], kernels[:, at])
 
-    if total == step:
-        prod = contract(cols[...], kernels[...])
-    else:
-        prod = lax.fori_loop(0, total // step, turn, jnp.zeros((256, 256), F32))
+    return lax.fori_loop(0, n_chunk // 16, turn, jnp.zeros((256, 256), F32))
+
+
+def image_rows(prod, targets, own, scale):
     both = prod[:128, :128] + (prod[128:, :128] + prod[:128, 128:])
     two = pltpu.roll(both, 64, 1)
 
@@ -166,9 +175,7 @@
         pl.loop(0, count)(put)
 
 
-def pack_kernel(n_col, *refs):
-    velocity, points, area, self_term, index, weight, me, out, tgt = refs[:9]
-    near = refs[9:]
+def pack_kernel(velocity, points, area, self_term, out, tgt):
     field = velocity[...]
     spot = points[...]
     rows = []
@@ -188,37 +195,36 @@
 
     each_wide(out.shape[0] // FIRST, put)
 
+
+def extra_kernel(half_chunks, me, *refs):
+    near, out = refs[:-1], refs[-1]
     row, col = me[1], me[2]
-    half = index.shape[0] // 2
-    low = low_half((half, 128))
-    for o in range(n_col):
-        to = col ^ o
-        at = lines_of(to // 2)
-        odd = to % 2 == 1
-        at_source = index[:, at]
-        at_source = (((at_source // 64) ^ row) * 64 + at_source % 64).astype(F32)
-        for i, value in enumerate((at_source, weight[:, at])):
+    lines = lax.broadcasted_iota(jnp.int32, (128, 128), 0).astype(F32)
+    for o, lists in enumerate(near):
+        count = lists.shape[0] // 2
+        half = count // 2
+        low = low_half((half, 128))
+        odd = col % 2 == 1
+        both = lists[:, lines_of(col // 2)]
+        place = both[:count].astype(jnp.int32)
+        place = (((place // 64) ^ row) * 64 + place % 64).astype(F32)
+        packed = []
+        for value in (place, both[count:]):
             top, bottom = value[:half], value[half:]
             lower = jnp.where(low, top, pltpu.roll(bottom, 64, 1))
             upper = jnp.where(low, pltpu.roll(top, 64, 1), bottom)
-            near[o][i] = jnp.where(odd, upper, lower)
-
-
-def extra_kernel(half_chunks, *refs):
-    near, out = refs[:-1], refs[-1]
-    lines = lax.broadcasted_iota(jnp.int32, (128, 128), 0)
-    for o, pair in enumerate(near):
-        index, weight = pair[0], pair[1]
+            packed.append(jnp.where(odd, upper, lower))
+        index, weight = packed
 
         def build(u):
-            line = (lines + u * 128).astype(F32)
+            line = lines + (u * 128.0 if isinstance(u, int) else (u * 128).astype(F32))
             total = jnp.zeros((128, 128), F32)
-            for k in range(index.shape[0]):
+            for k in range(half):
                 total = total + jnp.where(line == index[k : k + 1], weight[k : k + 1], 0.0)
             turned = total.T
             out[o * half_chunks + u] = turned[:64] + turned[64:]
 
-        pl.loop(0, half_chunks)(build)
+        each(half_chunks, build)
 
 
 def first_kernel(
@@ -240,11 +246,11 @@
         total.add(chunk, 0, vec, vec)
         write_columns(cols, spot, chunk, vec)
 
-    each(n_chunk, unpack)
     turned = tgt[...].T
     x = [jnp.broadcast_to(turned[:64, a : a + 1], (64, 128)) for a in range(3)]
 
     def build(chunk):
+        unpack(chunk)
         y = places[chunk]
         d = [x[a] - y[k : k + 1] for a, k in enumerate(ORDER)]
         dist = d[0] * d[0] + d[1] * d[1] + d[2] * d[2]
@@ -257,12 +263,12 @@
         kernels[0:128, at] = high
         kernels[128:256, at] = (value - high.astype(F32)).astype(BF16)
 
-    each(n_chunk, build)
+    prod = products(n_chunk, build, cols, kernels)
     norm = jnp.sqrt(total.get(0))
     scale = 1.0 / norm
     norm_out[0] = norm
     norm_out[1] = scale
-    write_piece(apply_rows(cols, kernels, tgt, basis[0], scale), out)
+    write_piece(image_rows(prod, tgt, basis[0], scale), out)
 
 
 def middle_kernel(n_row, n_col, n_base, final, piece, *refs):
@@ -315,11 +321,11 @@
             for j in range(n_base):
                 sums.add(chunk, n_base + 1 + j, vec, old[j])
 
-    each(n_chunk, columns)
+    prod = products(n_chunk, columns, cols, kernels)
     norm = jnp.sqrt(sums.get(n_base))
     scale = 1.0 / norm
     h_out[n_base] = norm
-    images = apply_rows(cols, kernels, tgt, basis[0], scale)
+    images = image_rows(prod, tgt, basis[0], scale)
     every = [*bases, basis]
     scales = [*scales, scale]
     for j, base in enumerate(every):
@@ -414,7 +420,7 @@
         out[HALF:, a, :] = density[4 : 4 + HALF, :64]
 
 
-def call(kernel, outs, scratch, operands, scalars=(), flops=0):
+def call(kernel, outs, scratch, operands, scalars=(), resident=(), flops=0):
     vmem = pl.BlockSpec(memory_space=pltpu.VMEM)
     smem = pl.BlockSpec(memory_space=pltpu.SMEM)
     count = len(operands)
@@ -422,7 +428,10 @@
     moved = sum(x.size * x.dtype.itemsize for x in operands)
     return pl.pallas_call(
         kernel,
-        out_shape=[jax.ShapeDtypeStruct(s, t) for s, t in outs],
+        out_shape=[
+            pltpu.VMEM(s, t) if i in resident else jax.ShapeDtypeStruct(s, t)
+            for i, (s, t) in enumerate(outs)
+        ],
         in_specs=specs,
         out_specs=[vmem] * len(outs),
         scratch_shapes=scratch,
@@ -441,33 +450,23 @@
     me = jnp.stack([row * n_col + col, row, col]).astype(jnp.int32)
     rhs = velocity.shape[0]
 
-    sources = [
-        velocity,
-        points,
-        panel_area[None],
-        self_term[None],
-        near_index.T,
-        near_weight.T,
-    ]
     message = ((n * LATER, 128), F32)
-    wide, tgt, *near = call(
-        functools.partial(pack_kernel, n_col),
-        [((n * FIRST, 128), F32), ((8, 128), F32)]
-        + [((2, near_index.shape[1] // 2, 128), F32)] * n_col,
+    wide, tgt = call(
+        pack_kernel,
+        [((n * FIRST, 128), F32), ((8, 128), F32)],
         [],
-        [*sources, me],
-        {6},
+        [velocity, points, panel_area[None], self_term[None]],
+        resident={0},
     )
-    near = [
-        lax.ppermute(pair, "col", xor_perm(n_col, o)) if o else pair
-        for o, pair in enumerate(near)
-    ]
     piece = spread(wide, n)
+    lists = jnp.concatenate([near_index.T.astype(F32), near_weight.T], axis=0)
+    near = [lists] + [lax.ppermute(lists, "col", xor_perm(n_col, o)) for o in range(1, n_col)]
     (extra,) = call(
         functools.partial(extra_kernel, n_row // 2),
         [((n_chunk, 64, 128), F32)],
         [],
-        near,
+        [me, *near],
+        {0},
         flops=10**9,
     )
 

time: 56.7 us -> 57.3 us (1.011)
  local copies, waits for them, and re-layouts: 0.68 us -> 2.08 us
  Pallas kernels: 10.1 us -> 9.09 us
    unnamed x12, local copies, waits for them, and re-layouts: 0.68 us -> 2.08 us
    pallas_call x6, Pallas kernels: 10.1 us -> 9.09 us  [call(): pl.pallas_call(kernel, out_shape=[pltpu.VMEM(s, t) if i in resident else...]
  transfers between devices with their start and end apart: 2 -> 2, of which waited for: 2 -> 2; matrix products, arithmetic and copies ran while one was open for 0% -> 0% of each run, Pallas kernels for 4% -> 3%
where the time goes in v7:
time: 57.3 us; the launch traced here: 56.9 us
  blocking collectives  31.4 us (55%)
  Pallas kernels  9.09 us (16%)
  starting transfers between devices  9.06 us (16%)
  waiting for transfers between devices  5.17 us (9%)
  local copies, waits for them, and re-layouts  2.08 us (4%)
    all_to_all x3, blocking collectives, spread(): return lax.all_to_all(wide, AXES, 0, 0, tiled=True).reshape(rows.shape)  31.4 us
    pallas_call x6, Pallas kernels, call(): pl.pallas_call(kernel, out_shape=[pltpu.VMEM(s, t) if i in resident else...  9.09 us
    all_to_all x1, starting transfers between devices, spread(): return lax.all_to_all(wide, AXES, 0, 0, tiled=True).reshape(rows.shape)  7.3 us
    all_to_all x1, waiting for transfers between devices, spread(): return lax.all_to_all(wide, AXES, 0, 0, tiled=True).reshape(rows.shape)  3.1 us
    ppermute x1, waiting for transfers between devices, body(): lax.ppermute(lists, 'col', xor_perm(n_col, o))  2.08 us
    unnamed x12, local copies, waits for them, and re-layouts  2.08 us
    ppermute x1, starting transfers between devices, body(): lax.ppermute(lists, 'col', xor_perm(n_col, o))  1.77 us
  transfers between devices with their start and end apart: 2, of which 2 were waited for; matrix products, arithmetic and copies ran while one was open for 0% of the time, Pallas kernels for 3%

profile of v7, /device:TPU:0, one launch (start us, length us, event | category | flops | bytes accessed | tf_op | source)
XLA Modules:
  0.0 56.9 jit_solution(13276077554507740947)
XLA Ops:
  0.0 0.0 copy-start.1
  0.0 0.0 copy-start.2
  0.0 0.0 copy-start.3
  0.0 0.7 %copy-done.1 = f32[3,64]{1,0:T(4,128)S(1)} copy-done((f32[3,64]{1,0:T(4,128)S(1)}, f32[3,64]{1,0:T(4,128)}, u32[]{:S(2)}) %copy-start.1) | copy-done | bytes 792
  0.7 0.0 copy-done.2
  0.7 0.0 copy-done.3
  0.7 0.0 copy-start
  0.7 0.7 %copy-done = f32[6,3,64]{2,1,0:T(4,128)S(1)} copy-done((f32[6,3,64]{2,1,0:T(4,128)S(1)}, f32[6,3,64]{2,1,0:T(4,128)}, u32[]{:S(2)}) %copy-start) | copy-done | bytes 4632
  1.4 0.8 %shard_map.64 = (f32[352,128]{1,0:T(8,128)}, f32[8,128]{1,0:T(8,128)S(1)}) custom-call(f32[6,3,64]{2,1,0:T(4,128)S(1)} %copy-done, f32[3,64]{1,0:T(4,128)S(1)} %copy-done.1, f32[1,64]{1,0:T(1,128)S(1)} %bitcast.25, f32[1,64]{1,0:T(1,128)S(1)} %bitcast.26), custom_call_target="tpu_custom_call" | custom-call | bytes 5888 | tf_op jit(solution)/shard_map/pallas_call | solution.py:429
  2.2 0.0 copy-start.4
  2.2 7.3 %all-to-all-start = ((f32[32,11,1,128]{3,2,1,0:T(1,128)}), f32[32,11,1,128]{3,2,1,0:T(1,128)S(1)}, u32[]{:S(2)}, u32[]{:S(2)}) async-start(f32[32,11,1,128]{3,2,1,0:T(1,128)} %bitcast.2), calls=%async_computation | async-start | bytes 360448 | tf_op jit(solution)/shard_map/all_to_all | solution.py:33
  9.5 0.0 copy-done.4
  9.5 0.0 copy-start.5
  9.5 0.7 %copy-done.5 = f32[128,16]{0,1:T(8,128)S(1)} copy-done((f32[128,16]{0,1:T(8,128)S(1)}, f32[128,16]{0,1:T(8,128)}, u32[]{:S(2)}) %copy-start.5) | copy-done | bytes 8216
  10.2 1.8 %collective-permute-start = (f32[32,128]{1,0:T(8,128)S(1)}, f32[32,128]{1,0:T(8,128)S(1)}, u32[]{:S(2)}, u32[]{:S(2)}) collective-permute-start(f32[32,128]{1,0:T(8,128)S(1)} %pad_maximum_fusion.refs_0_), channel_id=1, source_target_pairs={{0,1},{1,0},{2,3},{3,2},{4,5},{5,4},{6,7},{7,6},{8,9},{9,8},{10,11... | collective-permute-start | bytes 49160 | tf_op jit(solution)/shard_map/ppermute | solution.py:463
  12.0 0.1 pad_add_fusion.me.me_ref.refs_5_.refs_7_
  12.0 2.1 %collective-permute-done.refs_1_ = f32[32,128]{1,0:T(8,128)S(1)} collective-permute-done((f32[32,128]{1,0:T(8,128)S(1)}, f32[32,128]{1,0:T(8,128)S(1)}, u32[]{:S(2)}, u32[]{:S(2)}) %collective-permute-start) | collective-permute-done | bytes 16416 | tf_op jit(solution)/shard_map/ppermute | solution.py:463
  14.1 1.7 %shard_map.65.extra = f32[16,64,128]{2,1,0:T(8,128)S(1)} custom-call(s32[3]{0:T(128)S(1)} %pad_add_fusion.me.me_ref.refs_5_.refs_7_, f32[32,128]{1,0:T(8,128)S(1)} %pad_maximum_fusion.refs_0_, f32[32,128]{1,0:T(8,128)S(1)} %collective-permute-done.refs_1_), custom_call_target="tpu_custom_call" | custom-call | flops 1000000000 | bytes 32780 | tf_op jit(solution)/shard_map/pallas_call | solution.py:429
  15.8 3.1 %all-to-all-done = f32[32,11,1,128]{3,2,1,0:T(1,128)S(1)} async-done(((f32[32,11,1,128]{3,2,1,0:T(1,128)}), f32[32,11,1,128]{3,2,1,0:T(1,128)S(1)}, u32[]{:S(2)}, u32[]{:S(2)}) %all-to-all-start) | async-done | bytes 180256 | tf_op jit(solution)/shard_map/all_to_all | solution.py:33
  18.9 2.0 %shard_map.66 = (bf16[256,2048]{1,0:T(8,128)(2,1)S(1)}, f32[16,4,128]{2,1,0:T(4,128)S(1)}, f32[16,3,8,128]{3,2,1,0:T(8,128)S(1)}, f32[2,8,128]{2,1,0:T(8,128)S(1)}, f32[320,128]{1,0:T(8,128)S(1)}) custom-call(f32[352,128]{1,0:T(8,128)S(1)} %bitcast.18, f32[16,64,128]{2,1,0:T(8,128)S(1)} %shard_map.65.extra, ...), custom_call_target="tpu_custom_call" | custom-call | bytes 708620 | tf_op jit(solution)/shard_map/pallas_call | solution.py:429
  20.9 11.7 %all_to_all.20 = f32[32,10,1,128]{3,2,1,0:T(1,128)S(1)} all-to-all(f32[32,10,1,128]{3,2,1,0:T(1,128)S(1)} %bitcast.21), channel_id=1, replica_groups=mesh['top'=4,'mid'=2,'core'=2,'col'=2] {'top','mid','core','col'}, dimensions={0} | all-to-all | bytes 327680 | tf_op jit(solution)/shard_map/all_to_all | solution.py:33
  32.6 1.8 %shard_map.67 = (f32[16,3,8,128]{3,2,1,0:T(8,128)S(1)}, f32[3,8,128]{2,1,0:T(8,128)S(1)}, f32[320,128]{1,0:T(8,128)S(1)}, f32[2,3,8,128]{3,2,1,0:T(8,128)}) custom-call(f32[320,128]{1,0:T(8,128)S(1)} %bitcast.20, f32[16,3,8,128]{3,2,1,0:T(8,128)S(1)} %get-tuple-element.21.refs_0_, f32[2,8,128]{2,1,0:T(8,128)S(1)} %get-tuple-element.22.refs_1_.refs_2_, ...), custom_call_target="tpu_custom_call" | custom-call | bytes 1454092 | tf_op jit(solution)/shard_map/pallas_call | solution.py:429
  34.4 10.8 %all_to_all.21 = f32[32,10,1,128]{3,2,1,0:T(1,128)S(1)} all-to-all(f32[32,10,1,128]{3,2,1,0:T(1,128)S(1)} %bitcast.22), channel_id=1, replica_groups=mesh['top'=4,'mid'=2,'core'=2,'col'=2] {'top','mid','core','col'}, dimensions={0} | all-to-all | bytes 327680 | tf_op jit(solution)/shard_map/all_to_all | solution.py:33
  45.2 2.1 %shard_map.68 = (f32[16,3,8,128]{3,2,1,0:T(8,128)}, f32[6,8,128]{2,1,0:T(8,128)S(1)}, f32[32,128]{1,0:T(8,128)S(1)}, f32[3,3,8,128]{3,2,1,0:T(8,128)S(1)}) custom-call(f32[320,128]{1,0:T(8,128)S(1)} %bitcast.19, f32[16,3,8,128]{3,2,1,0:T(8,128)S(1)} %get-tuple-element.21.refs_0_, f32[16,3,8,128]{3,2,1,0:T(8,128)S(1)} %get-tuple-element.26.refs_1_, ...), custom_call_target="tpu_custom_call" | custom-call | bytes 1662988 | tf_op jit(solution)/shard_map/pallas_call | solution.py:429
  47.3 8.9 %all_to_all.22 = f32[32,1,1,128]{3,2,1,0:T(1,128)S(1)} all-to-all(f32[32,1,1,128]{3,2,1,0:T(1,128)S(1)} %bitcast.24), channel_id=1, replica_groups=mesh['top'=4,'mid'=2,'core'=2,'col'=2] {'top','mid','core','col'}, dimensions={0} | all-to-all | bytes 32768 | tf_op jit(solution)/shard_map/all_to_all | solution.py:33
  56.2 0.7 %shard_map.69 = f32[6,3,64]{2,1,0:T(4,128)} custom-call(f32[32,128]{1,0:T(8,128)S(1)} %bitcast.23, f32[3,3,8,128]{3,2,1,0:T(8,128)S(1)} %get-tuple-element.29.own, f32[3,8,128]{2,1,0:T(8,128)S(1)} %get-tuple-element.27.refs_3_.refs_0_, f32[6,8,128]{2,1,0:T(8,128)S(1)} %get-tuple-element.30.refs_1_, f32[2,8,128]{2,1,0:T(8,128)S(1)} %get-tuple-element.22.refs_1_.refs_2_), custom_call_target="tpu_custom_call" | custom-call | bytes 98304 | tf_op jit(solution)/shard_map/pallas_call | solution.py:429
  (2 shorter events, 0.0 us)
Async XLA Ops:
  0.0 0.7 %copy-start.1 = (f32[3,64]{1,0:T(4,128)S(1)}, f32[3,64]{1,0:T(4,128)}, u32[]{:S(2)}) copy-start(f32[3,64]{1,0:T(4,128)} %points.1) | copy-start | bytes 2308
  0.0 0.7 %copy-start.2 = (f32[64]{0:T(128)S(1)}, f32[64]{0:T(128)}, u32[]{:S(2)}) copy-start(f32[64]{0:T(128)} %param.8) | copy-start | bytes 772
  0.0 0.7 %copy-start.3 = (f32[64]{0:T(128)S(1)}, f32[64]{0:T(128)}, u32[]{:S(2)}) copy-start(f32[64]{0:T(128)} %param.9) | copy-start | bytes 772
  0.7 0.7 %copy-start = (f32[6,3,64]{2,1,0:T(4,128)S(1)}, f32[6,3,64]{2,1,0:T(4,128)}, u32[]{:S(2)}) copy-start(f32[6,3,64]{2,1,0:T(4,128)} %velocity.1) | copy-start | bytes 13828
  2.2 7.3 %copy-start.4 = (s32[128,16]{0,1:T(8,128)S(1)}, s32[128,16]{0,1:T(8,128)}, u32[]{:S(2)}) copy-start(s32[128,16]{0,1:T(8,128)} %param.10) | copy-start | bytes 24580
  2.2 16.7 %all-to-all-start = ((f32[32,11,1,128]{3,2,1,0:T(1,128)}), f32[32,11,1,128]{3,2,1,0:T(1,128)S(1)}, u32[]{:S(2)}, u32[]{:S(2)}) async-start(f32[32,11,1,128]{3,2,1,0:T(1,128)} %bitcast.2), calls=%async_computation | async-start | bytes 360448 | tf_op jit(solution)/shard_map/all_to_all | solution.py:33
  9.5 0.7 %copy-start.5 = (f32[128,16]{0,1:T(8,128)S(1)}, f32[128,16]{0,1:T(8,128)}, u32[]{:S(2)}) copy-start(f32[128,16]{0,1:T(8,128)} %param.11) | copy-start | bytes 24580
  10.2 3.9 %collective-permute-start = (f32[32,128]{1,0:T(8,128)S(1)}, f32[32,128]{1,0:T(8,128)S(1)}, u32[]{:S(2)}, u32[]{:S(2)}) collective-permute-start(f32[32,128]{1,0:T(8,128)S(1)} %pad_maximum_fusion.refs_0_), channel_id=1, source_target_pairs={{0,1},{1,0},{2,3},{3,2},{4,5},{5,4},{6,7},{7,6},{8,9},{9,8},{10,11... | collective-permute-start | bytes 49160 | tf_op jit(solution)/shard_map/ppermute | solution.py:463

commit v8 on v7

--- a/solution.py
+++ b/solution.py
@@ -175,7 +175,21 @@
         pl.loop(0, count)(put)
 
 
-def pack_kernel(velocity, points, area, self_term, out, tgt):
+def pack_kernel(*refs):
+    sources, outs, held, sems = refs[:6], refs[6:9], refs[9:15], refs[15]
+    out, tgt, lists = outs
+    copies = [
+        pltpu.make_async_copy(src, dst, sems.at[i])
+        for i, (src, dst) in enumerate(zip(sources, held))
+    ]
+    for copy in copies:
+        copy.start()
+    for copy in copies:
+        copy.wait()
+    velocity, points, area, self_term, index, weight = held
+    count = index.shape[0]
+    lists[:count] = index[...].astype(F32)
+    lists[count:] = weight[...]
     field = velocity[...]
     spot = points[...]
     rows = []
@@ -273,7 +287,10 @@
 
 def middle_kernel(n_row, n_col, n_base, final, piece, *refs):
     bases, norms = refs[:n_base], refs[n_base : 2 * n_base]
-    kernels, places, tgt, me_ref, basis, h_out, out, own, cols, *held = refs[2 * n_base :]
+    if final:
+        kernels, places, tgt, me_ref, own, h_out, out, basis, cols, *held = refs[2 * n_base :]
+    else:
+        kernels, places, tgt, me_ref, basis, h_out, out, cols, *held = refs[2 * n_base :]
     n_chunk = n_row * n_col // 2
     me = me_ref[0]
     scales = [norm[norm.shape[0] - 1] for norm in norms]
@@ -326,15 +343,14 @@
     scale = 1.0 / norm
     h_out[n_base] = norm
     images = image_rows(prod, tgt, basis[0], scale)
-    every = [*bases, basis]
-    scales = [*scales, scale]
-    for j, base in enumerate(every):
-        for a in range(3):
-            own[j, a] = base[0, a] * scales[j]
     if not final:
         h_out[n_base + 1] = scale
         write_piece(images, out)
         return
+    every = [*bases, basis]
+    for j, base in enumerate(every):
+        for a in range(3):
+            own[j, a] = base[0, a] * [*scales, scale][j]
     for j in range(n_base):
         gram[j, n_base] = sums.get(n_base + 1 + j) * (scale * scales[j])
     for at, pair in enumerate(PAIRS):
@@ -420,18 +436,16 @@
         out[HALF:, a, :] = density[4 : 4 + HALF, :64]
 
 
-def call(kernel, outs, scratch, operands, scalars=(), resident=(), flops=0):
+def call(kernel, outs, scratch, operands, scalars=(), far=(), flops=0):
     vmem = pl.BlockSpec(memory_space=pltpu.VMEM)
     smem = pl.BlockSpec(memory_space=pltpu.SMEM)
     count = len(operands)
-    specs = [smem if i in scalars else vmem for i in range(count)]
+    hbm = pl.BlockSpec(memory_space=pltpu.HBM)
+    specs = [smem if i in scalars else hbm if i in far else vmem for i in range(count)]
     moved = sum(x.size * x.dtype.itemsize for x in operands)
     return pl.pallas_call(
         kernel,
-        out_shape=[
-            pltpu.VMEM(s, t) if i in resident else jax.ShapeDtypeStruct(s, t)
-            for i, (s, t) in enumerate(outs)
-        ],
+        out_shape=[jax.ShapeDtypeStruct(s, t) for s, t in outs],
         in_specs=specs,
         out_specs=[vmem] * len(outs),
         scratch_shapes=scratch,
@@ -451,15 +465,26 @@
     rhs = velocity.shape[0]
 
     message = ((n * LATER, 128), F32)
-    wide, tgt = call(
+    sources = [
+        velocity,
+        points,
+        panel_area[None],
+        self_term[None],
+        near_index.T,
+        near_weight.T,
+    ]
+    wide, tgt, lists = call(
         pack_kernel,
-        [((n * FIRST, 128), F32), ((8, 128), F32)],
-        [],
-        [velocity, points, panel_area[None], self_term[None]],
-        resident={0},
+        [
+            ((n * FIRST, 128), F32),
+            ((8, 128), F32),
+            ((2 * near_index.shape[1], near_index.shape[0]), F32),
+        ],
+        [pltpu.VMEM(x.shape, x.dtype) for x in sources] + [pltpu.SemaphoreType.DMA((6,))],
+        [pltpu.with_memory_space_constraint(x, pltpu.HBM) for x in sources],
+        far=range(6),
     )
     piece = spread(wide, n)
-    lists = jnp.concatenate([near_index.T.astype(F32), near_weight.T], axis=0)
     near = [lists] + [lax.ppermute(lists, "col", xor_perm(n_col, o)) for o in range(1, n_col)]
     (extra,) = call(
         functools.partial(extra_kernel, n_row // 2),
@@ -491,23 +516,22 @@
     for k in range(1, ITERS):
         final = k == ITERS - 1
         piece = spread(wide, n)
-        basis, column, wide, own = call(
+        main, column, wide = call(
             functools.partial(middle_kernel, n_row, n_col, k, final),
             [
-                (vec_shape, F32),
+                ((ITERS, 3, ROWS, 128) if final else vec_shape, F32),
                 ((k + 1 + (len(PAIRS) if final else 1), ROWS, 128), F32),
                 ((n, 128), F32) if final else message,
-                ((k + 1, 3, ROWS, 128), F32),
             ],
-            [cols, *held],
+            [*([pltpu.VMEM(vec_shape, F32)] if final else []), cols, *held],
             [piece, *bases, *columns, kernels, places, tgt, me],
             {2 * k + 4},
         )
-        bases.append(basis)
+        bases.append(main)
         columns.append(column)
     sums = spread(wide, n)
     (density,) = call(
-        last_kernel, [((rhs, 3, 64), F32)], [], [sums, own, *columns[1:], columns[0]]
+        last_kernel, [((rhs, 3, 64), F32)], [], [sums, bases[-1], *columns[1:], columns[0]]
     )
     return density
 

time: 57.3 us -> 55.1 us (0.962)
  local copies, waits for them, and re-layouts: 2.08 us -> 0 us
  blocking collectives: 31.4 us -> 30.7 us
  waiting for transfers between devices: 5.17 us -> 5.82 us
    unnamed x12 -> x0, local copies, waits for them, and re-layouts: 2.08 us -> none
    all_to_all x1, waiting for transfers between devices: 3.1 us -> 3.91 us  [spread(): return lax.all_to_all(wide, AXES, 0, 0, tiled=True).reshape(rows.shape)]
    all_to_all x3, blocking collectives: 31.4 us -> 30.7 us  [spread(): return lax.all_to_all(wide, AXES, 0, 0, tiled=True).reshape(rows.shape)]
where the time goes in v8:
time: 55.1 us; the launch traced here: 54.8 us
  blocking collectives  30.7 us (56%)
  starting transfers between devices  9.14 us (17%)
  Pallas kernels  9.04 us (16%)
  waiting for transfers between devices  5.82 us (11%)
    all_to_all x3, blocking collectives, spread(): return lax.all_to_all(wide, AXES, 0, 0, tiled=True).reshape(rows.shape)  30.7 us
    pallas_call x6, Pallas kernels, call(): pl.pallas_call(kernel, out_shape=[jax.ShapeDtypeStruct(s, t) for s, t in...  9.04 us
    all_to_all x1, starting transfers between devices, spread(): return lax.all_to_all(wide, AXES, 0, 0, tiled=True).reshape(rows.shape)  7.3 us
    all_to_all x1, waiting for transfers between devices, spread(): return lax.all_to_all(wide, AXES, 0, 0, tiled=True).reshape(rows.shape)  3.91 us
    ppermute x1, waiting for transfers between devices, body(): lax.ppermute(lists, 'col', xor_perm(n_col, o))  1.91 us
    ppermute x1, starting transfers between devices, body(): lax.ppermute(lists, 'col', xor_perm(n_col, o))  1.83 us
  transfers between devices with their start and end apart: 2, of which 2 were waited for; matrix products, arithmetic and copies ran while one was open for 0% of the time, Pallas kernels for 3%

profile of v8, /device:TPU:0, one launch (start us, length us, event | category | flops | bytes accessed | tf_op | source)
XLA Modules:
  0.0 54.8 jit_solution(7404989128055262755)
XLA Ops:
  0.0 1.6 %shard_map.64 = (f32[352,128]{1,0:T(8,128)}, f32[8,128]{1,0:T(8,128)S(1)}, f32[32,128]{1,0:T(8,128)S(1)}) custom-call(f32[6,3,64]{2,1,0:T(4,128)} %refs_0_.1, f32[3,64]{1,0:T(4,128)} %refs_1_.1, f32[1,64]{1,0:T(1,128)} %bitcast.26, f32[1,64]{1,0:T(1,128)} %bitcast.27, s32[16,128]{1,0:T(8,128)} %bitcast.24, f32[16,128]{1,0:T(8,128)} %bitcast.25), custom_call_target="tpu_custom_call" | custom-call | bytes 22272 | tf_op jit(solution)/shard_map/pallas_call | solution.py:446
  1.6 7.3 %all-to-all-start = ((f32[32,11,1,128]{3,2,1,0:T(1,128)}), f32[32,11,1,128]{3,2,1,0:T(1,128)S(1)}, u32[]{:S(2)}, u32[]{:S(2)}) async-start(f32[32,11,1,128]{3,2,1,0:T(1,128)} %bitcast.4), calls=%async_computation | async-start | bytes 360448 | tf_op jit(solution)/shard_map/all_to_all | solution.py:33
  8.9 1.8 %collective-permute-start = (f32[32,128]{1,0:T(8,128)S(1)}, f32[32,128]{1,0:T(8,128)S(1)}, u32[]{:S(2)}, u32[]{:S(2)}) collective-permute-start(f32[32,128]{1,0:T(8,128)S(1)} %get-tuple-element.20.refs_0_), channel_id=1, source_target_pairs={{0,1},{1,0},{2,3},{3,2},{4,5},{5,4},{6,7},{7,6},{8,9},{9,8},{10,11... | collective-permute-start | bytes 49160 | tf_op jit(solution)/shard_map/ppermute | solution.py:488
  10.7 0.1 pad_add_fusion.me.me_ref.refs_5_.refs_7_
  10.8 1.9 %collective-permute-done.refs_1_ = f32[32,128]{1,0:T(8,128)S(1)} collective-permute-done((f32[32,128]{1,0:T(8,128)S(1)}, f32[32,128]{1,0:T(8,128)S(1)}, u32[]{:S(2)}, u32[]{:S(2)}) %collective-permute-start) | collective-permute-done | bytes 16416 | tf_op jit(solution)/shard_map/ppermute | solution.py:488
  12.7 1.7 %shard_map.65.extra = f32[16,64,128]{2,1,0:T(8,128)S(1)} custom-call(s32[3]{0:T(128)S(1)} %pad_add_fusion.me.me_ref.refs_5_.refs_7_, f32[32,128]{1,0:T(8,128)S(1)} %get-tuple-element.20.refs_0_, f32[32,128]{1,0:T(8,128)S(1)} %collective-permute-done.refs_1_), custom_call_target="tpu_custom_call" | custom-call | flops 1000000000 | bytes 32780 | tf_op jit(solution)/shard_map/pallas_call | solution.py:446
  14.4 3.9 %all-to-all-done = f32[32,11,1,128]{3,2,1,0:T(1,128)S(1)} async-done(((f32[32,11,1,128]{3,2,1,0:T(1,128)}), f32[32,11,1,128]{3,2,1,0:T(1,128)S(1)}, u32[]{:S(2)}, u32[]{:S(2)}) %all-to-all-start) | async-done | bytes 180256 | tf_op jit(solution)/shard_map/all_to_all | solution.py:33
  18.3 2.0 %shard_map.66 = (bf16[256,2048]{1,0:T(8,128)(2,1)S(1)}, f32[16,4,128]{2,1,0:T(4,128)S(1)}, f32[16,3,8,128]{3,2,1,0:T(8,128)S(1)}, f32[2,8,128]{2,1,0:T(8,128)S(1)}, f32[320,128]{1,0:T(8,128)S(1)}) custom-call(f32[352,128]{1,0:T(8,128)S(1)} %bitcast.17, f32[16,64,128]{2,1,0:T(8,128)S(1)} %shard_map.65.extra, ...), custom_call_target="tpu_custom_call" | custom-call | bytes 708620 | tf_op jit(solution)/shard_map/pallas_call | solution.py:446
  20.3 10.9 %all_to_all.20 = f32[32,10,1,128]{3,2,1,0:T(1,128)S(1)} all-to-all(f32[32,10,1,128]{3,2,1,0:T(1,128)S(1)} %bitcast.20), channel_id=1, replica_groups=mesh['top'=4,'mid'=2,'core'=2,'col'=2] {'top','mid','core','col'}, dimensions={0} | all-to-all | bytes 327680 | tf_op jit(solution)/shard_map/all_to_all | solution.py:33
  31.2 1.5 %shard_map.67 = (f32[16,3,8,128]{3,2,1,0:T(8,128)S(1)}, f32[3,8,128]{2,1,0:T(8,128)S(1)}, f32[320,128]{1,0:T(8,128)S(1)}) custom-call(f32[320,128]{1,0:T(8,128)S(1)} %bitcast.19, f32[16,3,8,128]{3,2,1,0:T(8,128)S(1)} %get-tuple-element.23.refs_0_, f32[2,8,128]{2,1,0:T(8,128)S(1)} %get-tuple-element.24.refs_1_.refs_2_, ...), custom_call_target="tpu_custom_call" | custom-call | bytes 1454092 | tf_op jit(solution)/shard_map/pallas_call | solution.py:446
  32.7 10.8 %all_to_all.21 = f32[32,10,1,128]{3,2,1,0:T(1,128)S(1)} all-to-all(f32[32,10,1,128]{3,2,1,0:T(1,128)S(1)} %bitcast.21), channel_id=1, replica_groups=mesh['top'=4,'mid'=2,'core'=2,'col'=2] {'top','mid','core','col'}, dimensions={0} | all-to-all | bytes 327680 | tf_op jit(solution)/shard_map/all_to_all | solution.py:33
  43.6 1.5 %shard_map.68 = (f32[3,3,8,128]{3,2,1,0:T(8,128)S(1)}, f32[6,8,128]{2,1,0:T(8,128)S(1)}, f32[32,128]{1,0:T(8,128)S(1)}) custom-call(f32[320,128]{1,0:T(8,128)S(1)} %bitcast.18, f32[16,3,8,128]{3,2,1,0:T(8,128)S(1)} %get-tuple-element.23.refs_0_, f32[16,3,8,128]{3,2,1,0:T(8,128)S(1)} %get-tuple-element.28.refs_1_, ...), custom_call_target="tpu_custom_call" | custom-call | bytes 1662988 | tf_op jit(solution)/shard_map/pallas_call | solution.py:446
  45.1 8.9 %all_to_all.22 = f32[32,1,1,128]{3,2,1,0:T(1,128)S(1)} all-to-all(f32[32,1,1,128]{3,2,1,0:T(1,128)S(1)} %bitcast.23), channel_id=1, replica_groups=mesh['top'=4,'mid'=2,'core'=2,'col'=2] {'top','mid','core','col'}, dimensions={0} | all-to-all | bytes 32768 | tf_op jit(solution)/shard_map/all_to_all | solution.py:33
  54.0 0.7 %shard_map.69 = f32[6,3,64]{2,1,0:T(4,128)} custom-call(f32[32,128]{1,0:T(8,128)S(1)} %bitcast.22, f32[3,3,8,128]{3,2,1,0:T(8,128)S(1)} %get-tuple-element.31.own, f32[3,8,128]{2,1,0:T(8,128)S(1)} %get-tuple-element.29.refs_3_.refs_0_, f32[6,8,128]{2,1,0:T(8,128)S(1)} %get-tuple-element.32.refs_1_, f32[2,8,128]{2,1,0:T(8,128)S(1)} %get-tuple-element.24.refs_1_.refs_2_), custom_call_target="tpu_custom_call" | custom-call | bytes 98304 | tf_op jit(solution)/shard_map/pallas_call | solution.py:446
Async XLA Ops:
  1.6 16.7 %all-to-all-start = ((f32[32,11,1,128]{3,2,1,0:T(1,128)}), f32[32,11,1,128]{3,2,1,0:T(1,128)S(1)}, u32[]{:S(2)}, u32[]{:S(2)}) async-start(f32[32,11,1,128]{3,2,1,0:T(1,128)} %bitcast.4), calls=%async_computation | async-start | bytes 360448 | tf_op jit(solution)/shard_map/all_to_all | solution.py:33
  8.9 3.8 %collective-permute-start = (f32[32,128]{1,0:T(8,128)S(1)}, f32[32,128]{1,0:T(8,128)S(1)}, u32[]{:S(2)}, u32[]{:S(2)}) collective-permute-start(f32[32,128]{1,0:T(8,128)S(1)} %get-tuple-element.20.refs_0_), channel_id=1, source_target_pairs={{0,1},{1,0},{2,3},{3,2},{4,5},{5,4},{6,7},{7,6},{8,9},{9,8},{10,11... | collective-permute-start | bytes 49160 | tf_op jit(solution)/shard_map/ppermute | solution.py:488

commit v9 on v8

--- a/solution.py
+++ b/solution.py
@@ -119,15 +119,9 @@
 
 def products(n_chunk, columns, cols, kernels):
     if n_chunk <= 16:
-        group = n_chunk // 4
-        prod = None
-        for begin in range(0, n_chunk, group):
-            for chunk in range(begin, begin + group):
-                columns(chunk)
-            at = pl.ds(begin * 128, group * 128)
-            part = contract(cols[:, at], kernels[:, at])
-            prod = part if prod is None else prod + part
-        return prod
+        for chunk in range(n_chunk):
+            columns(chunk)
+        return contract(cols[...], kernels[...])
     pl.loop(0, n_chunk)(columns)
 
     def turn(i, acc):
@@ -137,7 +131,7 @@
     return lax.fori_loop(0, n_chunk // 16, turn, jnp.zeros((256, 256), F32))
 
 
-def image_rows(prod, targets, own, scale):
+def image_rows(prod, targets, own):
     both = prod[:128, :128] + (prod[128:, :128] + prod[:128, 128:])
     two = pltpu.roll(both, 64, 1)
 
@@ -150,7 +144,7 @@
     for a in range(3):
         cross = sum(x[b] * group(4 + 3 * a + b) for b in range(3))
         image = both[8 * a : 8 * a + 8] + x[a] * along - cross + group(13 + a)
-        images.append((image + targets[3:4] * own[a]) * scale)
+        images.append(image + targets[3:4] * own[a])
     return images
 
 
@@ -242,7 +236,7 @@
 
 
 def first_kernel(
-    n_row, n_col, piece, extra, tgt, me_ref, kernels, places, basis, norm_out, out, cols, *sums
+    n_row, n_col, piece, extra, tgt, me_ref, kernels, places, basis, mine, norm_out, out, cols, *sums
 ):
     n_chunk = n_row * n_col // 2
     me = me_ref[0]
@@ -282,15 +276,19 @@
     scale = 1.0 / norm
     norm_out[0] = norm
     norm_out[1] = scale
-    write_piece(image_rows(prod, tgt, basis[0], scale), out)
+    images = [image * scale for image in image_rows(prod, tgt, basis[0])]
+    for a in range(3):
+        mine[a] = images[a]
+    write_piece(images, out)
 
 
 def middle_kernel(n_row, n_col, n_base, final, piece, *refs):
-    bases, norms = refs[:n_base], refs[n_base : 2 * n_base]
+    bases, norms, before = (refs[i * n_base : (i + 1) * n_base] for i in range(3))
+    kernels, places, tgt, me_ref, *rest = refs[3 * n_base :]
     if final:
-        kernels, places, tgt, me_ref, own, h_out, out, basis, cols, *held = refs[2 * n_base :]
+        own, h_out, out, basis, cols, *held = rest
     else:
-        kernels, places, tgt, me_ref, basis, h_out, out, cols, *held = refs[2 * n_base :]
+        basis, mine, h_out, out, cols, *held = rest
     n_chunk = n_row * n_col // 2
     me = me_ref[0]
     scales = [norm[norm.shape[0] - 1] for norm in norms]
@@ -305,12 +303,14 @@
         old = [[base[chunk, a] for a in range(3)] for base in bases]
         for a in range(3):
             basis[chunk, a] = vec[a]
+        write_columns(cols, places[chunk], chunk, vec)
         for j in range(n_base):
             sums.add(chunk, j, vec, old[j])
         for at, (i, j) in enumerate(cross):
             sums.add(chunk, 2 * n_base + 1 + at, old[i], old[j])
 
-    each(n_chunk, unpack)
+    prod = products(n_chunk, unpack, cols, kernels)
+    raw = image_rows(prod, tgt, basis[0])
     gram = {}
     for at, (i, j) in enumerate(cross):
         gram[j, i] = sums.get(2 * n_base + 1 + at) * (scales[i] * scales[j])
@@ -323,7 +323,7 @@
         h_out[j] = h
     factors = [h * scale for h, scale in zip(column, scales)]
 
-    def columns(chunk):
+    def take(chunk):
         old = [[base[chunk, a] for a in range(3)] for base in bases]
         vec = []
         for a in range(3):
@@ -333,17 +333,21 @@
             vec.append(value)
             basis[chunk, a] = value
         sums.add(chunk, n_base, vec, vec)
-        write_columns(cols, places[chunk], chunk, vec)
         if final:
             for j in range(n_base):
                 sums.add(chunk, n_base + 1 + j, vec, old[j])
 
-    prod = products(n_chunk, columns, cols, kernels)
+    each(n_chunk, take)
     norm = jnp.sqrt(sums.get(n_base))
     scale = 1.0 / norm
     h_out[n_base] = norm
-    images = image_rows(prod, tgt, basis[0], scale)
+    images = [
+        (raw[a] - sum(column[j] * before[j][a] for j in range(n_base))) * scale
+        for a in range(3)
+    ]
     if not final:
+        for a in range(3):
+            mine[a] = images[a]
         h_out[n_base + 1] = scale
         write_piece(images, out)
         return
@@ -498,12 +502,13 @@
     vec_shape = (n_chunk, 3, ROWS, 128)
     cols = pltpu.VMEM((256, total), BF16)
     held = [] if n_chunk <= 16 else [pltpu.VMEM((8, ROWS, 128), F32)]
-    kernels, places, basis, norm, wide = call(
+    kernels, places, basis, image, norm, wide = call(
         functools.partial(first_kernel, n_row, n_col),
         [
             ((256, total), BF16),
             ((n_chunk, 4, 128), F32),
             (vec_shape, F32),
+            ((3, ROWS, 128), F32),
             ((2, ROWS, 128), F32),
             message,
         ],
@@ -513,22 +518,25 @@
     )
     bases = [basis]
     columns = [norm]
+    images = [image]
     for k in range(1, ITERS):
         final = k == ITERS - 1
         piece = spread(wide, n)
-        main, column, wide = call(
+        main, *image, column, wide = call(
             functools.partial(middle_kernel, n_row, n_col, k, final),
             [
                 ((ITERS, 3, ROWS, 128) if final else vec_shape, F32),
+                *([] if final else [((3, ROWS, 128), F32)]),
                 ((k + 1 + (len(PAIRS) if final else 1), ROWS, 128), F32),
                 ((n, 128), F32) if final else message,
             ],
             [*([pltpu.VMEM(vec_shape, F32)] if final else []), cols, *held],
-            [piece, *bases, *columns, kernels, places, tgt, me],
-            {2 * k + 4},
+            [piece, *bases, *columns, *images, kernels, places, tgt, me],
+            {3 * k + 4},
         )
         bases.append(main)
         columns.append(column)
+        images += image
     sums = spread(wide, n)
     (density,) = call(
         last_kernel, [((rhs, 3, 64), F32)], [], [sums, bases[-1], *columns[1:], columns[0]]

time: 55.1 us -> 55 us (level)
  no operation moved by 1% of the time
where the time goes in v9:
time: 55 us; the launch traced here: 54.8 us
  blocking collectives  30.7 us (56%)
  starting transfers between devices  9.14 us (17%)
  Pallas kernels  9.03 us (16%)
  waiting for transfers between devices  5.82 us (11%)
    all_to_all x3, blocking collectives, spread(): return lax.all_to_all(wide, AXES, 0, 0, tiled=True).reshape(rows.shape)  30.7 us
    pallas_call x6, Pallas kernels, call(): pl.pallas_call(kernel, out_shape=[jax.ShapeDtypeStruct(s, t) for s, t in...  9.03 us
    all_to_all x1, starting transfers between devices, spread(): return lax.all_to_all(wide, AXES, 0, 0, tiled=True).reshape(rows.shape)  7.3 us
    all_to_all x1, waiting for transfers between devices, spread(): return lax.all_to_all(wide, AXES, 0, 0, tiled=True).reshape(rows.shape)  3.91 us
    ppermute x1, waiting for transfers between devices, body(): lax.ppermute(lists, 'col', xor_perm(n_col, o))  1.91 us
    ppermute x1, starting transfers between devices, body(): lax.ppermute(lists, 'col', xor_perm(n_col, o))  1.83 us
  transfers between devices with their start and end apart: 2, of which 2 were waited for; matrix products, arithmetic and copies ran while one was open for 0% of the time, Pallas kernels for 3%

profile of v9, /device:TPU:0, one launch (start us, length us, event | category | flops | bytes accessed | tf_op | source)
XLA Modules:
  0.0 54.8 jit_solution(1575310878547958282)
XLA Ops:
  0.0 1.6 %shard_map.64 = (f32[352,128]{1,0:T(8,128)}, f32[8,128]{1,0:T(8,128)S(1)}, f32[32,128]{1,0:T(8,128)S(1)}) custom-call(f32[6,3,64]{2,1,0:T(4,128)} %refs_0_.1, f32[3,64]{1,0:T(4,128)} %refs_1_.1, f32[1,64]{1,0:T(1,128)} %bitcast.26, f32[1,64]{1,0:T(1,128)} %bitcast.27, s32[16,128]{1,0:T(8,128)} %bitcast.24, f32[16,128]{1,0:T(8,128)} %bitcast.25), custom_call_target="tpu_custom_call" | custom-call | bytes 22272 | tf_op jit(solution)/shard_map/pallas_call | solution.py:450
  1.6 7.3 %all-to-all-start = ((f32[32,11,1,128]{3,2,1,0:T(1,128)}), f32[32,11,1,128]{3,2,1,0:T(1,128)S(1)}, u32[]{:S(2)}, u32[]{:S(2)}) async-start(f32[32,11,1,128]{3,2,1,0:T(1,128)} %bitcast.4), calls=%async_computation | async-start | bytes 360448 | tf_op jit(solution)/shard_map/all_to_all | solution.py:33
  8.9 1.8 %collective-permute-start = (f32[32,128]{1,0:T(8,128)S(1)}, f32[32,128]{1,0:T(8,128)S(1)}, u32[]{:S(2)}, u32[]{:S(2)}) collective-permute-start(f32[32,128]{1,0:T(8,128)S(1)} %get-tuple-element.22.refs_0_), channel_id=1, source_target_pairs={{0,1},{1,0},{2,3},{3,2},{4,5},{5,4},{6,7},{7,6},{8,9},{9,8},{10,11... | collective-permute-start | bytes 49160 | tf_op jit(solution)/shard_map/ppermute | solution.py:492
  10.7 0.1 pad_add_fusion.me.me_ref.refs_6_.refs_9_
  10.8 1.9 %collective-permute-done.refs_1_ = f32[32,128]{1,0:T(8,128)S(1)} collective-permute-done((f32[32,128]{1,0:T(8,128)S(1)}, f32[32,128]{1,0:T(8,128)S(1)}, u32[]{:S(2)}, u32[]{:S(2)}) %collective-permute-start) | collective-permute-done | bytes 16416 | tf_op jit(solution)/shard_map/ppermute | solution.py:492
  12.7 1.7 %shard_map.65.extra = f32[16,64,128]{2,1,0:T(8,128)S(1)} custom-call(s32[3]{0:T(128)S(1)} %pad_add_fusion.me.me_ref.refs_6_.refs_9_, f32[32,128]{1,0:T(8,128)S(1)} %get-tuple-element.22.refs_0_, f32[32,128]{1,0:T(8,128)S(1)} %collective-permute-done.refs_1_), custom_call_target="tpu_custom_call" | custom-call | flops 1000000000 | bytes 32780 | tf_op jit(solution)/shard_map/pallas_call | solution.py:450
  14.4 3.9 %all-to-all-done = f32[32,11,1,128]{3,2,1,0:T(1,128)S(1)} async-done(((f32[32,11,1,128]{3,2,1,0:T(1,128)}), f32[32,11,1,128]{3,2,1,0:T(1,128)S(1)}, u32[]{:S(2)}, u32[]{:S(2)}) %all-to-all-start) | async-done | bytes 180256 | tf_op jit(solution)/shard_map/all_to_all | solution.py:33
  18.3 2.0 %shard_map.66 = (bf16[256,2048]{1,0:T(8,128)(2,1)S(1)}, f32[16,4,128]{2,1,0:T(4,128)S(1)}, f32[16,3,8,128]{3,2,1,0:T(8,128)S(1)}, f32[3,8,128]{2,1,0:T(8,128)S(1...) custom-call(f32[352,128]{1,0:T(8,128)S(1)} %bitcast.17, f32[16,64,128]{2,1,0:T(8,128)S(1)} %shard_map.65.extra, ...), custom_call_target="tpu_custom_call" | custom-call | bytes 708620 | tf_op jit(solution)/shard_map/pallas_call | solution.py:450
  20.4 10.9 %all_to_all.20 = f32[32,10,1,128]{3,2,1,0:T(1,128)S(1)} all-to-all(f32[32,10,1,128]{3,2,1,0:T(1,128)S(1)} %bitcast.20), channel_id=1, replica_groups=mesh['top'=4,'mid'=2,'core'=2,'col'=2] {'top','mid','core','col'}, dimensions={0} | all-to-all | bytes 327680 | tf_op jit(solution)/shard_map/all_to_all | solution.py:33
  31.3 1.5 %shard_map.67 = (f32[16,3,8,128]{3,2,1,0:T(8,128)S(1)}, f32[3,8,128]{2,1,0:T(8,128)S(1)}, f32[3,8,128]{2,1,0:T(8,128)S(1)}, f32[320,128]{1,0:T(8,128)S(1)}) custom-call(f32[320,128]{1,0:T(8,128)S(1)} %bitcast.19, f32[16,3,8,128]{3,2,1,0:T(8,128)S(1)} %get-tuple-element.25.refs_0_, f32[2,8,128]{2,1,0:T(8,128)S(1)} %get-tuple-element.26.refs_1_.refs_2_, ...), custom_call_target="tpu_custom_call" | custom-call | bytes 1466380 | tf_op jit(solution)/shard_map/pallas_call | solution.py:450
  32.8 10.8 %all_to_all.21 = f32[32,10,1,128]{3,2,1,0:T(1,128)S(1)} all-to-all(f32[32,10,1,128]{3,2,1,0:T(1,128)S(1)} %bitcast.21), channel_id=1, replica_groups=mesh['top'=4,'mid'=2,'core'=2,'col'=2] {'top','mid','core','col'}, dimensions={0} | all-to-all | bytes 327680 | tf_op jit(solution)/shard_map/all_to_all | solution.py:33
  43.6 1.5 %shard_map.68 = (f32[3,3,8,128]{3,2,1,0:T(8,128)S(1)}, f32[6,8,128]{2,1,0:T(8,128)S(1)}, f32[32,128]{1,0:T(8,128)S(1)}) custom-call(f32[320,128]{1,0:T(8,128)S(1)} %bitcast.18, f32[16,3,8,128]{3,2,1,0:T(8,128)S(1)} %get-tuple-element.25.refs_0_, f32[16,3,8,128]{3,2,1,0:T(8,128)S(1)} %get-tuple-element.31.refs_1_, ...), custom_call_target="tpu_custom_call" | custom-call | bytes 1687564 | tf_op jit(solution)/shard_map/pallas_call | solution.py:450
  45.1 8.9 %all_to_all.22 = f32[32,1,1,128]{3,2,1,0:T(1,128)S(1)} all-to-all(f32[32,1,1,128]{3,2,1,0:T(1,128)S(1)} %bitcast.23), channel_id=1, replica_groups=mesh['top'=4,'mid'=2,'core'=2,'col'=2] {'top','mid','core','col'}, dimensions={0} | all-to-all | bytes 32768 | tf_op jit(solution)/shard_map/all_to_all | solution.py:33
  54.0 0.7 %shard_map.69 = f32[6,3,64]{2,1,0:T(4,128)} custom-call(f32[32,128]{1,0:T(8,128)S(1)} %bitcast.22, f32[3,3,8,128]{3,2,1,0:T(8,128)S(1)} %get-tuple-element.35.own, f32[3,8,128]{2,1,0:T(8,128)S(1)} %get-tuple-element.32.refs_3_.refs_0_, f32[6,8,128]{2,1,0:T(8,128)S(1)} %get-tuple-element.36.refs_1_, f32[2,8,128]{2,1,0:T(8,128)S(1)} %get-tuple-element.26.refs_1_.refs_2_), custom_call_target="tpu_custom_call" | custom-call | bytes 98304 | tf_op jit(solution)/shard_map/pallas_call | solution.py:450
Async XLA Ops:
  1.6 16.7 %all-to-all-start = ((f32[32,11,1,128]{3,2,1,0:T(1,128)}), f32[32,11,1,128]{3,2,1,0:T(1,128)S(1)}, u32[]{:S(2)}, u32[]{:S(2)}) async-start(f32[32,11,1,128]{3,2,1,0:T(1,128)} %bitcast.4), calls=%async_computation | async-start | bytes 360448 | tf_op jit(solution)/shard_map/all_to_all | solution.py:33
  8.9 3.8 %collective-permute-start = (f32[32,128]{1,0:T(8,128)S(1)}, f32[32,128]{1,0:T(8,128)S(1)}, u32[]{:S(2)}, u32[]{:S(2)}) collective-permute-start(f32[32,128]{1,0:T(8,128)S(1)} %get-tuple-element.22.refs_0_), channel_id=1, source_target_pairs={{0,1},{1,0},{2,3},{3,2},{4,5},{5,4},{6,7},{7,6},{8,9},{9,8},{10,11... | collective-permute-start | bytes 49160 | tf_op jit(solution)/shard_map/ppermute | solution.py:492

commit v10 on v8

--- a/solution.py
+++ b/solution.py
@@ -112,33 +112,28 @@
     cols[128:256, at] = low
 
 
-def contract(left, right):
-    dims = (((1,), (1,)), ((), ()))
-    return lax.dot_general(left, right, dims, preferred_element_type=F32)
+def contract(cols, kernels):
+    first = jnp.dot(cols[:128], kernels, preferred_element_type=F32)
+    second = jnp.dot(cols[128:], kernels[:, :128], preferred_element_type=F32)
+    return first[:, :128] + (second + first[:, 128:])
 
 
 def products(n_chunk, columns, cols, kernels):
     if n_chunk <= 16:
-        group = n_chunk // 4
-        prod = None
-        for begin in range(0, n_chunk, group):
-            for chunk in range(begin, begin + group):
-                columns(chunk)
-            at = pl.ds(begin * 128, group * 128)
-            part = contract(cols[:, at], kernels[:, at])
-            prod = part if prod is None else prod + part
-        return prod
+        for chunk in range(n_chunk):
+            columns(chunk)
+        return contract(cols[...], kernels[...])
     pl.loop(0, n_chunk)(columns)
 
     def turn(i, acc):
         at = pl.ds(pl.multiple_of(i * 2048, 2048), 2048)
-        return acc + contract(cols[:, at], kernels[:, at])
-
-    return lax.fori_loop(0, n_chunk // 16, turn, jnp.zeros((256, 256), F32))
+        return acc + contract(cols[:, at], kernels[at, :])
+
+    return lax.fori_loop(0, n_chunk // 16, turn, jnp.zeros((128, 128), F32))
 
 
 def image_rows(prod, targets, own, scale):
-    both = prod[:128, :128] + (prod[128:, :128] + prod[:128, 128:])
+    both = prod
     two = pltpu.roll(both, 64, 1)
 
     def group(k):
@@ -271,11 +266,11 @@
         root = lax.rsqrt(dist + BLOB_SQ)
         two = (y[3:4] * INV_EIGHT_PI) * root * root * root
         one = (dist + 2.0 * BLOB_SQ) * two + extra[chunk]
-        value = jnp.concatenate([one, two], axis=0)
+        value = jnp.concatenate([one, two], axis=0).T
         high = value.astype(BF16)
         at = lines_of(chunk)
-        kernels[0:128, at] = high
-        kernels[128:256, at] = (value - high.astype(F32)).astype(BF16)
+        kernels[at, 0:128] = high
+        kernels[at, 128:256] = (value - high.astype(F32)).astype(BF16)
 
     prod = products(n_chunk, build, cols, kernels)
     norm = jnp.sqrt(total.get(0))
@@ -501,7 +496,7 @@
     kernels, places, basis, norm, wide = call(
         functools.partial(first_kernel, n_row, n_col),
         [
-            ((256, total), BF16),
+            ((total, 256), BF16),
             ((n_chunk, 4, 128), F32),
             (vec_shape, F32),
             ((2, ROWS, 128), F32),

time: 55.1 us -> 54.9 us (level)
  no operation moved by 1% of the time
where the time goes in v10:
time: 54.9 us; the launch traced here: 54.6 us
  blocking collectives  30.7 us (56%)
  starting transfers between devices  9.14 us (17%)
  Pallas kernels  8.84 us (16%)
  waiting for transfers between devices  5.82 us (11%)
    all_to_all x3, blocking collectives, spread(): return lax.all_to_all(wide, AXES, 0, 0, tiled=True).reshape(rows.shape)  30.7 us
    pallas_call x6, Pallas kernels, call(): pl.pallas_call(kernel, out_shape=[jax.ShapeDtypeStruct(s, t) for s, t in...  8.84 us
    all_to_all x1, starting transfers between devices, spread(): return lax.all_to_all(wide, AXES, 0, 0, tiled=True).reshape(rows.shape)  7.3 us
    all_to_all x1, waiting for transfers between devices, spread(): return lax.all_to_all(wide, AXES, 0, 0, tiled=True).reshape(rows.shape)  3.91 us
    ppermute x1, waiting for transfers between devices, body(): lax.ppermute(lists, 'col', xor_perm(n_col, o))  1.91 us
    ppermute x1, starting transfers between devices, body(): lax.ppermute(lists, 'col', xor_perm(n_col, o))  1.83 us
  transfers between devices with their start and end apart: 2, of which 2 were waited for; matrix products, arithmetic and copies ran while one was open for 0% of the time, Pallas kernels for 3%

profile of v10, /device:TPU:0, one launch (start us, length us, event | category | flops | bytes accessed | tf_op | source)
XLA Modules:
  0.0 54.6 jit_solution(17844631420745068384)
XLA Ops:
  0.0 1.6 %shard_map.64 = (f32[352,128]{1,0:T(8,128)}, f32[8,128]{1,0:T(8,128)S(1)}, f32[32,128]{1,0:T(8,128)S(1)}) custom-call(f32[6,3,64]{2,1,0:T(4,128)} %refs_0_.1, f32[3,64]{1,0:T(4,128)} %refs_1_.1, f32[1,64]{1,0:T(1,128)} %bitcast.26, f32[1,64]{1,0:T(1,128)} %bitcast.27, s32[16,128]{1,0:T(8,128)} %bitcast.24, f32[16,128]{1,0:T(8,128)} %bitcast.25), custom_call_target="tpu_custom_call" | custom-call | bytes 22272 | tf_op jit(solution)/shard_map/pallas_call | solution.py:441
  1.6 7.3 %all-to-all-start = ((f32[32,11,1,128]{3,2,1,0:T(1,128)}), f32[32,11,1,128]{3,2,1,0:T(1,128)S(1)}, u32[]{:S(2)}, u32[]{:S(2)}) async-start(f32[32,11,1,128]{3,2,1,0:T(1,128)} %bitcast.4), calls=%async_computation | async-start | bytes 360448 | tf_op jit(solution)/shard_map/all_to_all | solution.py:33
  8.9 1.8 %collective-permute-start = (f32[32,128]{1,0:T(8,128)S(1)}, f32[32,128]{1,0:T(8,128)S(1)}, u32[]{:S(2)}, u32[]{:S(2)}) collective-permute-start(f32[32,128]{1,0:T(8,128)S(1)} %get-tuple-element.20.refs_0_), channel_id=1, source_target_pairs={{0,1},{1,0},{2,3},{3,2},{4,5},{5,4},{6,7},{7,6},{8,9},{9,8},{10,11... | collective-permute-start | bytes 49160 | tf_op jit(solution)/shard_map/ppermute | solution.py:483
  10.7 0.1 pad_add_fusion.me.me_ref.refs_5_.refs_7_
  10.8 1.9 %collective-permute-done.refs_1_ = f32[32,128]{1,0:T(8,128)S(1)} collective-permute-done((f32[32,128]{1,0:T(8,128)S(1)}, f32[32,128]{1,0:T(8,128)S(1)}, u32[]{:S(2)}, u32[]{:S(2)}) %collective-permute-start) | collective-permute-done | bytes 16416 | tf_op jit(solution)/shard_map/ppermute | solution.py:483
  12.7 1.7 %shard_map.65.extra = f32[16,64,128]{2,1,0:T(8,128)S(1)} custom-call(s32[3]{0:T(128)S(1)} %pad_add_fusion.me.me_ref.refs_5_.refs_7_, f32[32,128]{1,0:T(8,128)S(1)} %get-tuple-element.20.refs_0_, f32[32,128]{1,0:T(8,128)S(1)} %collective-permute-done.refs_1_), custom_call_target="tpu_custom_call" | custom-call | flops 1000000000 | bytes 32780 | tf_op jit(solution)/shard_map/pallas_call | solution.py:441
  14.4 3.9 %all-to-all-done = f32[32,11,1,128]{3,2,1,0:T(1,128)S(1)} async-done(((f32[32,11,1,128]{3,2,1,0:T(1,128)}), f32[32,11,1,128]{3,2,1,0:T(1,128)S(1)}, u32[]{:S(2)}, u32[]{:S(2)}) %all-to-all-start) | async-done | bytes 180256 | tf_op jit(solution)/shard_map/all_to_all | solution.py:33
  18.3 1.9 %shard_map.66 = (bf16[2048,256]{1,0:T(8,128)(2,1)S(1)}, f32[16,4,128]{2,1,0:T(4,128)S(1)}, f32[16,3,8,128]{3,2,1,0:T(8,128)S(1)}, f32[2,8,128]{2,1,0:T(8,128)S(1)}, f32[320,128]{1,0:T(8,128)S(1)}) custom-call(f32[352,128]{1,0:T(8,128)S(1)} %bitcast.17, f32[16,64,128]{2,1,0:T(8,128)S(1)} %shard_map.65.extra, ...), custom_call_target="tpu_custom_call" | custom-call | bytes 708620 | tf_op jit(solution)/shard_map/pallas_call | solution.py:441
  20.2 10.9 %all_to_all.20 = f32[32,10,1,128]{3,2,1,0:T(1,128)S(1)} all-to-all(f32[32,10,1,128]{3,2,1,0:T(1,128)S(1)} %bitcast.20), channel_id=1, replica_groups=mesh['top'=4,'mid'=2,'core'=2,'col'=2] {'top','mid','core','col'}, dimensions={0} | all-to-all | bytes 327680 | tf_op jit(solution)/shard_map/all_to_all | solution.py:33
  31.1 1.5 %shard_map.67 = (f32[16,3,8,128]{3,2,1,0:T(8,128)S(1)}, f32[3,8,128]{2,1,0:T(8,128)S(1)}, f32[320,128]{1,0:T(8,128)S(1)}) custom-call(f32[320,128]{1,0:T(8,128)S(1)} %bitcast.19, f32[16,3,8,128]{3,2,1,0:T(8,128)S(1)} %get-tuple-element.23.refs_0_, f32[2,8,128]{2,1,0:T(8,128)S(1)} %get-tuple-element.24.refs_1_.refs_2_, ...), custom_call_target="tpu_custom_call" | custom-call | bytes 1454092 | tf_op jit(solution)/shard_map/pallas_call | solution.py:441
  32.6 10.8 %all_to_all.21 = f32[32,10,1,128]{3,2,1,0:T(1,128)S(1)} all-to-all(f32[32,10,1,128]{3,2,1,0:T(1,128)S(1)} %bitcast.21), channel_id=1, replica_groups=mesh['top'=4,'mid'=2,'core'=2,'col'=2] {'top','mid','core','col'}, dimensions={0} | all-to-all | bytes 327680 | tf_op jit(solution)/shard_map/all_to_all | solution.py:33
  43.5 1.5 %shard_map.68 = (f32[3,3,8,128]{3,2,1,0:T(8,128)S(1)}, f32[6,8,128]{2,1,0:T(8,128)S(1)}, f32[32,128]{1,0:T(8,128)S(1)}) custom-call(f32[320,128]{1,0:T(8,128)S(1)} %bitcast.18, f32[16,3,8,128]{3,2,1,0:T(8,128)S(1)} %get-tuple-element.23.refs_0_, f32[16,3,8,128]{3,2,1,0:T(8,128)S(1)} %get-tuple-element.28.refs_1_, ...), custom_call_target="tpu_custom_call" | custom-call | bytes 1662988 | tf_op jit(solution)/shard_map/pallas_call | solution.py:441
  44.9 8.9 %all_to_all.22 = f32[32,1,1,128]{3,2,1,0:T(1,128)S(1)} all-to-all(f32[32,1,1,128]{3,2,1,0:T(1,128)S(1)} %bitcast.23), channel_id=1, replica_groups=mesh['top'=4,'mid'=2,'core'=2,'col'=2] {'top','mid','core','col'}, dimensions={0} | all-to-all | bytes 32768 | tf_op jit(solution)/shard_map/all_to_all | solution.py:33
  53.8 0.7 %shard_map.69 = f32[6,3,64]{2,1,0:T(4,128)} custom-call(f32[32,128]{1,0:T(8,128)S(1)} %bitcast.22, f32[3,3,8,128]{3,2,1,0:T(8,128)S(1)} %get-tuple-element.31.own, f32[3,8,128]{2,1,0:T(8,128)S(1)} %get-tuple-element.29.refs_3_.refs_0_, f32[6,8,128]{2,1,0:T(8,128)S(1)} %get-tuple-element.32.refs_1_, f32[2,8,128]{2,1,0:T(8,128)S(1)} %get-tuple-element.24.refs_1_.refs_2_), custom_call_target="tpu_custom_call" | custom-call | bytes 98304 | tf_op jit(solution)/shard_map/pallas_call | solution.py:441
Async XLA Ops:
  1.6 16.7 %all-to-all-start = ((f32[32,11,1,128]{3,2,1,0:T(1,128)}), f32[32,11,1,128]{3,2,1,0:T(1,128)S(1)}, u32[]{:S(2)}, u32[]{:S(2)}) async-start(f32[32,11,1,128]{3,2,1,0:T(1,128)} %bitcast.4), calls=%async_computation | async-start | bytes 360448 | tf_op jit(solution)/shard_map/all_to_all | solution.py:33
  8.9 3.8 %collective-permute-start = (f32[32,128]{1,0:T(8,128)S(1)}, f32[32,128]{1,0:T(8,128)S(1)}, u32[]{:S(2)}, u32[]{:S(2)}) collective-permute-start(f32[32,128]{1,0:T(8,128)S(1)} %get-tuple-element.20.refs_0_), channel_id=1, source_target_pairs={{0,1},{1,0},{2,3},{3,2},{4,5},{5,4},{6,7},{7,6},{8,9},{9,8},{10,11... | collective-permute-start | bytes 49160 | tf_op jit(solution)/shard_map/ppermute | solution.py:483

commit v11 on v10

--- a/solution.py
+++ b/solution.py
@@ -97,6 +97,12 @@
     return pl.ds(pl.multiple_of(chunk * 128, 128), 128)
 
 
+def halves(value):
+    scaled = value * 65537.0
+    high = scaled - (scaled - value)
+    return high.astype(BF16), (value - high).astype(BF16)
+
+
 def write_columns(cols, y, chunk, vec):
     ys = [y[a : a + 1] for a in ORDER]
     f = [vec[a] for a in range(3)]
@@ -105,8 +111,7 @@
     groups += [ys[p] * f[v] for p in range(3) for v in range(3)]
     groups += [ys[a] * g for a in range(3)]
     full = jnp.concatenate(groups, axis=0)
-    high = full.astype(BF16)
-    low = (full - high.astype(F32)).astype(BF16)
+    high, low = halves(full)
     at = lines_of(chunk)
     cols[0:128, at] = high
     cols[128:256, at] = low
@@ -267,10 +272,10 @@
         two = (y[3:4] * INV_EIGHT_PI) * root * root * root
         one = (dist + 2.0 * BLOB_SQ) * two + extra[chunk]
         value = jnp.concatenate([one, two], axis=0).T
-        high = value.astype(BF16)
+        high, low = halves(value)
         at = lines_of(chunk)
         kernels[at, 0:128] = high
-        kernels[at, 128:256] = (value - high.astype(F32)).astype(BF16)
+        kernels[at, 128:256] = low
 
     prod = products(n_chunk, build, cols, kernels)
     norm = jnp.sqrt(total.get(0))

time: 54.9 us -> 55.2 us (level)
  no operation moved by 1% of the time
where the time goes in v11:
time: 55.2 us; the launch traced here: 54.9 us
  blocking collectives  30.7 us (56%)
  Pallas kernels  9.2 us (17%)
  starting transfers between devices  9.14 us (17%)
  waiting for transfers between devices  5.82 us (11%)
    all_to_all x3, blocking collectives, spread(): return lax.all_to_all(wide, AXES, 0, 0, tiled=True).reshape(rows.shape)  30.7 us
    pallas_call x6, Pallas kernels, call(): pl.pallas_call(kernel, out_shape=[jax.ShapeDtypeStruct(s, t) for s, t in...  9.2 us
    all_to_all x1, starting transfers between devices, spread(): return lax.all_to_all(wide, AXES, 0, 0, tiled=True).reshape(rows.shape)  7.3 us
    all_to_all x1, waiting for transfers between devices, spread(): return lax.all_to_all(wide, AXES, 0, 0, tiled=True).reshape(rows.shape)  3.91 us
    ppermute x1, waiting for transfers between devices, body(): lax.ppermute(lists, 'col', xor_perm(n_col, o))  1.91 us
    ppermute x1, starting transfers between devices, body(): lax.ppermute(lists, 'col', xor_perm(n_col, o))  1.83 us
  transfers between devices with their start and end apart: 2, of which 2 were waited for; matrix products, arithmetic and copies ran while one was open for 0% of the time, Pallas kernels for 3%

profile of v11, /device:TPU:0, one launch (start us, length us, event | category | flops | bytes accessed | tf_op | source)
XLA Modules:
  0.0 54.9 jit_solution(12817117966514030655)
XLA Ops:
  0.0 1.6 %shard_map.64 = (f32[352,128]{1,0:T(8,128)}, f32[8,128]{1,0:T(8,128)S(1)}, f32[32,128]{1,0:T(8,128)S(1)}) custom-call(f32[6,3,64]{2,1,0:T(4,128)} %refs_0_.1, f32[3,64]{1,0:T(4,128)} %refs_1_.1, f32[1,64]{1,0:T(1,128)} %bitcast.26, f32[1,64]{1,0:T(1,128)} %bitcast.27, s32[16,128]{1,0:T(8,128)} %bitcast.24, f32[16,128]{1,0:T(8,128)} %bitcast.25), custom_call_target="tpu_custom_call" | custom-call | bytes 22272 | tf_op jit(solution)/shard_map/pallas_call | solution.py:446
  1.6 7.3 %all-to-all-start = ((f32[32,11,1,128]{3,2,1,0:T(1,128)}), f32[32,11,1,128]{3,2,1,0:T(1,128)S(1)}, u32[]{:S(2)}, u32[]{:S(2)}) async-start(f32[32,11,1,128]{3,2,1,0:T(1,128)} %bitcast.4), calls=%async_computation | async-start | bytes 360448 | tf_op jit(solution)/shard_map/all_to_all | solution.py:33
  8.9 1.8 %collective-permute-start = (f32[32,128]{1,0:T(8,128)S(1)}, f32[32,128]{1,0:T(8,128)S(1)}, u32[]{:S(2)}, u32[]{:S(2)}) collective-permute-start(f32[32,128]{1,0:T(8,128)S(1)} %get-tuple-element.20.refs_0_), channel_id=1, source_target_pairs={{0,1},{1,0},{2,3},{3,2},{4,5},{5,4},{6,7},{7,6},{8,9},{9,8},{10,11... | collective-permute-start | bytes 49160 | tf_op jit(solution)/shard_map/ppermute | solution.py:488
  10.7 0.1 pad_add_fusion.me.me_ref.refs_5_.refs_7_
  10.8 1.9 %collective-permute-done.refs_1_ = f32[32,128]{1,0:T(8,128)S(1)} collective-permute-done((f32[32,128]{1,0:T(8,128)S(1)}, f32[32,128]{1,0:T(8,128)S(1)}, u32[]{:S(2)}, u32[]{:S(2)}) %collective-permute-start) | collective-permute-done | bytes 16416 | tf_op jit(solution)/shard_map/ppermute | solution.py:488
  12.7 1.7 %shard_map.65.extra = f32[16,64,128]{2,1,0:T(8,128)S(1)} custom-call(s32[3]{0:T(128)S(1)} %pad_add_fusion.me.me_ref.refs_5_.refs_7_, f32[32,128]{1,0:T(8,128)S(1)} %get-tuple-element.20.refs_0_, f32[32,128]{1,0:T(8,128)S(1)} %collective-permute-done.refs_1_), custom_call_target="tpu_custom_call" | custom-call | flops 1000000000 | bytes 32780 | tf_op jit(solution)/shard_map/pallas_call | solution.py:446
  14.4 3.9 %all-to-all-done = f32[32,11,1,128]{3,2,1,0:T(1,128)S(1)} async-done(((f32[32,11,1,128]{3,2,1,0:T(1,128)}), f32[32,11,1,128]{3,2,1,0:T(1,128)S(1)}, u32[]{:S(2)}, u32[]{:S(2)}) %all-to-all-start) | async-done | bytes 180256 | tf_op jit(solution)/shard_map/all_to_all | solution.py:33
  18.3 2.0 %shard_map.66 = (bf16[2048,256]{1,0:T(8,128)(2,1)S(1)}, f32[16,4,128]{2,1,0:T(4,128)S(1)}, f32[16,3,8,128]{3,2,1,0:T(8,128)S(1)}, f32[2,8,128]{2,1,0:T(8,128)S(1)}, f32[320,128]{1,0:T(8,128)S(1)}) custom-call(f32[352,128]{1,0:T(8,128)S(1)} %bitcast.17, f32[16,64,128]{2,1,0:T(8,128)S(1)} %shard_map.65.extra, ...), custom_call_target="tpu_custom_call" | custom-call | bytes 708620 | tf_op jit(solution)/shard_map/pallas_call | solution.py:446
  20.3 10.9 %all_to_all.20 = f32[32,10,1,128]{3,2,1,0:T(1,128)S(1)} all-to-all(f32[32,10,1,128]{3,2,1,0:T(1,128)S(1)} %bitcast.20), channel_id=1, replica_groups=mesh['top'=4,'mid'=2,'core'=2,'col'=2] {'top','mid','core','col'}, dimensions={0} | all-to-all | bytes 327680 | tf_op jit(solution)/shard_map/all_to_all | solution.py:33
  31.3 1.6 %shard_map.67 = (f32[16,3,8,128]{3,2,1,0:T(8,128)S(1)}, f32[3,8,128]{2,1,0:T(8,128)S(1)}, f32[320,128]{1,0:T(8,128)S(1)}) custom-call(f32[320,128]{1,0:T(8,128)S(1)} %bitcast.19, f32[16,3,8,128]{3,2,1,0:T(8,128)S(1)} %get-tuple-element.23.refs_0_, f32[2,8,128]{2,1,0:T(8,128)S(1)} %get-tuple-element.24.refs_1_.refs_2_, ...), custom_call_target="tpu_custom_call" | custom-call | bytes 1454092 | tf_op jit(solution)/shard_map/pallas_call | solution.py:446
  32.8 10.8 %all_to_all.21 = f32[32,10,1,128]{3,2,1,0:T(1,128)S(1)} all-to-all(f32[32,10,1,128]{3,2,1,0:T(1,128)S(1)} %bitcast.21), channel_id=1, replica_groups=mesh['top'=4,'mid'=2,'core'=2,'col'=2] {'top','mid','core','col'}, dimensions={0} | all-to-all | bytes 327680 | tf_op jit(solution)/shard_map/all_to_all | solution.py:33
  43.7 1.6 %shard_map.68 = (f32[3,3,8,128]{3,2,1,0:T(8,128)S(1)}, f32[6,8,128]{2,1,0:T(8,128)S(1)}, f32[32,128]{1,0:T(8,128)S(1)}) custom-call(f32[320,128]{1,0:T(8,128)S(1)} %bitcast.18, f32[16,3,8,128]{3,2,1,0:T(8,128)S(1)} %get-tuple-element.23.refs_0_, f32[16,3,8,128]{3,2,1,0:T(8,128)S(1)} %get-tuple-element.28.refs_1_, ...), custom_call_target="tpu_custom_call" | custom-call | bytes 1662988 | tf_op jit(solution)/shard_map/pallas_call | solution.py:446
  45.3 8.9 %all_to_all.22 = f32[32,1,1,128]{3,2,1,0:T(1,128)S(1)} all-to-all(f32[32,1,1,128]{3,2,1,0:T(1,128)S(1)} %bitcast.23), channel_id=1, replica_groups=mesh['top'=4,'mid'=2,'core'=2,'col'=2] {'top','mid','core','col'}, dimensions={0} | all-to-all | bytes 32768 | tf_op jit(solution)/shard_map/all_to_all | solution.py:33
  54.2 0.7 %shard_map.69 = f32[6,3,64]{2,1,0:T(4,128)} custom-call(f32[32,128]{1,0:T(8,128)S(1)} %bitcast.22, f32[3,3,8,128]{3,2,1,0:T(8,128)S(1)} %get-tuple-element.31.own, f32[3,8,128]{2,1,0:T(8,128)S(1)} %get-tuple-element.29.refs_3_.refs_0_, f32[6,8,128]{2,1,0:T(8,128)S(1)} %get-tuple-element.32.refs_1_, f32[2,8,128]{2,1,0:T(8,128)S(1)} %get-tuple-element.24.refs_1_.refs_2_), custom_call_target="tpu_custom_call" | custom-call | bytes 98304 | tf_op jit(solution)/shard_map/pallas_call | solution.py:446
Async XLA Ops:
  1.6 16.7 %all-to-all-start = ((f32[32,11,1,128]{3,2,1,0:T(1,128)}), f32[32,11,1,128]{3,2,1,0:T(1,128)S(1)}, u32[]{:S(2)}, u32[]{:S(2)}) async-start(f32[32,11,1,128]{3,2,1,0:T(1,128)} %bitcast.4), calls=%async_computation | async-start | bytes 360448 | tf_op jit(solution)/shard_map/all_to_all | solution.py:33
  8.9 3.8 %collective-permute-start = (f32[32,128]{1,0:T(8,128)S(1)}, f32[32,128]{1,0:T(8,128)S(1)}, u32[]{:S(2)}, u32[]{:S(2)}) collective-permute-start(f32[32,128]{1,0:T(8,128)S(1)} %get-tuple-element.20.refs_0_), channel_id=1, source_target_pairs={{0,1},{1,0},{2,3},{3,2},{4,5},{5,4},{6,7},{7,6},{8,9},{9,8},{10,11... | collective-permute-start | bytes 49160 | tf_op jit(solution)/shard_map/ppermute | solution.py:488

commit v12 on v10

--- a/solution.py
+++ b/solution.py
@@ -13,6 +13,7 @@
 INV_EIGHT_PI = 1.0 / (8.0 * math.pi)
 ROWS = 8
 HALF = 3
+UNROLL = 4
 FIRST, LATER = 11, 10
 ORDER = (0, 2, 1)
 AXES = ("top", "mid", "core", "col")
@@ -41,30 +42,22 @@
         pl.loop(0, count)(step)
 
 
-class Sums:
-    def __init__(self, count, refs):
-        self.refs = refs
-        self.parts = [[None] * 4 for _ in range(count)]
-        if refs is not None:
-            for at in range(count):
-                refs[at] = jnp.zeros((ROWS, 128), F32)
-
-    def add(self, chunk, at, left, right):
-        part = sum(left[a] * right[a] for a in range(3))
-        if self.refs is not None:
-            self.refs[at] = self.refs[at] + part
-            return
-        held = self.parts[at]
-        slot = chunk % 4
-        held[slot] = part if held[slot] is None else held[slot] + part
-
-    def get(self, at):
-        if self.refs is not None:
-            total = self.refs[at]
-        else:
-            held = self.parts[at]
-            total = (held[0] + held[1]) + (held[2] + held[3])
-        return jnp.broadcast_to(jnp.sum(total, axis=1, keepdims=True), (ROWS, 128))
+def sweep(n_chunk, count, step):
+    def turn(i, sums):
+        for inner in range(UNROLL):
+            parts = step(i * UNROLL + inner)
+            sums = [held + part for held, part in zip(sums, parts)]
+        return sums
+
+    zeros = [jnp.zeros((ROWS, 128), F32)] * count
+    sums = lax.fori_loop(0, n_chunk // UNROLL, turn, zeros)
+    return [
+        jnp.broadcast_to(jnp.sum(held, axis=1, keepdims=True), (ROWS, 128)) for held in sums
+    ]
+
+
+def along(left, right):
+    return sum(left[a] * right[a] for a in range(3))
 
 
 def chunk_parts(piece, chunk, me, n_row, n_col, size, at, count):
@@ -118,12 +111,9 @@
     return first[:, :128] + (second + first[:, 128:])
 
 
-def products(n_chunk, columns, cols, kernels):
+def products(n_chunk, cols, kernels):
     if n_chunk <= 16:
-        for chunk in range(n_chunk):
-            columns(chunk)
         return contract(cols[...], kernels[...])
-    pl.loop(0, n_chunk)(columns)
 
     def turn(i, acc):
         at = pl.ds(pl.multiple_of(i * 2048, 2048), 2048)
@@ -237,11 +227,10 @@
 
 
 def first_kernel(
-    n_row, n_col, piece, extra, tgt, me_ref, kernels, places, basis, norm_out, out, cols, *sums
+    n_row, n_col, piece, extra, tgt, me_ref, kernels, places, basis, norm_out, out, cols
 ):
     n_chunk = n_row * n_col // 2
     me = me_ref[0]
-    total = Sums(1, sums[0] if sums else None)
 
     def unpack(chunk):
         vec = [
@@ -252,14 +241,14 @@
         places[chunk] = spot
         for a in range(3):
             basis[chunk, a] = vec[a]
-        total.add(chunk, 0, vec, vec)
         write_columns(cols, spot, chunk, vec)
+        return along(vec, vec)
 
     turned = tgt[...].T
     x = [jnp.broadcast_to(turned[:64, a : a + 1], (64, 128)) for a in range(3)]
 
     def build(chunk):
-        unpack(chunk)
+        square = unpack(chunk)
         y = places[chunk]
         d = [x[a] - y[k : k + 1] for a, k in enumerate(ORDER)]
         dist = d[0] * d[0] + d[1] * d[1] + d[2] * d[2]
@@ -271,9 +260,11 @@
         at = lines_of(chunk)
         kernels[at, 0:128] = high
         kernels[at, 128:256] = (value - high.astype(F32)).astype(BF16)
-
-    prod = products(n_chunk, build, cols, kernels)
-    norm = jnp.sqrt(total.get(0))
+        return [square]
+
+    (square,) = sweep(n_chunk, 1, build)
+    prod = products(n_chunk, cols, kernels)
+    norm = jnp.sqrt(square)
     scale = 1.0 / norm
     norm_out[0] = norm
     norm_out[1] = scale
@@ -283,14 +274,13 @@
 def middle_kernel(n_row, n_col, n_base, final, piece, *refs):
     bases, norms = refs[:n_base], refs[n_base : 2 * n_base]
     if final:
-        kernels, places, tgt, me_ref, own, h_out, out, basis, cols, *held = refs[2 * n_base :]
+        kernels, places, tgt, me_ref, own, h_out, out, basis, cols = refs[2 * n_base :]
     else:
-        kernels, places, tgt, me_ref, basis, h_out, out, cols, *held = refs[2 * n_base :]
+        kernels, places, tgt, me_ref, basis, h_out, out, cols = refs[2 * n_base :]
     n_chunk = n_row * n_col // 2
     me = me_ref[0]
     scales = [norm[norm.shape[0] - 1] for norm in norms]
     cross = [(i, j) for i in range(n_base) for j in range(i)]
-    sums = Sums(2 * n_base + 1 + len(cross), held[0] if held else None)
 
     def unpack(chunk):
         vec = [
@@ -300,18 +290,16 @@
         old = [[base[chunk, a] for a in range(3)] for base in bases]
         for a in range(3):
             basis[chunk, a] = vec[a]
-        for j in range(n_base):
-            sums.add(chunk, j, vec, old[j])
-        for at, (i, j) in enumerate(cross):
-            sums.add(chunk, 2 * n_base + 1 + at, old[i], old[j])
-
-    each(n_chunk, unpack)
+        parts = [along(vec, old[j]) for j in range(n_base)]
+        return parts + [along(old[i], old[j]) for i, j in cross]
+
+    inner = sweep(n_chunk, n_base + len(cross), unpack)
     gram = {}
     for at, (i, j) in enumerate(cross):
-        gram[j, i] = sums.get(2 * n_base + 1 + at) * (scales[i] * scales[j])
+        gram[j, i] = inner[n_base + at] * (scales[i] * scales[j])
     column = []
     for j in range(n_base):
-        h = sums.get(j) * scales[j]
+        h = inner[j] * scales[j]
         for i in range(j):
             h = h - column[i] * gram[i, j]
         column.append(h)
@@ -327,14 +315,13 @@
                 value = value - factors[j] * old[j][a]
             vec.append(value)
             basis[chunk, a] = value
-        sums.add(chunk, n_base, vec, vec)
         write_columns(cols, places[chunk], chunk, vec)
-        if final:
-            for j in range(n_base):
-                sums.add(chunk, n_base + 1 + j, vec, old[j])
-
-    prod = products(n_chunk, columns, cols, kernels)
-    norm = jnp.sqrt(sums.get(n_base))
+        parts = [along(vec, vec)]
+        return parts + ([along(vec, old[j]) for j in range(n_base)] if final else [])
+
+    square, *mixed = sweep(n_chunk, 1 + (n_base if final else 0), columns)
+    prod = products(n_chunk, cols, kernels)
+    norm = jnp.sqrt(square)
     scale = 1.0 / norm
     h_out[n_base] = norm
     images = image_rows(prod, tgt, basis[0], scale)
@@ -347,7 +334,7 @@
         for a in range(3):
             own[j, a] = base[0, a] * [*scales, scale][j]
     for j in range(n_base):
-        gram[j, n_base] = sums.get(n_base + 1 + j) * (scale * scales[j])
+        gram[j, n_base] = mixed[j] * (scale * scales[j])
     for at, pair in enumerate(PAIRS):
         h_out[n_base + 1 + at] = gram[pair]
     low = low_half((ROWS, 128))
@@ -492,7 +479,6 @@
 
     vec_shape = (n_chunk, 3, ROWS, 128)
     cols = pltpu.VMEM((256, total), BF16)
-    held = [] if n_chunk <= 16 else [pltpu.VMEM((8, ROWS, 128), F32)]
     kernels, places, basis, norm, wide = call(
         functools.partial(first_kernel, n_row, n_col),
         [
@@ -502,7 +488,7 @@
             ((2, ROWS, 128), F32),
             message,
         ],
-        [cols, *held],
+        [cols],
         [piece, extra, tgt, me],
         {3},
     )
@@ -518,7 +504,7 @@
                 ((k + 1 + (len(PAIRS) if final else 1), ROWS, 128), F32),
                 ((n, 128), F32) if final else message,
             ],
-            [*([pltpu.VMEM(vec_shape, F32)] if final else []), cols, *held],
+            [*([pltpu.VMEM(vec_shape, F32)] if final else []), cols],
             [piece, *bases, *columns, kernels, places, tgt, me],
             {2 * k + 4},
         )

time: 54.9 us -> 56.8 us (1.035)
  Pallas kernels: 8.84 us -> 10.8 us
    pallas_call x6, Pallas kernels: 8.84 us -> 10.8 us  [call(): pl.pallas_call(kernel, out_shape=[jax.ShapeDtypeStruct(s, t) for s, t in...]
where the time goes in v12:
time: 56.8 us; the launch traced here: 56.5 us
  blocking collectives  30.7 us (54%)
  Pallas kernels  10.8 us (19%)
  starting transfers between devices  9.14 us (16%)
  waiting for transfers between devices  5.82 us (10%)
    all_to_all x3, blocking collectives, spread(): return lax.all_to_all(wide, AXES, 0, 0, tiled=True).reshape(rows.shape)  30.7 us
    pallas_call x6, Pallas kernels, call(): pl.pallas_call(kernel, out_shape=[jax.ShapeDtypeStruct(s, t) for s, t in...  10.8 us
    all_to_all x1, starting transfers between devices, spread(): return lax.all_to_all(wide, AXES, 0, 0, tiled=True).reshape(rows.shape)  7.3 us
    all_to_all x1, waiting for transfers between devices, spread(): return lax.all_to_all(wide, AXES, 0, 0, tiled=True).reshape(rows.shape)  3.91 us
    ppermute x1, waiting for transfers between devices, body(): lax.ppermute(lists, 'col', xor_perm(n_col, o))  1.91 us
    ppermute x1, starting transfers between devices, body(): lax.ppermute(lists, 'col', xor_perm(n_col, o))  1.83 us
  transfers between devices with their start and end apart: 2, of which 2 were waited for; matrix products, arithmetic and copies ran while one was open for 0% of the time, Pallas kernels for 3%

profile of v12, /device:TPU:0, one launch (start us, length us, event | category | flops | bytes accessed | tf_op | source)
XLA Modules:
  0.0 56.5 jit_solution(13027995572975710405)
XLA Ops:
  0.0 1.6 %shard_map.64 = (f32[352,128]{1,0:T(8,128)}, f32[8,128]{1,0:T(8,128)S(1)}, f32[32,128]{1,0:T(8,128)S(1)}) custom-call(f32[6,3,64]{2,1,0:T(4,128)} %refs_0_.1, f32[3,64]{1,0:T(4,128)} %refs_1_.1, f32[1,64]{1,0:T(1,128)} %bitcast.26, f32[1,64]{1,0:T(1,128)} %bitcast.27, s32[16,128]{1,0:T(8,128)} %bitcast.24, f32[16,128]{1,0:T(8,128)} %bitcast.25), custom_call_target="tpu_custom_call" | custom-call | bytes 22272 | tf_op jit(solution)/shard_map/pallas_call | solution.py:428
  1.6 7.3 %all-to-all-start = ((f32[32,11,1,128]{3,2,1,0:T(1,128)}), f32[32,11,1,128]{3,2,1,0:T(1,128)S(1)}, u32[]{:S(2)}, u32[]{:S(2)}) async-start(f32[32,11,1,128]{3,2,1,0:T(1,128)} %bitcast.4), calls=%async_computation | async-start | bytes 360448 | tf_op jit(solution)/shard_map/all_to_all | solution.py:34
  8.9 1.8 %collective-permute-start = (f32[32,128]{1,0:T(8,128)S(1)}, f32[32,128]{1,0:T(8,128)S(1)}, u32[]{:S(2)}, u32[]{:S(2)}) collective-permute-start(f32[32,128]{1,0:T(8,128)S(1)} %get-tuple-element.20.refs_0_), channel_id=1, source_target_pairs={{0,1},{1,0},{2,3},{3,2},{4,5},{5,4},{6,7},{7,6},{8,9},{9,8},{10,11... | collective-permute-start | bytes 49160 | tf_op jit(solution)/shard_map/ppermute | solution.py:470
  10.7 0.1 pad_add_fusion.me.me_ref.refs_5_.refs_7_
  10.8 1.9 %collective-permute-done.refs_1_ = f32[32,128]{1,0:T(8,128)S(1)} collective-permute-done((f32[32,128]{1,0:T(8,128)S(1)}, f32[32,128]{1,0:T(8,128)S(1)}, u32[]{:S(2)}, u32[]{:S(2)}) %collective-permute-start) | collective-permute-done | bytes 16416 | tf_op jit(solution)/shard_map/ppermute | solution.py:470
  12.7 1.7 %shard_map.65.extra = f32[16,64,128]{2,1,0:T(8,128)S(1)} custom-call(s32[3]{0:T(128)S(1)} %pad_add_fusion.me.me_ref.refs_5_.refs_7_, f32[32,128]{1,0:T(8,128)S(1)} %get-tuple-element.20.refs_0_, f32[32,128]{1,0:T(8,128)S(1)} %collective-permute-done.refs_1_), custom_call_target="tpu_custom_call" | custom-call | flops 1000000000 | bytes 32780 | tf_op jit(solution)/shard_map/pallas_call | solution.py:428
  14.4 3.9 %all-to-all-done = f32[32,11,1,128]{3,2,1,0:T(1,128)S(1)} async-done(((f32[32,11,1,128]{3,2,1,0:T(1,128)}), f32[32,11,1,128]{3,2,1,0:T(1,128)S(1)}, u32[]{:S(2)}, u32[]{:S(2)}) %all-to-all-start) | async-done | bytes 180256 | tf_op jit(solution)/shard_map/all_to_all | solution.py:34
  18.3 2.7 %shard_map.66 = (bf16[2048,256]{1,0:T(8,128)(2,1)S(1)}, f32[16,4,128]{2,1,0:T(4,128)S(1)}, f32[16,3,8,128]{3,2,1,0:T(8,128)S(1)}, f32[2,8,128]{2,1,0:T(8,128)S(1)}, f32[320,128]{1,0:T(8,128)S(1)}) custom-call(f32[352,128]{1,0:T(8,128)S(1)} %bitcast.17, f32[16,64,128]{2,1,0:T(8,128)S(1)} %shard_map.65.extra, ...), custom_call_target="tpu_custom_call" | custom-call | bytes 708620 | tf_op jit(solution)/shard_map/pallas_call | solution.py:428
  21.0 10.9 %all_to_all.20 = f32[32,10,1,128]{3,2,1,0:T(1,128)S(1)} all-to-all(f32[32,10,1,128]{3,2,1,0:T(1,128)S(1)} %bitcast.20), channel_id=1, replica_groups=mesh['top'=4,'mid'=2,'core'=2,'col'=2] {'top','mid','core','col'}, dimensions={0} | all-to-all | bytes 327680 | tf_op jit(solution)/shard_map/all_to_all | solution.py:34
  31.9 2.0 %shard_map.67 = (f32[16,3,8,128]{3,2,1,0:T(8,128)S(1)}, f32[3,8,128]{2,1,0:T(8,128)S(1)}, f32[320,128]{1,0:T(8,128)S(1)}) custom-call(f32[320,128]{1,0:T(8,128)S(1)} %bitcast.19, f32[16,3,8,128]{3,2,1,0:T(8,128)S(1)} %get-tuple-element.23.refs_0_, f32[2,8,128]{2,1,0:T(8,128)S(1)} %get-tuple-element.24.refs_1_.refs_2_, ...), custom_call_target="tpu_custom_call" | custom-call | bytes 1454092 | tf_op jit(solution)/shard_map/pallas_call | solution.py:428
  33.9 10.8 %all_to_all.21 = f32[32,10,1,128]{3,2,1,0:T(1,128)S(1)} all-to-all(f32[32,10,1,128]{3,2,1,0:T(1,128)S(1)} %bitcast.21), channel_id=1, replica_groups=mesh['top'=4,'mid'=2,'core'=2,'col'=2] {'top','mid','core','col'}, dimensions={0} | all-to-all | bytes 327680 | tf_op jit(solution)/shard_map/all_to_all | solution.py:34
  44.8 2.1 %shard_map.68 = (f32[3,3,8,128]{3,2,1,0:T(8,128)S(1)}, f32[6,8,128]{2,1,0:T(8,128)S(1)}, f32[32,128]{1,0:T(8,128)S(1)}) custom-call(f32[320,128]{1,0:T(8,128)S(1)} %bitcast.18, f32[16,3,8,128]{3,2,1,0:T(8,128)S(1)} %get-tuple-element.23.refs_0_, f32[16,3,8,128]{3,2,1,0:T(8,128)S(1)} %get-tuple-element.28.refs_1_, ...), custom_call_target="tpu_custom_call" | custom-call | bytes 1662988 | tf_op jit(solution)/shard_map/pallas_call | solution.py:428
  46.9 8.9 %all_to_all.22 = f32[32,1,1,128]{3,2,1,0:T(1,128)S(1)} all-to-all(f32[32,1,1,128]{3,2,1,0:T(1,128)S(1)} %bitcast.23), channel_id=1, replica_groups=mesh['top'=4,'mid'=2,'core'=2,'col'=2] {'top','mid','core','col'}, dimensions={0} | all-to-all | bytes 32768 | tf_op jit(solution)/shard_map/all_to_all | solution.py:34
  55.8 0.7 %shard_map.69 = f32[6,3,64]{2,1,0:T(4,128)} custom-call(f32[32,128]{1,0:T(8,128)S(1)} %bitcast.22, f32[3,3,8,128]{3,2,1,0:T(8,128)S(1)} %get-tuple-element.31.own, f32[3,8,128]{2,1,0:T(8,128)S(1)} %get-tuple-element.29.refs_3_.refs_0_, f32[6,8,128]{2,1,0:T(8,128)S(1)} %get-tuple-element.32.refs_1_, f32[2,8,128]{2,1,0:T(8,128)S(1)} %get-tuple-element.24.refs_1_.refs_2_), custom_call_target="tpu_custom_call" | custom-call | bytes 98304 | tf_op jit(solution)/shard_map/pallas_call | solution.py:428
Async XLA Ops:
  1.6 16.7 %all-to-all-start = ((f32[32,11,1,128]{3,2,1,0:T(1,128)}), f32[32,11,1,128]{3,2,1,0:T(1,128)S(1)}, u32[]{:S(2)}, u32[]{:S(2)}) async-start(f32[32,11,1,128]{3,2,1,0:T(1,128)} %bitcast.4), calls=%async_computation | async-start | bytes 360448 | tf_op jit(solution)/shard_map/all_to_all | solution.py:34
  8.9 3.8 %collective-permute-start = (f32[32,128]{1,0:T(8,128)S(1)}, f32[32,128]{1,0:T(8,128)S(1)}, u32[]{:S(2)}, u32[]{:S(2)}) collective-permute-start(f32[32,128]{1,0:T(8,128)S(1)} %get-tuple-element.20.refs_0_), channel_id=1, source_target_pairs={{0,1},{1,0},{2,3},{3,2},{4,5},{5,4},{6,7},{7,6},{8,9},{9,8},{10,11... | collective-permute-start | bytes 49160 | tf_op jit(solution)/shard_map/ppermute | solution.py:470

commit v13 on v10

--- a/solution.py
+++ b/solution.py
@@ -154,12 +154,13 @@
     for image in images:
         top, bottom = image[:4], pltpu.roll(image[4:], 64, 1)
         rows.append(jnp.where(low_half((4, 128)), top, bottom))
+    message = jnp.concatenate([rows[0][:HALF], rows[1][:HALF], rows[2]], axis=0)
+    block = jnp.concatenate([message] * 4, axis=0)
 
     def put(m):
-        for a in range(3):
-            out[pl.ds(m * LATER + HALF * a, 4)] = rows[a]
-
-    each_wide(out.shape[0] // LATER, put)
+        out[pl.ds(m * 4 * LATER, 4 * LATER)] = block
+
+    each_wide(out.shape[0] // (4 * LATER), put)
 
 
 def each_wide(count, put):
@@ -171,8 +172,8 @@
 
 
 def pack_kernel(*refs):
-    sources, outs, held, sems = refs[:6], refs[6:9], refs[9:15], refs[15]
-    out, tgt, lists = outs
+    sources, (out, tgt, lists), held = refs[:6], refs[6:9], refs[9:15]
+    block, sems = refs[15:]
     copies = [
         pltpu.make_async_copy(src, dst, sems.at[i])
         for i, (src, dst) in enumerate(zip(sources, held))
@@ -183,8 +184,6 @@
         copy.wait()
     velocity, points, area, self_term, index, weight = held
     count = index.shape[0]
-    lists[:count] = index[...].astype(F32)
-    lists[count:] = weight[...]
     field = velocity[...]
     spot = points[...]
     rows = []
@@ -198,47 +197,55 @@
     right = jnp.concatenate([spot[1:2], area[...]], axis=0)
     rows.append(jnp.concatenate([left, right], axis=1))
     message = jnp.concatenate(rows, axis=0)
-
-    def put(m):
-        out[pl.ds(m * FIRST, FIRST)] = message
-
-    each_wide(out.shape[0] // FIRST, put)
-
-
-def extra_kernel(half_chunks, me, *refs):
-    near, out = refs[:-1], refs[-1]
+    size = block.shape[0]
+    block[...] = jnp.concatenate([message] * 8, axis=0)
+    copies = [
+        pltpu.make_async_copy(block, out.at[pl.ds(i * size, size)], sems.at[6 + i])
+        for i in range(out.shape[0] // size)
+    ]
+    for copy in copies:
+        copy.start()
+    lists[:count] = index[...].astype(F32)
+    lists[count:] = weight[...]
+    for copy in copies:
+        copy.wait()
+
+
+def extra_kernel(me, lists, out):
     row, col = me[1], me[2]
     lines = lax.broadcasted_iota(jnp.int32, (128, 128), 0).astype(F32)
-    for o, lists in enumerate(near):
-        count = lists.shape[0] // 2
-        half = count // 2
-        low = low_half((half, 128))
-        odd = col % 2 == 1
-        both = lists[:, lines_of(col // 2)]
-        place = both[:count].astype(jnp.int32)
-        place = (((place // 64) ^ row) * 64 + place % 64).astype(F32)
-        packed = []
-        for value in (place, both[count:]):
-            top, bottom = value[:half], value[half:]
-            lower = jnp.where(low, top, pltpu.roll(bottom, 64, 1))
-            upper = jnp.where(low, pltpu.roll(top, 64, 1), bottom)
-            packed.append(jnp.where(odd, upper, lower))
-        index, weight = packed
-
-        def build(u):
-            line = lines + (u * 128.0 if isinstance(u, int) else (u * 128).astype(F32))
-            total = jnp.zeros((128, 128), F32)
-            for k in range(half):
-                total = total + jnp.where(line == index[k : k + 1], weight[k : k + 1], 0.0)
-            turned = total.T
-            out[o * half_chunks + u] = turned[:64] + turned[64:]
-
-        each(half_chunks, build)
+    count = lists.shape[0] // 2
+    half = count // 2
+    low = low_half((half, 128))
+    odd = col % 2 == 1
+    both = lists[:, lines_of(col // 2)]
+    place = both[:count].astype(jnp.int32)
+    place = (((place // 64) ^ row) * 64 + place % 64).astype(F32)
+    packed = []
+    for value in (place, both[count:]):
+        top, bottom = value[:half], value[half:]
+        lower = jnp.where(low, top, pltpu.roll(bottom, 64, 1))
+        upper = jnp.where(low, pltpu.roll(top, 64, 1), bottom)
+        packed.append(jnp.where(odd, upper, lower))
+    index, weight = packed
+
+    def build(u):
+        line = lines + (u * 128.0 if isinstance(u, int) else (u * 128).astype(F32))
+        total = jnp.zeros((128, 128), F32)
+        for k in range(half):
+            total = total + jnp.where(line == index[k : k + 1], weight[k : k + 1], 0.0)
+        turned = total.T
+        out[u] = turned[:64] + turned[64:]
+
+    each(out.shape[0], build)
 
 
 def first_kernel(
-    n_row, n_col, piece, extra, tgt, me_ref, kernels, places, basis, norm_out, out, cols, *sums
+    n_row, n_col, piece, *refs
 ):
+    extra = refs[:n_col]
+    tgt, me_ref, kernels, places, basis, norm_out, out, cols, *sums = refs[n_col:]
+    half = n_row // 2
     n_chunk = n_row * n_col // 2
     me = me_ref[0]
     total = Sums(1, sums[0] if sums else None)
@@ -265,7 +272,13 @@
         dist = d[0] * d[0] + d[1] * d[1] + d[2] * d[2]
         root = lax.rsqrt(dist + BLOB_SQ)
         two = (y[3:4] * INV_EIGHT_PI) * root * root * root
-        one = (dist + 2.0 * BLOB_SQ) * two + extra[chunk]
+        one = (dist + 2.0 * BLOB_SQ) * two
+        if isinstance(chunk, int):
+            one = one + extra[chunk // half][chunk % half]
+        else:
+            for o in range(n_col):
+                mine = extra[o][chunk % half]
+                one = one + jnp.where(chunk // half == o, mine, 0.0)
         value = jnp.concatenate([one, two], axis=0).T
         high = value.astype(BF16)
         at = lines_of(chunk)
@@ -431,7 +444,7 @@
         out[HALF:, a, :] = density[4 : 4 + HALF, :64]
 
 
-def call(kernel, outs, scratch, operands, scalars=(), far=(), flops=0):
+def call(kernel, outs, scratch, operands, scalars=(), far=(), spread_out=False, flops=0):
     vmem = pl.BlockSpec(memory_space=pltpu.VMEM)
     smem = pl.BlockSpec(memory_space=pltpu.SMEM)
     count = len(operands)
@@ -442,7 +455,7 @@
         kernel,
         out_shape=[jax.ShapeDtypeStruct(s, t) for s, t in outs],
         in_specs=specs,
-        out_specs=[vmem] * len(outs),
+        out_specs=[pl.BlockSpec(memory_space=pl.ANY) if spread_out and i == 0 else vmem for i in range(len(outs))],
         scratch_shapes=scratch,
         cost_estimate=pl.CostEstimate(flops=flops, bytes_accessed=moved, transcendentals=0),
         compiler_params=pltpu.CompilerParams(vmem_limit_bytes=48 * 1024 * 1024),
@@ -475,20 +488,25 @@
             ((8, 128), F32),
             ((2 * near_index.shape[1], near_index.shape[0]), F32),
         ],
-        [pltpu.VMEM(x.shape, x.dtype) for x in sources] + [pltpu.SemaphoreType.DMA((6,))],
+        [pltpu.VMEM(x.shape, x.dtype) for x in sources]
+        + [pltpu.VMEM((8 * FIRST, 128), F32), pltpu.SemaphoreType.DMA((6 + n // 8,))],
         [pltpu.with_memory_space_constraint(x, pltpu.HBM) for x in sources],
         far=range(6),
+        spread_out=True,
     )
     piece = spread(wide, n)
     near = [lists] + [lax.ppermute(lists, "col", xor_perm(n_col, o)) for o in range(1, n_col)]
-    (extra,) = call(
-        functools.partial(extra_kernel, n_row // 2),
-        [((n_chunk, 64, 128), F32)],
-        [],
-        [me, *near],
-        {0},
-        flops=10**9,
-    )
+    extra = [
+        call(
+            extra_kernel,
+            [((n_row // 2, 64, 128), F32)],
+            [],
+            [me, pair],
+            {0},
+            flops=10**8,
+        )[0]
+        for pair in near
+    ]
 
     vec_shape = (n_chunk, 3, ROWS, 128)
     cols = pltpu.VMEM((256, total), BF16)
@@ -503,8 +521,8 @@
             message,
         ],
         [cols, *held],
-        [piece, extra, tgt, me],
-        {3},
+        [piece, *extra, tgt, me],
+        {n_col + 2},
     )
     bases = [basis]
     columns = [norm]

time: 54.9 us -> 54.8 us (level)
  Pallas kernels: 8.84 us -> 9.42 us
  waiting for transfers between devices: 5.82 us -> 5.25 us
    ppermute x1, waiting for transfers between devices: 1.91 us -> 0.79 us  [body(): lax.ppermute(lists, 'col', xor_perm(n_col, o))]
    pallas_call x6 -> x7, Pallas kernels: 8.84 us -> 9.42 us  [call(): pl.pallas_call(kernel, out_shape=[jax.ShapeDtypeStruct(s, t) for s, t in...]
  transfers between devices with their start and end apart: 2 -> 2, of which waited for: 2 -> 2; matrix products, arithmetic and copies ran while one was open for 0% -> 0% of each run, Pallas kernels for 3% -> 4%
where the time goes in v13:
time: 54.8 us; the launch traced here: 54.5 us
  blocking collectives  30.6 us (56%)
  Pallas kernels  9.42 us (17%)
  starting transfers between devices  9.14 us (17%)
  waiting for transfers between devices  5.25 us (10%)
    all_to_all x3, blocking collectives, spread(): return lax.all_to_all(wide, AXES, 0, 0, tiled=True).reshape(rows.shape)  30.6 us
    pallas_call x7, Pallas kernels, call(): pl.pallas_call(kernel, out_shape=[jax.ShapeDtypeStruct(s, t) for s, t in...  9.42 us
    all_to_all x1, starting transfers between devices, spread(): return lax.all_to_all(wide, AXES, 0, 0, tiled=True).reshape(rows.shape)  7.3 us
    all_to_all x1, waiting for transfers between devices, spread(): return lax.all_to_all(wide, AXES, 0, 0, tiled=True).reshape(rows.shape)  4.46 us
    ppermute x1, starting transfers between devices, body(): lax.ppermute(lists, 'col', xor_perm(n_col, o))  1.83 us
  transfers between devices with their start and end apart: 2, of which 2 were waited for; matrix products, arithmetic and copies ran while one was open for 0% of the time, Pallas kernels for 4%

profile of v13, /device:TPU:0, one launch (start us, length us, event | category | flops | bytes accessed | tf_op | source)
XLA Modules:
  0.0 54.5 jit_solution(1856470349798078023)
XLA Ops:
  0.0 1.6 %shard_map.64 = (f32[352,128]{1,0:T(8,128)}, f32[8,128]{1,0:T(8,128)S(1)}, f32[32,128]{1,0:T(8,128)S(1)}) custom-call(f32[6,3,64]{2,1,0:T(4,128)} %refs_0_.1, f32[3,64]{1,0:T(4,128)} %refs_1_.1, f32[1,64]{1,0:T(1,128)} %bitcast.26, f32[1,64]{1,0:T(1,128)} %bitcast.27, s32[16,128]{1,0:T(8,128)} %bitcast.24, f32[16,128]{1,0:T(8,128)} %bitcast.25), custom_call_target="tpu_custom_call" | custom-call | bytes 22272 | tf_op jit(solution)/shard_map/pallas_call | solution.py:454
  1.6 7.3 %all-to-all-start = ((f32[32,11,1,128]{3,2,1,0:T(1,128)}), f32[32,11,1,128]{3,2,1,0:T(1,128)S(1)}, u32[]{:S(2)}, u32[]{:S(2)}) async-start(f32[32,11,1,128]{3,2,1,0:T(1,128)} %bitcast.4), calls=%async_computation | async-start | bytes 360448 | tf_op jit(solution)/shard_map/all_to_all | solution.py:33
  8.9 1.8 %collective-permute-start = (f32[32,128]{1,0:T(8,128)S(1)}, f32[32,128]{1,0:T(8,128)S(1)}, u32[]{:S(2)}, u32[]{:S(2)}) collective-permute-start(f32[32,128]{1,0:T(8,128)S(1)} %get-tuple-element.20.lists), channel_id=1, source_target_pairs={{0,1},{1,0},{2,3},{3,2},{4,5},{5,4},{6,7},{7,6},{8,9},{9,8},{10,11... | collective-permute-start | bytes 49160 | tf_op jit(solution)/shard_map/ppermute | solution.py:498
  10.8 0.1 pad_add_fusion.me.refs_3_.refs_5_.refs_7_
  10.8 1.1 %shard_map.65.refs_0_ = f32[8,64,128]{2,1,0:T(8,128)S(1)} custom-call(s32[3]{0:T(128)S(1)} %pad_add_fusion.me.refs_3_.refs_5_.refs_7_, f32[32,128]{1,0:T(8,128)S(1)} %get-tuple-element.20.lists), custom_call_target="tpu_custom_call" | custom-call | flops 100000000 | bytes 16396 | tf_op jit(solution)/shard_map/pallas_call | solution.py:454
  12.0 0.8 %collective-permute-done.lists = f32[32,128]{1,0:T(8,128)S(1)} collective-permute-done((f32[32,128]{1,0:T(8,128)S(1)}, f32[32,128]{1,0:T(8,128)S(1)}, u32[]{:S(2)}, u32[]{:S(2)}) %collective-permute-start) | collective-permute-done | bytes 16416 | tf_op jit(solution)/shard_map/ppermute | solution.py:498
  12.8 1.1 %shard_map.66.refs_1_ = f32[8,64,128]{2,1,0:T(8,128)S(1)} custom-call(s32[3]{0:T(128)S(1)} %pad_add_fusion.me.refs_3_.refs_5_.refs_7_, f32[32,128]{1,0:T(8,128)S(1)} %collective-permute-done.lists), custom_call_target="tpu_custom_call" | custom-call | flops 100000000 | bytes 16396 | tf_op jit(solution)/shard_map/pallas_call | solution.py:454
  13.9 4.5 %all-to-all-done = f32[32,11,1,128]{3,2,1,0:T(1,128)S(1)} async-done(((f32[32,11,1,128]{3,2,1,0:T(1,128)}), f32[32,11,1,128]{3,2,1,0:T(1,128)S(1)}, u32[]{:S(2)}, u32[]{:S(2)}) %all-to-all-start) | async-done | bytes 180256 | tf_op jit(solution)/shard_map/all_to_all | solution.py:33
  18.3 1.9 %shard_map.67 = (bf16[2048,256]{1,0:T(8,128)(2,1)S(1)}, f32[16,4,128]{2,1,0:T(4,128)S(1)}, f32[16,3,8,128]{3,2,1,0:T(8,128)S(1)}, f32[2,8,128]{2,1,0:T(8,128)S(1)}, f32[320,128]{1,0:T(8,128)S(1)}) custom-call(f32[352,128]{1,0:T(8,128)S(1)} %bitcast.17, f32[8,64,128]{2,1,0:T(8,128)S(1)} %shard_map.65.refs_0_, f32[8,64,128]{2,1,0:T(8,128)S(1)} %shard_map.66.refs_1_, ...), custom_call_target="tpu_custom_call" | custom-call | bytes 708620 | tf_op jit(solution)/shard_map/pallas_call | solution.py:454
  20.2 10.8 %all_to_all.20 = f32[32,10,1,128]{3,2,1,0:T(1,128)S(1)} all-to-all(f32[32,10,1,128]{3,2,1,0:T(1,128)S(1)} %bitcast.20), channel_id=1, replica_groups=mesh['top'=4,'mid'=2,'core'=2,'col'=2] {'top','mid','core','col'}, dimensions={0} | all-to-all | bytes 327680 | tf_op jit(solution)/shard_map/all_to_all | solution.py:33
  31.1 1.4 %shard_map.68 = (f32[16,3,8,128]{3,2,1,0:T(8,128)S(1)}, f32[3,8,128]{2,1,0:T(8,128)S(1)}, f32[320,128]{1,0:T(8,128)S(1)}) custom-call(f32[320,128]{1,0:T(8,128)S(1)} %bitcast.19, f32[16,3,8,128]{3,2,1,0:T(8,128)S(1)} %get-tuple-element.23.refs_0_, f32[2,8,128]{2,1,0:T(8,128)S(1)} %get-tuple-element.24.refs_1_.refs_2_, ...), custom_call_target="tpu_custom_call" | custom-call | bytes 1454092 | tf_op jit(solution)/shard_map/pallas_call | solution.py:454
  32.5 10.8 %all_to_all.21 = f32[32,10,1,128]{3,2,1,0:T(1,128)S(1)} all-to-all(f32[32,10,1,128]{3,2,1,0:T(1,128)S(1)} %bitcast.21), channel_id=1, replica_groups=mesh['top'=4,'mid'=2,'core'=2,'col'=2] {'top','mid','core','col'}, dimensions={0} | all-to-all | bytes 327680 | tf_op jit(solution)/shard_map/all_to_all | solution.py:33
  43.4 1.5 %shard_map.69 = (f32[3,3,8,128]{3,2,1,0:T(8,128)S(1)}, f32[6,8,128]{2,1,0:T(8,128)S(1)}, f32[32,128]{1,0:T(8,128)S(1)}) custom-call(f32[320,128]{1,0:T(8,128)S(1)} %bitcast.18, f32[16,3,8,128]{3,2,1,0:T(8,128)S(1)} %get-tuple-element.23.refs_0_, f32[16,3,8,128]{3,2,1,0:T(8,128)S(1)} %get-tuple-element.28.refs_1_, ...), custom_call_target="tpu_custom_call" | custom-call | bytes 1662988 | tf_op jit(solution)/shard_map/pallas_call | solution.py:454
  44.9 8.9 %all_to_all.22 = f32[32,1,1,128]{3,2,1,0:T(1,128)S(1)} all-to-all(f32[32,1,1,128]{3,2,1,0:T(1,128)S(1)} %bitcast.23), channel_id=1, replica_groups=mesh['top'=4,'mid'=2,'core'=2,'col'=2] {'top','mid','core','col'}, dimensions={0} | all-to-all | bytes 32768 | tf_op jit(solution)/shard_map/all_to_all | solution.py:33
  53.8 0.7 %shard_map.70 = f32[6,3,64]{2,1,0:T(4,128)} custom-call(f32[32,128]{1,0:T(8,128)S(1)} %bitcast.22, f32[3,3,8,128]{3,2,1,0:T(8,128)S(1)} %get-tuple-element.31.own, f32[3,8,128]{2,1,0:T(8,128)S(1)} %get-tuple-element.29.refs_3_.refs_0_, f32[6,8,128]{2,1,0:T(8,128)S(1)} %get-tuple-element.32.refs_1_, f32[2,8,128]{2,1,0:T(8,128)S(1)} %get-tuple-element.24.refs_1_.refs_2_), custom_call_target="tpu_custom_call" | custom-call | bytes 98304 | tf_op jit(solution)/shard_map/pallas_call | solution.py:454
Async XLA Ops:
  1.6 16.7 %all-to-all-start = ((f32[32,11,1,128]{3,2,1,0:T(1,128)}), f32[32,11,1,128]{3,2,1,0:T(1,128)S(1)}, u32[]{:S(2)}, u32[]{:S(2)}) async-start(f32[32,11,1,128]{3,2,1,0:T(1,128)} %bitcast.4), calls=%async_computation | async-start | bytes 360448 | tf_op jit(solution)/shard_map/all_to_all | solution.py:33
  8.9 3.8 %collective-permute-start = (f32[32,128]{1,0:T(8,128)S(1)}, f32[32,128]{1,0:T(8,128)S(1)}, u32[]{:S(2)}, u32[]{:S(2)}) collective-permute-start(f32[32,128]{1,0:T(8,128)S(1)} %get-tuple-element.20.lists), channel_id=1, source_target_pairs={{0,1},{1,0},{2,3},{3,2},{4,5},{5,4},{6,7},{7,6},{8,9},{9,8},{10,11... | collective-permute-start | bytes 49160 | tf_op jit(solution)/shard_map/ppermute | solution.py:498

commit v14 on v13

--- a/solution.py
+++ b/solution.py
@@ -13,7 +13,7 @@
 INV_EIGHT_PI = 1.0 / (8.0 * math.pi)
 ROWS = 8
 HALF = 3
-FIRST, LATER = 11, 10
+FIRST, LATER = 11, 9
 ORDER = (0, 2, 1)
 AXES = ("top", "mid", "core", "col")
 F32 = jnp.float32
@@ -71,12 +71,14 @@
     half = n_row // 2
     o = chunk // half
     u = chunk % half
-    even = piece[pl.ds((me ^ ((2 * u) * n_col + o)) * size + at, count)]
-    odd = piece[pl.ds((me ^ ((2 * u + 1) * n_col + o)) * size + at, count)]
+    early = max(at + count - size, 0)
+    even = piece[pl.ds((me ^ ((2 * u) * n_col + o)) * size + at - early, count)]
+    odd = piece[pl.ds((me ^ ((2 * u + 1) * n_col + o)) * size + at - early, count)]
     low = low_half((count, 128))
     first = jnp.where(low, even, pltpu.roll(odd, 64, 1))
     second = jnp.where(low, pltpu.roll(even, 64, 1), odd)
-    return jnp.concatenate([first, second], axis=0)
+    rows = jnp.concatenate([first, second], axis=0)
+    return pltpu.roll(rows, ROWS - early, 0) if early else rows
 
 
 PAIRS = [(i, j) for i in range(ITERS) for j in range(i + 1, ITERS)]
@@ -113,9 +115,8 @@
 
 
 def contract(cols, kernels):
-    first = jnp.dot(cols[:128], kernels, preferred_element_type=F32)
-    second = jnp.dot(cols[128:], kernels[:, :128], preferred_element_type=F32)
-    return first[:, :128] + (second + first[:, 128:])
+    prod = jnp.dot(cols, kernels, preferred_element_type=F32)
+    return prod[:128, :128] + (prod[128:, :128] + prod[:128, 128:])
 
 
 def products(n_chunk, columns, cols, kernels):
@@ -154,13 +155,13 @@
     for image in images:
         top, bottom = image[:4], pltpu.roll(image[4:], 64, 1)
         rows.append(jnp.where(low_half((4, 128)), top, bottom))
-    message = jnp.concatenate([rows[0][:HALF], rows[1][:HALF], rows[2]], axis=0)
-    block = jnp.concatenate([message] * 4, axis=0)
+    message = jnp.concatenate([row[:HALF] for row in rows], axis=0)
+    block = jnp.concatenate([message] * 8, axis=0)
 
     def put(m):
-        out[pl.ds(m * 4 * LATER, 4 * LATER)] = block
-
-    each_wide(out.shape[0] // (4 * LATER), put)
+        out[pl.ds(m * 8 * LATER, 8 * LATER)] = block
+
+    each_wide(out.shape[0] // (8 * LATER), put)
 
 
 def each_wide(count, put):
@@ -180,7 +181,7 @@
     ]
     for copy in copies:
         copy.start()
-    for copy in copies:
+    for copy in copies[:4]:
         copy.wait()
     velocity, points, area, self_term, index, weight = held
     count = index.shape[0]
@@ -199,15 +200,17 @@
     message = jnp.concatenate(rows, axis=0)
     size = block.shape[0]
     block[...] = jnp.concatenate([message] * 8, axis=0)
-    copies = [
+    leaving = [
         pltpu.make_async_copy(block, out.at[pl.ds(i * size, size)], sems.at[6 + i])
         for i in range(out.shape[0] // size)
     ]
-    for copy in copies:
+    for copy in leaving:
         copy.start()
+    for copy in copies[4:]:
+        copy.wait()
     lists[:count] = index[...].astype(F32)
     lists[count:] = weight[...]
-    for copy in copies:
+    for copy in leaving:
         copy.wait()
 
 

time: 54.8 us -> 54.4 us (level)
  no operation moved by 1% of the time
where the time goes in v14:
time: 54.4 us; the launch traced here: 54 us
  blocking collectives  30.1 us (55%)
  Pallas kernels  9.45 us (17%)
  starting transfers between devices  9.14 us (17%)
  waiting for transfers between devices  5.25 us (10%)
    all_to_all x3, blocking collectives, spread(): return lax.all_to_all(wide, AXES, 0, 0, tiled=True).reshape(rows.shape)  30.1 us
    pallas_call x7, Pallas kernels, call(): pl.pallas_call(kernel, out_shape=[jax.ShapeDtypeStruct(s, t) for s, t in...  9.45 us
    all_to_all x1, starting transfers between devices, spread(): return lax.all_to_all(wide, AXES, 0, 0, tiled=True).reshape(rows.shape)  7.3 us
    all_to_all x1, waiting for transfers between devices, spread(): return lax.all_to_all(wide, AXES, 0, 0, tiled=True).reshape(rows.shape)  4.46 us
    ppermute x1, starting transfers between devices, body(): lax.ppermute(lists, 'col', xor_perm(n_col, o))  1.83 us
  transfers between devices with their start and end apart: 2, of which 2 were waited for; matrix products, arithmetic and copies ran while one was open for 0% of the time, Pallas kernels for 4%

profile of v14, /device:TPU:0, one launch (start us, length us, event | category | flops | bytes accessed | tf_op | source)
XLA Modules:
  0.0 54.0 jit_solution(12680094876228751911)
XLA Ops:
  0.0 1.5 %shard_map.64 = (f32[352,128]{1,0:T(8,128)}, f32[8,128]{1,0:T(8,128)S(1)}, f32[32,128]{1,0:T(8,128)S(1)}) custom-call(f32[6,3,64]{2,1,0:T(4,128)} %refs_0_.1, f32[3,64]{1,0:T(4,128)} %refs_1_.1, f32[1,64]{1,0:T(1,128)} %bitcast.26, f32[1,64]{1,0:T(1,128)} %bitcast.27, s32[16,128]{1,0:T(8,128)} %bitcast.24, f32[16,128]{1,0:T(8,128)} %bitcast.25), custom_call_target="tpu_custom_call" | custom-call | bytes 22272 | tf_op jit(solution)/shard_map/pallas_call | solution.py:457
  1.5 7.3 %all-to-all-start = ((f32[32,11,1,128]{3,2,1,0:T(1,128)}), f32[32,11,1,128]{3,2,1,0:T(1,128)S(1)}, u32[]{:S(2)}, u32[]{:S(2)}) async-start(f32[32,11,1,128]{3,2,1,0:T(1,128)} %bitcast.4), calls=%async_computation | async-start | bytes 360448 | tf_op jit(solution)/shard_map/all_to_all | solution.py:33
  8.9 1.8 %collective-permute-start = (f32[32,128]{1,0:T(8,128)S(1)}, f32[32,128]{1,0:T(8,128)S(1)}, u32[]{:S(2)}, u32[]{:S(2)}) collective-permute-start(f32[32,128]{1,0:T(8,128)S(1)} %get-tuple-element.20.lists), channel_id=1, source_target_pairs={{0,1},{1,0},{2,3},{3,2},{4,5},{5,4},{6,7},{7,6},{8,9},{9,8},{10,11... | collective-permute-start | bytes 49160 | tf_op jit(solution)/shard_map/ppermute | solution.py:501
  10.7 0.1 pad_add_fusion.me.refs_3_.refs_5_.refs_7_
  10.8 1.1 %shard_map.65.refs_0_ = f32[8,64,128]{2,1,0:T(8,128)S(1)} custom-call(s32[3]{0:T(128)S(1)} %pad_add_fusion.me.refs_3_.refs_5_.refs_7_, f32[32,128]{1,0:T(8,128)S(1)} %get-tuple-element.20.lists), custom_call_target="tpu_custom_call" | custom-call | flops 100000000 | bytes 16396 | tf_op jit(solution)/shard_map/pallas_call | solution.py:457
  11.9 0.8 %collective-permute-done.lists = f32[32,128]{1,0:T(8,128)S(1)} collective-permute-done((f32[32,128]{1,0:T(8,128)S(1)}, f32[32,128]{1,0:T(8,128)S(1)}, u32[]{:S(2)}, u32[]{:S(2)}) %collective-permute-start) | collective-permute-done | bytes 16416 | tf_op jit(solution)/shard_map/ppermute | solution.py:501
  12.7 1.1 %shard_map.66.refs_1_ = f32[8,64,128]{2,1,0:T(8,128)S(1)} custom-call(s32[3]{0:T(128)S(1)} %pad_add_fusion.me.refs_3_.refs_5_.refs_7_, f32[32,128]{1,0:T(8,128)S(1)} %collective-permute-done.lists), custom_call_target="tpu_custom_call" | custom-call | flops 100000000 | bytes 16396 | tf_op jit(solution)/shard_map/pallas_call | solution.py:457
  13.8 4.5 %all-to-all-done = f32[32,11,1,128]{3,2,1,0:T(1,128)S(1)} async-done(((f32[32,11,1,128]{3,2,1,0:T(1,128)}), f32[32,11,1,128]{3,2,1,0:T(1,128)S(1)}, u32[]{:S(2)}, u32[]{:S(2)}) %all-to-all-start) | async-done | bytes 180256 | tf_op jit(solution)/shard_map/all_to_all | solution.py:33
  18.3 2.0 %shard_map.67 = (bf16[2048,256]{1,0:T(8,128)(2,1)S(1)}, f32[16,4,128]{2,1,0:T(4,128)S(1)}, f32[16,3,8,128]{3,2,1,0:T(8,128)S(1)}, f32[2,8,128]{2,1,0:T(8,128)S(1)}, f32[288,128]{1,0:T(8,128)S(1)}) custom-call(f32[352,128]{1,0:T(8,128)S(1)} %bitcast.17, f32[8,64,128]{2,1,0:T(8,128)S(1)} %shard_map.65.refs_0_, f32[8,64,128]{2,1,0:T(8,128)S(1)} %shard_map.66.refs_1_, ...), custom_call_target="tpu_custom_call" | custom-call | bytes 708620 | tf_op jit(solution)/shard_map/pallas_call | solution.py:457
  20.3 10.6 %all_to_all.20 = f32[32,9,1,128]{3,2,1,0:T(1,128)S(1)} all-to-all(f32[32,9,1,128]{3,2,1,0:T(1,128)S(1)} %bitcast.20), channel_id=1, replica_groups=mesh['top'=4,'mid'=2,'core'=2,'col'=2] {'top','mid','core','col'}, dimensions={0} | all-to-all | bytes 294912 | tf_op jit(solution)/shard_map/all_to_all | solution.py:33
  30.8 1.5 %shard_map.68 = (f32[16,3,8,128]{3,2,1,0:T(8,128)S(1)}, f32[3,8,128]{2,1,0:T(8,128)S(1)}, f32[288,128]{1,0:T(8,128)S(1)}) custom-call(f32[288,128]{1,0:T(8,128)S(1)} %bitcast.19, f32[16,3,8,128]{3,2,1,0:T(8,128)S(1)} %get-tuple-element.23.refs_0_, f32[2,8,128]{2,1,0:T(8,128)S(1)} %get-tuple-element.24.refs_1_.refs_2_, ...), custom_call_target="tpu_custom_call" | custom-call | bytes 1437708 | tf_op jit(solution)/shard_map/pallas_call | solution.py:457
  32.3 10.6 %all_to_all.21 = f32[32,9,1,128]{3,2,1,0:T(1,128)S(1)} all-to-all(f32[32,9,1,128]{3,2,1,0:T(1,128)S(1)} %bitcast.21), channel_id=1, replica_groups=mesh['top'=4,'mid'=2,'core'=2,'col'=2] {'top','mid','core','col'}, dimensions={0} | all-to-all | bytes 294912 | tf_op jit(solution)/shard_map/all_to_all | solution.py:33
  42.9 1.5 %shard_map.69 = (f32[3,3,8,128]{3,2,1,0:T(8,128)S(1)}, f32[6,8,128]{2,1,0:T(8,128)S(1)}, f32[32,128]{1,0:T(8,128)S(1)}) custom-call(f32[288,128]{1,0:T(8,128)S(1)} %bitcast.18, f32[16,3,8,128]{3,2,1,0:T(8,128)S(1)} %get-tuple-element.23.refs_0_, f32[16,3,8,128]{3,2,1,0:T(8,128)S(1)} %get-tuple-element.28.refs_1_, ...), custom_call_target="tpu_custom_call" | custom-call | bytes 1646604 | tf_op jit(solution)/shard_map/pallas_call | solution.py:457
  44.4 8.9 %all_to_all.22 = f32[32,1,1,128]{3,2,1,0:T(1,128)S(1)} all-to-all(f32[32,1,1,128]{3,2,1,0:T(1,128)S(1)} %bitcast.23), channel_id=1, replica_groups=mesh['top'=4,'mid'=2,'core'=2,'col'=2] {'top','mid','core','col'}, dimensions={0} | all-to-all | bytes 32768 | tf_op jit(solution)/shard_map/all_to_all | solution.py:33
  53.3 0.7 %shard_map.70 = f32[6,3,64]{2,1,0:T(4,128)} custom-call(f32[32,128]{1,0:T(8,128)S(1)} %bitcast.22, f32[3,3,8,128]{3,2,1,0:T(8,128)S(1)} %get-tuple-element.31.own, f32[3,8,128]{2,1,0:T(8,128)S(1)} %get-tuple-element.29.refs_3_.refs_0_, f32[6,8,128]{2,1,0:T(8,128)S(1)} %get-tuple-element.32.refs_1_, f32[2,8,128]{2,1,0:T(8,128)S(1)} %get-tuple-element.24.refs_1_.refs_2_), custom_call_target="tpu_custom_call" | custom-call | bytes 98304 | tf_op jit(solution)/shard_map/pallas_call | solution.py:457
Async XLA Ops:
  1.5 16.7 %all-to-all-start = ((f32[32,11,1,128]{3,2,1,0:T(1,128)}), f32[32,11,1,128]{3,2,1,0:T(1,128)S(1)}, u32[]{:S(2)}, u32[]{:S(2)}) async-start(f32[32,11,1,128]{3,2,1,0:T(1,128)} %bitcast.4), calls=%async_computation | async-start | bytes 360448 | tf_op jit(solution)/shard_map/all_to_all | solution.py:33
  8.9 3.8 %collective-permute-start = (f32[32,128]{1,0:T(8,128)S(1)}, f32[32,128]{1,0:T(8,128)S(1)}, u32[]{:S(2)}, u32[]{:S(2)}) collective-permute-start(f32[32,128]{1,0:T(8,128)S(1)} %get-tuple-element.20.lists), channel_id=1, source_target_pairs={{0,1},{1,0},{2,3},{3,2},{4,5},{5,4},{6,7},{7,6},{8,9},{9,8},{10,11... | collective-permute-start | bytes 49160 | tf_op jit(solution)/shard_map/ppermute | solution.py:501

commit v15 on v14

--- a/solution.py
+++ b/solution.py
@@ -99,24 +99,18 @@
     return pl.ds(pl.multiple_of(chunk * 128, 128), 128)
 
 
-def write_columns(cols, y, chunk, vec):
-    ys = [y[a : a + 1] for a in ORDER]
-    f = [vec[a] for a in range(3)]
-    g = ys[0] * f[0] + ys[1] * f[1] + ys[2] * f[2]
-    groups = f + [g]
-    groups += [ys[p] * f[v] for p in range(3) for v in range(3)]
-    groups += [ys[a] * g for a in range(3)]
-    full = jnp.concatenate(groups, axis=0)
+def write_columns(cols, y, chunk, f):
+    inner = sum(y[k : k + 1] * f[a] for a, k in enumerate(ORDER))
+    full = jnp.concatenate([*f, inner], axis=0)
     high = full.astype(BF16)
-    low = (full - high.astype(F32)).astype(BF16)
     at = lines_of(chunk)
-    cols[0:128, at] = high
-    cols[128:256, at] = low
+    cols[0:32, at] = high
+    cols[32:64, at] = (full - high.astype(F32)).astype(BF16)
 
 
 def contract(cols, kernels):
     prod = jnp.dot(cols, kernels, preferred_element_type=F32)
-    return prod[:128, :128] + (prod[128:, :128] + prod[:128, 128:])
+    return prod[:32, :256] + (prod[32:, :256] + prod[:32, 256:])
 
 
 def products(n_chunk, columns, cols, kernels):
@@ -130,24 +124,17 @@
         at = pl.ds(pl.multiple_of(i * 2048, 2048), 2048)
         return acc + contract(cols[:, at], kernels[at, :])
 
-    return lax.fori_loop(0, n_chunk // 16, turn, jnp.zeros((128, 128), F32))
+    return lax.fori_loop(0, n_chunk // 16, turn, jnp.zeros((32, 256), F32))
 
 
 def image_rows(prod, targets, own, scale):
-    both = prod
-    two = pltpu.roll(both, 64, 1)
-
-    def group(k):
-        return two[8 * k : 8 * k + 8]
-
+    left = [prod[8 * k : 8 * k + 8, :128] for k in range(4)]
+    right = [prod[8 * k : 8 * k + 8, 128:] for k in range(4)]
     x = [targets[a : a + 1] for a in range(3)]
-    images = []
-    along = x[0] * group(0) + x[1] * group(1) + x[2] * group(2) - group(3)
-    for a in range(3):
-        cross = sum(x[b] * group(4 + 3 * a + b) for b in range(3))
-        image = both[8 * a : 8 * a + 8] + x[a] * along - cross + group(13 + a)
-        images.append((image + targets[3:4] * own[a]) * scale)
-    return images
+    first = x[0] * left[0] + x[1] * left[1] + x[2] * left[2] - left[3]
+    other = x[0] * right[0] + x[1] * right[1] + x[2] * right[2] - right[3]
+    parts = [pltpu.roll(first, 64, 1), other, pltpu.roll(other, 64, 1)]
+    return [(left[a] + parts[a] + targets[3:4] * own[a]) * scale for a in range(3)]
 
 
 def write_piece(images, out):
@@ -282,11 +269,13 @@
             for o in range(n_col):
                 mine = extra[o][chunk % half]
                 one = one + jnp.where(chunk // half == o, mine, 0.0)
-        value = jnp.concatenate([one, two], axis=0).T
-        high = value.astype(BF16)
+        moved = [two * part for part in d]
         at = lines_of(chunk)
-        kernels[at, 0:128] = high
-        kernels[at, 128:256] = (value - high.astype(F32)).astype(BF16)
+        for k, pair in enumerate(([one, moved[0]], moved[1:])):
+            value = jnp.concatenate(pair, axis=0).T
+            high = value.astype(BF16)
+            kernels[at, 128 * k : 128 * k + 128] = high
+            kernels[at, 256 + 128 * k : 384 + 128 * k] = (value - high.astype(F32)).astype(BF16)
 
     prod = products(n_chunk, build, cols, kernels)
     norm = jnp.sqrt(total.get(0))
@@ -512,12 +501,12 @@
     ]
 
     vec_shape = (n_chunk, 3, ROWS, 128)
-    cols = pltpu.VMEM((256, total), BF16)
+    cols = pltpu.VMEM((64, total), BF16)
     held = [] if n_chunk <= 16 else [pltpu.VMEM((8, ROWS, 128), F32)]
     kernels, places, basis, norm, wide = call(
         functools.partial(first_kernel, n_row, n_col),
         [
-            ((total, 256), BF16),
+            ((total, 512), BF16),
             ((n_chunk, 4, 128), F32),
             (vec_shape, F32),
             ((2, ROWS, 128), F32),

time: 54.4 us -> 54.5 us (level)
  no operation moved by 1% of the time
where the time goes in v15:
time: 54.5 us; the launch traced here: 54.2 us
  blocking collectives  30.1 us (55%)
  Pallas kernels  9.58 us (18%)
  starting transfers between devices  9.14 us (17%)
  waiting for transfers between devices  5.25 us (10%)
    all_to_all x3, blocking collectives, spread(): return lax.all_to_all(wide, AXES, 0, 0, tiled=True).reshape(rows.shape)  30.1 us
    pallas_call x7, Pallas kernels, call(): pl.pallas_call(kernel, out_shape=[jax.ShapeDtypeStruct(s, t) for s, t in...  9.58 us
    all_to_all x1, starting transfers between devices, spread(): return lax.all_to_all(wide, AXES, 0, 0, tiled=True).reshape(rows.shape)  7.3 us
    all_to_all x1, waiting for transfers between devices, spread(): return lax.all_to_all(wide, AXES, 0, 0, tiled=True).reshape(rows.shape)  4.46 us
    ppermute x1, starting transfers between devices, body(): lax.ppermute(lists, 'col', xor_perm(n_col, o))  1.83 us
  transfers between devices with their start and end apart: 2, of which 2 were waited for; matrix products, arithmetic and copies ran while one was open for 0% of the time, Pallas kernels for 4%

profile of v15, /device:TPU:0, one launch (start us, length us, event | category | flops | bytes accessed | tf_op | source)
XLA Modules:
  0.0 54.2 jit_solution(11733210126242112861)
XLA Ops:
  0.0 1.5 %shard_map.64 = (f32[352,128]{1,0:T(8,128)}, f32[8,128]{1,0:T(8,128)S(1)}, f32[32,128]{1,0:T(8,128)S(1)}) custom-call(f32[6,3,64]{2,1,0:T(4,128)} %refs_0_.1, f32[3,64]{1,0:T(4,128)} %refs_1_.1, f32[1,64]{1,0:T(1,128)} %bitcast.26, f32[1,64]{1,0:T(1,128)} %bitcast.27, s32[16,128]{1,0:T(8,128)} %bitcast.24, f32[16,128]{1,0:T(8,128)} %bitcast.25), custom_call_target="tpu_custom_call" | custom-call | bytes 22272 | tf_op jit(solution)/shard_map/pallas_call | solution.py:446
  1.5 7.3 %all-to-all-start = ((f32[32,11,1,128]{3,2,1,0:T(1,128)}), f32[32,11,1,128]{3,2,1,0:T(1,128)S(1)}, u32[]{:S(2)}, u32[]{:S(2)}) async-start(f32[32,11,1,128]{3,2,1,0:T(1,128)} %bitcast.4), calls=%async_computation | async-start | bytes 360448 | tf_op jit(solution)/shard_map/all_to_all | solution.py:33
  8.9 1.8 %collective-permute-start = (f32[32,128]{1,0:T(8,128)S(1)}, f32[32,128]{1,0:T(8,128)S(1)}, u32[]{:S(2)}, u32[]{:S(2)}) collective-permute-start(f32[32,128]{1,0:T(8,128)S(1)} %get-tuple-element.20.lists), channel_id=1, source_target_pairs={{0,1},{1,0},{2,3},{3,2},{4,5},{5,4},{6,7},{7,6},{8,9},{9,8},{10,11... | collective-permute-start | bytes 49160 | tf_op jit(solution)/shard_map/ppermute | solution.py:490
  10.7 0.1 pad_add_fusion.me.refs_3_.refs_5_.refs_7_
  10.8 1.1 %shard_map.65.refs_0_ = f32[8,64,128]{2,1,0:T(8,128)S(1)} custom-call(s32[3]{0:T(128)S(1)} %pad_add_fusion.me.refs_3_.refs_5_.refs_7_, f32[32,128]{1,0:T(8,128)S(1)} %get-tuple-element.20.lists), custom_call_target="tpu_custom_call" | custom-call | flops 100000000 | bytes 16396 | tf_op jit(solution)/shard_map/pallas_call | solution.py:446
  11.9 0.8 %collective-permute-done.lists = f32[32,128]{1,0:T(8,128)S(1)} collective-permute-done((f32[32,128]{1,0:T(8,128)S(1)}, f32[32,128]{1,0:T(8,128)S(1)}, u32[]{:S(2)}, u32[]{:S(2)}) %collective-permute-start) | collective-permute-done | bytes 16416 | tf_op jit(solution)/shard_map/ppermute | solution.py:490
  12.7 1.1 %shard_map.66.refs_1_ = f32[8,64,128]{2,1,0:T(8,128)S(1)} custom-call(s32[3]{0:T(128)S(1)} %pad_add_fusion.me.refs_3_.refs_5_.refs_7_, f32[32,128]{1,0:T(8,128)S(1)} %collective-permute-done.lists), custom_call_target="tpu_custom_call" | custom-call | flops 100000000 | bytes 16396 | tf_op jit(solution)/shard_map/pallas_call | solution.py:446
  13.8 4.5 %all-to-all-done = f32[32,11,1,128]{3,2,1,0:T(1,128)S(1)} async-done(((f32[32,11,1,128]{3,2,1,0:T(1,128)}), f32[32,11,1,128]{3,2,1,0:T(1,128)S(1)}, u32[]{:S(2)}, u32[]{:S(2)}) %all-to-all-start) | async-done | bytes 180256 | tf_op jit(solution)/shard_map/all_to_all | solution.py:33
  18.3 2.1 %shard_map.67 = (bf16[2048,512]{1,0:T(8,128)(2,1)S(1)}, f32[16,4,128]{2,1,0:T(4,128)S(1)}, f32[16,3,8,128]{3,2,1,0:T(8,128)S(1)}, f32[2,8,128]{2,1,0:T(8,128)S(1)}, f32[288,128]{1,0:T(8,128)S(1)}) custom-call(f32[352,128]{1,0:T(8,128)S(1)} %bitcast.17, f32[8,64,128]{2,1,0:T(8,128)S(1)} %shard_map.65.refs_0_, f32[8,64,128]{2,1,0:T(8,128)S(1)} %shard_map.66.refs_1_, ...), custom_call_target="tpu_custom_call" | custom-call | bytes 708620 | tf_op jit(solution)/shard_map/pallas_call | solution.py:446
  20.3 10.6 %all_to_all.20 = f32[32,9,1,128]{3,2,1,0:T(1,128)S(1)} all-to-all(f32[32,9,1,128]{3,2,1,0:T(1,128)S(1)} %bitcast.20), channel_id=1, replica_groups=mesh['top'=4,'mid'=2,'core'=2,'col'=2] {'top','mid','core','col'}, dimensions={0} | all-to-all | bytes 294912 | tf_op jit(solution)/shard_map/all_to_all | solution.py:33
  30.9 1.5 %shard_map.68 = (f32[16,3,8,128]{3,2,1,0:T(8,128)S(1)}, f32[3,8,128]{2,1,0:T(8,128)S(1)}, f32[288,128]{1,0:T(8,128)S(1)}) custom-call(f32[288,128]{1,0:T(8,128)S(1)} %bitcast.19, f32[16,3,8,128]{3,2,1,0:T(8,128)S(1)} %get-tuple-element.23.refs_0_, f32[2,8,128]{2,1,0:T(8,128)S(1)} %get-tuple-element.24.refs_1_.refs_2_, ...), custom_call_target="tpu_custom_call" | custom-call | bytes 2486284 | tf_op jit(solution)/shard_map/pallas_call | solution.py:446
  32.4 10.6 %all_to_all.21 = f32[32,9,1,128]{3,2,1,0:T(1,128)S(1)} all-to-all(f32[32,9,1,128]{3,2,1,0:T(1,128)S(1)} %bitcast.21), channel_id=1, replica_groups=mesh['top'=4,'mid'=2,'core'=2,'col'=2] {'top','mid','core','col'}, dimensions={0} | all-to-all | bytes 294912 | tf_op jit(solution)/shard_map/all_to_all | solution.py:33
  43.0 1.5 %shard_map.69 = (f32[3,3,8,128]{3,2,1,0:T(8,128)S(1)}, f32[6,8,128]{2,1,0:T(8,128)S(1)}, f32[32,128]{1,0:T(8,128)S(1)}) custom-call(f32[288,128]{1,0:T(8,128)S(1)} %bitcast.18, f32[16,3,8,128]{3,2,1,0:T(8,128)S(1)} %get-tuple-element.23.refs_0_, f32[16,3,8,128]{3,2,1,0:T(8,128)S(1)} %get-tuple-element.28.refs_1_, ...), custom_call_target="tpu_custom_call" | custom-call | bytes 2695180 | tf_op jit(solution)/shard_map/pallas_call | solution.py:446
  44.5 8.9 %all_to_all.22 = f32[32,1,1,128]{3,2,1,0:T(1,128)S(1)} all-to-all(f32[32,1,1,128]{3,2,1,0:T(1,128)S(1)} %bitcast.23), channel_id=1, replica_groups=mesh['top'=4,'mid'=2,'core'=2,'col'=2] {'top','mid','core','col'}, dimensions={0} | all-to-all | bytes 32768 | tf_op jit(solution)/shard_map/all_to_all | solution.py:33
  53.4 0.7 %shard_map.70 = f32[6,3,64]{2,1,0:T(4,128)} custom-call(f32[32,128]{1,0:T(8,128)S(1)} %bitcast.22, f32[3,3,8,128]{3,2,1,0:T(8,128)S(1)} %get-tuple-element.31.own, f32[3,8,128]{2,1,0:T(8,128)S(1)} %get-tuple-element.29.refs_3_.refs_0_, f32[6,8,128]{2,1,0:T(8,128)S(1)} %get-tuple-element.32.refs_1_, f32[2,8,128]{2,1,0:T(8,128)S(1)} %get-tuple-element.24.refs_1_.refs_2_), custom_call_target="tpu_custom_call" | custom-call | bytes 98304 | tf_op jit(solution)/shard_map/pallas_call | solution.py:446
Async XLA Ops:
  1.5 16.7 %all-to-all-start = ((f32[32,11,1,128]{3,2,1,0:T(1,128)}), f32[32,11,1,128]{3,2,1,0:T(1,128)S(1)}, u32[]{:S(2)}, u32[]{:S(2)}) async-start(f32[32,11,1,128]{3,2,1,0:T(1,128)} %bitcast.4), calls=%async_computation | async-start | bytes 360448 | tf_op jit(solution)/shard_map/all_to_all | solution.py:33
  8.9 3.8 %collective-permute-start = (f32[32,128]{1,0:T(8,128)S(1)}, f32[32,128]{1,0:T(8,128)S(1)}, u32[]{:S(2)}, u32[]{:S(2)}) collective-permute-start(f32[32,128]{1,0:T(8,128)S(1)} %get-tuple-element.20.lists), channel_id=1, source_target_pairs={{0,1},{1,0},{2,3},{3,2},{4,5},{5,4},{6,7},{7,6},{8,9},{9,8},{10,11... | collective-permute-start | bytes 49160 | tf_op jit(solution)/shard_map/ppermute | solution.py:490

commit v16 on v15

--- a/solution.py
+++ b/solution.py
@@ -18,6 +18,12 @@
 AXES = ("top", "mid", "core", "col")
 F32 = jnp.float32
 BF16 = jnp.bfloat16
+
+
+def position(sizes):
+    top, mid, core, col = (lax.axis_index(axis) for axis in AXES)
+    row = (top * sizes[1] + mid) * sizes[2] + core
+    return row * sizes[3] + col, row, col
 
 
 def low_half(shape):
@@ -201,8 +207,8 @@
         copy.wait()
 
 
-def extra_kernel(me, lists, out):
-    row, col = me[1], me[2]
+def extra_kernel(sizes, lists, out):
+    _, row, col = position(sizes)
     lines = lax.broadcasted_iota(jnp.int32, (128, 128), 0).astype(F32)
     count = lists.shape[0] // 2
     half = count // 2
@@ -230,14 +236,13 @@
     each(out.shape[0], build)
 
 
-def first_kernel(
-    n_row, n_col, piece, *refs
-):
+def first_kernel(sizes, piece, *refs):
+    n_row, n_col = sizes[0] * sizes[1] * sizes[2], sizes[3]
     extra = refs[:n_col]
-    tgt, me_ref, kernels, places, basis, norm_out, out, cols, *sums = refs[n_col:]
+    tgt, kernels, places, basis, norm_out, out, cols, *sums = refs[n_col:]
     half = n_row // 2
     n_chunk = n_row * n_col // 2
-    me = me_ref[0]
+    me, _, _ = position(sizes)
     total = Sums(1, sums[0] if sums else None)
 
     def unpack(chunk):
@@ -285,14 +290,15 @@
     write_piece(image_rows(prod, tgt, basis[0], scale), out)
 
 
-def middle_kernel(n_row, n_col, n_base, final, piece, *refs):
+def middle_kernel(sizes, n_base, final, piece, *refs):
+    n_row, n_col = sizes[0] * sizes[1] * sizes[2], sizes[3]
     bases, norms = refs[:n_base], refs[n_base : 2 * n_base]
     if final:
-        kernels, places, tgt, me_ref, own, h_out, out, basis, cols, *held = refs[2 * n_base :]
+        kernels, places, tgt, own, h_out, out, basis, cols, *held = refs[2 * n_base :]
     else:
-        kernels, places, tgt, me_ref, basis, h_out, out, cols, *held = refs[2 * n_base :]
+        kernels, places, tgt, basis, h_out, out, cols, *held = refs[2 * n_base :]
     n_chunk = n_row * n_col // 2
-    me = me_ref[0]
+    me, _, _ = position(sizes)
     scales = [norm[norm.shape[0] - 1] for norm in norms]
     cross = [(i, j) for i in range(n_base) for j in range(i)]
     sums = Sums(2 * n_base + 1 + len(cross), held[0] if held else None)
@@ -436,12 +442,11 @@
         out[HALF:, a, :] = density[4 : 4 + HALF, :64]
 
 
-def call(kernel, outs, scratch, operands, scalars=(), far=(), spread_out=False, flops=0):
+def call(kernel, outs, scratch, operands, far=(), spread_out=False, flops=0):
     vmem = pl.BlockSpec(memory_space=pltpu.VMEM)
-    smem = pl.BlockSpec(memory_space=pltpu.SMEM)
     count = len(operands)
     hbm = pl.BlockSpec(memory_space=pltpu.HBM)
-    specs = [smem if i in scalars else hbm if i in far else vmem for i in range(count)]
+    specs = [hbm if i in far else vmem for i in range(count)]
     moved = sum(x.size * x.dtype.itemsize for x in operands)
     return pl.pallas_call(
         kernel,
@@ -459,9 +464,6 @@
     n = n_row * n_col
     n_chunk = n // 2
     total = n * 64
-    row = lax.axis_index(AXES[:3])
-    col = lax.axis_index("col")
-    me = jnp.stack([row * n_col + col, row, col]).astype(jnp.int32)
     rhs = velocity.shape[0]
 
     message = ((n * LATER, 128), F32)
@@ -490,11 +492,10 @@
     near = [lists] + [lax.ppermute(lists, "col", xor_perm(n_col, o)) for o in range(1, n_col)]
     extra = [
         call(
-            extra_kernel,
+            functools.partial(extra_kernel, sizes),
             [((n_row // 2, 64, 128), F32)],
             [],
-            [me, pair],
-            {0},
+            [pair],
             flops=10**8,
         )[0]
         for pair in near
@@ -504,7 +505,7 @@
     cols = pltpu.VMEM((64, total), BF16)
     held = [] if n_chunk <= 16 else [pltpu.VMEM((8, ROWS, 128), F32)]
     kernels, places, basis, norm, wide = call(
-        functools.partial(first_kernel, n_row, n_col),
+        functools.partial(first_kernel, sizes),
         [
             ((total, 512), BF16),
             ((n_chunk, 4, 128), F32),
@@ -513,8 +514,7 @@
             message,
         ],
         [cols, *held],
-        [piece, *extra, tgt, me],
-        {n_col + 2},
+        [piece, *extra, tgt],
     )
     bases = [basis]
     columns = [norm]
@@ -522,15 +522,14 @@
         final = k == ITERS - 1
         piece = spread(wide, n)
         main, column, wide = call(
-            functools.partial(middle_kernel, n_row, n_col, k, final),
+            functools.partial(middle_kernel, sizes, k, final),
             [
                 ((ITERS, 3, ROWS, 128) if final else vec_shape, F32),
                 ((k + 1 + (len(PAIRS) if final else 1), ROWS, 128), F32),
                 ((n, 128), F32) if final else message,
             ],
             [*([pltpu.VMEM(vec_shape, F32)] if final else []), cols, *held],
-            [piece, *bases, *columns, kernels, places, tgt, me],
-            {2 * k + 4},
+            [piece, *bases, *columns, kernels, places, tgt],
         )
         bases.append(main)
         columns.append(column)

time: 54.5 us -> 52.9 us (0.971)
  Pallas kernels: 9.58 us -> 6.91 us
  waiting for transfers between devices: 5.25 us -> 6.42 us
    pallas_call x7, Pallas kernels: 9.58 us -> 6.91 us  [call(): pl.pallas_call(kernel, out_shape=[jax.ShapeDtypeStruct(s, t) for s, t in...]
    ppermute x1, waiting for transfers between devices: 0.79 us -> 1.42 us  [body(): lax.ppermute(lists, 'col', xor_perm(n_col, o))]
    all_to_all x1, waiting for transfers between devices: 4.46 us -> 5 us  [spread(): return lax.all_to_all(wide, AXES, 0, 0, tiled=True).reshape(rows.shape)]
  transfers between devices with their start and end apart: 2 -> 2, of which waited for: 2 -> 2; matrix products, arithmetic and copies ran while one was open for 0% -> 0% of each run, Pallas kernels for 4% -> 2%
where the time goes in v16:
time: 52.9 us; the launch traced here: 52.6 us
  blocking collectives  30.1 us (57%)
  starting transfers between devices  9.14 us (17%)
  Pallas kernels  6.91 us (13%)
  waiting for transfers between devices  6.42 us (12%)
    all_to_all x3, blocking collectives, spread(): return lax.all_to_all(wide, AXES, 0, 0, tiled=True).reshape(rows.shape)  30.1 us
    all_to_all x1, starting transfers between devices, spread(): return lax.all_to_all(wide, AXES, 0, 0, tiled=True).reshape(rows.shape)  7.3 us
    pallas_call x7, Pallas kernels, call(): pl.pallas_call(kernel, out_shape=[jax.ShapeDtypeStruct(s, t) for s, t in...  6.91 us
    all_to_all x1, waiting for transfers between devices, spread(): return lax.all_to_all(wide, AXES, 0, 0, tiled=True).reshape(rows.shape)  5 us
    ppermute x1, starting transfers between devices, body(): lax.ppermute(lists, 'col', xor_perm(n_col, o))  1.83 us
    ppermute x1, waiting for transfers between devices, body(): lax.ppermute(lists, 'col', xor_perm(n_col, o))  1.42 us
  transfers between devices with their start and end apart: 2, of which 2 were waited for; matrix products, arithmetic and copies ran while one was open for 0% of the time, Pallas kernels for 2%

profile of v16, /device:TPU:0, one launch (start us, length us, event | category | flops | bytes accessed | tf_op | source)
XLA Modules:
  0.0 52.6 jit_solution(12937697371466317794)
XLA Ops:
  0.0 1.5 %shard_map.64 = (f32[352,128]{1,0:T(8,128)}, f32[8,128]{1,0:T(8,128)S(1)}, f32[32,128]{1,0:T(8,128)S(1)}) custom-call(f32[6,3,64]{2,1,0:T(4,128)} %refs_0_.1, f32[3,64]{1,0:T(4,128)} %refs_1_.1, f32[1,64]{1,0:T(1,128)} %bitcast.23, f32[1,64]{1,0:T(1,128)} %bitcast.24, s32[16,128]{1,0:T(8,128)} %bitcast.21, f32[16,128]{1,0:T(8,128)} %bitcast.22), custom_call_target="tpu_custom_call" | custom-call | bytes 22272 | tf_op jit(solution)/shard_map/pallas_call | solution.py:451
  1.5 7.3 %all-to-all-start = ((f32[32,11,1,128]{3,2,1,0:T(1,128)}), f32[32,11,1,128]{3,2,1,0:T(1,128)S(1)}, u32[]{:S(2)}, u32[]{:S(2)}) async-start(f32[32,11,1,128]{3,2,1,0:T(1,128)} %bitcast.4), calls=%async_computation | async-start | bytes 360448 | tf_op jit(solution)/shard_map/all_to_all | solution.py:39
  8.9 1.8 %collective-permute-start = (f32[32,128]{1,0:T(8,128)S(1)}, f32[32,128]{1,0:T(8,128)S(1)}, u32[]{:S(2)}, u32[]{:S(2)}) collective-permute-start(f32[32,128]{1,0:T(8,128)S(1)} %get-tuple-element.20.lists), channel_id=1, source_target_pairs={{0,1},{1,0},{2,3},{3,2},{4,5},{5,4},{6,7},{7,6},{8,9},{9,8},{10,11... | collective-permute-start | bytes 49160 | tf_op jit(solution)/shard_map/ppermute | solution.py:492
  10.7 0.6 %shard_map.65.refs_0_ = f32[8,64,128]{2,1,0:T(8,128)S(1)} custom-call(f32[32,128]{1,0:T(8,128)S(1)} %get-tuple-element.20.lists), custom_call_target="tpu_custom_call" | custom-call | flops 100000000 | bytes 16384 | tf_op jit(solution)/shard_map/pallas_call | solution.py:451
  11.3 1.4 %collective-permute-done.lists = f32[32,128]{1,0:T(8,128)S(1)} collective-permute-done((f32[32,128]{1,0:T(8,128)S(1)}, f32[32,128]{1,0:T(8,128)S(1)}, u32[]{:S(2)}, u32[]{:S(2)}) %collective-permute-start) | collective-permute-done | bytes 16416 | tf_op jit(solution)/shard_map/ppermute | solution.py:492
  12.7 0.6 %shard_map.66.refs_1_ = f32[8,64,128]{2,1,0:T(8,128)S(1)} custom-call(f32[32,128]{1,0:T(8,128)S(1)} %collective-permute-done.lists), custom_call_target="tpu_custom_call" | custom-call | flops 100000000 | bytes 16384 | tf_op jit(solution)/shard_map/pallas_call | solution.py:451
  13.2 5.0 %all-to-all-done = f32[32,11,1,128]{3,2,1,0:T(1,128)S(1)} async-done(((f32[32,11,1,128]{3,2,1,0:T(1,128)}), f32[32,11,1,128]{3,2,1,0:T(1,128)S(1)}, u32[]{:S(2)}, u32[]{:S(2)}) %all-to-all-start) | async-done | bytes 180256 | tf_op jit(solution)/shard_map/all_to_all | solution.py:39
  18.3 1.6 %shard_map.67 = (bf16[2048,512]{1,0:T(8,128)(2,1)S(1)}, f32[16,4,128]{2,1,0:T(4,128)S(1)}, f32[16,3,8,128]{3,2,1,0:T(8,128)S(1)}, f32[2,8,128]{2,1,0:T(8,128)S(1)}, f32[288,128]{1,0:T(8,128)S(1)}) custom-call(f32[352,128]{1,0:T(8,128)S(1)} %bitcast.14, f32[8,64,128]{2,1,0:T(8,128)S(1)} %shard_map.65.refs_0_, f32[8,64,128]{2,1,0:T(8,128)S(1)} %shard_map.66.refs_1_, ...), custom_call_target="tpu_custom_call" | custom-call | bytes 708608 | tf_op jit(solution)/shard_map/pallas_call | solution.py:451
  19.8 10.6 %all_to_all.20 = f32[32,9,1,128]{3,2,1,0:T(1,128)S(1)} all-to-all(f32[32,9,1,128]{3,2,1,0:T(1,128)S(1)} %bitcast.17), channel_id=1, replica_groups=mesh['top'=4,'mid'=2,'core'=2,'col'=2] {'top','mid','core','col'}, dimensions={0} | all-to-all | bytes 294912 | tf_op jit(solution)/shard_map/all_to_all | solution.py:39
  30.4 0.9 %shard_map.68 = (f32[16,3,8,128]{3,2,1,0:T(8,128)S(1)}, f32[3,8,128]{2,1,0:T(8,128)S(1)}, f32[288,128]{1,0:T(8,128)S(1)}) custom-call(f32[288,128]{1,0:T(8,128)S(1)} %bitcast.15, f32[16,3,8,128]{3,2,1,0:T(8,128)S(1)} %get-tuple-element.23.refs_0_, f32[2,8,128]{2,1,0:T(8,128)S(1)} %get-tuple-element.24.refs_1_.refs_2_, ...), custom_call_target="tpu_custom_call" | custom-call | bytes 2486272 | tf_op jit(solution)/shard_map/pallas_call | solution.py:451
  31.4 10.6 %all_to_all.21 = f32[32,9,1,128]{3,2,1,0:T(1,128)S(1)} all-to-all(f32[32,9,1,128]{3,2,1,0:T(1,128)S(1)} %bitcast.18), channel_id=1, replica_groups=mesh['top'=4,'mid'=2,'core'=2,'col'=2] {'top','mid','core','col'}, dimensions={0} | all-to-all | bytes 294912 | tf_op jit(solution)/shard_map/all_to_all | solution.py:39
  41.9 1.0 %shard_map.69 = (f32[3,3,8,128]{3,2,1,0:T(8,128)S(1)}, f32[6,8,128]{2,1,0:T(8,128)S(1)}, f32[32,128]{1,0:T(8,128)S(1)}) custom-call(f32[288,128]{1,0:T(8,128)S(1)} %bitcast.16, f32[16,3,8,128]{3,2,1,0:T(8,128)S(1)} %get-tuple-element.23.refs_0_, f32[16,3,8,128]{3,2,1,0:T(8,128)S(1)} %get-tuple-element.28.refs_1_, ...), custom_call_target="tpu_custom_call" | custom-call | bytes 2695168 | tf_op jit(solution)/shard_map/pallas_call | solution.py:451
  43.0 8.9 %all_to_all.22 = f32[32,1,1,128]{3,2,1,0:T(1,128)S(1)} all-to-all(f32[32,1,1,128]{3,2,1,0:T(1,128)S(1)} %bitcast.20), channel_id=1, replica_groups=mesh['top'=4,'mid'=2,'core'=2,'col'=2] {'top','mid','core','col'}, dimensions={0} | all-to-all | bytes 32768 | tf_op jit(solution)/shard_map/all_to_all | solution.py:39
  51.9 0.7 %shard_map.70 = f32[6,3,64]{2,1,0:T(4,128)} custom-call(f32[32,128]{1,0:T(8,128)S(1)} %bitcast.19, f32[3,3,8,128]{3,2,1,0:T(8,128)S(1)} %get-tuple-element.31.own, f32[3,8,128]{2,1,0:T(8,128)S(1)} %get-tuple-element.29.refs_3_.refs_0_, f32[6,8,128]{2,1,0:T(8,128)S(1)} %get-tuple-element.32.refs_1_, f32[2,8,128]{2,1,0:T(8,128)S(1)} %get-tuple-element.24.refs_1_.refs_2_), custom_call_target="tpu_custom_call" | custom-call | bytes 98304 | tf_op jit(solution)/shard_map/pallas_call | solution.py:451
Async XLA Ops:
  1.5 16.7 %all-to-all-start = ((f32[32,11,1,128]{3,2,1,0:T(1,128)}), f32[32,11,1,128]{3,2,1,0:T(1,128)S(1)}, u32[]{:S(2)}, u32[]{:S(2)}) async-start(f32[32,11,1,128]{3,2,1,0:T(1,128)} %bitcast.4), calls=%async_computation | async-start | bytes 360448 | tf_op jit(solution)/shard_map/all_to_all | solution.py:39
  8.9 3.8 %collective-permute-start = (f32[32,128]{1,0:T(8,128)S(1)}, f32[32,128]{1,0:T(8,128)S(1)}, u32[]{:S(2)}, u32[]{:S(2)}) collective-permute-start(f32[32,128]{1,0:T(8,128)S(1)} %get-tuple-element.20.lists), channel_id=1, source_target_pairs={{0,1},{1,0},{2,3},{3,2},{4,5},{5,4},{6,7},{7,6},{8,9},{9,8},{10,11... | collective-permute-start | bytes 49160 | tf_op jit(solution)/shard_map/ppermute | solution.py:492

commit v17 on v16

--- a/solution.py
+++ b/solution.py
@@ -326,7 +326,8 @@
         for i in range(j):
             h = h - column[i] * gram[i, j]
         column.append(h)
-        h_out[j] = h
+        if not final:
+            h_out[j] = h
     factors = [h * scale for h, scale in zip(column, scales)]
 
     def columns(chunk):
@@ -347,9 +348,9 @@
     prod = products(n_chunk, columns, cols, kernels)
     norm = jnp.sqrt(sums.get(n_base))
     scale = 1.0 / norm
-    h_out[n_base] = norm
     images = image_rows(prod, tgt, basis[0], scale)
     if not final:
+        h_out[n_base] = norm
         h_out[n_base + 1] = scale
         write_piece(images, out)
         return
@@ -359,8 +360,13 @@
             own[j, a] = base[0, a] * [*scales, scale][j]
     for j in range(n_base):
         gram[j, n_base] = sums.get(n_base + 1 + j) * (scale * scales[j])
-    for at, pair in enumerate(PAIRS):
-        h_out[n_base + 1 + at] = gram[pair]
+    hessen = {(i, n_base - 1): value for i, value in enumerate([*column, norm])}
+    for k in range(1, n_base):
+        for i in range(k + 1):
+            hessen[i, k - 1] = norms[k][i]
+    known = rotate_known(hessen, norms[0][0], ITERS)
+    for at, value in enumerate(known + [gram[pair] for pair in PAIRS]):
+        h_out[at] = value
     low = low_half((ROWS, 128))
     row = jnp.zeros((ROWS, 128), F32)
     for j in range(ITERS + 1):
@@ -368,74 +374,77 @@
         part = sum(images[a] * other[a] for a in range(3))
         part = row_sum(jnp.where(low, part, 0.0))
         row = row + jnp.where(place_of(j), part, 0.0)
-    row = jnp.sum(row, axis=0, keepdims=True)
+    row = jnp.broadcast_to(jnp.sum(row, axis=0, keepdims=True), (8, 128))
 
     def put(m):
-        out[pl.ds(m, 1)] = row
-
-    each_wide(out.shape[0], put)
-
-
-def solve_small(hessen, start_norm, count):
-    zero = jnp.zeros_like(start_norm)
-    target = [start_norm] + [zero] * count
-    cosines = []
-    sines = []
-    triangle = {}
-    for k in range(count):
+        out[pl.ds(m * 8, 8)] = row
+
+    each_wide(out.shape[0] // 8, put)
+
+
+def rotate_known(hessen, start_norm, count):
+    target = [start_norm]
+    turns = []
+    above = []
+    inverses = []
+    for k in range(count - 1):
         column = [hessen[i, k] for i in range(k + 2)]
-        for j in range(k):
-            first_val = column[j]
-            second_val = column[j + 1]
-            column[j] = cosines[j] * first_val + sines[j] * second_val
-            column[j + 1] = cosines[j] * second_val - sines[j] * first_val
-        radius = jnp.sqrt(column[k] * column[k] + column[k + 1] * column[k + 1])
-        cosine = column[k] / radius
-        sine = column[k + 1] / radius
-        cosines.append(cosine)
-        sines.append(sine)
-        for i in range(k):
-            triangle[i, k] = column[i]
-        triangle[k, k] = radius
-        target[k + 1] = -sine * target[k]
-        target[k] = cosine * target[k]
+        for j, (cosine, sine) in enumerate(turns):
+            first_val, second_val = column[j], column[j + 1]
+            column[j] = cosine * first_val + sine * second_val
+            column[j + 1] = cosine * second_val - sine * first_val
+        inverse = 1.0 / jnp.sqrt(column[k] * column[k] + column[k + 1] * column[k + 1])
+        turns.append((column[k] * inverse, column[k + 1] * inverse))
+        above += column[:k]
+        inverses.append(inverse)
+        target.append(-turns[k][1] * target[k])
+        target[k] = turns[k][0] * target[k]
+    return [value for turn in turns for value in turn] + above + inverses + target
+
+
+def solve_last(known, column, square, count):
+    size = count - 1
+    turns, known = known[: 2 * size], known[2 * size :]
+    above, known = known[: size * (size - 1) // 2], known[size * (size - 1) // 2 :]
+    inverses, target = known[:size], known[size:]
+    column = list(column)
+    for j in range(size):
+        cosine, sine = turns[2 * j], turns[2 * j + 1]
+        first_val, second_val = column[j], column[j + 1]
+        column[j] = cosine * first_val + sine * second_val
+        column[j + 1] = cosine * second_val - sine * first_val
+    last = column[size]
     coeffs = [None] * count
-    for k in range(count - 1, -1, -1):
-        accum = target[k]
-        for i in range(k + 1, count):
-            accum = accum - triangle[k, i] * coeffs[i]
-        coeffs[k] = accum / triangle[k, k]
+    coeffs[size] = target[size] * last / (last * last + square)
+    for k in range(size - 1, -1, -1):
+        accum = target[k] - column[k] * coeffs[size]
+        for i in range(k + 1, size):
+            accum = accum - above[i * (i - 1) // 2 + k] * coeffs[i]
+        coeffs[k] = accum * inverses[k]
     return coeffs
 
 
-def last_kernel(sums, own, *refs):
-    columns = refs[: ITERS - 1]
-    norm, out = refs[ITERS - 1 :]
-    hessen = {}
-    for k in range(ITERS - 1):
-        for j in range(k + 2):
-            hessen[j, k] = columns[k][j]
+KNOWN = 2 * (ITERS - 1) + (ITERS - 1) * (ITERS - 2) // 2 + (ITERS - 1) + ITERS
+
+
+def last_kernel(sums, own, held, out):
+    known = [held[i] for i in range(KNOWN)]
     gram = {(j, j): 1.0 for j in range(ITERS)}
     for at, (i, j) in enumerate(PAIRS):
-        gram[i, j] = gram[j, i] = columns[-1][ITERS + at]
+        gram[i, j] = gram[j, i] = held[KNOWN + at]
     row = jnp.broadcast_to(jnp.sum(sums[...], axis=0, keepdims=True), (ROWS, 128))
     inner = [
         jnp.broadcast_to(row_sum(jnp.where(place_of(j), row, 0.0)), (ROWS, 128))
         for j in range(ITERS + 1)
     ]
+    column = []
+    for j in range(ITERS):
+        column.append(inner[j] - sum(column[i] * gram[i, j] for i in range(j)))
     square = inner[ITERS]
     for j in range(ITERS):
-        h = inner[j]
-        for i in range(j):
-            h = h - hessen[i, ITERS - 1] * gram[i, j]
-        hessen[j, ITERS - 1] = h
-    for j in range(ITERS):
-        rest = -2.0 * inner[j]
-        for i in range(ITERS):
-            rest = rest + hessen[i, ITERS - 1] * gram[i, j]
-        square = square + hessen[j, ITERS - 1] * rest
-    hessen[ITERS, ITERS - 1] = jnp.sqrt(jnp.maximum(square, 0.0))
-    coeffs = solve_small(hessen, norm[0], ITERS)
+        rest = sum(column[i] * gram[i, j] for i in range(ITERS)) - 2.0 * inner[j]
+        square = square + column[j] * rest
+    coeffs = solve_last(known, column, jnp.maximum(square, 0.0), ITERS)
     for a in range(3):
         density = sum(coeffs[k] * own[k, a] for k in range(ITERS))
         out[:HALF, a, :] = density[:HALF, :64]
@@ -525,7 +534,7 @@
             functools.partial(middle_kernel, sizes, k, final),
             [
                 ((ITERS, 3, ROWS, 128) if final else vec_shape, F32),
-                ((k + 1 + (len(PAIRS) if final else 1), ROWS, 128), F32),
+                ((KNOWN + len(PAIRS) if final else k + 2, ROWS, 128), F32),
                 ((n, 128), F32) if final else message,
             ],
             [*([pltpu.VMEM(vec_shape, F32)] if final else []), cols, *held],
@@ -535,7 +544,7 @@
         columns.append(column)
     sums = spread(wide, n)
     (density,) = call(
-        last_kernel, [((rhs, 3, 64), F32)], [], [sums, bases[-1], *columns[1:], columns[0]]
+        last_kernel, [((rhs, 3, 64), F32)], [], [sums, bases[-1], columns[-1]]
     )
     return density
 

time: 52.9 us -> 52.9 us (level)
  no operation moved by 1% of the time
where the time goes in v17:
time: 52.9 us; the launch traced here: 52.6 us
  blocking collectives  30.1 us (57%)
  starting transfers between devices  9.14 us (17%)
  Pallas kernels  6.89 us (13%)
  waiting for transfers between devices  6.42 us (12%)
    all_to_all x3, blocking collectives, spread(): return lax.all_to_all(wide, AXES, 0, 0, tiled=True).reshape(rows.shape)  30.1 us
    all_to_all x1, starting transfers between devices, spread(): return lax.all_to_all(wide, AXES, 0, 0, tiled=True).reshape(rows.shape)  7.3 us
    pallas_call x7, Pallas kernels, call(): pl.pallas_call(kernel, out_shape=[jax.ShapeDtypeStruct(s, t) for s, t in...  6.89 us
    all_to_all x1, waiting for transfers between devices, spread(): return lax.all_to_all(wide, AXES, 0, 0, tiled=True).reshape(rows.shape)  5 us
    ppermute x1, starting transfers between devices, body(): lax.ppermute(lists, 'col', xor_perm(n_col, o))  1.83 us
    ppermute x1, waiting for transfers between devices, body(): lax.ppermute(lists, 'col', xor_perm(n_col, o))  1.42 us
  transfers between devices with their start and end apart: 2, of which 2 were waited for; matrix products, arithmetic and copies ran while one was open for 0% of the time, Pallas kernels for 2%

profile of v17, /device:TPU:0, one launch (start us, length us, event | category | flops | bytes accessed | tf_op | source)
XLA Modules:
  0.0 52.6 jit_solution(14808663369990526811)
XLA Ops:
  0.0 1.5 %shard_map.64 = (f32[352,128]{1,0:T(8,128)}, f32[8,128]{1,0:T(8,128)S(1)}, f32[32,128]{1,0:T(8,128)S(1)}) custom-call(f32[6,3,64]{2,1,0:T(4,128)} %refs_0_.1, f32[3,64]{1,0:T(4,128)} %refs_1_.1, f32[1,64]{1,0:T(1,128)} %bitcast.23, f32[1,64]{1,0:T(1,128)} %bitcast.24, s32[16,128]{1,0:T(8,128)} %bitcast.21, f32[16,128]{1,0:T(8,128)} %bitcast.22), custom_call_target="tpu_custom_call" | custom-call | bytes 22272 | tf_op jit(solution)/shard_map/pallas_call | solution.py:460
  1.5 7.3 %all-to-all-start = ((f32[32,11,1,128]{3,2,1,0:T(1,128)}), f32[32,11,1,128]{3,2,1,0:T(1,128)S(1)}, u32[]{:S(2)}, u32[]{:S(2)}) async-start(f32[32,11,1,128]{3,2,1,0:T(1,128)} %bitcast.4), calls=%async_computation | async-start | bytes 360448 | tf_op jit(solution)/shard_map/all_to_all | solution.py:39
  8.9 1.8 %collective-permute-start = (f32[32,128]{1,0:T(8,128)S(1)}, f32[32,128]{1,0:T(8,128)S(1)}, u32[]{:S(2)}, u32[]{:S(2)}) collective-permute-start(f32[32,128]{1,0:T(8,128)S(1)} %get-tuple-element.20.lists), channel_id=1, source_target_pairs={{0,1},{1,0},{2,3},{3,2},{4,5},{5,4},{6,7},{7,6},{8,9},{9,8},{10,11... | collective-permute-start | bytes 49160 | tf_op jit(solution)/shard_map/ppermute | solution.py:501
  10.7 0.6 %shard_map.65.refs_0_ = f32[8,64,128]{2,1,0:T(8,128)S(1)} custom-call(f32[32,128]{1,0:T(8,128)S(1)} %get-tuple-element.20.lists), custom_call_target="tpu_custom_call" | custom-call | flops 100000000 | bytes 16384 | tf_op jit(solution)/shard_map/pallas_call | solution.py:460
  11.3 1.4 %collective-permute-done.lists = f32[32,128]{1,0:T(8,128)S(1)} collective-permute-done((f32[32,128]{1,0:T(8,128)S(1)}, f32[32,128]{1,0:T(8,128)S(1)}, u32[]{:S(2)}, u32[]{:S(2)}) %collective-permute-start) | collective-permute-done | bytes 16416 | tf_op jit(solution)/shard_map/ppermute | solution.py:501
  12.7 0.6 %shard_map.66.refs_1_ = f32[8,64,128]{2,1,0:T(8,128)S(1)} custom-call(f32[32,128]{1,0:T(8,128)S(1)} %collective-permute-done.lists), custom_call_target="tpu_custom_call" | custom-call | flops 100000000 | bytes 16384 | tf_op jit(solution)/shard_map/pallas_call | solution.py:460
  13.2 5.0 %all-to-all-done = f32[32,11,1,128]{3,2,1,0:T(1,128)S(1)} async-done(((f32[32,11,1,128]{3,2,1,0:T(1,128)}), f32[32,11,1,128]{3,2,1,0:T(1,128)S(1)}, u32[]{:S(2)}, u32[]{:S(2)}) %all-to-all-start) | async-done | bytes 180256 | tf_op jit(solution)/shard_map/all_to_all | solution.py:39
  18.3 1.6 %shard_map.67 = (bf16[2048,512]{1,0:T(8,128)(2,1)S(1)}, f32[16,4,128]{2,1,0:T(4,128)S(1)}, f32[16,3,8,128]{3,2,1,0:T(8,128)S(1)}, f32[2,8,128]{2,1,0:T(8,128)S(1)}, f32[288,128]{1,0:T(8,128)S(1)}) custom-call(f32[352,128]{1,0:T(8,128)S(1)} %bitcast.14, f32[8,64,128]{2,1,0:T(8,128)S(1)} %shard_map.65.refs_0_, f32[8,64,128]{2,1,0:T(8,128)S(1)} %shard_map.66.refs_1_, ...), custom_call_target="tpu_custom_call" | custom-call | bytes 708608 | tf_op jit(solution)/shard_map/pallas_call | solution.py:460
  19.8 10.6 %all_to_all.20 = f32[32,9,1,128]{3,2,1,0:T(1,128)S(1)} all-to-all(f32[32,9,1,128]{3,2,1,0:T(1,128)S(1)} %bitcast.17), channel_id=1, replica_groups=mesh['top'=4,'mid'=2,'core'=2,'col'=2] {'top','mid','core','col'}, dimensions={0} | all-to-all | bytes 294912 | tf_op jit(solution)/shard_map/all_to_all | solution.py:39
  30.4 0.9 %shard_map.68 = (f32[16,3,8,128]{3,2,1,0:T(8,128)S(1)}, f32[3,8,128]{2,1,0:T(8,128)S(1)}, f32[288,128]{1,0:T(8,128)S(1)}) custom-call(f32[288,128]{1,0:T(8,128)S(1)} %bitcast.15, f32[16,3,8,128]{3,2,1,0:T(8,128)S(1)} %get-tuple-element.23.refs_0_, f32[2,8,128]{2,1,0:T(8,128)S(1)} %get-tuple-element.24.refs_1_.refs_2_, ...), custom_call_target="tpu_custom_call" | custom-call | bytes 2486272 | tf_op jit(solution)/shard_map/pallas_call | solution.py:460
  31.4 10.6 %all_to_all.21 = f32[32,9,1,128]{3,2,1,0:T(1,128)S(1)} all-to-all(f32[32,9,1,128]{3,2,1,0:T(1,128)S(1)} %bitcast.18), channel_id=1, replica_groups=mesh['top'=4,'mid'=2,'core'=2,'col'=2] {'top','mid','core','col'}, dimensions={0} | all-to-all | bytes 294912 | tf_op jit(solution)/shard_map/all_to_all | solution.py:39
  41.9 1.0 %shard_map.69 = (f32[3,3,8,128]{3,2,1,0:T(8,128)S(1)}, f32[13,8,128]{2,1,0:T(8,128)S(1)}, f32[32,128]{1,0:T(8,128)S(1)}) custom-call(f32[288,128]{1,0:T(8,128)S(1)} %bitcast.16, f32[16,3,8,128]{3,2,1,0:T(8,128)S(1)} %get-tuple-element.23.refs_0_, f32[16,3,8,128]{3,2,1,0:T(8,128)S(1)} %get-tuple-element.28.refs_1_, ...), custom_call_target="tpu_custom_call" | custom-call | bytes 2695168 | tf_op jit(solution)/shard_map/pallas_call | solution.py:460
  42.9 8.9 %all_to_all.22 = f32[32,1,1,128]{3,2,1,0:T(1,128)S(1)} all-to-all(f32[32,1,1,128]{3,2,1,0:T(1,128)S(1)} %bitcast.20), channel_id=1, replica_groups=mesh['top'=4,'mid'=2,'core'=2,'col'=2] {'top','mid','core','col'}, dimensions={0} | all-to-all | bytes 32768 | tf_op jit(solution)/shard_map/all_to_all | solution.py:39
  51.8 0.7 %shard_map.70 = f32[6,3,64]{2,1,0:T(4,128)} custom-call(f32[32,128]{1,0:T(8,128)S(1)} %bitcast.19, f32[3,3,8,128]{3,2,1,0:T(8,128)S(1)} %get-tuple-element.31.own, f32[13,8,128]{2,1,0:T(8,128)S(1)} %get-tuple-element.32.held), custom_call_target="tpu_custom_call" | custom-call | bytes 106496 | tf_op jit(solution)/shard_map/pallas_call | solution.py:460
Async XLA Ops:
  1.5 16.7 %all-to-all-start = ((f32[32,11,1,128]{3,2,1,0:T(1,128)}), f32[32,11,1,128]{3,2,1,0:T(1,128)S(1)}, u32[]{:S(2)}, u32[]{:S(2)}) async-start(f32[32,11,1,128]{3,2,1,0:T(1,128)} %bitcast.4), calls=%async_computation | async-start | bytes 360448 | tf_op jit(solution)/shard_map/all_to_all | solution.py:39
  8.9 3.8 %collective-permute-start = (f32[32,128]{1,0:T(8,128)S(1)}, f32[32,128]{1,0:T(8,128)S(1)}, u32[]{:S(2)}, u32[]{:S(2)}) collective-permute-start(f32[32,128]{1,0:T(8,128)S(1)} %get-tuple-element.20.lists), channel_id=1, source_target_pairs={{0,1},{1,0},{2,3},{3,2},{4,5},{5,4},{6,7},{7,6},{8,9},{9,8},{10,11... | collective-permute-start | bytes 49160 | tf_op jit(solution)/shard_map/ppermute | solution.py:501

commit v18 on v17

--- a/solution.py
+++ b/solution.py
@@ -174,19 +174,14 @@
     ]
     for copy in copies:
         copy.start()
-    for copy in copies[:4]:
+    for copy in copies[:3]:
         copy.wait()
     velocity, points, area, self_term, index, weight = held
     count = index.shape[0]
-    field = velocity[...]
+    rows = [
+        jnp.concatenate([velocity[:HALF, a, :], velocity[HALF:, a, :]], axis=1) for a in range(3)
+    ]
     spot = points[...]
-    rows = []
-    for a in range(3):
-        vec = field[:, a, :]
-        rows.append(jnp.concatenate([vec[:HALF], vec[HALF:]], axis=1))
-    mine = jnp.concatenate([spot, self_term[...]], axis=0)
-    mine = jnp.concatenate([mine, mine], axis=1)
-    tgt[...] = jnp.concatenate([mine, mine], axis=0)
     left = jnp.concatenate([spot[0:1], spot[2:3]], axis=0)
     right = jnp.concatenate([spot[1:2], area[...]], axis=0)
     rows.append(jnp.concatenate([left, right], axis=1))
@@ -199,8 +194,11 @@
     ]
     for copy in leaving:
         copy.start()
-    for copy in copies[4:]:
+    for copy in copies[3:]:
         copy.wait()
+    mine = jnp.concatenate([spot, self_term[...]], axis=0)
+    mine = jnp.concatenate([mine, mine], axis=1)
+    tgt[...] = jnp.concatenate([mine, mine], axis=0)
     lists[:count] = index[...].astype(F32)
     lists[count:] = weight[...]
     for copy in leaving:

time: 52.9 us -> 52.9 us (level)
  no operation moved by 1% of the time
where the time goes in v18:
time: 52.9 us; the launch traced here: 52.5 us
  blocking collectives  30.1 us (57%)
  starting transfers between devices  9.14 us (17%)
  Pallas kernels  6.88 us (13%)
  waiting for transfers between devices  6.42 us (12%)
    all_to_all x3, blocking collectives, spread(): return lax.all_to_all(wide, AXES, 0, 0, tiled=True).reshape(rows.shape)  30.1 us
    all_to_all x1, starting transfers between devices, spread(): return lax.all_to_all(wide, AXES, 0, 0, tiled=True).reshape(rows.shape)  7.3 us
    pallas_call x7, Pallas kernels, call(): pl.pallas_call(kernel, out_shape=[jax.ShapeDtypeStruct(s, t) for s, t in...  6.88 us
    all_to_all x1, waiting for transfers between devices, spread(): return lax.all_to_all(wide, AXES, 0, 0, tiled=True).reshape(rows.shape)  5 us
    ppermute x1, starting transfers between devices, body(): lax.ppermute(lists, 'col', xor_perm(n_col, o))  1.83 us
    ppermute x1, waiting for transfers between devices, body(): lax.ppermute(lists, 'col', xor_perm(n_col, o))  1.42 us
  transfers between devices with their start and end apart: 2, of which 2 were waited for; matrix products, arithmetic and copies ran while one was open for 0% of the time, Pallas kernels for 2%

profile of v18, /device:TPU:0, one launch (start us, length us, event | category | flops | bytes accessed | tf_op | source)
XLA Modules:
  0.0 52.5 jit_solution(11429392463453067985)
XLA Ops:
  0.0 1.5 %shard_map.64 = (f32[352,128]{1,0:T(8,128)}, f32[8,128]{1,0:T(8,128)S(1)}, f32[32,128]{1,0:T(8,128)S(1)}) custom-call(f32[6,3,64]{2,1,0:T(4,128)} %refs_0_.1, f32[3,64]{1,0:T(4,128)} %refs_1_.1, f32[1,64]{1,0:T(1,128)} %bitcast.23, f32[1,64]{1,0:T(1,128)} %bitcast.24, s32[16,128]{1,0:T(8,128)} %bitcast.21, f32[16,128]{1,0:T(8,128)} %bitcast.22), custom_call_target="tpu_custom_call" | custom-call | bytes 22272 | tf_op jit(solution)/shard_map/pallas_call | solution.py:458
  1.5 7.3 %all-to-all-start = ((f32[32,11,1,128]{3,2,1,0:T(1,128)}), f32[32,11,1,128]{3,2,1,0:T(1,128)S(1)}, u32[]{:S(2)}, u32[]{:S(2)}) async-start(f32[32,11,1,128]{3,2,1,0:T(1,128)} %bitcast.4), calls=%async_computation | async-start | bytes 360448 | tf_op jit(solution)/shard_map/all_to_all | solution.py:39
  8.9 1.8 %collective-permute-start = (f32[32,128]{1,0:T(8,128)S(1)}, f32[32,128]{1,0:T(8,128)S(1)}, u32[]{:S(2)}, u32[]{:S(2)}) collective-permute-start(f32[32,128]{1,0:T(8,128)S(1)} %get-tuple-element.20.lists), channel_id=1, source_target_pairs={{0,1},{1,0},{2,3},{3,2},{4,5},{5,4},{6,7},{7,6},{8,9},{9,8},{10,11... | collective-permute-start | bytes 49160 | tf_op jit(solution)/shard_map/ppermute | solution.py:499
  10.7 0.6 %shard_map.65.refs_0_ = f32[8,64,128]{2,1,0:T(8,128)S(1)} custom-call(f32[32,128]{1,0:T(8,128)S(1)} %get-tuple-element.20.lists), custom_call_target="tpu_custom_call" | custom-call | flops 100000000 | bytes 16384 | tf_op jit(solution)/shard_map/pallas_call | solution.py:458
  11.3 1.4 %collective-permute-done.lists = f32[32,128]{1,0:T(8,128)S(1)} collective-permute-done((f32[32,128]{1,0:T(8,128)S(1)}, f32[32,128]{1,0:T(8,128)S(1)}, u32[]{:S(2)}, u32[]{:S(2)}) %collective-permute-start) | collective-permute-done | bytes 16416 | tf_op jit(solution)/shard_map/ppermute | solution.py:499
  12.7 0.6 %shard_map.66.refs_1_ = f32[8,64,128]{2,1,0:T(8,128)S(1)} custom-call(f32[32,128]{1,0:T(8,128)S(1)} %collective-permute-done.lists), custom_call_target="tpu_custom_call" | custom-call | flops 100000000 | bytes 16384 | tf_op jit(solution)/shard_map/pallas_call | solution.py:458
  13.2 5.0 %all-to-all-done = f32[32,11,1,128]{3,2,1,0:T(1,128)S(1)} async-done(((f32[32,11,1,128]{3,2,1,0:T(1,128)}), f32[32,11,1,128]{3,2,1,0:T(1,128)S(1)}, u32[]{:S(2)}, u32[]{:S(2)}) %all-to-all-start) | async-done | bytes 180256 | tf_op jit(solution)/shard_map/all_to_all | solution.py:39
  18.3 1.6 %shard_map.67 = (bf16[2048,512]{1,0:T(8,128)(2,1)S(1)}, f32[16,4,128]{2,1,0:T(4,128)S(1)}, f32[16,3,8,128]{3,2,1,0:T(8,128)S(1)}, f32[2,8,128]{2,1,0:T(8,128)S(1)}, f32[288,128]{1,0:T(8,128)S(1)}) custom-call(f32[352,128]{1,0:T(8,128)S(1)} %bitcast.14, f32[8,64,128]{2,1,0:T(8,128)S(1)} %shard_map.65.refs_0_, f32[8,64,128]{2,1,0:T(8,128)S(1)} %shard_map.66.refs_1_, ...), custom_call_target="tpu_custom_call" | custom-call | bytes 708608 | tf_op jit(solution)/shard_map/pallas_call | solution.py:458
  19.8 10.6 %all_to_all.20 = f32[32,9,1,128]{3,2,1,0:T(1,128)S(1)} all-to-all(f32[32,9,1,128]{3,2,1,0:T(1,128)S(1)} %bitcast.17), channel_id=1, replica_groups=mesh['top'=4,'mid'=2,'core'=2,'col'=2] {'top','mid','core','col'}, dimensions={0} | all-to-all | bytes 294912 | tf_op jit(solution)/shard_map/all_to_all | solution.py:39
  30.4 0.9 %shard_map.68 = (f32[16,3,8,128]{3,2,1,0:T(8,128)S(1)}, f32[3,8,128]{2,1,0:T(8,128)S(1)}, f32[288,128]{1,0:T(8,128)S(1)}) custom-call(f32[288,128]{1,0:T(8,128)S(1)} %bitcast.15, f32[16,3,8,128]{3,2,1,0:T(8,128)S(1)} %get-tuple-element.23.refs_0_, f32[2,8,128]{2,1,0:T(8,128)S(1)} %get-tuple-element.24.refs_1_.refs_2_, ...), custom_call_target="tpu_custom_call" | custom-call | bytes 2486272 | tf_op jit(solution)/shard_map/pallas_call | solution.py:458
  31.4 10.6 %all_to_all.21 = f32[32,9,1,128]{3,2,1,0:T(1,128)S(1)} all-to-all(f32[32,9,1,128]{3,2,1,0:T(1,128)S(1)} %bitcast.18), channel_id=1, replica_groups=mesh['top'=4,'mid'=2,'core'=2,'col'=2] {'top','mid','core','col'}, dimensions={0} | all-to-all | bytes 294912 | tf_op jit(solution)/shard_map/all_to_all | solution.py:39
  41.9 1.0 %shard_map.69 = (f32[3,3,8,128]{3,2,1,0:T(8,128)S(1)}, f32[13,8,128]{2,1,0:T(8,128)S(1)}, f32[32,128]{1,0:T(8,128)S(1)}) custom-call(f32[288,128]{1,0:T(8,128)S(1)} %bitcast.16, f32[16,3,8,128]{3,2,1,0:T(8,128)S(1)} %get-tuple-element.23.refs_0_, f32[16,3,8,128]{3,2,1,0:T(8,128)S(1)} %get-tuple-element.28.refs_1_, ...), custom_call_target="tpu_custom_call" | custom-call | bytes 2695168 | tf_op jit(solution)/shard_map/pallas_call | solution.py:458
  42.9 8.9 %all_to_all.22 = f32[32,1,1,128]{3,2,1,0:T(1,128)S(1)} all-to-all(f32[32,1,1,128]{3,2,1,0:T(1,128)S(1)} %bitcast.20), channel_id=1, replica_groups=mesh['top'=4,'mid'=2,'core'=2,'col'=2] {'top','mid','core','col'}, dimensions={0} | all-to-all | bytes 32768 | tf_op jit(solution)/shard_map/all_to_all | solution.py:39
  51.8 0.7 %shard_map.70 = f32[6,3,64]{2,1,0:T(4,128)} custom-call(f32[32,128]{1,0:T(8,128)S(1)} %bitcast.19, f32[3,3,8,128]{3,2,1,0:T(8,128)S(1)} %get-tuple-element.31.own, f32[13,8,128]{2,1,0:T(8,128)S(1)} %get-tuple-element.32.held), custom_call_target="tpu_custom_call" | custom-call | bytes 106496 | tf_op jit(solution)/shard_map/pallas_call | solution.py:458
Async XLA Ops:
  1.5 16.7 %all-to-all-start = ((f32[32,11,1,128]{3,2,1,0:T(1,128)}), f32[32,11,1,128]{3,2,1,0:T(1,128)S(1)}, u32[]{:S(2)}, u32[]{:S(2)}) async-start(f32[32,11,1,128]{3,2,1,0:T(1,128)} %bitcast.4), calls=%async_computation | async-start | bytes 360448 | tf_op jit(solution)/shard_map/all_to_all | solution.py:39
  8.9 3.8 %collective-permute-start = (f32[32,128]{1,0:T(8,128)S(1)}, f32[32,128]{1,0:T(8,128)S(1)}, u32[]{:S(2)}, u32[]{:S(2)}) collective-permute-start(f32[32,128]{1,0:T(8,128)S(1)} %get-tuple-element.20.lists), channel_id=1, source_target_pairs={{0,1},{1,0},{2,3},{3,2},{4,5},{5,4},{6,7},{7,6},{8,9},{9,8},{10,11... | collective-permute-start | bytes 49160 | tf_op jit(solution)/shard_map/ppermute | solution.py:499

commit v19 on v18

--- a/solution.py
+++ b/solution.py
@@ -115,8 +115,9 @@
 
 
 def contract(cols, kernels):
-    prod = jnp.dot(cols, kernels, preferred_element_type=F32)
-    return prod[:32, :256] + (prod[32:, :256] + prod[:32, 256:])
+    first = jnp.dot(cols, kernels[:, :256], preferred_element_type=F32)
+    second = jnp.dot(cols[:32], kernels[:, 256:], preferred_element_type=F32)
+    return first[:32] + (first[32:] + second)
 
 
 def products(n_chunk, columns, cols, kernels):

time: 52.9 us -> 52.9 us (level)
  no operation moved by 1% of the time
where the time goes in v19:
time: 52.9 us; the launch traced here: 52.5 us
  blocking collectives  30.1 us (57%)
  starting transfers between devices  9.14 us (17%)
  Pallas kernels  6.86 us (13%)
  waiting for transfers between devices  6.42 us (12%)
    all_to_all x3, blocking collectives, spread(): return lax.all_to_all(wide, AXES, 0, 0, tiled=True).reshape(rows.shape)  30.1 us
    all_to_all x1, starting transfers between devices, spread(): return lax.all_to_all(wide, AXES, 0, 0, tiled=True).reshape(rows.shape)  7.3 us
    pallas_call x7, Pallas kernels, call(): pl.pallas_call(kernel, out_shape=[jax.ShapeDtypeStruct(s, t) for s, t in...  6.86 us
    all_to_all x1, waiting for transfers between devices, spread(): return lax.all_to_all(wide, AXES, 0, 0, tiled=True).reshape(rows.shape)  5 us
    ppermute x1, starting transfers between devices, body(): lax.ppermute(lists, 'col', xor_perm(n_col, o))  1.83 us
    ppermute x1, waiting for transfers between devices, body(): lax.ppermute(lists, 'col', xor_perm(n_col, o))  1.42 us
  transfers between devices with their start and end apart: 2, of which 2 were waited for; matrix products, arithmetic and copies ran while one was open for 0% of the time, Pallas kernels for 2%

profile of v19, /device:TPU:0, one launch (start us, length us, event | category | flops | bytes accessed | tf_op | source)
XLA Modules:
  0.0 52.5 jit_solution(692011945468273994)
XLA Ops:
  0.0 1.5 %shard_map.64 = (f32[352,128]{1,0:T(8,128)}, f32[8,128]{1,0:T(8,128)S(1)}, f32[32,128]{1,0:T(8,128)S(1)}) custom-call(f32[6,3,64]{2,1,0:T(4,128)} %refs_0_.1, f32[3,64]{1,0:T(4,128)} %refs_1_.1, f32[1,64]{1,0:T(1,128)} %bitcast.23, f32[1,64]{1,0:T(1,128)} %bitcast.24, s32[16,128]{1,0:T(8,128)} %bitcast.21, f32[16,128]{1,0:T(8,128)} %bitcast.22), custom_call_target="tpu_custom_call" | custom-call | bytes 22272 | tf_op jit(solution)/shard_map/pallas_call | solution.py:459
  1.5 7.3 %all-to-all-start = ((f32[32,11,1,128]{3,2,1,0:T(1,128)}), f32[32,11,1,128]{3,2,1,0:T(1,128)S(1)}, u32[]{:S(2)}, u32[]{:S(2)}) async-start(f32[32,11,1,128]{3,2,1,0:T(1,128)} %bitcast.4), calls=%async_computation | async-start | bytes 360448 | tf_op jit(solution)/shard_map/all_to_all | solution.py:39
  8.9 1.8 %collective-permute-start = (f32[32,128]{1,0:T(8,128)S(1)}, f32[32,128]{1,0:T(8,128)S(1)}, u32[]{:S(2)}, u32[]{:S(2)}) collective-permute-start(f32[32,128]{1,0:T(8,128)S(1)} %get-tuple-element.20.lists), channel_id=1, source_target_pairs={{0,1},{1,0},{2,3},{3,2},{4,5},{5,4},{6,7},{7,6},{8,9},{9,8},{10,11... | collective-permute-start | bytes 49160 | tf_op jit(solution)/shard_map/ppermute | solution.py:500
  10.7 0.6 %shard_map.65.refs_0_ = f32[8,64,128]{2,1,0:T(8,128)S(1)} custom-call(f32[32,128]{1,0:T(8,128)S(1)} %get-tuple-element.20.lists), custom_call_target="tpu_custom_call" | custom-call | flops 100000000 | bytes 16384 | tf_op jit(solution)/shard_map/pallas_call | solution.py:459
  11.3 1.4 %collective-permute-done.lists = f32[32,128]{1,0:T(8,128)S(1)} collective-permute-done((f32[32,128]{1,0:T(8,128)S(1)}, f32[32,128]{1,0:T(8,128)S(1)}, u32[]{:S(2)}, u32[]{:S(2)}) %collective-permute-start) | collective-permute-done | bytes 16416 | tf_op jit(solution)/shard_map/ppermute | solution.py:500
  12.7 0.6 %shard_map.66.refs_1_ = f32[8,64,128]{2,1,0:T(8,128)S(1)} custom-call(f32[32,128]{1,0:T(8,128)S(1)} %collective-permute-done.lists), custom_call_target="tpu_custom_call" | custom-call | flops 100000000 | bytes 16384 | tf_op jit(solution)/shard_map/pallas_call | solution.py:459
  13.2 5.0 %all-to-all-done = f32[32,11,1,128]{3,2,1,0:T(1,128)S(1)} async-done(((f32[32,11,1,128]{3,2,1,0:T(1,128)}), f32[32,11,1,128]{3,2,1,0:T(1,128)S(1)}, u32[]{:S(2)}, u32[]{:S(2)}) %all-to-all-start) | async-done | bytes 180256 | tf_op jit(solution)/shard_map/all_to_all | solution.py:39
  18.3 1.6 %shard_map.67 = (bf16[2048,512]{1,0:T(8,128)(2,1)S(1)}, f32[16,4,128]{2,1,0:T(4,128)S(1)}, f32[16,3,8,128]{3,2,1,0:T(8,128)S(1)}, f32[2,8,128]{2,1,0:T(8,128)S(1)}, f32[288,128]{1,0:T(8,128)S(1)}) custom-call(f32[352,128]{1,0:T(8,128)S(1)} %bitcast.14, f32[8,64,128]{2,1,0:T(8,128)S(1)} %shard_map.65.refs_0_, f32[8,64,128]{2,1,0:T(8,128)S(1)} %shard_map.66.refs_1_, ...), custom_call_target="tpu_custom_call" | custom-call | bytes 708608 | tf_op jit(solution)/shard_map/pallas_call | solution.py:459
  19.8 10.6 %all_to_all.20 = f32[32,9,1,128]{3,2,1,0:T(1,128)S(1)} all-to-all(f32[32,9,1,128]{3,2,1,0:T(1,128)S(1)} %bitcast.17), channel_id=1, replica_groups=mesh['top'=4,'mid'=2,'core'=2,'col'=2] {'top','mid','core','col'}, dimensions={0} | all-to-all | bytes 294912 | tf_op jit(solution)/shard_map/all_to_all | solution.py:39
  30.4 0.9 %shard_map.68 = (f32[16,3,8,128]{3,2,1,0:T(8,128)S(1)}, f32[3,8,128]{2,1,0:T(8,128)S(1)}, f32[288,128]{1,0:T(8,128)S(1)}) custom-call(f32[288,128]{1,0:T(8,128)S(1)} %bitcast.15, f32[16,3,8,128]{3,2,1,0:T(8,128)S(1)} %get-tuple-element.23.refs_0_, f32[2,8,128]{2,1,0:T(8,128)S(1)} %get-tuple-element.24.refs_1_.refs_2_, ...), custom_call_target="tpu_custom_call" | custom-call | bytes 2486272 | tf_op jit(solution)/shard_map/pallas_call | solution.py:459
  31.3 10.6 %all_to_all.21 = f32[32,9,1,128]{3,2,1,0:T(1,128)S(1)} all-to-all(f32[32,9,1,128]{3,2,1,0:T(1,128)S(1)} %bitcast.18), channel_id=1, replica_groups=mesh['top'=4,'mid'=2,'core'=2,'col'=2] {'top','mid','core','col'}, dimensions={0} | all-to-all | bytes 294912 | tf_op jit(solution)/shard_map/all_to_all | solution.py:39
  41.9 1.0 %shard_map.69 = (f32[3,3,8,128]{3,2,1,0:T(8,128)S(1)}, f32[13,8,128]{2,1,0:T(8,128)S(1)}, f32[32,128]{1,0:T(8,128)S(1)}) custom-call(f32[288,128]{1,0:T(8,128)S(1)} %bitcast.16, f32[16,3,8,128]{3,2,1,0:T(8,128)S(1)} %get-tuple-element.23.refs_0_, f32[16,3,8,128]{3,2,1,0:T(8,128)S(1)} %get-tuple-element.28.refs_1_, ...), custom_call_target="tpu_custom_call" | custom-call | bytes 2695168 | tf_op jit(solution)/shard_map/pallas_call | solution.py:459
  42.9 8.9 %all_to_all.22 = f32[32,1,1,128]{3,2,1,0:T(1,128)S(1)} all-to-all(f32[32,1,1,128]{3,2,1,0:T(1,128)S(1)} %bitcast.20), channel_id=1, replica_groups=mesh['top'=4,'mid'=2,'core'=2,'col'=2] {'top','mid','core','col'}, dimensions={0} | all-to-all | bytes 32768 | tf_op jit(solution)/shard_map/all_to_all | solution.py:39
  51.8 0.7 %shard_map.70 = f32[6,3,64]{2,1,0:T(4,128)} custom-call(f32[32,128]{1,0:T(8,128)S(1)} %bitcast.19, f32[3,3,8,128]{3,2,1,0:T(8,128)S(1)} %get-tuple-element.31.own, f32[13,8,128]{2,1,0:T(8,128)S(1)} %get-tuple-element.32.held), custom_call_target="tpu_custom_call" | custom-call | bytes 106496 | tf_op jit(solution)/shard_map/pallas_call | solution.py:459
Async XLA Ops:
  1.5 16.7 %all-to-all-start = ((f32[32,11,1,128]{3,2,1,0:T(1,128)}), f32[32,11,1,128]{3,2,1,0:T(1,128)S(1)}, u32[]{:S(2)}, u32[]{:S(2)}) async-start(f32[32,11,1,128]{3,2,1,0:T(1,128)} %bitcast.4), calls=%async_computation | async-start | bytes 360448 | tf_op jit(solution)/shard_map/all_to_all | solution.py:39
  8.9 3.8 %collective-permute-start = (f32[32,128]{1,0:T(8,128)S(1)}, f32[32,128]{1,0:T(8,128)S(1)}, u32[]{:S(2)}, u32[]{:S(2)}) collective-permute-start(f32[32,128]{1,0:T(8,128)S(1)} %get-tuple-element.20.lists), channel_id=1, source_target_pairs={{0,1},{1,0},{2,3},{3,2},{4,5},{5,4},{6,7},{7,6},{8,9},{9,8},{10,11... | collective-permute-start | bytes 49160 | tf_op jit(solution)/shard_map/ppermute | solution.py:500

commit v20 on v19

--- a/solution.py
+++ b/solution.py
@@ -238,7 +238,7 @@
 def first_kernel(sizes, piece, *refs):
     n_row, n_col = sizes[0] * sizes[1] * sizes[2], sizes[3]
     extra = refs[:n_col]
-    tgt, kernels, places, basis, norm_out, out, cols, *sums = refs[n_col:]
+    tgt, kernels, places, basis, mine, norm_out, out, cols, *sums = refs[n_col:]
     half = n_row // 2
     n_chunk = n_row * n_col // 2
     me, _, _ = position(sizes)
@@ -286,16 +286,19 @@
     scale = 1.0 / norm
     norm_out[0] = norm
     norm_out[1] = scale
-    write_piece(image_rows(prod, tgt, basis[0], scale), out)
+    images = image_rows(prod, tgt, basis[0], scale)
+    for a in range(3):
+        mine[a] = images[a]
+    write_piece(images, out)
 
 
 def middle_kernel(sizes, n_base, final, piece, *refs):
     n_row, n_col = sizes[0] * sizes[1] * sizes[2], sizes[3]
-    bases, norms = refs[:n_base], refs[n_base : 2 * n_base]
+    bases, norms, before = (refs[i * n_base : (i + 1) * n_base] for i in range(3))
     if final:
-        kernels, places, tgt, own, h_out, out, basis, cols, *held = refs[2 * n_base :]
+        kernels, places, tgt, own, h_out, out, basis, cols, *held = refs[3 * n_base :]
     else:
-        kernels, places, tgt, basis, h_out, out, cols, *held = refs[2 * n_base :]
+        kernels, places, tgt, basis, mine, h_out, out, cols, *held = refs[3 * n_base :]
     n_chunk = n_row * n_col // 2
     me, _, _ = position(sizes)
     scales = [norm[norm.shape[0] - 1] for norm in norms]
@@ -310,12 +313,14 @@
         old = [[base[chunk, a] for a in range(3)] for base in bases]
         for a in range(3):
             basis[chunk, a] = vec[a]
+        write_columns(cols, places[chunk], chunk, vec)
         for j in range(n_base):
             sums.add(chunk, j, vec, old[j])
         for at, (i, j) in enumerate(cross):
             sums.add(chunk, 2 * n_base + 1 + at, old[i], old[j])
 
-    each(n_chunk, unpack)
+    prod = products(n_chunk, unpack, cols, kernels)
+    raw = image_rows(prod, tgt, basis[0], 1.0)
     gram = {}
     for at, (i, j) in enumerate(cross):
         gram[j, i] = sums.get(2 * n_base + 1 + at) * (scales[i] * scales[j])
@@ -339,16 +344,20 @@
             vec.append(value)
             basis[chunk, a] = value
         sums.add(chunk, n_base, vec, vec)
-        write_columns(cols, places[chunk], chunk, vec)
         if final:
             for j in range(n_base):
                 sums.add(chunk, n_base + 1 + j, vec, old[j])
 
-    prod = products(n_chunk, columns, cols, kernels)
+    each(n_chunk, columns)
     norm = jnp.sqrt(sums.get(n_base))
     scale = 1.0 / norm
-    images = image_rows(prod, tgt, basis[0], scale)
+    images = [
+        (raw[a] - sum(column[j] * before[j][a] for j in range(n_base))) * scale
+        for a in range(3)
+    ]
     if not final:
+        for a in range(3):
+            mine[a] = images[a]
         h_out[n_base] = norm
         h_out[n_base + 1] = scale
         write_piece(images, out)
@@ -512,12 +521,13 @@
     vec_shape = (n_chunk, 3, ROWS, 128)
     cols = pltpu.VMEM((64, total), BF16)
     held = [] if n_chunk <= 16 else [pltpu.VMEM((8, ROWS, 128), F32)]
-    kernels, places, basis, norm, wide = call(
+    kernels, places, basis, image, norm, wide = call(
         functools.partial(first_kernel, sizes),
         [
             ((total, 512), BF16),
             ((n_chunk, 4, 128), F32),
             (vec_shape, F32),
+            ((3, ROWS, 128), F32),
             ((2, ROWS, 128), F32),
             message,
         ],
@@ -526,21 +536,24 @@
     )
     bases = [basis]
     columns = [norm]
+    images = [image]
     for k in range(1, ITERS):
         final = k == ITERS - 1
         piece = spread(wide, n)
-        main, column, wide = call(
+        main, *image, column, wide = call(
             functools.partial(middle_kernel, sizes, k, final),
             [
                 ((ITERS, 3, ROWS, 128) if final else vec_shape, F32),
+                *([] if final else [((3, ROWS, 128), F32)]),
                 ((KNOWN + len(PAIRS) if final else k + 2, ROWS, 128), F32),
                 ((n, 128), F32) if final else message,
             ],
             [*([pltpu.VMEM(vec_shape, F32)] if final else []), cols, *held],
-            [piece, *bases, *columns, kernels, places, tgt],
+            [piece, *bases, *columns, *images, kernels, places, tgt],
         )
         bases.append(main)
         columns.append(column)
+        images += image
     sums = spread(wide, n)
     (density,) = call(
         last_kernel, [((rhs, 3, 64), F32)], [], [sums, bases[-1], columns[-1]]

time: 52.9 us -> 52.5 us (level)
  no operation moved by 1% of the time
where the time goes in v20:
time: 52.5 us; the launch traced here: 52.1 us
  blocking collectives  30.1 us (57%)
  starting transfers between devices  9.14 us (17%)
  Pallas kernels  6.47 us (12%)
  waiting for transfers between devices  6.42 us (12%)
    all_to_all x3, blocking collectives, spread(): return lax.all_to_all(wide, AXES, 0, 0, tiled=True).reshape(rows.shape)  30.1 us
    all_to_all x1, starting transfers between devices, spread(): return lax.all_to_all(wide, AXES, 0, 0, tiled=True).reshape(rows.shape)  7.3 us
    pallas_call x7, Pallas kernels, call(): pl.pallas_call(kernel, out_shape=[jax.ShapeDtypeStruct(s, t) for s, t in...  6.47 us
    all_to_all x1, waiting for transfers between devices, spread(): return lax.all_to_all(wide, AXES, 0, 0, tiled=True).reshape(rows.shape)  5 us
    ppermute x1, starting transfers between devices, body(): lax.ppermute(lists, 'col', xor_perm(n_col, o))  1.83 us
    ppermute x1, waiting for transfers between devices, body(): lax.ppermute(lists, 'col', xor_perm(n_col, o))  1.42 us
  transfers between devices with their start and end apart: 2, of which 2 were waited for; matrix products, arithmetic and copies ran while one was open for 0% of the time, Pallas kernels for 2%

profile of v20, /device:TPU:0, one launch (start us, length us, event | category | flops | bytes accessed | tf_op | source)
XLA Modules:
  0.0 52.1 jit_solution(6758371903669353163)
XLA Ops:
  0.0 1.5 %shard_map.64 = (f32[352,128]{1,0:T(8,128)}, f32[8,128]{1,0:T(8,128)S(1)}, f32[32,128]{1,0:T(8,128)S(1)}) custom-call(f32[6,3,64]{2,1,0:T(4,128)} %refs_0_.1, f32[3,64]{1,0:T(4,128)} %refs_1_.1, f32[1,64]{1,0:T(1,128)} %bitcast.23, f32[1,64]{1,0:T(1,128)} %bitcast.24, s32[16,128]{1,0:T(8,128)} %bitcast.21, f32[16,128]{1,0:T(8,128)} %bitcast.22), custom_call_target="tpu_custom_call" | custom-call | bytes 22272 | tf_op jit(solution)/shard_map/pallas_call | solution.py:468
  1.5 7.3 %all-to-all-start = ((f32[32,11,1,128]{3,2,1,0:T(1,128)}), f32[32,11,1,128]{3,2,1,0:T(1,128)S(1)}, u32[]{:S(2)}, u32[]{:S(2)}) async-start(f32[32,11,1,128]{3,2,1,0:T(1,128)} %bitcast.4), calls=%async_computation | async-start | bytes 360448 | tf_op jit(solution)/shard_map/all_to_all | solution.py:39
  8.9 1.8 %collective-permute-start = (f32[32,128]{1,0:T(8,128)S(1)}, f32[32,128]{1,0:T(8,128)S(1)}, u32[]{:S(2)}, u32[]{:S(2)}) collective-permute-start(f32[32,128]{1,0:T(8,128)S(1)} %get-tuple-element.22.lists), channel_id=1, source_target_pairs={{0,1},{1,0},{2,3},{3,2},{4,5},{5,4},{6,7},{7,6},{8,9},{9,8},{10,11... | collective-permute-start | bytes 49160 | tf_op jit(solution)/shard_map/ppermute | solution.py:509
  10.7 0.6 %shard_map.65.refs_0_ = f32[8,64,128]{2,1,0:T(8,128)S(1)} custom-call(f32[32,128]{1,0:T(8,128)S(1)} %get-tuple-element.22.lists), custom_call_target="tpu_custom_call" | custom-call | flops 100000000 | bytes 16384 | tf_op jit(solution)/shard_map/pallas_call | solution.py:468
  11.3 1.4 %collective-permute-done.lists = f32[32,128]{1,0:T(8,128)S(1)} collective-permute-done((f32[32,128]{1,0:T(8,128)S(1)}, f32[32,128]{1,0:T(8,128)S(1)}, u32[]{:S(2)}, u32[]{:S(2)}) %collective-permute-start) | collective-permute-done | bytes 16416 | tf_op jit(solution)/shard_map/ppermute | solution.py:509
  12.7 0.6 %shard_map.66.refs_1_ = f32[8,64,128]{2,1,0:T(8,128)S(1)} custom-call(f32[32,128]{1,0:T(8,128)S(1)} %collective-permute-done.lists), custom_call_target="tpu_custom_call" | custom-call | flops 100000000 | bytes 16384 | tf_op jit(solution)/shard_map/pallas_call | solution.py:468
  13.2 5.0 %all-to-all-done = f32[32,11,1,128]{3,2,1,0:T(1,128)S(1)} async-done(((f32[32,11,1,128]{3,2,1,0:T(1,128)}), f32[32,11,1,128]{3,2,1,0:T(1,128)S(1)}, u32[]{:S(2)}, u32[]{:S(2)}) %all-to-all-start) | async-done | bytes 180256 | tf_op jit(solution)/shard_map/all_to_all | solution.py:39
  18.3 1.6 %shard_map.67 = (bf16[2048,512]{1,0:T(8,128)(2,1)S(1)}, f32[16,4,128]{2,1,0:T(4,128)S(1)}, f32[16,3,8,128]{3,2,1,0:T(8,128)S(1)}, f32[3,8,128]{2,1,0:T(8,128)S(1...) custom-call(f32[352,128]{1,0:T(8,128)S(1)} %bitcast.14, f32[8,64,128]{2,1,0:T(8,128)S(1)} %shard_map.65.refs_0_, ...), custom_call_target="tpu_custom_call" | custom-call | bytes 708608 | tf_op jit(solution)/shard_map/pallas_call | solution.py:468
  19.8 10.6 %all_to_all.20 = f32[32,9,1,128]{3,2,1,0:T(1,128)S(1)} all-to-all(f32[32,9,1,128]{3,2,1,0:T(1,128)S(1)} %bitcast.17), channel_id=1, replica_groups=mesh['top'=4,'mid'=2,'core'=2,'col'=2] {'top','mid','core','col'}, dimensions={0} | all-to-all | bytes 294912 | tf_op jit(solution)/shard_map/all_to_all | solution.py:39
  30.4 0.7 %shard_map.68 = (f32[16,3,8,128]{3,2,1,0:T(8,128)S(1)}, f32[3,8,128]{2,1,0:T(8,128)S(1)}, f32[3,8,128]{2,1,0:T(8,128)S(1)}, f32[288,128]{1,0:T(8,128)S(1)}) custom-call(f32[288,128]{1,0:T(8,128)S(1)} %bitcast.15, f32[16,3,8,128]{3,2,1,0:T(8,128)S(1)} %get-tuple-element.25.refs_0_, f32[2,8,128]{2,1,0:T(8,128)S(1)} %get-tuple-element.26.refs_1_.refs_2_, ...), custom_call_target="tpu_custom_call" | custom-call | bytes 2498560 | tf_op jit(solution)/shard_map/pallas_call | solution.py:468
  31.1 10.6 %all_to_all.21 = f32[32,9,1,128]{3,2,1,0:T(1,128)S(1)} all-to-all(f32[32,9,1,128]{3,2,1,0:T(1,128)S(1)} %bitcast.18), channel_id=1, replica_groups=mesh['top'=4,'mid'=2,'core'=2,'col'=2] {'top','mid','core','col'}, dimensions={0} | all-to-all | bytes 294912 | tf_op jit(solution)/shard_map/all_to_all | solution.py:39
  41.7 0.8 %shard_map.69 = (f32[3,3,8,128]{3,2,1,0:T(8,128)S(1)}, f32[13,8,128]{2,1,0:T(8,128)S(1)}, f32[32,128]{1,0:T(8,128)S(1)}) custom-call(f32[288,128]{1,0:T(8,128)S(1)} %bitcast.16, f32[16,3,8,128]{3,2,1,0:T(8,128)S(1)} %get-tuple-element.25.refs_0_, f32[16,3,8,128]{3,2,1,0:T(8,128)S(1)} %get-tuple-element.31.refs_1_, ...), custom_call_target="tpu_custom_call" | custom-call | bytes 2719744 | tf_op jit(solution)/shard_map/pallas_call | solution.py:468
  42.5 8.9 %all_to_all.22 = f32[32,1,1,128]{3,2,1,0:T(1,128)S(1)} all-to-all(f32[32,1,1,128]{3,2,1,0:T(1,128)S(1)} %bitcast.20), channel_id=1, replica_groups=mesh['top'=4,'mid'=2,'core'=2,'col'=2] {'top','mid','core','col'}, dimensions={0} | all-to-all | bytes 32768 | tf_op jit(solution)/shard_map/all_to_all | solution.py:39
  51.4 0.7 %shard_map.70 = f32[6,3,64]{2,1,0:T(4,128)} custom-call(f32[32,128]{1,0:T(8,128)S(1)} %bitcast.19, f32[3,3,8,128]{3,2,1,0:T(8,128)S(1)} %get-tuple-element.35.own, f32[13,8,128]{2,1,0:T(8,128)S(1)} %get-tuple-element.36.held), custom_call_target="tpu_custom_call" | custom-call | bytes 106496 | tf_op jit(solution)/shard_map/pallas_call | solution.py:468
Async XLA Ops:
  1.5 16.7 %all-to-all-start = ((f32[32,11,1,128]{3,2,1,0:T(1,128)}), f32[32,11,1,128]{3,2,1,0:T(1,128)S(1)}, u32[]{:S(2)}, u32[]{:S(2)}) async-start(f32[32,11,1,128]{3,2,1,0:T(1,128)} %bitcast.4), calls=%async_computation | async-start | bytes 360448 | tf_op jit(solution)/shard_map/all_to_all | solution.py:39
  8.9 3.8 %collective-permute-start = (f32[32,128]{1,0:T(8,128)S(1)}, f32[32,128]{1,0:T(8,128)S(1)}, u32[]{:S(2)}, u32[]{:S(2)}) collective-permute-start(f32[32,128]{1,0:T(8,128)S(1)} %get-tuple-element.22.lists), channel_id=1, source_target_pairs={{0,1},{1,0},{2,3},{3,2},{4,5},{5,4},{6,7},{7,6},{8,9},{9,8},{10,11... | collective-permute-start | bytes 49160 | tf_op jit(solution)/shard_map/ppermute | solution.py:509
